TPU v7x, 32 devices: a whole 2x2x4 slice. The times are simulated.
32 devices in a mesh: scan: 2 (over x), slab: 16 (over z, y, core).
Axes of the slice: x: 2, y: 2, z: 4, core: 2. Of those that a mesh axis runs over, the one named last changes fastest.
Arguments:
- volume: float32 [64, 64, 1024], P(('scan', 'slab')), parts along dimension 0, may hold values from 0.3 to 3
- measured: float32 [96, 8, 1024], P(('scan', 'slab')), parts along dimension 0, may hold values from 0.3 to 3
- view_angle: int32 [16], P('scan'), parts along dimension 0, may hold values from 0 to 179
- view_lift: int32 [16], P('scan'), parts along dimension 0, may hold values from -6 to 6, as said below
- subset: int32 [8], P('scan'), parts along dimension 0, may hold values from 0 to 7, as said below
Outputs:
- residual: float32 [96, 8, 1024], P(('scan', 'slab')), parts along dimension 0
- updated: float32 [64, 64, 1024], P(('scan', 'slab')), parts along dimension 0
There are 2 independent parts, one for each index of `scan`. A program takes and returns all parts, laid end to end along the dimension named above; each array names one. Nothing has to cross between parts.
Inputs may be any that keep to these rules, and one draw needn't show every extreme that they name: `view_lift`: in every scan some view has shift 6 and another has shift -6. `subset`: 4 different view numbers.
All inputs are finite; a program needn't handle non-finite values.
Results may differ from a plain program's by a relative error of at most 0.0003.
Values sent between devices are 32-bit elements; how exact they have to be, the bound alone decides.
No kernel may reach another device: no remote copies, remote signals or barrier semaphores. Data moves between devices by JAX's collectives and lax.ppermute only.
A program may use at most 64 MiB of HBM per device.

v0:
```python
import math

import jax
import jax.numpy as jnp
from jax import lax
from jax.sharding import PartitionSpec as P

ANGLES = 180


PITCH = 0.9
MAG_BASE = 1.5
ECCENTRIC = 0.12
LEN_FLOOR = 0.25


def passed_along(block, axis, distance):
    devices = range(lax.axis_size(axis))
    route = [(i - distance, i) for i in devices if i - distance in devices]
    return lax.ppermute(block, axis, route)


def view_geometry(angle_index, height):
    radians = (angle_index.astype(jnp.float32) + 0.5) * (0.5 * math.pi / ANGLES) - 0.25 * math.pi
    cosine = jnp.cos(radians)
    tangent = jnp.tan(radians)
    magnify = MAG_BASE / (1.0 - ECCENTRIC * jnp.sin(2.0 * radians + 1.0))
    return (cosine, tangent, magnify, height.astype(jnp.float32))


def cone_weights(row_index, slice_index, magnify, height, rows_total, slices_total):
    sample = (
        (row_index[None, :] + 0.5 - rows_total / 2 - height[:, None]) / magnify[:, None]
        + slices_total / 2
        - 0.5
    )
    return jnp.maximum(0.0, 1.0 - jnp.abs(sample[:, :, None] - slice_index[None, None, :]))


def column_weights(cosine, column_count, cell_count):
    center = (
        (jnp.arange(column_count, dtype=jnp.float32) + 0.5 - column_count / 2)
        * (PITCH * cell_count / column_count)
        / cosine
        + cell_count / 2
        - 0.5
    )
    position = jnp.arange(cell_count, dtype=jnp.float32)
    return jnp.maximum(0.0, 1.0 - jnp.abs(position[None, :] - center[:, None]))


def shift_rows(padded, amounts, bit_count):
    current = padded
    width_all = padded.shape[-1]
    for bit_place in range(bit_count):
        stride = 1 << bit_place
        filler = jnp.zeros(current.shape[:-1] + (stride,), current.dtype)
        advanced = jnp.concatenate([current[..., stride:], filler], axis=-1)
        chosen_bit = jnp.bitwise_and(jnp.right_shift(amounts, bit_place), 1) == 1
        current = jnp.where(chosen_bit[:, None], advanced, current)
    return current


def shear_forward(field, tangent):
    row_count, cell_count = (field.shape[-2], field.shape[-1])
    offset = (jnp.arange(row_count, dtype=jnp.float32) + 0.5 - row_count / 2) * tangent
    step_whole = jnp.floor(offset)
    fraction = offset - step_whole
    margin = row_count // 2 + 2
    padded = jnp.pad(field, [(0, 0)] * (field.ndim - 1) + [(margin, margin)])
    amounts = step_whole.astype(jnp.int32) + margin
    shifted = shift_rows(padded, amounts, (row_count + 2).bit_length())
    lower_tap = shifted[..., :cell_count]
    upper_tap = shifted[..., 1 : cell_count + 1]
    return (1.0 - fraction)[:, None] * lower_tap + fraction[:, None] * upper_tap


def shear_adjoint(profile, tangent, row_count):
    cell_count = profile.shape[-1]
    offset = (jnp.arange(row_count, dtype=jnp.float32) + 0.5 - row_count / 2) * tangent
    step_whole = jnp.floor(offset)
    fraction = offset - step_whole
    margin = row_count // 2 + 2
    padded = jnp.pad(profile, [(0, 0)] * (profile.ndim - 1) + [(margin, margin)])
    spread_rows = jnp.broadcast_to(
        padded[..., None, :], padded.shape[:-1] + (row_count, padded.shape[-1])
    )
    amounts = margin - step_whole.astype(jnp.int32) - 1
    shifted = shift_rows(spread_rows, amounts, (row_count + 2).bit_length())
    lower_tap = shifted[..., 1 : cell_count + 1]
    upper_tap = shifted[..., :cell_count]
    return (1.0 - fraction)[:, None] * lower_tap + fraction[:, None] * upper_tap


def per_device(volume, measured, view_angle, view_lift, subset):
    highest = lax.Precision.HIGHEST
    slab_count = lax.axis_size("slab")
    slab_index = lax.axis_index("slab")
    slab_depth, row_count, cell_count = volume.shape
    row_share, view_count, column_count = measured.shape
    subset_count = subset.shape[0]
    total_rows = row_share * slab_count
    total_slices = slab_depth * slab_count
    reach_max = 3 * slab_count // 20 + 4
    cosine, tangent, magnify, height = view_geometry(view_angle, view_lift)
    own_slices = (slab_index * slab_depth + jnp.arange(slab_depth, dtype=jnp.int32)).astype(
        jnp.float32
    )
    own_rows = (slab_index * row_share + jnp.arange(row_share, dtype=jnp.int32)).astype(jnp.float32)
    unit_field = jnp.ones((row_count, cell_count), jnp.float32)

    def one_view(packed):
        cosine_one, tangent_one = packed
        factor = 1.0 / (row_count * cosine_one)
        collapsed = jnp.sum(shear_forward(volume, tangent_one), axis=1) * factor
        column_map = column_weights(cosine_one, column_count, cell_count)
        profile = jnp.dot(collapsed, column_map.T, precision=highest)
        coverage_in = jnp.sum(shear_forward(unit_field, tangent_one), axis=0) * factor
        coverage = jnp.dot(column_map, coverage_in, precision=highest)
        return (profile, coverage)

    profiles, coverage = lax.map(one_view, (cosine, tangent))

    def add_slices(running, received, row_start):
        amount = received.shape[1]
        slice_index = (row_start + jnp.arange(amount, dtype=jnp.int32)).astype(jnp.float32)
        cone_map = cone_weights(own_rows, slice_index, magnify, height, total_rows, total_slices)
        return running + jnp.einsum("vrz,vzu->rvu", cone_map, received, precision=highest)

    initial = jnp.zeros((row_share, view_count, column_count), jnp.float32)
    projection = add_slices(initial, profiles, slab_index * slab_depth)
    for offset in range(-reach_max, reach_max + 1):
        if offset != 0:
            incoming = passed_along(profiles, "slab", offset)
            projection = add_slices(projection, incoming, (slab_index - offset) * slab_depth)
    all_slices = jnp.arange(total_slices, dtype=jnp.float32)
    row_cone = cone_weights(own_rows, all_slices, magnify, height, total_rows, total_slices)
    row_total = jnp.sum(row_cone, axis=2)
    ray_length = jnp.transpose(row_total)[:, :, None] * coverage[None, :, :]
    residual = (measured - projection) / jnp.maximum(ray_length, LEN_FLOOR)
    selector = subset[:, None] == jnp.arange(view_count, dtype=jnp.int32)[None, :]
    chosen = jnp.einsum("rvu,kv->rku", residual, selector.astype(jnp.float32), precision=highest)
    cosine_sub = jnp.sum(jnp.where(selector, cosine[None, :], 0.0), axis=1)
    tangent_sub = jnp.sum(jnp.where(selector, tangent[None, :], 0.0), axis=1)
    magnify_sub = jnp.sum(jnp.where(selector, magnify[None, :], 0.0), axis=1)
    height_sub = jnp.sum(jnp.where(selector, height[None, :], 0.0), axis=1)

    def add_rows(running, received, row_start):
        amount = received.shape[0]
        row_index = (row_start + jnp.arange(amount, dtype=jnp.int32)).astype(jnp.float32)
        cone_map = cone_weights(
            row_index, own_slices, magnify_sub, height_sub, total_rows, total_slices
        )
        return running + jnp.einsum("krz,rku->kzu", cone_map, received, precision=highest)

    initial_back = jnp.zeros((subset_count, slab_depth, column_count), jnp.float32)
    spread = add_rows(initial_back, chosen, slab_index * row_share)
    for offset in range(-reach_max, reach_max + 1):
        if offset != 0:
            incoming_rows = passed_along(chosen, "slab", offset)
            spread = add_rows(spread, incoming_rows, (slab_index - offset) * row_share)
    all_rows = jnp.arange(total_rows, dtype=jnp.float32)
    column_cone = cone_weights(
        all_rows, own_slices, magnify_sub, height_sub, total_rows, total_slices
    )
    slice_total = jnp.sum(column_cone, axis=1)
    accumulated = jnp.zeros(volume.shape, jnp.float32)
    weight = jnp.zeros(volume.shape, jnp.float32)
    for member in range(subset_count):
        factor = 1.0 / (row_count * cosine_sub[member])
        column_map = column_weights(cosine_sub[member], column_count, cell_count)
        profile = jnp.dot(spread[member], column_map, precision=highest) * factor
        accumulated = accumulated + shear_adjoint(profile, tangent_sub[member], row_count)
        edge_line = jnp.sum(column_map, axis=0) * factor
        weight = (
            weight
            + slice_total[member][:, None, None]
            * shear_adjoint(edge_line, tangent_sub[member], row_count)[None]
        )
    updated = volume + accumulated / jnp.maximum(weight, LEN_FLOOR * subset_count / row_count)
    return (residual, updated)


def solution(mesh):
    in_specs = (
        P(("scan", "slab"), None, None),
        P(("scan", "slab"), None, None),
        P("scan"),
        P("scan"),
        P("scan"),
    )
    out_specs = (P(("scan", "slab"), None, None), P(("scan", "slab"), None, None))
    return jax.shard_map(
        per_device, mesh=mesh, in_specs=in_specs, out_specs=out_specs, check_vma=False
    )
```

profile of v0, /device:TPU:17, one launch (start us, length us, event | category | flops | bytes accessed | tf_op | source)
XLA Modules:
  0.0 321.2 jit_solution(1031020605554507242)
XLA Ops:
  1.4 160.4 %while.16 = (s32[]{:T(128)}, f32[8,2,1024]{2,1,0:T(2,128)S(1)}, f32[8,1024]{1,0:T(8,128)S(1)}, f32[8]{0:T(128)S(1)}, f32[2,64,1024]{2,1,0:T(8,128)}, /*index=5*/...) while((s32[]{:T(128)}, f32[8,2,1024]{2,1,0:T(2,128)S(1)}, ...), condition=%wide.region_3.4_spmd, body=%wide.region_0.3_spmd.sunk | while | flops 48608132 | bytes 31388556 | solution.py:122
  11.4 3.8 %fusion.423 = f32[8,2,1024]{2,1,0:T(2,128)S(1)} fusion(f32[8,2,1024]{2,1,0:T(2,128)S(1)} %get-tuple-element.271, s32[]{:T(128)S(6)} %copy.91, f32[1024]{0:T(1024)S(1)} %divide_add_fusion.21, f32[2,1024]{1,0:T(2,128)S(1)} %fusion.422, f32[]{:T(128)S(6)} %div.377), kind=kOutput, calls=%fused_computation.10.clone.1 | convolution fusion | flops 29362176 | bytes 20488 | tf_op jit(solution)/shard_map/while/body/eval_jaxpr/dot_general | solution.py:117
  17.2 4.2 %fusion.425 = f32[1,1024]{1,0:T(1,128)S(1)} fusion(f32[1024,1]{0,1:T(1,128)S(1)} %bitcast.65, f32[1024]{0:T(1024)S(1)} %divide_add_fusion.21), kind=kOutput, calls=%fused_computation.1.clone.1 | convolution fusion | flops 16777216 | bytes 12288 | tf_op jit(solution)/shard_map/while/body/eval_jaxpr/dot_general | solution.py:119
  31.4 3.8 %fusion.423 = f32[8,2,1024]{2,1,0:T(2,128)S(1)} fusion(f32[8,2,1024]{2,1,0:T(2,128)S(1)} %get-tuple-element.271, s32[]{:T(128)S(6)} %copy.91, f32[1024]{0:T(1024)S(1)} %divide_add_fusion.21, f32[2,1024]{1,0:T(2,128)S(1)} %fusion.422, f32[]{:T(128)S(6)} %div.377), kind=kOutput, calls=%fused_computation.10.clone.1 | convolution fusion | flops 29362176 | bytes 20488 | tf_op jit(solution)/shard_map/while/body/eval_jaxpr/dot_general | solution.py:117
  37.2 4.2 %fusion.425 = f32[1,1024]{1,0:T(1,128)S(1)} fusion(f32[1024,1]{0,1:T(1,128)S(1)} %bitcast.65, f32[1024]{0:T(1024)S(1)} %divide_add_fusion.21), kind=kOutput, calls=%fused_computation.1.clone.1 | convolution fusion | flops 16777216 | bytes 12288 | tf_op jit(solution)/shard_map/while/body/eval_jaxpr/dot_general | solution.py:119
  51.5 3.8 %fusion.423 = f32[8,2,1024]{2,1,0:T(2,128)S(1)} fusion(f32[8,2,1024]{2,1,0:T(2,128)S(1)} %get-tuple-element.271, s32[]{:T(128)S(6)} %copy.91, f32[1024]{0:T(1024)S(1)} %divide_add_fusion.21, f32[2,1024]{1,0:T(2,128)S(1)} %fusion.422, f32[]{:T(128)S(6)} %div.377), kind=kOutput, calls=%fused_computation.10.clone.1 | convolution fusion | flops 29362176 | bytes 20488 | tf_op jit(solution)/shard_map/while/body/eval_jaxpr/dot_general | solution.py:117
  57.3 4.2 %fusion.425 = f32[1,1024]{1,0:T(1,128)S(1)} fusion(f32[1024,1]{0,1:T(1,128)S(1)} %bitcast.65, f32[1024]{0:T(1024)S(1)} %divide_add_fusion.21), kind=kOutput, calls=%fused_computation.1.clone.1 | convolution fusion | flops 16777216 | bytes 12288 | tf_op jit(solution)/shard_map/while/body/eval_jaxpr/dot_general | solution.py:119
  71.5 3.8 %fusion.423 = f32[8,2,1024]{2,1,0:T(2,128)S(1)} fusion(f32[8,2,1024]{2,1,0:T(2,128)S(1)} %get-tuple-element.271, s32[]{:T(128)S(6)} %copy.91, f32[1024]{0:T(1024)S(1)} %divide_add_fusion.21, f32[2,1024]{1,0:T(2,128)S(1)} %fusion.422, f32[]{:T(128)S(6)} %div.377), kind=kOutput, calls=%fused_computation.10.clone.1 | convolution fusion | flops 29362176 | bytes 20488 | tf_op jit(solution)/shard_map/while/body/eval_jaxpr/dot_general | solution.py:117
  77.3 4.2 %fusion.425 = f32[1,1024]{1,0:T(1,128)S(1)} fusion(f32[1024,1]{0,1:T(1,128)S(1)} %bitcast.65, f32[1024]{0:T(1024)S(1)} %divide_add_fusion.21), kind=kOutput, calls=%fused_computation.1.clone.1 | convolution fusion | flops 16777216 | bytes 12288 | tf_op jit(solution)/shard_map/while/body/eval_jaxpr/dot_general | solution.py:119
  91.6 3.8 %fusion.423 = f32[8,2,1024]{2,1,0:T(2,128)S(1)} fusion(f32[8,2,1024]{2,1,0:T(2,128)S(1)} %get-tuple-element.271, s32[]{:T(128)S(6)} %copy.91, f32[1024]{0:T(1024)S(1)} %divide_add_fusion.21, f32[2,1024]{1,0:T(2,128)S(1)} %fusion.422, f32[]{:T(128)S(6)} %div.377), kind=kOutput, calls=%fused_computation.10.clone.1 | convolution fusion | flops 29362176 | bytes 20488 | tf_op jit(solution)/shard_map/while/body/eval_jaxpr/dot_general | solution.py:117
  97.4 4.2 %fusion.425 = f32[1,1024]{1,0:T(1,128)S(1)} fusion(f32[1024,1]{0,1:T(1,128)S(1)} %bitcast.65, f32[1024]{0:T(1024)S(1)} %divide_add_fusion.21), kind=kOutput, calls=%fused_computation.1.clone.1 | convolution fusion | flops 16777216 | bytes 12288 | tf_op jit(solution)/shard_map/while/body/eval_jaxpr/dot_general | solution.py:119
  111.6 3.8 %fusion.423 = f32[8,2,1024]{2,1,0:T(2,128)S(1)} fusion(f32[8,2,1024]{2,1,0:T(2,128)S(1)} %get-tuple-element.271, s32[]{:T(128)S(6)} %copy.91, f32[1024]{0:T(1024)S(1)} %divide_add_fusion.21, f32[2,1024]{1,0:T(2,128)S(1)} %fusion.422, f32[]{:T(128)S(6)} %div.377), kind=kOutput, calls=%fused_computation.10.clone.1 | convolution fusion | flops 29362176 | bytes 20488 | tf_op jit(solution)/shard_map/while/body/eval_jaxpr/dot_general | solution.py:117
  117.4 4.2 %fusion.425 = f32[1,1024]{1,0:T(1,128)S(1)} fusion(f32[1024,1]{0,1:T(1,128)S(1)} %bitcast.65, f32[1024]{0:T(1024)S(1)} %divide_add_fusion.21), kind=kOutput, calls=%fused_computation.1.clone.1 | convolution fusion | flops 16777216 | bytes 12288 | tf_op jit(solution)/shard_map/while/body/eval_jaxpr/dot_general | solution.py:119
  131.7 3.8 %fusion.423 = f32[8,2,1024]{2,1,0:T(2,128)S(1)} fusion(f32[8,2,1024]{2,1,0:T(2,128)S(1)} %get-tuple-element.271, s32[]{:T(128)S(6)} %copy.91, f32[1024]{0:T(1024)S(1)} %divide_add_fusion.21, f32[2,1024]{1,0:T(2,128)S(1)} %fusion.422, f32[]{:T(128)S(6)} %div.377), kind=kOutput, calls=%fused_computation.10.clone.1 | convolution fusion | flops 29362176 | bytes 20488 | tf_op jit(solution)/shard_map/while/body/eval_jaxpr/dot_general | solution.py:117
  137.4 4.2 %fusion.425 = f32[1,1024]{1,0:T(1,128)S(1)} fusion(f32[1024,1]{0,1:T(1,128)S(1)} %bitcast.65, f32[1024]{0:T(1024)S(1)} %divide_add_fusion.21), kind=kOutput, calls=%fused_computation.1.clone.1 | convolution fusion | flops 16777216 | bytes 12288 | tf_op jit(solution)/shard_map/while/body/eval_jaxpr/dot_general | solution.py:119
  151.7 3.8 %fusion.423 = f32[8,2,1024]{2,1,0:T(2,128)S(1)} fusion(f32[8,2,1024]{2,1,0:T(2,128)S(1)} %get-tuple-element.271, s32[]{:T(128)S(6)} %copy.91, f32[1024]{0:T(1024)S(1)} %divide_add_fusion.21, f32[2,1024]{1,0:T(2,128)S(1)} %fusion.422, f32[]{:T(128)S(6)} %div.377), kind=kOutput, calls=%fused_computation.10.clone.1 | convolution fusion | flops 29362176 | bytes 20488 | tf_op jit(solution)/shard_map/while/body/eval_jaxpr/dot_general | solution.py:117
  157.5 4.2 %fusion.425 = f32[1,1024]{1,0:T(1,128)S(1)} fusion(f32[1024,1]{0,1:T(1,128)S(1)} %bitcast.65, f32[1024]{0:T(1024)S(1)} %divide_add_fusion.21), kind=kOutput, calls=%fused_computation.1.clone.1 | convolution fusion | flops 16777216 | bytes 12288 | tf_op jit(solution)/shard_map/while/body/eval_jaxpr/dot_general | solution.py:119
  161.8 4.2 %collective-permute-start.11 = (f32[8,2,1024]{2,1,0:T(2,128)S(1)}, f32[8,2,1024]{2,1,0:T(2,128)S(1)}, u32[]{:S(2)}, u32[]{:S(2)}) collective-permute-start(f32[8,2,1024]{2,1,0:T(2,128)S(1)} %get-tuple-element.130), channel_id=1, source_target_pairs={{0,6},{1,7},{2,8},{3,9},{4,10},{5,11},{6,12},{7,13},{8,14},{9,15},... | collective-permute-start | bytes 196616 | tf_op jit(solution)/shard_map/ppermute | solution.py:20
  171.7 5.6 %collective-permute-start = (f32[8,2,1024]{2,1,0:T(2,128)S(1)}, f32[8,2,1024]{2,1,0:T(2,128)S(1)}, u32[]{:S(2)}, u32[]{:S(2)}) collective-permute-start(f32[8,2,1024]{2,1,0:T(2,128)S(1)} %get-tuple-element.130), channel_id=1, source_target_pairs={{6,0},{7,1},{8,2},{9,3},{10,4},{11,5},{12,6},{13,7},{14,8},{15,9},... | collective-permute-start | bytes 196616 | tf_op jit(solution)/shard_map/ppermute | solution.py:20
  221.9 4.0 %collective-permute-start.6 = (f32[8,2,1024]{2,1,0:T(2,128)S(1)}, f32[8,2,1024]{2,1,0:T(2,128)S(1)}, u32[]{:S(2)}, u32[]{:S(2)}) collective-permute-start(f32[8,2,1024]{2,1,0:T(2,128)S(1)} %get-tuple-element.130), channel_id=1, source_target_pairs={{0,1},{1,2},{2,3},{3,4},{4,5},{5,6},{6,7},{7,8},{8,9},{9,10},{10,1... | collective-permute-start | bytes 196616 | tf_op jit(solution)/shard_map/ppermute | solution.py:20
  228.9 3.2 collective-permute-start.4
  232.6 5.2 %collective-permute-start.3 = (f32[8,2,1024]{2,1,0:T(2,128)S(1)}, f32[8,2,1024]{2,1,0:T(2,128)S(1)}, u32[]{:S(2)}, u32[]{:S(2)}) collective-permute-start(f32[8,2,1024]{2,1,0:T(2,128)S(1)} %get-tuple-element.130), channel_id=1, source_target_pairs={{3,0},{4,1},{5,2},{6,3},{7,4},{8,5},{9,6},{10,7},{11,8},{12,9},{13... | collective-permute-start | bytes 196616 | tf_op jit(solution)/shard_map/ppermute | solution.py:20
  245.3 2.1 collective-permute-done.1
  256.1 5.4 %collective-permute-start.12 = (f32[3,4,1024]{2,1,0:T(4,128)S(1)}, f32[3,4,1024]{2,1,0:T(4,128)S(1)}, u32[]{:S(2)}, u32[]{:S(2)}) collective-permute-start(f32[3,4,1024]{2,1,0:T(4,128)S(1)} %convolution_bitcast_fusion), channel_id=1, source_target_pairs={{6,0},{7,1},{8,2},{9,3},{10,4},{11,5},{12,6},{13,7},{14,8},{15,9},... | collective-permute-start | bytes 147464 | tf_op jit(solution)/shard_map/ppermute | solution.py:20
  264.9 4.5 %collective-permute-start.18 = (f32[3,4,1024]{2,1,0:T(4,128)S(1)}, f32[3,4,1024]{2,1,0:T(4,128)S(1)}, u32[]{:S(2)}, u32[]{:S(2)}) collective-permute-start(f32[3,4,1024]{2,1,0:T(4,128)S(1)} %convolution_bitcast_fusion), channel_id=1, source_target_pairs={{0,1},{1,2},{2,3},{3,4},{4,5},{5,6},{6,7},{7,8},{8,9},{9,10},{10,1... | collective-permute-start | bytes 147464 | tf_op jit(solution)/shard_map/ppermute | solution.py:20
  272.1 3.3 %collective-permute-start.16 = (f32[3,4,1024]{2,1,0:T(4,128)S(1)}, f32[3,4,1024]{2,1,0:T(4,128)S(1)}, u32[]{:S(2)}, u32[]{:S(2)}) collective-permute-start(f32[3,4,1024]{2,1,0:T(4,128)S(1)} %convolution_bitcast_fusion), channel_id=1, source_target_pairs={{2,0},{3,1},{4,2},{5,3},{6,4},{7,5},{8,6},{9,7},{10,8},{11,9},{12,... | collective-permute-start | bytes 147464 | tf_op jit(solution)/shard_map/ppermute | solution.py:20
  275.7 6.4 %collective-permute-start.15 = (f32[3,4,1024]{2,1,0:T(4,128)S(1)}, f32[3,4,1024]{2,1,0:T(4,128)S(1)}, u32[]{:S(2)}, u32[]{:S(2)}) collective-permute-start(f32[3,4,1024]{2,1,0:T(4,128)S(1)} %convolution_bitcast_fusion), channel_id=1, source_target_pairs={{3,0},{4,1},{5,2},{6,3},{7,4},{8,5},{9,6},{10,7},{11,8},{12,9},{13... | collective-permute-start | bytes 147464 | tf_op jit(solution)/shard_map/ppermute | solution.py:20
  284.7 10.7 %collective-permute-start.13 = (f32[3,4,1024]{2,1,0:T(4,128)S(1)}, f32[3,4,1024]{2,1,0:T(4,128)S(1)}, u32[]{:S(2)}, u32[]{:S(2)}) collective-permute-start(f32[3,4,1024]{2,1,0:T(4,128)S(1)} %convolution_bitcast_fusion), channel_id=1, source_target_pairs={{5,0},{6,1},{7,2},{8,3},{9,4},{10,5},{11,6},{12,7},{13,8},{14,9},{... | collective-permute-start | bytes 147464 | tf_op jit(solution)/shard_map/ppermute | solution.py:20
  297.5 2.7 fusion.67
  300.3 2.7 fusion.66
  303.2 2.7 fusion.65
  306.0 2.7 fusion.64
  (651 shorter events, 180.0 us)
Async XLA Ops:
  1.4 176.0 %copy-start.5 = (s32[8]{0:T(128)S(1)}, s32[8]{0:T(128)}, u32[]{:S(2)}) copy-start(s32[8]{0:T(128)} %param.10) | copy-start | bytes 100
  1.4 176.4 %copy-start.3 = (s32[4]{0:T(128)S(1)}, s32[4]{0:T(128)}, u32[]{:S(2)}) copy-start(s32[4]{0:T(128)} %param.11) | copy-start | bytes 52
  1.4 3.9 %copy-start = (f32[2,64,1024]{2,1,0:T(8,128)S(1)}, f32[2,64,1024]{2,1,0:T(8,128)}, u32[]{:S(2)}) copy-start(f32[2,64,1024]{2,1,0:T(8,128)} %get-tuple-element.285) | copy-start | bytes 1572868 | tf_op jit(solution)/shard_map/while
  21.4 3.9 %copy-start = (f32[2,64,1024]{2,1,0:T(8,128)S(1)}, f32[2,64,1024]{2,1,0:T(8,128)}, u32[]{:S(2)}) copy-start(f32[2,64,1024]{2,1,0:T(8,128)} %get-tuple-element.285) | copy-start | bytes 1572868 | tf_op jit(solution)/shard_map/while
  41.5 3.9 %copy-start = (f32[2,64,1024]{2,1,0:T(8,128)S(1)}, f32[2,64,1024]{2,1,0:T(8,128)}, u32[]{:S(2)}) copy-start(f32[2,64,1024]{2,1,0:T(8,128)} %get-tuple-element.285) | copy-start | bytes 1572868 | tf_op jit(solution)/shard_map/while
  61.5 3.9 %copy-start = (f32[2,64,1024]{2,1,0:T(8,128)S(1)}, f32[2,64,1024]{2,1,0:T(8,128)}, u32[]{:S(2)}) copy-start(f32[2,64,1024]{2,1,0:T(8,128)} %get-tuple-element.285) | copy-start | bytes 1572868 | tf_op jit(solution)/shard_map/while
  161.8 60.2 %collective-permute-start.11 = (f32[8,2,1024]{2,1,0:T(2,128)S(1)}, f32[8,2,1024]{2,1,0:T(2,128)S(1)}, u32[]{:S(2)}, u32[]{:S(2)}) collective-permute-start(f32[8,2,1024]{2,1,0:T(2,128)S(1)} %get-tuple-element.130), channel_id=1, source_target_pairs={{0,6},{1,7},{2,8},{3,9},{4,10},{5,11},{6,12},{7,13},{8,14},{9,15},... | collective-permute-start | bytes 196616 | tf_op jit(solution)/shard_map/ppermute | solution.py:20
  165.9 60.5 %collective-permute-start.10 = (f32[8,2,1024]{2,1,0:T(2,128)S(1)}, f32[8,2,1024]{2,1,0:T(2,128)S(1)}, u32[]{:S(2)}, u32[]{:S(2)}) collective-permute-start(f32[8,2,1024]{2,1,0:T(2,128)S(1)} %get-tuple-element.130), channel_id=1, source_target_pairs={{0,5},{1,6},{2,7},{3,8},{4,9},{5,10},{6,11},{7,12},{8,13},{9,14},{... | collective-permute-start | bytes 196616 | tf_op jit(solution)/shard_map/ppermute | solution.py:20
  167.9 61.0 %collective-permute-start.9 = (f32[8,2,1024]{2,1,0:T(2,128)S(1)}, f32[8,2,1024]{2,1,0:T(2,128)S(1)}, u32[]{:S(2)}, u32[]{:S(2)}) collective-permute-start(f32[8,2,1024]{2,1,0:T(2,128)S(1)} %get-tuple-element.130), channel_id=1, source_target_pairs={{0,4},{1,5},{2,6},{3,7},{4,8},{5,9},{6,10},{7,11},{8,12},{9,13},{1... | collective-permute-start | bytes 196616 | tf_op jit(solution)/shard_map/ppermute | solution.py:20
  169.8 62.8 %collective-permute-start.8 = (f32[8,2,1024]{2,1,0:T(2,128)S(1)}, f32[8,2,1024]{2,1,0:T(2,128)S(1)}, u32[]{:S(2)}, u32[]{:S(2)}) collective-permute-start(f32[8,2,1024]{2,1,0:T(2,128)S(1)} %get-tuple-element.130), channel_id=1, source_target_pairs={{0,3},{1,4},{2,5},{3,6},{4,7},{5,8},{6,9},{7,10},{8,11},{9,12},{10... | collective-permute-start | bytes 196616 | tf_op jit(solution)/shard_map/ppermute | solution.py:20
  171.7 47.8 %collective-permute-start = (f32[8,2,1024]{2,1,0:T(2,128)S(1)}, f32[8,2,1024]{2,1,0:T(2,128)S(1)}, u32[]{:S(2)}, u32[]{:S(2)}) collective-permute-start(f32[8,2,1024]{2,1,0:T(2,128)S(1)} %get-tuple-element.130), channel_id=1, source_target_pairs={{6,0},{7,1},{8,2},{9,3},{10,4},{11,5},{12,6},{13,7},{14,8},{15,9},... | collective-permute-start | bytes 196616 | tf_op jit(solution)/shard_map/ppermute | solution.py:20
  219.5 18.8 %collective-permute-start.7 = (f32[8,2,1024]{2,1,0:T(2,128)S(1)}, f32[8,2,1024]{2,1,0:T(2,128)S(1)}, u32[]{:S(2)}, u32[]{:S(2)}) collective-permute-start(f32[8,2,1024]{2,1,0:T(2,128)S(1)} %get-tuple-element.130), channel_id=1, source_target_pairs={{0,2},{1,3},{2,4},{3,5},{4,6},{5,7},{6,8},{7,9},{8,10},{9,11},{10,... | collective-permute-start | bytes 196616 | tf_op jit(solution)/shard_map/ppermute | solution.py:20
  221.9 18.9 %collective-permute-start.6 = (f32[8,2,1024]{2,1,0:T(2,128)S(1)}, f32[8,2,1024]{2,1,0:T(2,128)S(1)}, u32[]{:S(2)}, u32[]{:S(2)}) collective-permute-start(f32[8,2,1024]{2,1,0:T(2,128)S(1)} %get-tuple-element.130), channel_id=1, source_target_pairs={{0,1},{1,2},{2,3},{3,4},{4,5},{5,6},{6,7},{7,8},{8,9},{9,10},{10,1... | collective-permute-start | bytes 196616 | tf_op jit(solution)/shard_map/ppermute | solution.py:20
  226.4 16.8 %collective-permute-start.5 = (f32[8,2,1024]{2,1,0:T(2,128)S(1)}, f32[8,2,1024]{2,1,0:T(2,128)S(1)}, u32[]{:S(2)}, u32[]{:S(2)}) collective-permute-start(f32[8,2,1024]{2,1,0:T(2,128)S(1)} %get-tuple-element.130), channel_id=1, source_target_pairs={{1,0},{2,1},{3,2},{4,3},{5,4},{6,5},{7,6},{8,7},{9,8},{10,9},{11,1... | collective-permute-start | bytes 196616 | tf_op jit(solution)/shard_map/ppermute | solution.py:20
  228.9 14.9 %collective-permute-start.4 = (f32[8,2,1024]{2,1,0:T(2,128)S(1)}, f32[8,2,1024]{2,1,0:T(2,128)S(1)}, u32[]{:S(2)}, u32[]{:S(2)}) collective-permute-start(f32[8,2,1024]{2,1,0:T(2,128)S(1)} %get-tuple-element.130), channel_id=1, source_target_pairs={{2,0},{3,1},{4,2},{5,3},{6,4},{7,5},{8,6},{9,7},{10,8},{11,9},{12,... | collective-permute-start | bytes 196616 | tf_op jit(solution)/shard_map/ppermute | solution.py:20
  232.6 11.7 %collective-permute-start.3 = (f32[8,2,1024]{2,1,0:T(2,128)S(1)}, f32[8,2,1024]{2,1,0:T(2,128)S(1)}, u32[]{:S(2)}, u32[]{:S(2)}) collective-permute-start(f32[8,2,1024]{2,1,0:T(2,128)S(1)} %get-tuple-element.130), channel_id=1, source_target_pairs={{3,0},{4,1},{5,2},{6,3},{7,4},{8,5},{9,6},{10,7},{11,8},{12,9},{13... | collective-permute-start | bytes 196616 | tf_op jit(solution)/shard_map/ppermute | solution.py:20
  238.3 9.1 %copy-start.4 = (f32[3,8,1024]{2,1,0:T(8,128)S(1)}, f32[3,8,1024]{2,1,0:T(8,128)}, u32[]{:S(2)}) copy-start(f32[3,8,1024]{2,1,0:T(8,128)} %param.8) | copy-start | bytes 294916
  238.3 6.5 %collective-permute-start.2 = (f32[8,2,1024]{2,1,0:T(2,128)S(1)}, f32[8,2,1024]{2,1,0:T(2,128)S(1)}, u32[]{:S(2)}, u32[]{:S(2)}) collective-permute-start(f32[8,2,1024]{2,1,0:T(2,128)S(1)} %get-tuple-element.130), channel_id=1, source_target_pairs={{4,0},{5,1},{6,2},{7,3},{8,4},{9,5},{10,6},{11,7},{12,8},{13,9},{1... | collective-permute-start | bytes 196616 | tf_op jit(solution)/shard_map/ppermute | solution.py:20
  240.9 6.5 %collective-permute-start.1 = (f32[8,2,1024]{2,1,0:T(2,128)S(1)}, f32[8,2,1024]{2,1,0:T(2,128)S(1)}, u32[]{:S(2)}, u32[]{:S(2)}) collective-permute-start(f32[8,2,1024]{2,1,0:T(2,128)S(1)} %get-tuple-element.130), channel_id=1, source_target_pairs={{5,0},{6,1},{7,2},{8,3},{9,4},{10,5},{11,6},{12,7},{13,8},{14,9},{... | collective-permute-start | bytes 196616 | tf_op jit(solution)/shard_map/ppermute | solution.py:20
  248.1 48.3 %copy-start.2 = (f32[3,8,1024]{2,1,0:T(8,128)}, f32[3,8,1024]{2,1,0:T(8,128)S(1)}, u32[]{:S(2)}) copy-start(f32[3,8,1024]{2,1,0:T(8,128)S(1)} %copy.58) | copy-start | bytes 294916
  248.4 16.5 %collective-permute-start.23 = (f32[3,4,1024]{2,1,0:T(4,128)S(1)}, f32[3,4,1024]{2,1,0:T(4,128)S(1)}, u32[]{:S(2)}, u32[]{:S(2)}) collective-permute-start(f32[3,4,1024]{2,1,0:T(4,128)S(1)} %convolution_bitcast_fusion), channel_id=1, source_target_pairs={{0,6},{1,7},{2,8},{3,9},{4,10},{5,11},{6,12},{7,13},{8,14},{9,15},... | collective-permute-start | bytes 147464 | tf_op jit(solution)/shard_map/ppermute | solution.py:20
  250.3 19.5 %collective-permute-start.22 = (f32[3,4,1024]{2,1,0:T(4,128)S(1)}, f32[3,4,1024]{2,1,0:T(4,128)S(1)}, u32[]{:S(2)}, u32[]{:S(2)}) collective-permute-start(f32[3,4,1024]{2,1,0:T(4,128)S(1)} %convolution_bitcast_fusion), channel_id=1, source_target_pairs={{0,5},{1,6},{2,7},{3,8},{4,9},{5,10},{6,11},{7,12},{8,13},{9,14},{... | collective-permute-start | bytes 147464 | tf_op jit(solution)/shard_map/ppermute | solution.py:20
  252.2 19.8 %collective-permute-start.21 = (f32[3,4,1024]{2,1,0:T(4,128)S(1)}, f32[3,4,1024]{2,1,0:T(4,128)S(1)}, u32[]{:S(2)}, u32[]{:S(2)}) collective-permute-start(f32[3,4,1024]{2,1,0:T(4,128)S(1)} %convolution_bitcast_fusion), channel_id=1, source_target_pairs={{0,4},{1,5},{2,6},{3,7},{4,8},{5,9},{6,10},{7,11},{8,12},{9,13},{1... | collective-permute-start | bytes 147464 | tf_op jit(solution)/shard_map/ppermute | solution.py:20
  254.2 21.6 %collective-permute-start.20 = (f32[3,4,1024]{2,1,0:T(4,128)S(1)}, f32[3,4,1024]{2,1,0:T(4,128)S(1)}, u32[]{:S(2)}, u32[]{:S(2)}) collective-permute-start(f32[3,4,1024]{2,1,0:T(4,128)S(1)} %convolution_bitcast_fusion), channel_id=1, source_target_pairs={{0,3},{1,4},{2,5},{3,6},{4,7},{5,8},{6,9},{7,10},{8,11},{9,12},{10... | collective-permute-start | bytes 147464 | tf_op jit(solution)/shard_map/ppermute | solution.py:20
  256.1 6.6 %collective-permute-start.12 = (f32[3,4,1024]{2,1,0:T(4,128)S(1)}, f32[3,4,1024]{2,1,0:T(4,128)S(1)}, u32[]{:S(2)}, u32[]{:S(2)}) collective-permute-start(f32[3,4,1024]{2,1,0:T(4,128)S(1)} %convolution_bitcast_fusion), channel_id=1, source_target_pairs={{6,0},{7,1},{8,2},{9,3},{10,4},{11,5},{12,6},{13,7},{14,8},{15,9},... | collective-permute-start | bytes 147464 | tf_op jit(solution)/shard_map/ppermute | solution.py:20
  262.7 19.8 %collective-permute-start.19 = (f32[3,4,1024]{2,1,0:T(4,128)S(1)}, f32[3,4,1024]{2,1,0:T(4,128)S(1)}, u32[]{:S(2)}, u32[]{:S(2)}) collective-permute-start(f32[3,4,1024]{2,1,0:T(4,128)S(1)} %convolution_bitcast_fusion), channel_id=1, source_target_pairs={{0,2},{1,3},{2,4},{3,5},{4,6},{5,7},{6,8},{7,9},{8,10},{9,11},{10,... | collective-permute-start | bytes 147464 | tf_op jit(solution)/shard_map/ppermute | solution.py:20
  264.9 19.8 %collective-permute-start.18 = (f32[3,4,1024]{2,1,0:T(4,128)S(1)}, f32[3,4,1024]{2,1,0:T(4,128)S(1)}, u32[]{:S(2)}, u32[]{:S(2)}) collective-permute-start(f32[3,4,1024]{2,1,0:T(4,128)S(1)} %convolution_bitcast_fusion), channel_id=1, source_target_pairs={{0,1},{1,2},{2,3},{3,4},{4,5},{5,6},{6,7},{7,8},{8,9},{9,10},{10,1... | collective-permute-start | bytes 147464 | tf_op jit(solution)/shard_map/ppermute | solution.py:20
  269.8 26.0 %collective-permute-start.17 = (f32[3,4,1024]{2,1,0:T(4,128)S(1)}, f32[3,4,1024]{2,1,0:T(4,128)S(1)}, u32[]{:S(2)}, u32[]{:S(2)}) collective-permute-start(f32[3,4,1024]{2,1,0:T(4,128)S(1)} %convolution_bitcast_fusion), channel_id=1, source_target_pairs={{1,0},{2,1},{3,2},{4,3},{5,4},{6,5},{7,6},{8,7},{9,8},{10,9},{11,1... | collective-permute-start | bytes 147464 | tf_op jit(solution)/shard_map/ppermute | solution.py:20
  272.1 24.0 %collective-permute-start.16 = (f32[3,4,1024]{2,1,0:T(4,128)S(1)}, f32[3,4,1024]{2,1,0:T(4,128)S(1)}, u32[]{:S(2)}, u32[]{:S(2)}) collective-permute-start(f32[3,4,1024]{2,1,0:T(4,128)S(1)} %convolution_bitcast_fusion), channel_id=1, source_target_pairs={{2,0},{3,1},{4,2},{5,3},{6,4},{7,5},{8,6},{9,7},{10,8},{11,9},{12,... | collective-permute-start | bytes 147464 | tf_op jit(solution)/shard_map/ppermute | solution.py:20
  275.7 20.7 %collective-permute-start.15 = (f32[3,4,1024]{2,1,0:T(4,128)S(1)}, f32[3,4,1024]{2,1,0:T(4,128)S(1)}, u32[]{:S(2)}, u32[]{:S(2)}) collective-permute-start(f32[3,4,1024]{2,1,0:T(4,128)S(1)} %convolution_bitcast_fusion), channel_id=1, source_target_pairs={{3,0},{4,1},{5,2},{6,3},{7,4},{8,5},{9,6},{10,7},{11,8},{12,9},{13... | collective-permute-start | bytes 147464 | tf_op jit(solution)/shard_map/ppermute | solution.py:20
  282.5 14.3 %collective-permute-start.14 = (f32[3,4,1024]{2,1,0:T(4,128)S(1)}, f32[3,4,1024]{2,1,0:T(4,128)S(1)}, u32[]{:S(2)}, u32[]{:S(2)}) collective-permute-start(f32[3,4,1024]{2,1,0:T(4,128)S(1)} %convolution_bitcast_fusion), channel_id=1, source_target_pairs={{4,0},{5,1},{6,2},{7,3},{8,4},{9,5},{10,6},{11,7},{12,8},{13,9},{1... | collective-permute-start | bytes 147464 | tf_op jit(solution)/shard_map/ppermute | solution.py:20
  284.7 12.4 %collective-permute-start.13 = (f32[3,4,1024]{2,1,0:T(4,128)S(1)}, f32[3,4,1024]{2,1,0:T(4,128)S(1)}, u32[]{:S(2)}, u32[]{:S(2)}) collective-permute-start(f32[3,4,1024]{2,1,0:T(4,128)S(1)} %convolution_bitcast_fusion), channel_id=1, source_target_pairs={{5,0},{6,1},{7,2},{8,3},{9,4},{10,5},{11,6},{12,7},{13,8},{14,9},{... | collective-permute-start | bytes 147464 | tf_op jit(solution)/shard_map/ppermute | solution.py:20
  (5 other events, 16.6 us)
where the time goes:
time: 327 us; the launch traced here: 321 us
  other arithmetic  89.9 us (27%)
  matrix products  85.3 us (26%)
  starting transfers between devices  79.5 us (24%)
  local copies, waits for them, and re-layouts  51.1 us (16%)
  loops' own time  7.27 us (2%)
  between operations  5.19 us (2%)
    ppermute x24, starting transfers between devices, passed_along(): return lax.ppermute(block, axis, route)  79.5 us
    eq x60, other arithmetic, shift_rows(): chosen_bit = jnp.bitwise_and(jnp.right_shift(amounts, bit_place), 1) == 1  41 us
    slice x168, local copies, waits for them, and re-layouts, shift_rows(): advanced = jnp.concatenate([current[..., stride:], filler], axis=-1)  36.6 us
    dot_general x8, matrix products, one_view(): coverage = jnp.dot(column_map, coverage_in, precision=highest)  33.2 us
    dot_general x8, matrix products, one_view(): profile = jnp.dot(collapsed, column_map.T, precision=highest)  30.4 us
    select_n x168, other arithmetic, shift_rows(): current = jnp.where(chosen_bit[:, None], advanced, current)  20.4 us
    dot_general x4, matrix products, per_device(): profile = jnp.dot(spread[member], column_map, precision=highest) * factor  10.7 us
    dynamic_slice x16, local copies, waits for them, and re-layouts, per_device(): profiles, coverage = lax.map(one_view, (cosine, tangent))  10 us
  transfers between devices with their start and end apart: 24, of which 2 were waited for; matrix products, arithmetic and copies ran while one was open for 15% of the time, Pallas kernels for 0%

commit v1 on v0

v1 whole, which is shorter than its diff:
```python
import functools
import math

import jax
import jax.numpy as jnp
import numpy as np
from jax import lax
from jax.experimental import pallas as pl
from jax.experimental.pallas import tpu as pltpu
from jax.sharding import PartitionSpec as P

ANGLES = 180
LIFT = 6
PITCH = 0.9
MAG_BASE = 1.5
ECCENTRIC = 0.12
LEN_FLOOR = 0.25
LANES = 128
SUBLANES = 8
F32 = jnp.float32


def angle_table():
    radians = (np.arange(ANGLES) + 0.5) * (0.5 * math.pi / ANGLES) - 0.25 * math.pi
    magnify = MAG_BASE / (1.0 - ECCENTRIC * np.sin(2.0 * radians + 1.0))
    return np.cos(radians), magnify


def slab_reach(slab_count, slab_depth, row_share):
    _, magnify = angle_table()
    total_rows, total_slices = row_share * slab_count, slab_depth * slab_count
    rows = np.arange(total_rows)
    reach = 0
    for lift in range(-LIFT, LIFT + 1):
        sample = (rows[None] + 0.5 - total_rows / 2 - lift) / magnify[:, None] + total_slices / 2 - 0.5
        for tap in (np.floor(sample - 1e-3), np.floor(sample + 1e-3) + 1):
            inside = (tap >= 0) & (tap < total_slices)
            distance = np.abs(tap // slab_depth - rows[None] // row_share)
            reach = max(reach, int(distance[inside].max()))
    return reach


def lane_index():
    return lax.broadcasted_iota(jnp.int32, (SUBLANES, LANES), 1)


def sublane_index():
    return lax.broadcasted_iota(jnp.int32, (SUBLANES, LANES), 0)


def angle_facts(index):
    x = (index.astype(F32) + 0.5) * (0.5 * math.pi / ANGLES) - 0.25 * math.pi
    s = x * x
    sine = x * (1.0 + s * (-1 / 6 + s * (1 / 120 + s * (-1 / 5040 + s * (1 / 362880)))))
    cosine = 1.0 + s * (-1 / 2 + s * (1 / 24 + s * (-1 / 720 + s * (1 / 40320 + s * (-1 / 3628800)))))
    double = 2.0 * sine * cosine * math.cos(1.0) + (1.0 - 2.0 * sine * sine) * math.sin(1.0)
    return cosine, sine / cosine, (1.0 - ECCENTRIC * double) * (1.0 / MAG_BASE)


def spread_scalars(read, count, place):
    out = jnp.full((SUBLANES, LANES), read(0), jnp.int32)
    for item in range(1, count):
        out = jnp.where(place == item, read(item), out)
    return out


def pick(tile, index):
    return jnp.take_along_axis(tile, index, axis=1, mode="promise_in_bounds")


def next_lane(tile, following):
    lane = lane_index()
    return jnp.where(lane < LANES - 1, pltpu.roll(tile, LANES - 1, 1), pltpu.roll(following, LANES - 1, 1))


def rows_summed(parts):
    sub = sublane_index()
    step = SUBLANES // 2
    while step:
        low = jnp.bitwise_and(sub, step) == 0
        half = len(parts) // 2
        parts = [
            jnp.where(low, a, pltpu.roll(b, step, 0)) + jnp.where(low, pltpu.roll(a, SUBLANES - step, 0), b)
            for a, b in zip(parts[:half], parts[half:])
        ]
        step //= 2
    return parts[0]


def tile_of(ref, lead, tile):
    return ref[lead + (slice(None), slice(tile * LANES, (tile + 1) * LANES))]


def column_center(column, cosine, column_count, cell_count):
    return (column + 0.5 - column_count / 2) * (PITCH * cell_count / column_count) / cosine + (
        cell_count / 2 - 0.5
    )


def shear_steps(group, row_count, tangent):
    row = (sublane_index() + group * SUBLANES).astype(F32)
    offset = (row + 0.5 - row_count / 2) * tangent
    whole = jnp.floor(offset)
    return whole.astype(jnp.int32), offset - whole


def project_kernel(
    angle_ref, subset_ref, volume_ref, measured_ref, block_ref, cover_ref, part_sum_ref, part_up_ref, cell_ref, slope_ref
):
    slab_depth, row_count, cell_count = volume_ref.shape
    row_share, view_count, column_count = measured_ref.shape
    subset_count = subset_ref.shape[0]
    half = row_count // 2
    tiles = cell_count // LANES
    groups = row_count // SUBLANES
    lane, sub = lane_index(), sublane_index()
    zero = jnp.zeros((SUBLANES, LANES), F32)
    width = column_count // 2

    for row in range(row_share):
        for member in range(subset_count):
            view = subset_ref[member]
            for side in range(2):
                block_ref[2 * slab_depth + row, side * subset_count + member : side * subset_count + member + 1, :] = (
                    measured_ref[row, pl.ds(view, 1), side * width : (side + 1) * width]
                )

    def one_view(view, carry):
        _, tangent, _ = angle_facts(jnp.full((SUBLANES, LANES), angle_ref[view], jnp.int32))
        first_sum, first_up, last_sum, last_up, all_up = zero, zero, zero, zero, zero
        for group in range(groups):
            whole, fraction = shear_steps(group, row_count, tangent)
            near = lane + (whole + half) < LANES
            first_sum += jnp.where(near, 0.0, 1.0)
            first_up += jnp.where(near, 0.0, fraction)
            last_sum += jnp.where(near, 1.0, 0.0)
            last_up += jnp.where(near, fraction, 0.0)
            all_up += fraction
        for tile, pair in ((0, (first_sum, first_up)), (tiles, (last_sum, last_up)), (1, (zero, all_up))):
            cut = slice(tile * LANES, (tile + 1) * LANES)
            part_sum_ref[slab_depth, view, :, cut], part_up_ref[slab_depth, view, :, cut] = pair
        for depth in range(slab_depth):
            sums, ups = [zero] * (tiles + 1), [zero] * (tiles + 1)
            for group in range(groups):
                whole, fraction = shear_steps(group, row_count, tangent)
                place = lane + (whole + half)
                index = jnp.bitwise_and(place, LANES - 1)
                near = place < LANES
                before = zero
                for tile in range(tiles + 1):
                    after = zero
                    if tile < tiles:
                        cells = volume_ref[
                            depth, group * SUBLANES : (group + 1) * SUBLANES, tile * LANES : (tile + 1) * LANES
                        ]
                        after = pick(cells, index)
                    moved = jnp.where(near, before, after)
                    sums[tile] = sums[tile] + moved
                    ups[tile] = ups[tile] + fraction * moved
                    before = after
            for tile in range(tiles + 1):
                cut = slice(tile * LANES, (tile + 1) * LANES)
                part_sum_ref[depth, view, :, cut] = sums[tile]
                part_up_ref[depth, view, :, cut] = ups[tile]
        return carry

    lax.fori_loop(0, view_count, one_view, 0)

    shift = LANES - half
    for depth in range(slab_depth + 1):
        collapsed = []
        held = lambda ref, tile: rows_summed([tile_of(ref, (depth, view), tile) for view in range(view_count)])
        if depth < slab_depth:
            sums = [held(part_sum_ref, tile) for tile in range(tiles + 1)]
            ups = [held(part_up_ref, tile) for tile in range(tiles + 1)]
        else:
            sums = [held(part_sum_ref, 0)] + [zero + float(row_count)] * (tiles - 1) + [held(part_sum_ref, tiles)]
            ups = [held(part_up_ref, 0)] + [held(part_up_ref, 1)] * (tiles - 1) + [held(part_up_ref, tiles)]
        ups.append(zero)
        for tile in range(tiles + 1):
            cells = sums[tile] - ups[tile] + next_lane(ups[tile], ups[tile + 1])
            cell = lane + (tile * LANES - shift)
            if tile in (0, tiles):
                cells = jnp.where((cell >= 0) & (cell < cell_count), cells, 0.0)
            collapsed.append(cells)
        collapsed.append(zero)
        for tile in range(tiles + 1):
            cut = slice(tile * LANES, (tile + 1) * LANES)
            cell_ref[depth, :, cut] = collapsed[tile]
            slope_ref[depth, :, cut] = next_lane(collapsed[tile], collapsed[tile + 1]) - collapsed[tile]

    cosine, _, _ = angle_facts(spread_scalars(lambda v: angle_ref[v], view_count, sub))
    factor = 1.0 / (row_count * cosine)
    least = angle_table()[0].min()
    for tile in range(column_count // LANES):
        column = (lane + tile * LANES).astype(F32)
        center = column_center(column, cosine, column_count, cell_count)
        whole = jnp.floor(center)
        fraction = center - whole
        place = jnp.clip(whole.astype(jnp.int32) + shift, shift - 2, shift + cell_count)
        block, index = jnp.right_shift(place, 7), jnp.bitwise_and(place, LANES - 1)
        ends = [column_center(tile * LANES + e, c, column_count, cell_count) for e in (0, LANES - 1) for c in (1.0, least)]
        low = min(max(math.floor(min(ends) - 1e-2) + shift, shift - 2), shift + cell_count) // LANES
        high = min(max(math.floor(max(ends) + 1e-2) + shift, shift - 2), shift + cell_count) // LANES
        for depth in range(slab_depth + 1):
            cells, slope = zero, zero
            for source in range(low, high + 1):
                here = block == source
                cells = jnp.where(here, pick(tile_of(cell_ref, (depth,), source), index), cells)
                slope = jnp.where(here, pick(tile_of(slope_ref, (depth,), source), index), slope)
            profile = (cells + fraction * slope) * factor
            if depth == slab_depth:
                cover_ref[:, tile * LANES : (tile + 1) * LANES] = profile
            else:
                side, inner = divmod(tile * LANES, width)
                block_ref[depth * 2 + side, :, inner : inner + LANES] = profile


def update_kernel(
    slab_count,
    reach,
    angle_ref,
    lift_ref,
    subset_ref,
    volume_ref,
    measured_ref,
    cover_ref,
    *refs,
):
    blocks = refs[: 2 * reach + 1]
    residual_ref, updated_ref, profile_ref, cover_sub_ref, spread_ref, cell_ref, slope_ref, edge_ref, bend_ref = refs[
        2 * reach + 1 :
    ]
    slab_depth, row_count, cell_count = volume_ref.shape
    row_share, view_count, column_count = measured_ref.shape
    subset_count = subset_ref.shape[0]
    total_rows, total_slices = row_share * slab_count, slab_depth * slab_count
    half = row_count // 2
    tiles, columns = cell_count // LANES, column_count // LANES
    width = column_count // 2
    lane, sub = lane_index(), sublane_index()
    zero = jnp.zeros((SUBLANES, LANES), F32)
    slab = lax.axis_index("slab")
    odd = lax.rem(slab, 2)
    toward = 2 * odd - 1
    origin = [slab] + [slab + toward * j for j in range(1, reach + 1)]
    origin += [slab - toward * j for j in range(1, reach + 1)]

    def cone(rows, lifts, flat):
        return (rows + 0.5 - total_rows / 2 - lifts) * flat + (total_slices / 2 - 0.5)

    def cone_total(sample):
        whole = jnp.floor(sample)
        fraction = sample - whole
        low = jnp.where((whole >= 0) & (whole < total_slices), 1.0 - fraction, 0.0)
        return low + jnp.where((whole >= -1) & (whole < total_slices - 1), fraction, 0.0)

    def column_of(tile, at):
        return jnp.broadcast_to(tile[:, at : at + 1], (SUBLANES, LANES))

    _, _, flat = angle_facts(spread_scalars(lambda v: angle_ref[v], view_count, sub))
    lifts = spread_scalars(lambda v: lift_ref[v], view_count, sub).astype(F32)
    source = jnp.right_shift(lane, slab_depth.bit_length() - 1) if slab_depth & (slab_depth - 1) == 0 else lane // slab_depth
    slices = spread_scalars(lambda b: origin[b], len(blocks), source) * slab_depth + (lane - source * slab_depth)
    slices = slices.astype(F32)
    for row in range(row_share):
        sample = cone((slab * row_share + row).astype(F32), lifts, flat)
        weights = jnp.maximum(0.0, 1.0 - jnp.abs(sample - slices))
        total = cone_total(sample)
        image = [zero] * columns
        for place, block in enumerate(blocks):
            for depth in range(slab_depth):
                weight = column_of(weights, place * slab_depth + depth)
                for tile in range(columns):
                    side, inner = divmod(tile * LANES, width)
                    image[tile] = image[tile] + weight * block[depth * 2 + side, :, inner : inner + LANES]
        for tile in range(columns):
            cut = slice(tile * LANES, (tile + 1) * LANES)
            length = total * cover_ref[:, cut]
            residual_ref[row, :, cut] = (measured_ref[row, :, cut] - image[tile]) / jnp.maximum(length, LEN_FLOOR)

    member_of = jnp.bitwise_and(sub, subset_count - 1)
    cosine, _, flat = angle_facts(spread_scalars(lambda k: angle_ref[subset_ref[k]], subset_count, member_of))
    lifts = spread_scalars(lambda k: lift_ref[subset_ref[k]], subset_count, member_of).astype(F32)
    factor = 1.0 / (row_count * cosine)
    for member in range(subset_count):
        view = pl.ds(subset_ref[member], 1)
        for side in range(2):
            at = slice(side * subset_count + member, side * subset_count + member + 1)
            cover_sub_ref[at, :] = cover_ref[view, side * width : (side + 1) * width]
            near = blocks[1][(slab_depth - 1) * 2 + side, view, :], blocks[1][side, view, :]
            mate = blocks[1 + reach][(slab_depth - 1) * 2 + side, view, :], blocks[1 + reach][side, view, :]
            profile_ref[0, at, :] = jnp.where(odd == 0, near[0], mate[0])
            for depth in range(slab_depth):
                profile_ref[1 + depth, at, :] = blocks[0][depth * 2 + side, view, :]
            profile_ref[1 + slab_depth, at, :] = jnp.where(odd == 0, mate[1], near[1])

    rows_here = row_share * len(blocks)
    source = sum(jnp.where(lane >= row_share * b, 1, 0) for b in range(1, len(blocks)))
    rows = spread_scalars(lambda b: origin[b], len(blocks), source) * row_share + (lane - source * row_share)
    real = (rows >= 0) & (rows < total_rows) & (lane < rows_here)
    sample = cone(rows.astype(F32), lifts, flat)
    total = cone_total(sample)
    weights = [
        jnp.where(real, jnp.maximum(0.0, 1.0 - jnp.abs(sample - (slab * slab_depth + z).astype(F32))), 0.0)
        for z in range(-1, slab_depth + 1)
    ]
    inner_tiles = width // LANES
    spread = [[zero] * inner_tiles for _ in range(slab_depth)]
    for place in range(rows_here):
        weight = [column_of(w, place) for w in weights]
        length = column_of(total, place)
        block, row = blocks[place // row_share], place % row_share
        for tile in range(inner_tiles):
            cut = slice(tile * LANES, (tile + 1) * LANES)
            image = weight[0] * profile_ref[0, :, cut]
            for z in range(1, slab_depth + 2):
                image = image + weight[z] * profile_ref[z, :, cut]
            rest = (block[2 * slab_depth + row, :, cut] - image) / jnp.maximum(
                length * cover_sub_ref[:, cut], LEN_FLOOR
            )
            for depth in range(slab_depth):
                spread[depth][tile] = spread[depth][tile] + weight[1 + depth] * rest
    for depth in range(slab_depth):
        for tile in range(inner_tiles):
            for side in range(2):
                spread_ref[
                    depth * subset_count : (depth + 1) * subset_count,
                    side * width + tile * LANES : side * width + (tile + 1) * LANES,
                ] = spread[depth][tile][side * subset_count : (side + 1) * subset_count]

    least = angle_table()[0].min()
    spacing = PITCH * cell_count / column_count
    shifted, edges = [], []
    for tile in range(tiles + 1):
        cell = (lane + (tile * LANES - half)).astype(F32)
        inside = (cell >= 0) & (cell < cell_count)
        first = jnp.floor((cell - (cell_count / 2 + 0.5)) * cosine * (1.0 / spacing) + (column_count / 2 - 0.5 - 1e-3)) + 1.0
        ends = [
            (tile * LANES - half + e - cell_count / 2 - 0.5) * c / spacing + column_count / 2 + 0.5
            for e in (0, LANES - 1)
            for c in (1.0, least)
        ]
        value, edge = zero, zero
        for tap in range(3):
            column = first + tap
            weight = jnp.maximum(0.0, 1.0 - jnp.abs(cell - column_center(column, cosine, column_count, cell_count)))
            weight = jnp.where(inside & (column >= 0) & (column < column_count), weight, 0.0)
            place = jnp.clip(column.astype(jnp.int32), 0, column_count - 1)
            block, index = jnp.right_shift(place, 7), jnp.bitwise_and(place, LANES - 1)
            low = min(max(math.floor(min(ends) + tap - 0.6), 0), column_count - 1) // LANES
            high = min(max(math.ceil(max(ends) + tap + 0.6), 0), column_count - 1) // LANES
            found = zero
            for at in range(low, high + 1):
                found = jnp.where(block == at, pick(tile_of(spread_ref, (), at), index), found)
            value = value + weight * found
            edge = edge + weight
        shifted.append(value * factor)
        edges.append(edge * factor)
    shifted.append(zero)
    edges.append(zero)
    for tile in range(tiles + 1):
        cut = slice(tile * LANES, (tile + 1) * LANES)
        cell_ref[:, cut] = shifted[tile]
        slope_ref[:, cut] = next_lane(shifted[tile], shifted[tile + 1]) - shifted[tile]
        edge_ref[:, cut] = edges[tile]
        bend_ref[:, cut] = next_lane(edges[tile], edges[tile + 1]) - edges[tile]

    slice_total = [jnp.sum(weights[1 + depth], axis=1, keepdims=True) for depth in range(slab_depth)]
    slice_total = [
        [jnp.broadcast_to(t[k : k + 1], (SUBLANES, LANES)) for k in range(subset_count)] for t in slice_total
    ]
    tangents = [
        angle_facts(jnp.full((SUBLANES, LANES), angle_ref[subset_ref[k]], jnp.int32))[1] for k in range(subset_count)
    ]

    def one_group(group, carry):
        band = pl.ds(pl.multiple_of(group * SUBLANES, SUBLANES), SUBLANES)
        steps = []
        for member in range(subset_count):
            whole, fraction = shear_steps(group, row_count, tangents[member])
            place = lane + (half - 1 - whole)
            steps.append((jnp.bitwise_and(place, LANES - 1), place < LANES, 1.0 - fraction))

        def sheared(base_ref, bend, row, member):
            index, near, share = steps[member]
            before = None
            out = []
            for tile in range(tiles + 1):
                cut = slice(tile * LANES, (tile + 1) * LANES)
                low = pick(jnp.broadcast_to(base_ref[row : row + 1, cut], (SUBLANES, LANES)), index)
                rise = pick(jnp.broadcast_to(bend[row : row + 1, cut], (SUBLANES, LANES)), index)
                after = low + share * rise
                if tile:
                    out.append(jnp.where(near, before, after))
                before = after
            return out

        weight = [[zero] * tiles for _ in range(slab_depth)]
        for member in range(subset_count):
            line = sheared(edge_ref, bend_ref, member, member)
            for depth in range(slab_depth):
                for tile in range(tiles):
                    weight[depth][tile] = weight[depth][tile] + slice_total[depth][member] * line[tile]
        for depth in range(slab_depth):
            for tile in range(tiles):
                updated_ref[depth, band, tile * LANES : (tile + 1) * LANES] = jnp.maximum(
                    weight[depth][tile], LEN_FLOOR * subset_count / row_count
                )
        for depth in range(slab_depth):
            back = [zero] * tiles
            for member in range(subset_count):
                line = sheared(cell_ref, slope_ref, depth * subset_count + member, member)
                back = [b + a for b, a in zip(back, line)]
            for tile in range(tiles):
                cut = slice(tile * LANES, (tile + 1) * LANES)
                updated_ref[depth, band, cut] = volume_ref[depth, band, cut] + back[tile] / updated_ref[depth, band, cut]
        return carry

    lax.fori_loop(0, row_count // SUBLANES, one_group, 0)


def swapped(block):
    return lax.ppermute(block, "slab", [(i, i ^ 1) for i in range(lax.axis_size("slab"))])


def from_side(block, distance):
    slabs = range(lax.axis_size("slab"))
    below = [(i - distance, i) for i in slabs if i % 2 == 0 and i - distance in slabs]
    above = [(i + distance, i) for i in slabs if i % 2 == 1 and i + distance in slabs]
    return lax.ppermute(block, "slab", below + above)


def per_device(volume, measured, view_angle, view_lift, subset):
    slab_count = lax.axis_size("slab")
    slab_depth, row_count, cell_count = volume.shape
    row_share, view_count, column_count = measured.shape
    subset_count = subset.shape[0]
    tiles = cell_count // LANES
    reach = slab_reach(slab_count, slab_depth, row_share)
    smem, vmem = pl.BlockSpec(memory_space=pltpu.SMEM), pl.BlockSpec(memory_space=pltpu.VMEM)
    wide = (tiles + 1) * LANES
    block_shape = (2 * slab_depth + row_share, SUBLANES, column_count // 2)
    own, cover = pl.pallas_call(
        project_kernel,
        out_shape=(
            jax.ShapeDtypeStruct(block_shape, F32),
            jax.ShapeDtypeStruct((view_count, column_count), F32),
        ),
        in_specs=[smem, smem, vmem, vmem],
        out_specs=(vmem, vmem),
        scratch_shapes=[pltpu.VMEM((slab_depth + 1, view_count, SUBLANES, wide), F32)] * 2
        + [pltpu.VMEM((slab_depth + 1, SUBLANES, wide), F32)] * 2,
        name="project",
    )(view_angle, subset, volume, measured)
    near = [from_side(own, j) for j in range(1, reach + 1)]
    mate = swapped(own)
    far = [mate] + [swapped(b) for b in near[:-1]]
    return pl.pallas_call(
        functools.partial(update_kernel, slab_count, reach),
        out_shape=(
            jax.ShapeDtypeStruct(measured.shape, F32),
            jax.ShapeDtypeStruct(volume.shape, F32),
        ),
        in_specs=[smem] * 3 + [vmem] * (3 + 1 + 2 * reach),
        out_specs=(vmem, vmem),
        scratch_shapes=[
            pltpu.VMEM((slab_depth + 2, SUBLANES, column_count // 2), F32),
            pltpu.VMEM((SUBLANES, column_count // 2), F32),
            pltpu.VMEM((SUBLANES, column_count), F32),
        ]
        + [pltpu.VMEM((SUBLANES, wide), F32)] * 4,
        name="update",
    )(view_angle, view_lift, subset, volume, measured, cover, own, *near, *far)


def solution(mesh):
    in_specs = (
        P(("scan", "slab"), None, None),
        P(("scan", "slab"), None, None),
        P("scan"),
        P("scan"),
        P("scan"),
    )
    out_specs = (P(("scan", "slab"), None, None), P(("scan", "slab"), None, None))
    return jax.shard_map(
        per_device, mesh=mesh, in_specs=in_specs, out_specs=out_specs, check_vma=False
    )
```

time: 327 us -> 26.2 us (0.08)
  the two profiles are of different devices: /device:TPU:17 before, /device:TPU:1 now
where the time goes in v1:
time: 26.2 us; the launch traced here: 26 us
  starting transfers between devices  12.2 us (47%)
  Pallas kernels  10.2 us (39%)
  waiting for transfers between devices  2.14 us (8%)
  between operations  0.74 us (3%)
  local copies, waits for them, and re-layouts  0.71 us (3%)
    ppermute x3, starting transfers between devices, from_side(): return lax.ppermute(block, 'slab', below + above)  11.5 us
    pallas_call x1, Pallas kernels, per_device(): pl.pallas_call(functools.partial(update_kernel, slab_count, reach), out_s...  5.73 us
    pallas_call x1, Pallas kernels, per_device(): pl.pallas_call(project_kernel, out_shape=(jax.ShapeDtypeStruct(block_shap...  4.5 us
    ppermute x3, waiting for transfers between devices, from_side(): return lax.ppermute(block, 'slab', below + above)  2.14 us
    unnamed x12, local copies, waits for them, and re-layouts  0.71 us
    ppermute x3, starting transfers between devices, swapped(): lax.ppermute(block, 'slab', [(i, i ^ 1) for i in range(lax.axis_size('sla...  0.62 us
  transfers between devices with their start and end apart: 6, of which 1 were waited for; matrix products, arithmetic and copies ran while one was open for 0% of the time, Pallas kernels for 0%

profile of v1, /device:TPU:1, one launch (start us, length us, event | category | flops | bytes accessed | tf_op | source)
XLA Modules:
  0.0 26.0 jit_solution(13735727500049884738)
XLA Ops:
  0.6 4.5 %project.1 = (f32[7,8,512]{2,1,0:T(8,128)}, f32[8,1024]{1,0:T(8,128)}) custom-call(s32[8]{0:T(128)} %angle_ref.3, s32[4]{0:T(128)} %subset_ref.3, f32[2,64,1024]{2,1,0:T(8,128)} %volume_ref.3, f32[3,8,1024]{2,1,0:T(8,128)} %measured_ref.3), custom_call_target="tpu_custom_call" | custom-call | tf_op jit(solution)/shard_map/project/pallas_call | solution.py:444
  5.1 1.3 %collective-permute-start.1 = (f32[7,8,512]{2,1,0:T(8,128)}, f32[7,8,512]{2,1,0:T(8,128)S(1)}, u32[]{:S(2)}, u32[]{:S(2)}) collective-permute-start(f32[7,8,512]{2,1,0:T(8,128)} %get-tuple-element.5.refs_0_), channel_id=1, source_target_pairs={{0,2},{2,4},{4,6},{6,8},{8,10},{10,12},{12,14},{3,1},{5,3},{7,5},{... | collective-permute-start | bytes 344072 | tf_op jit(solution)/shard_map/ppermute | solution.py:431
  6.4 6.7 %collective-permute-start = (f32[7,8,512]{2,1,0:T(8,128)}, f32[7,8,512]{2,1,0:T(8,128)S(1)}, u32[]{:S(2)}, u32[]{:S(2)}) collective-permute-start(f32[7,8,512]{2,1,0:T(8,128)} %get-tuple-element.5.refs_0_), channel_id=1, source_target_pairs={{1,2},{3,4},{5,6},{7,8},{9,10},{11,12},{13,14},{2,1},{4,3},{6,5},{... | collective-permute-start | bytes 344072 | tf_op jit(solution)/shard_map/ppermute | solution.py:431
  13.1 0.1 collective-permute-start.3
  13.2 3.6 %collective-permute-start.2 = (f32[7,8,512]{2,1,0:T(8,128)}, f32[7,8,512]{2,1,0:T(8,128)S(1)}, u32[]{:S(2)}, u32[]{:S(2)}) collective-permute-start(f32[7,8,512]{2,1,0:T(8,128)} %get-tuple-element.5.refs_0_), channel_id=1, source_target_pairs={{1,4},{3,6},{5,8},{7,10},{9,12},{11,14},{4,1},{6,3},{8,5},{10,7},{... | collective-permute-start | bytes 344072 | tf_op jit(solution)/shard_map/ppermute | solution.py:431
  16.8 0.0 collective-permute-done.1.refs_2_
  16.8 0.0 copy-start
  16.8 0.1 collective-permute-start.5
  16.9 0.0 collective-permute-done.refs_1_
  16.9 0.0 copy-start.1
  16.9 0.5 %collective-permute-start.4 = (f32[7,8,512]{2,1,0:T(8,128)S(1)}, f32[7,8,512]{2,1,0:T(8,128)S(1)}, u32[]{:S(2)}, u32[]{:S(2)}) collective-permute-start(f32[7,8,512]{2,1,0:T(8,128)S(1)} %collective-permute-done.refs_1_), channel_id=1, source_target_pairs={{0,1},{1,0},{2,3},{3,2},{4,5},{5,4},{6,7},{7,6},{8,9},{9,8},{10,11... | collective-permute-start | bytes 344072 | tf_op jit(solution)/shard_map/ppermute | solution.py:424
  17.4 0.0 collective-permute-done.3.refs_4_
  17.4 0.0 copy-start.2
  17.4 2.1 %collective-permute-done.2.refs_3_ = f32[7,8,512]{2,1,0:T(8,128)S(1)} collective-permute-done((f32[7,8,512]{2,1,0:T(8,128)}, f32[7,8,512]{2,1,0:T(8,128)S(1)}, u32[]{:S(2)}, u32[]{:S(2)}) %collective-permute-start.2) | collective-permute-done | bytes 114720 | tf_op jit(solution)/shard_map/ppermute | solution.py:431
  19.5 0.0 copy-start.3
  19.5 0.0 collective-permute-done.5.refs_6_
  19.5 0.0 copy-start.4
  19.5 0.0 collective-permute-done.4.refs_5_
  19.5 0.0 copy-start.5
  19.5 0.0 copy-done
  19.5 0.0 copy-done.1
  19.5 0.0 copy-done.2
  19.6 0.6 %copy-done.3 = f32[7,8,512]{2,1,0:T(8,128)} copy-done((f32[7,8,512]{2,1,0:T(8,128)}, f32[7,8,512]{2,1,0:T(8,128)S(1)}, u32[]{:S(2)}) %copy-start.3) | copy-done | bytes 114712
  20.2 0.0 copy-done.4
  20.2 0.1 copy-done.5
  20.2 5.7 %update.1 = (f32[3,8,1024]{2,1,0:T(8,128)}, f32[2,64,1024]{2,1,0:T(8,128)}) custom-call(s32[8]{0:T(128)} %angle_ref.3, s32[8]{0:T(128)} %lift_ref.1, s32[4]{0:T(128)} %subset_ref.3, f32[2,64,1024]{2,1,0:T(8,128)} %volume_ref.3, f32[3,8,1024]{2,1,0:T(8,128)} %measured_ref.3, f32[8,1024]{1,0:T(8,128)} %get-tuple-element.4.cover_ref, ...), custom_call_target="tpu_custom_call" | custom-call | tf_op jit(solution)/shard_map/update/pallas_call | solution.py:459
Async XLA Ops:
  5.1 11.6 %collective-permute-start.1 = (f32[7,8,512]{2,1,0:T(8,128)}, f32[7,8,512]{2,1,0:T(8,128)S(1)}, u32[]{:S(2)}, u32[]{:S(2)}) collective-permute-start(f32[7,8,512]{2,1,0:T(8,128)} %get-tuple-element.5.refs_0_), channel_id=1, source_target_pairs={{0,2},{2,4},{4,6},{6,8},{8,10},{10,12},{12,14},{3,1},{5,3},{7,5},{... | collective-permute-start | bytes 344072 | tf_op jit(solution)/shard_map/ppermute | solution.py:431
  6.4 10.4 %collective-permute-start = (f32[7,8,512]{2,1,0:T(8,128)}, f32[7,8,512]{2,1,0:T(8,128)S(1)}, u32[]{:S(2)}, u32[]{:S(2)}) collective-permute-start(f32[7,8,512]{2,1,0:T(8,128)} %get-tuple-element.5.refs_0_), channel_id=1, source_target_pairs={{1,2},{3,4},{5,6},{7,8},{9,10},{11,12},{13,14},{2,1},{4,3},{6,5},{... | collective-permute-start | bytes 344072 | tf_op jit(solution)/shard_map/ppermute | solution.py:431
  13.1 4.3 %collective-permute-start.3 = (f32[7,8,512]{2,1,0:T(8,128)}, f32[7,8,512]{2,1,0:T(8,128)S(1)}, u32[]{:S(2)}, u32[]{:S(2)}) collective-permute-start(f32[7,8,512]{2,1,0:T(8,128)} %get-tuple-element.5.refs_0_), channel_id=1, source_target_pairs={{0,1},{1,0},{2,3},{3,2},{4,5},{5,4},{6,7},{7,6},{8,9},{9,8},{10,11... | collective-permute-start | bytes 344072 | tf_op jit(solution)/shard_map/ppermute | solution.py:424
  13.2 6.3 %collective-permute-start.2 = (f32[7,8,512]{2,1,0:T(8,128)}, f32[7,8,512]{2,1,0:T(8,128)S(1)}, u32[]{:S(2)}, u32[]{:S(2)}) collective-permute-start(f32[7,8,512]{2,1,0:T(8,128)} %get-tuple-element.5.refs_0_), channel_id=1, source_target_pairs={{1,4},{3,6},{5,8},{7,10},{9,12},{11,14},{4,1},{6,3},{8,5},{10,7},{... | collective-permute-start | bytes 344072 | tf_op jit(solution)/shard_map/ppermute | solution.py:431
  16.8 2.8 %copy-start = (f32[7,8,512]{2,1,0:T(8,128)}, f32[7,8,512]{2,1,0:T(8,128)S(1)}, u32[]{:S(2)}) copy-start(f32[7,8,512]{2,1,0:T(8,128)S(1)} %collective-permute-done.1.refs_2_) | copy-start | bytes 344068
  16.8 2.7 %collective-permute-start.5 = (f32[7,8,512]{2,1,0:T(8,128)S(1)}, f32[7,8,512]{2,1,0:T(8,128)S(1)}, u32[]{:S(2)}, u32[]{:S(2)}) collective-permute-start(f32[7,8,512]{2,1,0:T(8,128)S(1)} %collective-permute-done.1.refs_2_), channel_id=1, source_target_pairs={{0,1},{1,0},{2,3},{3,2},{4,5},{5,4},{6,7},{7,6},{8,9},{9,8},{10,11... | collective-permute-start | bytes 344072 | tf_op jit(solution)/shard_map/ppermute | solution.py:424
  16.9 2.7 %copy-start.1 = (f32[7,8,512]{2,1,0:T(8,128)}, f32[7,8,512]{2,1,0:T(8,128)S(1)}, u32[]{:S(2)}) copy-start(f32[7,8,512]{2,1,0:T(8,128)S(1)} %collective-permute-done.refs_1_) | copy-start | bytes 344068
  16.9 2.6 %collective-permute-start.4 = (f32[7,8,512]{2,1,0:T(8,128)S(1)}, f32[7,8,512]{2,1,0:T(8,128)S(1)}, u32[]{:S(2)}, u32[]{:S(2)}) collective-permute-start(f32[7,8,512]{2,1,0:T(8,128)S(1)} %collective-permute-done.refs_1_), channel_id=1, source_target_pairs={{0,1},{1,0},{2,3},{3,2},{4,5},{5,4},{6,7},{7,6},{8,9},{9,8},{10,11... | collective-permute-start | bytes 344072 | tf_op jit(solution)/shard_map/ppermute | solution.py:424
  17.4 2.2 %copy-start.2 = (f32[7,8,512]{2,1,0:T(8,128)}, f32[7,8,512]{2,1,0:T(8,128)S(1)}, u32[]{:S(2)}) copy-start(f32[7,8,512]{2,1,0:T(8,128)S(1)} %collective-permute-done.3.refs_4_) | copy-start | bytes 344068
  19.5 0.7 %copy-start.3 = (f32[7,8,512]{2,1,0:T(8,128)}, f32[7,8,512]{2,1,0:T(8,128)S(1)}, u32[]{:S(2)}) copy-start(f32[7,8,512]{2,1,0:T(8,128)S(1)} %collective-permute-done.2.refs_3_) | copy-start | bytes 344068
  19.5 0.7 %copy-start.4 = (f32[7,8,512]{2,1,0:T(8,128)}, f32[7,8,512]{2,1,0:T(8,128)S(1)}, u32[]{:S(2)}) copy-start(f32[7,8,512]{2,1,0:T(8,128)S(1)} %collective-permute-done.5.refs_6_) | copy-start | bytes 344068
  19.5 0.7 %copy-start.5 = (f32[7,8,512]{2,1,0:T(8,128)}, f32[7,8,512]{2,1,0:T(8,128)S(1)}, u32[]{:S(2)}) copy-start(f32[7,8,512]{2,1,0:T(8,128)S(1)} %collective-permute-done.4.refs_5_) | copy-start | bytes 344068

commit v2 on v1

--- a/solution.py
+++ b/solution.py
@@ -262,10 +262,11 @@
     lifts = spread_scalars(lambda v: lift_ref[v], view_count, sub).astype(F32)
     source = jnp.right_shift(lane, slab_depth.bit_length() - 1) if slab_depth & (slab_depth - 1) == 0 else lane // slab_depth
     slices = spread_scalars(lambda b: origin[b], len(blocks), source) * slab_depth + (lane - source * slab_depth)
+    held = (slices >= 0) & (slices < total_slices)
     slices = slices.astype(F32)
     for row in range(row_share):
         sample = cone((slab * row_share + row).astype(F32), lifts, flat)
-        weights = jnp.maximum(0.0, 1.0 - jnp.abs(sample - slices))
+        weights = jnp.where(held, jnp.maximum(0.0, 1.0 - jnp.abs(sample - slices)), 0.0)
         total = cone_total(sample)
         image = [zero] * columns
         for place, block in enumerate(blocks):
@@ -301,10 +302,11 @@
     real = (rows >= 0) & (rows < total_rows) & (lane < rows_here)
     sample = cone(rows.astype(F32), lifts, flat)
     total = cone_total(sample)
-    weights = [
-        jnp.where(real, jnp.maximum(0.0, 1.0 - jnp.abs(sample - (slab * slab_depth + z).astype(F32))), 0.0)
-        for z in range(-1, slab_depth + 1)
-    ]
+    weights = []
+    for z in range(-1, slab_depth + 1):
+        at = slab * slab_depth + z
+        use = real & (at >= 0) & (at < total_slices)
+        weights.append(jnp.where(use, jnp.maximum(0.0, 1.0 - jnp.abs(sample - at.astype(F32))), 0.0))
     inner_tiles = width // LANES
     spread = [[zero] * inner_tiles for _ in range(slab_depth)]
     for place in range(rows_here):
@@ -426,9 +428,14 @@
 
 def from_side(block, distance):
     slabs = range(lax.axis_size("slab"))
-    below = [(i - distance, i) for i in slabs if i % 2 == 0 and i - distance in slabs]
-    above = [(i + distance, i) for i in slabs if i % 2 == 1 and i + distance in slabs]
-    return lax.ppermute(block, "slab", below + above)
+    pairs = [(i - distance, i) for i in slabs if i % 2 == 0 and i - distance in slabs]
+    pairs += [(i + distance, i) for i in slabs if i % 2 == 1 and i + distance in slabs]
+    idle = [i for i in slabs if i not in [p[0] for p in pairs]]
+    unmet = [i for i in slabs if i not in [p[1] for p in pairs]]
+    both = [i for i in idle if i in unmet]
+    pairs += [(i, i) for i in both]
+    pairs += list(zip([i for i in idle if i not in both], [i for i in unmet if i not in both]))
+    return lax.ppermute(block, "slab", pairs)
 
 
 def per_device(volume, measured, view_angle, view_lift, subset):
@@ -444,8 +451,8 @@
     own, cover = pl.pallas_call(
         project_kernel,
         out_shape=(
-            jax.ShapeDtypeStruct(block_shape, F32),
-            jax.ShapeDtypeStruct((view_count, column_count), F32),
+            pltpu.VMEM(block_shape, F32),
+            pltpu.VMEM((view_count, column_count), F32),
         ),
         in_specs=[smem, smem, vmem, vmem],
         out_specs=(vmem, vmem),
@@ -456,6 +463,7 @@
     near = [from_side(own, j) for j in range(1, reach + 1)]
     mate = swapped(own)
     far = [mate] + [swapped(b) for b in near[:-1]]
+    here = lambda x: pltpu.with_memory_space_constraint(x, pltpu.VMEM)
     return pl.pallas_call(
         functools.partial(update_kernel, slab_count, reach),
         out_shape=(
@@ -471,7 +479,7 @@
         ]
         + [pltpu.VMEM((SUBLANES, wide), F32)] * 4,
         name="update",
-    )(view_angle, view_lift, subset, volume, measured, cover, own, *near, *far)
+    )(view_angle, view_lift, subset, volume, measured, here(cover), *map(here, (own, *near, *far)))
 
 
 def solution(mesh):

time: 26.2 us -> 22.3 us (0.85)
  starting transfers between devices: 12.2 us -> 10.3 us
  Pallas kernels: 10.2 us -> 9.23 us
  local copies, waits for them, and re-layouts: 0.71 us -> 0 us
    ppermute x3, starting transfers between devices: 11.5 us -> 9.68 us  [from_side(): return lax.ppermute(block, 'slab', pairs)]
    unnamed x12 -> x0, local copies, waits for them, and re-layouts: 0.71 us -> none
    pallas_call x1, Pallas kernels: 4.5 us -> 3.86 us  [per_device(): pl.pallas_call(project_kernel, out_shape=(pltpu.VMEM(block_shape, F32), p...]
    pallas_call x1, Pallas kernels: 5.73 us -> 5.37 us  [per_device(): pl.pallas_call(functools.partial(update_kernel, slab_count, reach), out_s...]
where the time goes in v2:
time: 22.3 us; the launch traced here: 22.2 us
  starting transfers between devices  10.3 us (46%)
  Pallas kernels  9.23 us (41%)
  waiting for transfers between devices  1.95 us (9%)
  between operations  0.69 us (3%)
    ppermute x3, starting transfers between devices, from_side(): return lax.ppermute(block, 'slab', pairs)  9.68 us
    pallas_call x1, Pallas kernels, per_device(): pl.pallas_call(functools.partial(update_kernel, slab_count, reach), out_s...  5.37 us
    pallas_call x1, Pallas kernels, per_device(): pl.pallas_call(project_kernel, out_shape=(pltpu.VMEM(block_shape, F32), p...  3.86 us
    ppermute x3, waiting for transfers between devices, from_side(): return lax.ppermute(block, 'slab', pairs)  1.94 us
    ppermute x3, starting transfers between devices, swapped(): lax.ppermute(block, 'slab', [(i, i ^ 1) for i in range(lax.axis_size('sla...  0.63 us
  transfers between devices with their start and end apart: 6, of which 1 were waited for; matrix products, arithmetic and copies ran while one was open for 0% of the time, Pallas kernels for 0%

profile of v2, /device:TPU:1, one launch (start us, length us, event | category | flops | bytes accessed | tf_op | source)
XLA Modules:
  0.0 22.2 jit_solution(7775703525444618371)
XLA Ops:
  0.6 3.9 %project.1 = (f32[7,8,512]{2,1,0:T(8,128)S(1)}, f32[8,1024]{1,0:T(8,128)S(1)}) custom-call(s32[8]{0:T(128)} %angle_ref.3, s32[4]{0:T(128)} %subset_ref.3, f32[2,64,1024]{2,1,0:T(8,128)} %volume_ref.3, f32[3,8,1024]{2,1,0:T(8,128)} %measured_ref.3), custom_call_target="tpu_custom_call" | custom-call | tf_op jit(solution)/shard_map/project/pallas_call | solution.py:451
  4.5 0.1 collective-permute-start.1
  4.6 6.0 %collective-permute-start = (f32[7,8,512]{2,1,0:T(8,128)S(1)}, f32[7,8,512]{2,1,0:T(8,128)S(1)}, u32[]{:S(2)}, u32[]{:S(2)}) collective-permute-start(f32[7,8,512]{2,1,0:T(8,128)S(1)} %get-tuple-element.5.refs_0_), channel_id=1, source_target_pairs={{1,2},{3,4},{5,6},{7,8},{9,10},{11,12},{13,14},{2,1},{4,3},{6,5},{... | collective-permute-start | bytes 344072 | tf_op jit(solution)/shard_map/ppermute | solution.py:438
  10.6 0.1 collective-permute-start.3
  10.7 3.6 %collective-permute-start.2 = (f32[7,8,512]{2,1,0:T(8,128)S(1)}, f32[7,8,512]{2,1,0:T(8,128)S(1)}, u32[]{:S(2)}, u32[]{:S(2)}) collective-permute-start(f32[7,8,512]{2,1,0:T(8,128)S(1)} %get-tuple-element.5.refs_0_), channel_id=1, source_target_pairs={{1,4},{3,6},{5,8},{7,10},{9,12},{11,14},{4,1},{6,3},{8,5},{10,7},{... | collective-permute-start | bytes 344072 | tf_op jit(solution)/shard_map/ppermute | solution.py:438
  14.3 0.0 collective-permute-done.1.refs_2_
  14.3 0.1 collective-permute-start.5
  14.4 0.0 collective-permute-done.refs_1_
  14.4 0.5 %collective-permute-start.4 = (f32[7,8,512]{2,1,0:T(8,128)S(1)}, f32[7,8,512]{2,1,0:T(8,128)S(1)}, u32[]{:S(2)}, u32[]{:S(2)}) collective-permute-start(f32[7,8,512]{2,1,0:T(8,128)S(1)} %collective-permute-done.refs_1_), channel_id=1, source_target_pairs={{0,1},{1,0},{2,3},{3,2},{4,5},{5,4},{6,7},{7,6},{8,9},{9,8},{10,11... | collective-permute-start | bytes 344072 | tf_op jit(solution)/shard_map/ppermute | solution.py:426
  14.9 0.0 collective-permute-done.3.refs_4_
  14.9 1.9 %collective-permute-done.2.refs_3_ = f32[7,8,512]{2,1,0:T(8,128)S(1)} collective-permute-done((f32[7,8,512]{2,1,0:T(8,128)S(1)}, f32[7,8,512]{2,1,0:T(8,128)S(1)}, u32[]{:S(2)}, u32[]{:S(2)}) %collective-permute-start.2) | collective-permute-done | bytes 114720 | tf_op jit(solution)/shard_map/ppermute | solution.py:438
  16.8 0.0 collective-permute-done.5.refs_6_
  16.8 0.0 collective-permute-done.4.refs_5_
  16.8 5.4 %update.1 = (f32[3,8,1024]{2,1,0:T(8,128)}, f32[2,64,1024]{2,1,0:T(8,128)}) custom-call(s32[8]{0:T(128)} %angle_ref.3, s32[8]{0:T(128)} %lift_ref.1, s32[4]{0:T(128)} %subset_ref.3, f32[2,64,1024]{2,1,0:T(8,128)} %volume_ref.3, f32[3,8,1024]{2,1,0:T(8,128)} %measured_ref.3, f32[8,1024]{1,0:T(8,128)S(1)} %get-tuple-element.4.cover_ref, ...), custom_call_target="tpu_custom_call" | custom-call | tf_op jit(solution)/shard_map/update/pallas_call | solution.py:467
Async XLA Ops:
  4.5 9.8 %collective-permute-start.1 = (f32[7,8,512]{2,1,0:T(8,128)S(1)}, f32[7,8,512]{2,1,0:T(8,128)S(1)}, u32[]{:S(2)}, u32[]{:S(2)}) collective-permute-start(f32[7,8,512]{2,1,0:T(8,128)S(1)} %get-tuple-element.5.refs_0_), channel_id=1, source_target_pairs={{0,2},{2,4},{4,6},{6,8},{8,10},{10,12},{12,14},{3,1},{5,3},{7,5},{... | collective-permute-start | bytes 344072 | tf_op jit(solution)/shard_map/ppermute | solution.py:438
  4.6 9.7 %collective-permute-start = (f32[7,8,512]{2,1,0:T(8,128)S(1)}, f32[7,8,512]{2,1,0:T(8,128)S(1)}, u32[]{:S(2)}, u32[]{:S(2)}) collective-permute-start(f32[7,8,512]{2,1,0:T(8,128)S(1)} %get-tuple-element.5.refs_0_), channel_id=1, source_target_pairs={{1,2},{3,4},{5,6},{7,8},{9,10},{11,12},{13,14},{2,1},{4,3},{6,5},{... | collective-permute-start | bytes 344072 | tf_op jit(solution)/shard_map/ppermute | solution.py:438
  10.6 4.3 %collective-permute-start.3 = (f32[7,8,512]{2,1,0:T(8,128)S(1)}, f32[7,8,512]{2,1,0:T(8,128)S(1)}, u32[]{:S(2)}, u32[]{:S(2)}) collective-permute-start(f32[7,8,512]{2,1,0:T(8,128)S(1)} %get-tuple-element.5.refs_0_), channel_id=1, source_target_pairs={{0,1},{1,0},{2,3},{3,2},{4,5},{5,4},{6,7},{7,6},{8,9},{9,8},{10,11... | collective-permute-start | bytes 344072 | tf_op jit(solution)/shard_map/ppermute | solution.py:426
  10.7 6.1 %collective-permute-start.2 = (f32[7,8,512]{2,1,0:T(8,128)S(1)}, f32[7,8,512]{2,1,0:T(8,128)S(1)}, u32[]{:S(2)}, u32[]{:S(2)}) collective-permute-start(f32[7,8,512]{2,1,0:T(8,128)S(1)} %get-tuple-element.5.refs_0_), channel_id=1, source_target_pairs={{1,4},{3,6},{5,8},{7,10},{9,12},{11,14},{4,1},{6,3},{8,5},{10,7},{... | collective-permute-start | bytes 344072 | tf_op jit(solution)/shard_map/ppermute | solution.py:438
  14.3 2.5 %collective-permute-start.5 = (f32[7,8,512]{2,1,0:T(8,128)S(1)}, f32[7,8,512]{2,1,0:T(8,128)S(1)}, u32[]{:S(2)}, u32[]{:S(2)}) collective-permute-start(f32[7,8,512]{2,1,0:T(8,128)S(1)} %collective-permute-done.1.refs_2_), channel_id=1, source_target_pairs={{0,1},{1,0},{2,3},{3,2},{4,5},{5,4},{6,7},{7,6},{8,9},{9,8},{10,11... | collective-permute-start | bytes 344072 | tf_op jit(solution)/shard_map/ppermute | solution.py:426
  14.4 2.4 %collective-permute-start.4 = (f32[7,8,512]{2,1,0:T(8,128)S(1)}, f32[7,8,512]{2,1,0:T(8,128)S(1)}, u32[]{:S(2)}, u32[]{:S(2)}) collective-permute-start(f32[7,8,512]{2,1,0:T(8,128)S(1)} %collective-permute-done.refs_1_), channel_id=1, source_target_pairs={{0,1},{1,0},{2,3},{3,2},{4,5},{5,4},{6,7},{7,6},{8,9},{9,8},{10,11... | collective-permute-start | bytes 344072 | tf_op jit(solution)/shard_map/ppermute | solution.py:426

commit v3 on v2

--- a/solution.py
+++ b/solution.py
@@ -218,7 +218,7 @@
 
 def update_kernel(
     slab_count,
-    reach,
+    order,
     angle_ref,
     lift_ref,
     subset_ref,
@@ -227,9 +227,9 @@
     cover_ref,
     *refs,
 ):
-    blocks = refs[: 2 * reach + 1]
+    blocks = refs[: len(order)]
     residual_ref, updated_ref, profile_ref, cover_sub_ref, spread_ref, cell_ref, slope_ref, edge_ref, bend_ref = refs[
-        2 * reach + 1 :
+        len(order) :
     ]
     slab_depth, row_count, cell_count = volume_ref.shape
     row_share, view_count, column_count = measured_ref.shape
@@ -242,9 +242,8 @@
     zero = jnp.zeros((SUBLANES, LANES), F32)
     slab = lax.axis_index("slab")
     odd = lax.rem(slab, 2)
-    toward = 2 * odd - 1
-    origin = [slab] + [slab + toward * j for j in range(1, reach + 1)]
-    origin += [slab - toward * j for j in range(1, reach + 1)]
+    origin = [slab + (1 - 2 * odd) * away for away in order]
+    mate_block, other_block = (blocks[order.index(away)] for away in (1, -1))
 
     def cone(rows, lifts, flat):
         return (rows + 0.5 - total_rows / 2 - lifts) * flat + (total_slices / 2 - 0.5)
@@ -289,12 +288,12 @@
         for side in range(2):
             at = slice(side * subset_count + member, side * subset_count + member + 1)
             cover_sub_ref[at, :] = cover_ref[view, side * width : (side + 1) * width]
-            near = blocks[1][(slab_depth - 1) * 2 + side, view, :], blocks[1][side, view, :]
-            mate = blocks[1 + reach][(slab_depth - 1) * 2 + side, view, :], blocks[1 + reach][side, view, :]
-            profile_ref[0, at, :] = jnp.where(odd == 0, near[0], mate[0])
+            other = other_block[(slab_depth - 1) * 2 + side, view, :], other_block[side, view, :]
+            mate = mate_block[(slab_depth - 1) * 2 + side, view, :], mate_block[side, view, :]
+            profile_ref[0, at, :] = jnp.where(odd == 0, other[0], mate[0])
             for depth in range(slab_depth):
                 profile_ref[1 + depth, at, :] = blocks[0][depth * 2 + side, view, :]
-            profile_ref[1 + slab_depth, at, :] = jnp.where(odd == 0, mate[1], near[1])
+            profile_ref[1 + slab_depth, at, :] = jnp.where(odd == 0, mate[1], other[1])
 
     rows_here = row_share * len(blocks)
     source = sum(jnp.where(lane >= row_share * b, 1, 0) for b in range(1, len(blocks)))
@@ -426,16 +425,32 @@
     return lax.ppermute(block, "slab", [(i, i ^ 1) for i in range(lax.axis_size("slab"))])
 
 
-def from_side(block, distance):
+def from_chip(block, distance):
     slabs = range(lax.axis_size("slab"))
-    pairs = [(i - distance, i) for i in slabs if i % 2 == 0 and i - distance in slabs]
-    pairs += [(i + distance, i) for i in slabs if i % 2 == 1 and i + distance in slabs]
+    steps = [(i + 2 * distance * (1 - 2 * (i % 2)), i) for i in slabs]
+    pairs = [p for p in steps if p[0] in slabs]
     idle = [i for i in slabs if i not in [p[0] for p in pairs]]
     unmet = [i for i in slabs if i not in [p[1] for p in pairs]]
-    both = [i for i in idle if i in unmet]
-    pairs += [(i, i) for i in both]
-    pairs += list(zip([i for i in idle if i not in both], [i for i in unmet if i not in both]))
+    near = [i for i in idle if i ^ 1 in unmet]
+    pairs += [(i, i ^ 1) for i in near]
+    pairs += zip([i for i in idle if i not in near], [i for i in unmet if i ^ 1 not in near])
     return lax.ppermute(block, "slab", pairs)
+
+
+def gathered(own, reach):
+    received = {}
+    for distance in range(1, reach // 2 + 2):
+        for sign in (-1, 1):
+            if 2 * distance - (sign > 0) <= reach:
+                received[sign * distance] = from_chip(own, sign * distance)
+    blocks = {0: own, 1: swapped(own)}
+    for distance, block in received.items():
+        if 2 * abs(distance) <= reach:
+            blocks[2 * distance] = block
+        if abs(1 - 2 * distance) <= reach:
+            blocks[1 - 2 * distance] = swapped(block)
+    assert sorted(blocks) == list(range(-reach, reach + 1))
+    return blocks
 
 
 def per_device(volume, measured, view_angle, view_lift, subset):
@@ -460,12 +475,11 @@
         + [pltpu.VMEM((slab_depth + 1, SUBLANES, wide), F32)] * 2,
         name="project",
     )(view_angle, subset, volume, measured)
-    near = [from_side(own, j) for j in range(1, reach + 1)]
-    mate = swapped(own)
-    far = [mate] + [swapped(b) for b in near[:-1]]
+    blocks = gathered(own, reach)
+    order = tuple(blocks)
     here = lambda x: pltpu.with_memory_space_constraint(x, pltpu.VMEM)
     return pl.pallas_call(
-        functools.partial(update_kernel, slab_count, reach),
+        functools.partial(update_kernel, slab_count, order),
         out_shape=(
             jax.ShapeDtypeStruct(measured.shape, F32),
             jax.ShapeDtypeStruct(volume.shape, F32),
@@ -479,7 +493,7 @@
         ]
         + [pltpu.VMEM((SUBLANES, wide), F32)] * 4,
         name="update",
-    )(view_angle, view_lift, subset, volume, measured, here(cover), *map(here, (own, *near, *far)))
+    )(view_angle, view_lift, subset, volume, measured, here(cover), *map(here, blocks.values()))
 
 
 def solution(mesh):

time: 22.3 us -> 20.6 us (0.924)
  the two profiles are of different devices: /device:TPU:1 before, /device:TPU:0 now
where the time goes in v3:
time: 20.6 us; the launch traced here: 20.4 us
  Pallas kernels  9.23 us (45%)
  starting transfers between devices  7.27 us (35%)
  waiting for transfers between devices  3.3 us (16%)
  between operations  0.65 us (3%)
    pallas_call x1, Pallas kernels, per_device(): pl.pallas_call(functools.partial(update_kernel, slab_count, order), out_s...  5.37 us
    ppermute x4, starting transfers between devices, swapped(): lax.ppermute(block, 'slab', [(i, i ^ 1) for i in range(lax.axis_size('sla...  4.15 us
    pallas_call x1, Pallas kernels, per_device(): pl.pallas_call(project_kernel, out_shape=(pltpu.VMEM(block_shape, F32), p...  3.86 us
    ppermute x3, starting transfers between devices, from_chip(): return lax.ppermute(block, 'slab', pairs)  3.12 us
    ppermute x3, waiting for transfers between devices, from_chip(): return lax.ppermute(block, 'slab', pairs)  1.99 us
    ppermute x4, waiting for transfers between devices, swapped(): lax.ppermute(block, 'slab', [(i, i ^ 1) for i in range(lax.axis_size('sla...  1.31 us
  transfers between devices with their start and end apart: 7, of which 3 were waited for; matrix products, arithmetic and copies ran while one was open for 0% of the time, Pallas kernels for 0%

profile of v3, /device:TPU:0, one launch (start us, length us, event | category | flops | bytes accessed | tf_op | source)
XLA Modules:
  0.0 20.4 jit_solution(12639390778365907968)
XLA Ops:
  0.6 3.9 %project.1 = (f32[7,8,512]{2,1,0:T(8,128)S(1)}, f32[8,1024]{1,0:T(8,128)S(1)}) custom-call(s32[8]{0:T(128)} %angle_ref.3, s32[4]{0:T(128)} %subset_ref.3, f32[2,64,1024]{2,1,0:T(8,128)} %volume_ref.3, f32[3,8,1024]{2,1,0:T(8,128)} %measured_ref.3), custom_call_target="tpu_custom_call" | custom-call | tf_op jit(solution)/shard_map/project/pallas_call | solution.py:466
  4.5 0.5 %collective-permute-start.5 = (f32[7,8,512]{2,1,0:T(8,128)S(1)}, f32[7,8,512]{2,1,0:T(8,128)S(1)}, u32[]{:S(2)}, u32[]{:S(2)}) collective-permute-start(f32[7,8,512]{2,1,0:T(8,128)S(1)} %get-tuple-element.5.refs_0_), channel_id=1, source_target_pairs={{4,0},{6,2},{8,4},{1,5},{10,6},{3,7},{12,8},{5,9},{14,10},{7,11},{... | collective-permute-start | bytes 344072 | tf_op jit(solution)/shard_map/ppermute | solution.py:437
  5.0 2.1 %collective-permute-start.3 = (f32[7,8,512]{2,1,0:T(8,128)S(1)}, f32[7,8,512]{2,1,0:T(8,128)S(1)}, u32[]{:S(2)}, u32[]{:S(2)}) collective-permute-start(f32[7,8,512]{2,1,0:T(8,128)S(1)} %get-tuple-element.5.refs_0_), channel_id=1, source_target_pairs={{2,0},{4,2},{1,3},{6,4},{3,5},{8,6},{5,7},{10,8},{7,9},{12,10},{9,... | collective-permute-start | bytes 344072 | tf_op jit(solution)/shard_map/ppermute | solution.py:437
  7.1 0.5 %collective-permute-start.1 = (f32[7,8,512]{2,1,0:T(8,128)S(1)}, f32[7,8,512]{2,1,0:T(8,128)S(1)}, u32[]{:S(2)}, u32[]{:S(2)}) collective-permute-start(f32[7,8,512]{2,1,0:T(8,128)S(1)} %get-tuple-element.5.refs_0_), channel_id=1, source_target_pairs={{3,1},{0,2},{5,3},{2,4},{7,5},{4,6},{9,7},{6,8},{11,9},{8,10},{13,... | collective-permute-start | bytes 344072 | tf_op jit(solution)/shard_map/ppermute | solution.py:437
  7.6 0.7 %collective-permute-start = (f32[7,8,512]{2,1,0:T(8,128)S(1)}, f32[7,8,512]{2,1,0:T(8,128)S(1)}, u32[]{:S(2)}, u32[]{:S(2)}) collective-permute-start(f32[7,8,512]{2,1,0:T(8,128)S(1)} %get-tuple-element.5.refs_0_), channel_id=1, source_target_pairs={{0,1},{1,0},{2,3},{3,2},{4,5},{5,4},{6,7},{7,6},{8,9},{9,8},{10,11... | collective-permute-start | bytes 344072 | tf_op jit(solution)/shard_map/ppermute | solution.py:425
  8.3 2.0 %collective-permute-done.5 = f32[7,8,512]{2,1,0:T(8,128)S(1)} collective-permute-done((f32[7,8,512]{2,1,0:T(8,128)S(1)}, f32[7,8,512]{2,1,0:T(8,128)S(1)}, u32[]{:S(2)}, u32[]{:S(2)}) %collective-permute-start.5) | collective-permute-done | bytes 114720 | tf_op jit(solution)/shard_map/ppermute | solution.py:437
  10.3 0.0 collective-permute-start.6
  10.3 0.0 collective-permute-done.3.refs_4_
  10.3 3.4 %collective-permute-start.4 = (f32[7,8,512]{2,1,0:T(8,128)S(1)}, f32[7,8,512]{2,1,0:T(8,128)S(1)}, u32[]{:S(2)}, u32[]{:S(2)}) collective-permute-start(f32[7,8,512]{2,1,0:T(8,128)S(1)} %collective-permute-done.3.refs_4_), channel_id=1, source_target_pairs={{0,1},{1,0},{2,3},{3,2},{4,5},{5,4},{6,7},{7,6},{8,9},{9,8},{10,11... | collective-permute-start | bytes 344072 | tf_op jit(solution)/shard_map/ppermute | solution.py:425
  13.7 0.0 collective-permute-done.1.refs_2_
  13.8 0.0 collective-permute-start.2
  13.8 0.0 collective-permute-done.refs_1_
  13.8 0.0 collective-permute-done.6.refs_6_
  13.8 0.9 %collective-permute-done.4.refs_5_ = f32[7,8,512]{2,1,0:T(8,128)S(1)} collective-permute-done((f32[7,8,512]{2,1,0:T(8,128)S(1)}, f32[7,8,512]{2,1,0:T(8,128)S(1)}, u32[]{:S(2)}, u32[]{:S(2)}) %collective-permute-start.4) | collective-permute-done | bytes 114720 | tf_op jit(solution)/shard_map/ppermute | solution.py:425
  14.7 0.4 %collective-permute-done.2.refs_3_ = f32[7,8,512]{2,1,0:T(8,128)S(1)} collective-permute-done((f32[7,8,512]{2,1,0:T(8,128)S(1)}, f32[7,8,512]{2,1,0:T(8,128)S(1)}, u32[]{:S(2)}, u32[]{:S(2)}) %collective-permute-start.2) | collective-permute-done | bytes 114720 | tf_op jit(solution)/shard_map/ppermute | solution.py:425
  15.1 5.4 %update.1 = (f32[3,8,1024]{2,1,0:T(8,128)}, f32[2,64,1024]{2,1,0:T(8,128)}) custom-call(s32[8]{0:T(128)} %angle_ref.3, s32[8]{0:T(128)} %lift_ref.1, s32[4]{0:T(128)} %subset_ref.3, f32[2,64,1024]{2,1,0:T(8,128)} %volume_ref.3, f32[3,8,1024]{2,1,0:T(8,128)} %measured_ref.3, f32[8,1024]{1,0:T(8,128)S(1)} %get-tuple-element.4.cover_ref, ...), custom_call_target="tpu_custom_call" | custom-call | tf_op jit(solution)/shard_map/update/pallas_call | solution.py:481
Async XLA Ops:
  4.5 5.8 %collective-permute-start.5 = (f32[7,8,512]{2,1,0:T(8,128)S(1)}, f32[7,8,512]{2,1,0:T(8,128)S(1)}, u32[]{:S(2)}, u32[]{:S(2)}) collective-permute-start(f32[7,8,512]{2,1,0:T(8,128)S(1)} %get-tuple-element.5.refs_0_), channel_id=1, source_target_pairs={{4,0},{6,2},{8,4},{1,5},{10,6},{3,7},{12,8},{5,9},{14,10},{7,11},{... | collective-permute-start | bytes 344072 | tf_op jit(solution)/shard_map/ppermute | solution.py:437
  5.0 5.4 %collective-permute-start.3 = (f32[7,8,512]{2,1,0:T(8,128)S(1)}, f32[7,8,512]{2,1,0:T(8,128)S(1)}, u32[]{:S(2)}, u32[]{:S(2)}) collective-permute-start(f32[7,8,512]{2,1,0:T(8,128)S(1)} %get-tuple-element.5.refs_0_), channel_id=1, source_target_pairs={{2,0},{4,2},{1,3},{6,4},{3,5},{8,6},{5,7},{10,8},{7,9},{12,10},{9,... | collective-permute-start | bytes 344072 | tf_op jit(solution)/shard_map/ppermute | solution.py:437
  7.1 6.7 %collective-permute-start.1 = (f32[7,8,512]{2,1,0:T(8,128)S(1)}, f32[7,8,512]{2,1,0:T(8,128)S(1)}, u32[]{:S(2)}, u32[]{:S(2)}) collective-permute-start(f32[7,8,512]{2,1,0:T(8,128)S(1)} %get-tuple-element.5.refs_0_), channel_id=1, source_target_pairs={{3,1},{0,2},{5,3},{2,4},{7,5},{4,6},{9,7},{6,8},{11,9},{8,10},{13,... | collective-permute-start | bytes 344072 | tf_op jit(solution)/shard_map/ppermute | solution.py:437
  7.6 6.1 %collective-permute-start = (f32[7,8,512]{2,1,0:T(8,128)S(1)}, f32[7,8,512]{2,1,0:T(8,128)S(1)}, u32[]{:S(2)}, u32[]{:S(2)}) collective-permute-start(f32[7,8,512]{2,1,0:T(8,128)S(1)} %get-tuple-element.5.refs_0_), channel_id=1, source_target_pairs={{0,1},{1,0},{2,3},{3,2},{4,5},{5,4},{6,7},{7,6},{8,9},{9,8},{10,11... | collective-permute-start | bytes 344072 | tf_op jit(solution)/shard_map/ppermute | solution.py:425
  10.3 3.5 %collective-permute-start.6 = (f32[7,8,512]{2,1,0:T(8,128)S(1)}, f32[7,8,512]{2,1,0:T(8,128)S(1)}, u32[]{:S(2)}, u32[]{:S(2)}) collective-permute-start(f32[7,8,512]{2,1,0:T(8,128)S(1)} %collective-permute-done.5), channel_id=1, source_target_pairs={{0,1},{1,0},{2,3},{3,2},{4,5},{5,4},{6,7},{7,6},{8,9},{9,8},{10,11... | collective-permute-start | bytes 344072 | tf_op jit(solution)/shard_map/ppermute | solution.py:425
  10.3 4.4 %collective-permute-start.4 = (f32[7,8,512]{2,1,0:T(8,128)S(1)}, f32[7,8,512]{2,1,0:T(8,128)S(1)}, u32[]{:S(2)}, u32[]{:S(2)}) collective-permute-start(f32[7,8,512]{2,1,0:T(8,128)S(1)} %collective-permute-done.3.refs_4_), channel_id=1, source_target_pairs={{0,1},{1,0},{2,3},{3,2},{4,5},{5,4},{6,7},{7,6},{8,9},{9,8},{10,11... | collective-permute-start | bytes 344072 | tf_op jit(solution)/shard_map/ppermute | solution.py:425
  13.8 1.3 %collective-permute-start.2 = (f32[7,8,512]{2,1,0:T(8,128)S(1)}, f32[7,8,512]{2,1,0:T(8,128)S(1)}, u32[]{:S(2)}, u32[]{:S(2)}) collective-permute-start(f32[7,8,512]{2,1,0:T(8,128)S(1)} %collective-permute-done.1.refs_2_), channel_id=1, source_target_pairs={{0,1},{1,0},{2,3},{3,2},{4,5},{5,4},{6,7},{7,6},{8,9},{9,8},{10,11... | collective-permute-start | bytes 344072 | tf_op jit(solution)/shard_map/ppermute | solution.py:425

commit v4 on v3

--- a/solution.py
+++ b/solution.py
@@ -102,6 +102,104 @@
     offset = (row + 0.5 - row_count / 2) * tangent
     whole = jnp.floor(offset)
     return whole.astype(jnp.int32), offset - whole
+
+
+def cone_sample(rows, lifts, flat, total_rows, total_slices):
+    return (rows + 0.5 - total_rows / 2 - lifts) * flat + (total_slices / 2 - 0.5)
+
+
+def cone_total(sample, total_slices):
+    whole = jnp.floor(sample)
+    fraction = sample - whole
+    low = jnp.where((whole >= 0) & (whole < total_slices), 1.0 - fraction, 0.0)
+    return low + jnp.where((whole >= -1) & (whole < total_slices - 1), fraction, 0.0)
+
+
+def column_of(tile, at):
+    return jnp.broadcast_to(tile[:, at : at + 1], (SUBLANES, LANES))
+
+
+def subset_cone(slab, slab_count, order, slab_depth, row_share, flat, lifts):
+    lane = lane_index()
+    total_rows, total_slices = row_share * slab_count, slab_depth * slab_count
+    origin = slabs_of(slab, order)
+    source = sum(jnp.where(lane >= row_share * b, 1, 0) for b in range(1, len(order)))
+    rows = spread_scalars(lambda b: origin[b], len(order), source) * row_share + (lane - source * row_share)
+    real = (rows >= 0) & (rows < total_rows) & (lane < row_share * len(order))
+    sample = cone_sample(rows.astype(F32), lifts, flat, total_rows, total_slices)
+    weights = []
+    for z in range(-1, slab_depth + 1):
+        at = slab * slab_depth + z
+        use = real & (at >= 0) & (at < total_slices)
+        weights.append(jnp.where(use, jnp.maximum(0.0, 1.0 - jnp.abs(sample - at.astype(F32))), 0.0))
+    return sample, weights
+
+
+def slabs_of(slab, order):
+    return [slab + (1 - 2 * lax.rem(slab, 2)) * away for away in order]
+
+
+def adjoint_taps(tile, cosine, column_count, cell_count, half):
+    spacing = PITCH * cell_count / column_count
+    least = angle_table()[0].min()
+    lane = lane_index()
+    cell = (lane + (tile * LANES - half)).astype(F32)
+    inside = (cell >= 0) & (cell < cell_count)
+    first = jnp.floor((cell - (cell_count / 2 + 0.5)) * cosine * (1.0 / spacing) + (column_count / 2 - 0.5 - 1e-3)) + 1.0
+    ends = [
+        (tile * LANES - half + e - cell_count / 2 - 0.5) * c / spacing + column_count / 2 + 0.5
+        for e in (0, LANES - 1)
+        for c in (1.0, least)
+    ]
+    taps = []
+    for tap in range(3):
+        column = first + tap
+        weight = jnp.maximum(0.0, 1.0 - jnp.abs(cell - column_center(column, cosine, column_count, cell_count)))
+        weight = jnp.where(inside & (column >= 0) & (column < column_count), weight, 0.0)
+        place = jnp.clip(column.astype(jnp.int32), 0, column_count - 1)
+        low = min(max(math.floor(min(ends) + tap - 0.6), 0), column_count - 1) // LANES
+        high = min(max(math.ceil(max(ends) + tap + 0.6), 0), column_count - 1) // LANES
+        taps.append((place, weight, range(low, high + 1)))
+    return taps
+
+
+def store_line(line, base_ref, bend_ref):
+    line = line + [jnp.zeros((SUBLANES, LANES), F32)]
+    for tile in range(len(line) - 1):
+        cut = slice(tile * LANES, (tile + 1) * LANES)
+        base_ref[:, cut] = line[tile]
+        bend_ref[:, cut] = next_lane(line[tile], line[tile + 1]) - line[tile]
+
+
+def adjoint_steps(group, row_count, tangent):
+    whole, fraction = shear_steps(group, row_count, tangent)
+    place = lane_index() + (row_count // 2 - 1 - whole)
+    return jnp.bitwise_and(place, LANES - 1), place < LANES, 1.0 - fraction
+
+
+def sheared(base_ref, bend_ref, row, step, tiles):
+    index, near, share = step
+    before, out = None, []
+    for tile in range(tiles + 1):
+        cut = slice(tile * LANES, (tile + 1) * LANES)
+        low = pick(jnp.broadcast_to(base_ref[row : row + 1, cut], (SUBLANES, LANES)), index)
+        rise = pick(jnp.broadcast_to(bend_ref[row : row + 1, cut], (SUBLANES, LANES)), index)
+        after = low + share * rise
+        if tile:
+            out.append(jnp.where(near, before, after))
+        before = after
+    return out
+
+
+def subset_angles(angle_ref, lift_ref, subset_ref):
+    members = subset_ref.shape[0]
+    member = jnp.bitwise_and(sublane_index(), members - 1)
+    cosine, _, flat = angle_facts(spread_scalars(lambda k: angle_ref[subset_ref[k]], members, member))
+    lifts = spread_scalars(lambda k: lift_ref[subset_ref[k]], members, member).astype(F32)
+    tangents = [
+        angle_facts(jnp.full((SUBLANES, LANES), angle_ref[subset_ref[k]], jnp.int32))[1] for k in range(members)
+    ]
+    return cosine, flat, lifts, tangents
 
 
 def project_kernel(
@@ -216,6 +314,71 @@
                 block_ref[depth * 2 + side, :, inner : inner + LANES] = profile
 
 
+def divisor_kernel(
+    slab_count, order, angle_ref, lift_ref, subset_ref, cover_ref, bound_ref, own_ref, rows_ref, edge_ref, bend_ref, sub_ref
+):
+    slab_depth, row_count, cell_count = bound_ref.shape
+    row_share, view_count, column_count = own_ref.shape
+    subset_count = subset_ref.shape[0]
+    total_rows, total_slices = row_share * slab_count, slab_depth * slab_count
+    tiles, columns = cell_count // LANES, column_count // LANES
+    width = column_count // 2
+    sub = sublane_index()
+    zero = jnp.zeros((SUBLANES, LANES), F32)
+    slab = lax.axis_index("slab")
+
+    _, _, flat = angle_facts(spread_scalars(lambda v: angle_ref[v], view_count, sub))
+    lifts = spread_scalars(lambda v: lift_ref[v], view_count, sub).astype(F32)
+    for row in range(row_share):
+        sample = cone_sample((slab * row_share + row).astype(F32), lifts, flat, total_rows, total_slices)
+        total = cone_total(sample, total_slices)
+        for tile in range(columns):
+            cut = slice(tile * LANES, (tile + 1) * LANES)
+            own_ref[row, :, cut] = 1.0 / jnp.maximum(total * cover_ref[:, cut], LEN_FLOOR)
+
+    cosine, flat, lifts, tangents = subset_angles(angle_ref, lift_ref, subset_ref)
+    for member in range(subset_count):
+        view = pl.ds(subset_ref[member], 1)
+        for side in range(2):
+            at = slice(side * subset_count + member, side * subset_count + member + 1)
+            sub_ref[at, :] = cover_ref[view, side * width : (side + 1) * width]
+    sample, weights = subset_cone(slab, slab_count, order, slab_depth, row_share, flat, lifts)
+    total = cone_total(sample, total_slices)
+    for place in range(row_share * len(order)):
+        length = column_of(total, place)
+        for tile in range(width // LANES):
+            cut = slice(tile * LANES, (tile + 1) * LANES)
+            rows_ref[place, :, cut] = 1.0 / jnp.maximum(length * sub_ref[:, cut], LEN_FLOOR)
+
+    factor = 1.0 / (row_count * cosine)
+    line = []
+    for tile in range(tiles + 1):
+        taps = adjoint_taps(tile, cosine, column_count, cell_count, row_count // 2)
+        line.append(sum(weight for _, weight, _ in taps) * factor)
+    store_line(line, edge_ref, bend_ref)
+    slice_total = []
+    for depth in range(slab_depth):
+        t = jnp.sum(weights[1 + depth], axis=1, keepdims=True)
+        slice_total.append([jnp.broadcast_to(t[k : k + 1], (SUBLANES, LANES)) for k in range(subset_count)])
+
+    def one_group(group, carry):
+        band = pl.ds(pl.multiple_of(group * SUBLANES, SUBLANES), SUBLANES)
+        weight = [[zero] * tiles for _ in range(slab_depth)]
+        for member in range(subset_count):
+            line = sheared(edge_ref, bend_ref, member, adjoint_steps(group, row_count, tangents[member]), tiles)
+            for depth in range(slab_depth):
+                for tile in range(tiles):
+                    weight[depth][tile] = weight[depth][tile] + slice_total[depth][member] * line[tile]
+        for depth in range(slab_depth):
+            for tile in range(tiles):
+                bound_ref[depth, band, tile * LANES : (tile + 1) * LANES] = 1.0 / jnp.maximum(
+                    weight[depth][tile], LEN_FLOOR * subset_count / row_count
+                )
+        return carry
+
+    lax.fori_loop(0, row_count // SUBLANES, one_group, 0)
+
+
 def update_kernel(
     slab_count,
     order,
@@ -224,49 +387,35 @@
     subset_ref,
     volume_ref,
     measured_ref,
-    cover_ref,
+    bound_ref,
+    own_ref,
+    rows_ref,
     *refs,
 ):
     blocks = refs[: len(order)]
-    residual_ref, updated_ref, profile_ref, cover_sub_ref, spread_ref, cell_ref, slope_ref, edge_ref, bend_ref = refs[
-        len(order) :
-    ]
+    residual_ref, updated_ref, profile_ref, spread_ref, cell_ref, slope_ref = refs[len(order) :]
     slab_depth, row_count, cell_count = volume_ref.shape
     row_share, view_count, column_count = measured_ref.shape
     subset_count = subset_ref.shape[0]
     total_rows, total_slices = row_share * slab_count, slab_depth * slab_count
-    half = row_count // 2
     tiles, columns = cell_count // LANES, column_count // LANES
     width = column_count // 2
     lane, sub = lane_index(), sublane_index()
     zero = jnp.zeros((SUBLANES, LANES), F32)
     slab = lax.axis_index("slab")
     odd = lax.rem(slab, 2)
-    origin = [slab + (1 - 2 * odd) * away for away in order]
+    origin = slabs_of(slab, order)
     mate_block, other_block = (blocks[order.index(away)] for away in (1, -1))
-
-    def cone(rows, lifts, flat):
-        return (rows + 0.5 - total_rows / 2 - lifts) * flat + (total_slices / 2 - 0.5)
-
-    def cone_total(sample):
-        whole = jnp.floor(sample)
-        fraction = sample - whole
-        low = jnp.where((whole >= 0) & (whole < total_slices), 1.0 - fraction, 0.0)
-        return low + jnp.where((whole >= -1) & (whole < total_slices - 1), fraction, 0.0)
-
-    def column_of(tile, at):
-        return jnp.broadcast_to(tile[:, at : at + 1], (SUBLANES, LANES))
 
     _, _, flat = angle_facts(spread_scalars(lambda v: angle_ref[v], view_count, sub))
     lifts = spread_scalars(lambda v: lift_ref[v], view_count, sub).astype(F32)
-    source = jnp.right_shift(lane, slab_depth.bit_length() - 1) if slab_depth & (slab_depth - 1) == 0 else lane // slab_depth
-    slices = spread_scalars(lambda b: origin[b], len(blocks), source) * slab_depth + (lane - source * slab_depth)
+    source = sum(jnp.where(lane >= slab_depth * b, 1, 0) for b in range(1, len(order)))
+    slices = spread_scalars(lambda b: origin[b], len(order), source) * slab_depth + (lane - source * slab_depth)
     held = (slices >= 0) & (slices < total_slices)
     slices = slices.astype(F32)
     for row in range(row_share):
-        sample = cone((slab * row_share + row).astype(F32), lifts, flat)
+        sample = cone_sample((slab * row_share + row).astype(F32), lifts, flat, total_rows, total_slices)
         weights = jnp.where(held, jnp.maximum(0.0, 1.0 - jnp.abs(sample - slices)), 0.0)
-        total = cone_total(sample)
         image = [zero] * columns
         for place, block in enumerate(blocks):
             for depth in range(slab_depth):
@@ -276,18 +425,14 @@
                     image[tile] = image[tile] + weight * block[depth * 2 + side, :, inner : inner + LANES]
         for tile in range(columns):
             cut = slice(tile * LANES, (tile + 1) * LANES)
-            length = total * cover_ref[:, cut]
-            residual_ref[row, :, cut] = (measured_ref[row, :, cut] - image[tile]) / jnp.maximum(length, LEN_FLOOR)
-
-    member_of = jnp.bitwise_and(sub, subset_count - 1)
-    cosine, _, flat = angle_facts(spread_scalars(lambda k: angle_ref[subset_ref[k]], subset_count, member_of))
-    lifts = spread_scalars(lambda k: lift_ref[subset_ref[k]], subset_count, member_of).astype(F32)
+            residual_ref[row, :, cut] = (measured_ref[row, :, cut] - image[tile]) * own_ref[row, :, cut]
+
+    cosine, flat, lifts, tangents = subset_angles(angle_ref, lift_ref, subset_ref)
     factor = 1.0 / (row_count * cosine)
     for member in range(subset_count):
         view = pl.ds(subset_ref[member], 1)
         for side in range(2):
             at = slice(side * subset_count + member, side * subset_count + member + 1)
-            cover_sub_ref[at, :] = cover_ref[view, side * width : (side + 1) * width]
             other = other_block[(slab_depth - 1) * 2 + side, view, :], other_block[side, view, :]
             mate = mate_block[(slab_depth - 1) * 2 + side, view, :], mate_block[side, view, :]
             profile_ref[0, at, :] = jnp.where(odd == 0, other[0], mate[0])
@@ -295,31 +440,18 @@
                 profile_ref[1 + depth, at, :] = blocks[0][depth * 2 + side, view, :]
             profile_ref[1 + slab_depth, at, :] = jnp.where(odd == 0, mate[1], other[1])
 
-    rows_here = row_share * len(blocks)
-    source = sum(jnp.where(lane >= row_share * b, 1, 0) for b in range(1, len(blocks)))
-    rows = spread_scalars(lambda b: origin[b], len(blocks), source) * row_share + (lane - source * row_share)
-    real = (rows >= 0) & (rows < total_rows) & (lane < rows_here)
-    sample = cone(rows.astype(F32), lifts, flat)
-    total = cone_total(sample)
-    weights = []
-    for z in range(-1, slab_depth + 1):
-        at = slab * slab_depth + z
-        use = real & (at >= 0) & (at < total_slices)
-        weights.append(jnp.where(use, jnp.maximum(0.0, 1.0 - jnp.abs(sample - at.astype(F32))), 0.0))
+    _, weights = subset_cone(slab, slab_count, order, slab_depth, row_share, flat, lifts)
     inner_tiles = width // LANES
     spread = [[zero] * inner_tiles for _ in range(slab_depth)]
-    for place in range(rows_here):
+    for place in range(row_share * len(order)):
         weight = [column_of(w, place) for w in weights]
-        length = column_of(total, place)
         block, row = blocks[place // row_share], place % row_share
         for tile in range(inner_tiles):
             cut = slice(tile * LANES, (tile + 1) * LANES)
             image = weight[0] * profile_ref[0, :, cut]
             for z in range(1, slab_depth + 2):
                 image = image + weight[z] * profile_ref[z, :, cut]
-            rest = (block[2 * slab_depth + row, :, cut] - image) / jnp.maximum(
-                length * cover_sub_ref[:, cut], LEN_FLOOR
-            )
+            rest = (block[2 * slab_depth + row, :, cut] - image) * rows_ref[place, :, cut]
             for depth in range(slab_depth):
                 spread[depth][tile] = spread[depth][tile] + weight[1 + depth] * rest
     for depth in range(slab_depth):
@@ -330,92 +462,29 @@
                     side * width + tile * LANES : side * width + (tile + 1) * LANES,
                 ] = spread[depth][tile][side * subset_count : (side + 1) * subset_count]
 
-    least = angle_table()[0].min()
-    spacing = PITCH * cell_count / column_count
-    shifted, edges = [], []
+    line = []
     for tile in range(tiles + 1):
-        cell = (lane + (tile * LANES - half)).astype(F32)
-        inside = (cell >= 0) & (cell < cell_count)
-        first = jnp.floor((cell - (cell_count / 2 + 0.5)) * cosine * (1.0 / spacing) + (column_count / 2 - 0.5 - 1e-3)) + 1.0
-        ends = [
-            (tile * LANES - half + e - cell_count / 2 - 0.5) * c / spacing + column_count / 2 + 0.5
-            for e in (0, LANES - 1)
-            for c in (1.0, least)
-        ]
-        value, edge = zero, zero
-        for tap in range(3):
-            column = first + tap
-            weight = jnp.maximum(0.0, 1.0 - jnp.abs(cell - column_center(column, cosine, column_count, cell_count)))
-            weight = jnp.where(inside & (column >= 0) & (column < column_count), weight, 0.0)
-            place = jnp.clip(column.astype(jnp.int32), 0, column_count - 1)
+        value = zero
+        for place, weight, at_tiles in adjoint_taps(tile, cosine, column_count, cell_count, row_count // 2):
             block, index = jnp.right_shift(place, 7), jnp.bitwise_and(place, LANES - 1)
-            low = min(max(math.floor(min(ends) + tap - 0.6), 0), column_count - 1) // LANES
-            high = min(max(math.ceil(max(ends) + tap + 0.6), 0), column_count - 1) // LANES
             found = zero
-            for at in range(low, high + 1):
+            for at in at_tiles:
                 found = jnp.where(block == at, pick(tile_of(spread_ref, (), at), index), found)
             value = value + weight * found
-            edge = edge + weight
-        shifted.append(value * factor)
-        edges.append(edge * factor)
-    shifted.append(zero)
-    edges.append(zero)
-    for tile in range(tiles + 1):
-        cut = slice(tile * LANES, (tile + 1) * LANES)
-        cell_ref[:, cut] = shifted[tile]
-        slope_ref[:, cut] = next_lane(shifted[tile], shifted[tile + 1]) - shifted[tile]
-        edge_ref[:, cut] = edges[tile]
-        bend_ref[:, cut] = next_lane(edges[tile], edges[tile + 1]) - edges[tile]
-
-    slice_total = [jnp.sum(weights[1 + depth], axis=1, keepdims=True) for depth in range(slab_depth)]
-    slice_total = [
-        [jnp.broadcast_to(t[k : k + 1], (SUBLANES, LANES)) for k in range(subset_count)] for t in slice_total
-    ]
-    tangents = [
-        angle_facts(jnp.full((SUBLANES, LANES), angle_ref[subset_ref[k]], jnp.int32))[1] for k in range(subset_count)
-    ]
+        line.append(value * factor)
+    store_line(line, cell_ref, slope_ref)
 
     def one_group(group, carry):
         band = pl.ds(pl.multiple_of(group * SUBLANES, SUBLANES), SUBLANES)
-        steps = []
-        for member in range(subset_count):
-            whole, fraction = shear_steps(group, row_count, tangents[member])
-            place = lane + (half - 1 - whole)
-            steps.append((jnp.bitwise_and(place, LANES - 1), place < LANES, 1.0 - fraction))
-
-        def sheared(base_ref, bend, row, member):
-            index, near, share = steps[member]
-            before = None
-            out = []
-            for tile in range(tiles + 1):
-                cut = slice(tile * LANES, (tile + 1) * LANES)
-                low = pick(jnp.broadcast_to(base_ref[row : row + 1, cut], (SUBLANES, LANES)), index)
-                rise = pick(jnp.broadcast_to(bend[row : row + 1, cut], (SUBLANES, LANES)), index)
-                after = low + share * rise
-                if tile:
-                    out.append(jnp.where(near, before, after))
-                before = after
-            return out
-
-        weight = [[zero] * tiles for _ in range(slab_depth)]
-        for member in range(subset_count):
-            line = sheared(edge_ref, bend_ref, member, member)
-            for depth in range(slab_depth):
-                for tile in range(tiles):
-                    weight[depth][tile] = weight[depth][tile] + slice_total[depth][member] * line[tile]
-        for depth in range(slab_depth):
-            for tile in range(tiles):
-                updated_ref[depth, band, tile * LANES : (tile + 1) * LANES] = jnp.maximum(
-                    weight[depth][tile], LEN_FLOOR * subset_count / row_count
-                )
+        steps = [adjoint_steps(group, row_count, tangent) for tangent in tangents]
         for depth in range(slab_depth):
             back = [zero] * tiles
             for member in range(subset_count):
-                line = sheared(cell_ref, slope_ref, depth * subset_count + member, member)
+                line = sheared(cell_ref, slope_ref, depth * subset_count + member, steps[member], tiles)
                 back = [b + a for b, a in zip(back, line)]
             for tile in range(tiles):
                 cut = slice(tile * LANES, (tile + 1) * LANES)
-                updated_ref[depth, band, cut] = volume_ref[depth, band, cut] + back[tile] / updated_ref[depth, band, cut]
+                updated_ref[depth, band, cut] = volume_ref[depth, band, cut] + back[tile] * bound_ref[depth, band, cut]
         return carry
 
     lax.fori_loop(0, row_count // SUBLANES, one_group, 0)
@@ -437,20 +506,29 @@
     return lax.ppermute(block, "slab", pairs)
 
 
-def gathered(own, reach):
-    received = {}
-    for distance in range(1, reach // 2 + 2):
-        for sign in (-1, 1):
-            if 2 * distance - (sign > 0) <= reach:
-                received[sign * distance] = from_chip(own, sign * distance)
+def fetches(reach):
+    return [s * d for d in range(1, reach // 2 + 2) for s in (-1, 1) if 2 * d - (s > 0) <= reach]
+
+
+def window(reach):
+    order = [0, 1]
+    for distance in fetches(reach):
+        order += [at for at in (2 * distance, 1 - 2 * distance) if abs(at) <= reach]
+    assert sorted(order) == list(range(-reach, reach + 1))
+    return tuple(order)
+
+
+def gathered(own, reach, meanwhile):
+    received = [from_chip(own, distance) for distance in fetches(reach)]
     blocks = {0: own, 1: swapped(own)}
-    for distance, block in received.items():
+    done = meanwhile()
+    received, done = lax.optimization_barrier((received, done))
+    for distance, block in zip(fetches(reach), received):
         if 2 * abs(distance) <= reach:
             blocks[2 * distance] = block
         if abs(1 - 2 * distance) <= reach:
             blocks[1 - 2 * distance] = swapped(block)
-    assert sorted(blocks) == list(range(-reach, reach + 1))
-    return blocks
+    return [blocks[away] for away in window(reach)], done
 
 
 def per_device(volume, measured, view_angle, view_lift, subset):
@@ -475,25 +553,38 @@
         + [pltpu.VMEM((slab_depth + 1, SUBLANES, wide), F32)] * 2,
         name="project",
     )(view_angle, subset, volume, measured)
-    blocks = gathered(own, reach)
-    order = tuple(blocks)
     here = lambda x: pltpu.with_memory_space_constraint(x, pltpu.VMEM)
+    cover = here(cover)
+    order = window(reach)
+    divide = pl.pallas_call(
+        functools.partial(divisor_kernel, slab_count, order),
+        out_shape=(
+            pltpu.VMEM(volume.shape, F32),
+            pltpu.VMEM(measured.shape, F32),
+            pltpu.VMEM((row_share * len(order), SUBLANES, column_count // 2), F32),
+        ),
+        in_specs=[smem] * 3 + [vmem],
+        out_specs=(vmem,) * 3,
+        scratch_shapes=[pltpu.VMEM((SUBLANES, wide), F32)] * 2 + [pltpu.VMEM((SUBLANES, column_count // 2), F32)],
+        cost_estimate=pl.CostEstimate(flops=4_000_000, bytes_accessed=8_000_000, transcendentals=0),
+        name="divisors",
+    )
+    blocks, divisors = gathered(own, reach, lambda: divide(view_angle, view_lift, subset, cover))
     return pl.pallas_call(
         functools.partial(update_kernel, slab_count, order),
         out_shape=(
             jax.ShapeDtypeStruct(measured.shape, F32),
             jax.ShapeDtypeStruct(volume.shape, F32),
         ),
-        in_specs=[smem] * 3 + [vmem] * (3 + 1 + 2 * reach),
+        in_specs=[smem] * 3 + [vmem] * (5 + len(order)),
         out_specs=(vmem, vmem),
         scratch_shapes=[
             pltpu.VMEM((slab_depth + 2, SUBLANES, column_count // 2), F32),
-            pltpu.VMEM((SUBLANES, column_count // 2), F32),
             pltpu.VMEM((SUBLANES, column_count), F32),
         ]
-        + [pltpu.VMEM((SUBLANES, wide), F32)] * 4,
+        + [pltpu.VMEM((SUBLANES, wide), F32)] * 2,
         name="update",
-    )(view_angle, view_lift, subset, volume, measured, here(cover), *map(here, blocks.values()))
+    )(view_angle, view_lift, subset, volume, measured, *map(here, (*divisors, *blocks)))
 
 
 def solution(mesh):

time: 20.6 us -> 20.2 us (0.981)
  starting transfers between devices: 7.27 us -> 4.51 us
  Pallas kernels: 9.23 us -> 10.8 us
  waiting for transfers between devices: 3.3 us -> 4.07 us
    ppermute x4, starting transfers between devices: 4.15 us -> 1.38 us  [swapped(): lax.ppermute(block, 'slab', [(i, i ^ 1) for i in range(lax.axis_size('sla...]
    pallas_call x0 -> x1, Pallas kernels: none -> 2.33 us  [per_device(): divide(view_angle, view_lift, subset, cover)]
    ppermute x3, waiting for transfers between devices: 1.99 us -> 2.9 us  [from_chip(): return lax.ppermute(block, 'slab', pairs)]
    pallas_call x1, Pallas kernels: 5.37 us -> 4.63 us  [per_device(): pl.pallas_call(functools.partial(update_kernel, slab_count, order), out_s...]
  transfers between devices with their start and end apart: 7 -> 7, of which waited for: 3 -> 4; matrix products, arithmetic and copies ran while one was open for 0% -> 0% of each run, Pallas kernels for 0% -> 12%
where the time goes in v4:
time: 20.2 us; the launch traced here: 20.1 us
  Pallas kernels  10.8 us (53%)
  starting transfers between devices  4.51 us (22%)
  waiting for transfers between devices  4.07 us (20%)
  between operations  0.66 us (3%)
    pallas_call x1, Pallas kernels, per_device(): pl.pallas_call(functools.partial(update_kernel, slab_count, order), out_s...  4.63 us
    pallas_call x1, Pallas kernels, per_device(): pl.pallas_call(project_kernel, out_shape=(pltpu.VMEM(block_shape, F32), p...  3.86 us
    ppermute x3, starting transfers between devices, from_chip(): return lax.ppermute(block, 'slab', pairs)  3.12 us
    ppermute x3, waiting for transfers between devices, from_chip(): return lax.ppermute(block, 'slab', pairs)  2.9 us
    pallas_call x1, Pallas kernels, per_device(): divide(view_angle, view_lift, subset, cover)  2.33 us
    ppermute x4, starting transfers between devices, swapped(): lax.ppermute(block, 'slab', [(i, i ^ 1) for i in range(lax.axis_size('sla...  1.38 us
    ppermute x4, waiting for transfers between devices, swapped(): lax.ppermute(block, 'slab', [(i, i ^ 1) for i in range(lax.axis_size('sla...  1.16 us
  transfers between devices with their start and end apart: 7, of which 4 were waited for; matrix products, arithmetic and copies ran while one was open for 0% of the time, Pallas kernels for 12%

profile of v4, /device:TPU:0, one launch (start us, length us, event | category | flops | bytes accessed | tf_op | source)
XLA Modules:
  0.0 20.1 jit_solution(10779990828997012257)
XLA Ops:
  0.6 3.9 %project.1 = (f32[7,8,512]{2,1,0:T(8,128)S(1)}, f32[8,1024]{1,0:T(8,128)S(1)}) custom-call(s32[8]{0:T(128)} %angle_ref.5, s32[4]{0:T(128)} %subset_ref.5, f32[2,64,1024]{2,1,0:T(8,128)} %volume_ref.3, f32[3,8,1024]{2,1,0:T(8,128)} %measured_ref.3), custom_call_target="tpu_custom_call" | custom-call | tf_op jit(solution)/shard_map/project/pallas_call | solution.py:544
  4.5 0.5 %collective-permute-start.2 = (f32[7,8,512]{2,1,0:T(8,128)S(1)}, f32[7,8,512]{2,1,0:T(8,128)S(1)}, u32[]{:S(2)}, u32[]{:S(2)}) collective-permute-start(f32[7,8,512]{2,1,0:T(8,128)S(1)} %get-tuple-element.13.refs_0_), channel_id=1, source_target_pairs={{4,0},{6,2},{8,4},{1,5},{10,6},{3,7},{12,8},{5,9},{14,10},{7,11},{... | collective-permute-start | bytes 344072 | tf_op jit(solution)/shard_map/ppermute | solution.py:506
  5.0 2.1 %collective-permute-start.1 = (f32[7,8,512]{2,1,0:T(8,128)S(1)}, f32[7,8,512]{2,1,0:T(8,128)S(1)}, u32[]{:S(2)}, u32[]{:S(2)}) collective-permute-start(f32[7,8,512]{2,1,0:T(8,128)S(1)} %get-tuple-element.13.refs_0_), channel_id=1, source_target_pairs={{2,0},{4,2},{1,3},{6,4},{3,5},{8,6},{5,7},{10,8},{7,9},{12,10},{9,... | collective-permute-start | bytes 344072 | tf_op jit(solution)/shard_map/ppermute | solution.py:506
  7.1 0.5 %collective-permute-start = (f32[7,8,512]{2,1,0:T(8,128)S(1)}, f32[7,8,512]{2,1,0:T(8,128)S(1)}, u32[]{:S(2)}, u32[]{:S(2)}) collective-permute-start(f32[7,8,512]{2,1,0:T(8,128)S(1)} %get-tuple-element.13.refs_0_), channel_id=1, source_target_pairs={{3,1},{0,2},{5,3},{2,4},{7,5},{4,6},{9,7},{6,8},{11,9},{8,10},{13,... | collective-permute-start | bytes 344072 | tf_op jit(solution)/shard_map/ppermute | solution.py:506
  7.6 0.7 %collective-permute-start.3 = (f32[7,8,512]{2,1,0:T(8,128)S(1)}, f32[7,8,512]{2,1,0:T(8,128)S(1)}, u32[]{:S(2)}, u32[]{:S(2)}) collective-permute-start(f32[7,8,512]{2,1,0:T(8,128)S(1)} %get-tuple-element.13.refs_0_), channel_id=1, source_target_pairs={{0,1},{1,0},{2,3},{3,2},{4,5},{5,4},{6,7},{7,6},{8,9},{9,8},{10,11... | collective-permute-start | bytes 344072 | tf_op jit(solution)/shard_map/ppermute | solution.py:494
  8.3 2.3 %divisors.1 = (f32[2,64,1024]{2,1,0:T(8,128)S(1)}, f32[3,8,1024]{2,1,0:T(8,128)S(1)}, f32[21,8,512]{2,1,0:T(8,128)S(1)}) custom-call(s32[8]{0:T(128)} %angle_ref.5, s32[8]{0:T(128)} %lift_ref.3, s32[4]{0:T(128)} %subset_ref.5, f32[8,1024]{1,0:T(8,128)S(1)} %get-tuple-element.14.cover_ref), custom_call_target="tpu_custom_call" | custom-call | flops 4000000 | bytes 8000000 | tf_op jit(solution)/shard_map/divisors/pallas_call | solution.py:572
  10.7 0.0 collective-permute-done.2
  10.7 0.0 collective-permute-done.1.refs_4_
  10.7 2.9 %collective-permute-done.refs_2_ = f32[7,8,512]{2,1,0:T(8,128)S(1)} collective-permute-done((f32[7,8,512]{2,1,0:T(8,128)S(1)}, f32[7,8,512]{2,1,0:T(8,128)S(1)}, u32[]{:S(2)}, u32[]{:S(2)}) %collective-permute-start) | collective-permute-done | bytes 114720 | tf_op jit(solution)/shard_map/ppermute | solution.py:506
  13.6 0.2 collective-permute-start.6
  13.8 0.4 %collective-permute-start.4 = (f32[7,8,512]{2,1,0:T(8,128)S(1)}, f32[7,8,512]{2,1,0:T(8,128)S(1)}, u32[]{:S(2)}, u32[]{:S(2)}) collective-permute-start(f32[7,8,512]{2,1,0:T(8,128)S(1)} %collective-permute-done.refs_2_), channel_id=1, source_target_pairs={{0,1},{1,0},{2,3},{3,2},{4,5},{5,4},{6,7},{7,6},{8,9},{9,8},{10,11... | collective-permute-start | bytes 344072 | tf_op jit(solution)/shard_map/ppermute | solution.py:494
  14.1 0.2 collective-permute-start.5
  14.3 0.0 collective-permute-done.3.refs_1_
  14.3 0.7 %collective-permute-done.6.refs_6_ = f32[7,8,512]{2,1,0:T(8,128)S(1)} collective-permute-done((f32[7,8,512]{2,1,0:T(8,128)S(1)}, f32[7,8,512]{2,1,0:T(8,128)S(1)}, u32[]{:S(2)}, u32[]{:S(2)}) %collective-permute-start.6) | collective-permute-done | bytes 114720 | tf_op jit(solution)/shard_map/ppermute | solution.py:494
  14.9 0.2 collective-permute-done.4.refs_3_
  15.1 0.3 %collective-permute-done.5.refs_5_ = f32[7,8,512]{2,1,0:T(8,128)S(1)} collective-permute-done((f32[7,8,512]{2,1,0:T(8,128)S(1)}, f32[7,8,512]{2,1,0:T(8,128)S(1)}, u32[]{:S(2)}, u32[]{:S(2)}) %collective-permute-start.5) | collective-permute-done | bytes 114720 | tf_op jit(solution)/shard_map/ppermute | solution.py:494
  15.4 4.6 %update.1 = (f32[3,8,1024]{2,1,0:T(8,128)}, f32[2,64,1024]{2,1,0:T(8,128)}) custom-call(s32[8]{0:T(128)} %angle_ref.5, s32[8]{0:T(128)} %lift_ref.3, s32[4]{0:T(128)} %subset_ref.5, f32[2,64,1024]{2,1,0:T(8,128)} %volume_ref.3, f32[3,8,1024]{2,1,0:T(8,128)} %measured_ref.3, f32[2,64,1024]{2,1,0:T(8,128)S(1)} %get-tuple-element.18.bound_ref, ...), custom_call_target="tpu_custom_call" | custom-call | tf_op jit(solution)/shard_map/update/pallas_call | solution.py:573
Async XLA Ops:
  4.5 6.2 %collective-permute-start.2 = (f32[7,8,512]{2,1,0:T(8,128)S(1)}, f32[7,8,512]{2,1,0:T(8,128)S(1)}, u32[]{:S(2)}, u32[]{:S(2)}) collective-permute-start(f32[7,8,512]{2,1,0:T(8,128)S(1)} %get-tuple-element.13.refs_0_), channel_id=1, source_target_pairs={{4,0},{6,2},{8,4},{1,5},{10,6},{3,7},{12,8},{5,9},{14,10},{7,11},{... | collective-permute-start | bytes 344072 | tf_op jit(solution)/shard_map/ppermute | solution.py:506
  5.0 5.7 %collective-permute-start.1 = (f32[7,8,512]{2,1,0:T(8,128)S(1)}, f32[7,8,512]{2,1,0:T(8,128)S(1)}, u32[]{:S(2)}, u32[]{:S(2)}) collective-permute-start(f32[7,8,512]{2,1,0:T(8,128)S(1)} %get-tuple-element.13.refs_0_), channel_id=1, source_target_pairs={{2,0},{4,2},{1,3},{6,4},{3,5},{8,6},{5,7},{10,8},{7,9},{12,10},{9,... | collective-permute-start | bytes 344072 | tf_op jit(solution)/shard_map/ppermute | solution.py:506
  7.1 6.5 %collective-permute-start = (f32[7,8,512]{2,1,0:T(8,128)S(1)}, f32[7,8,512]{2,1,0:T(8,128)S(1)}, u32[]{:S(2)}, u32[]{:S(2)}) collective-permute-start(f32[7,8,512]{2,1,0:T(8,128)S(1)} %get-tuple-element.13.refs_0_), channel_id=1, source_target_pairs={{3,1},{0,2},{5,3},{2,4},{7,5},{4,6},{9,7},{6,8},{11,9},{8,10},{13,... | collective-permute-start | bytes 344072 | tf_op jit(solution)/shard_map/ppermute | solution.py:506
  7.6 6.6 %collective-permute-start.3 = (f32[7,8,512]{2,1,0:T(8,128)S(1)}, f32[7,8,512]{2,1,0:T(8,128)S(1)}, u32[]{:S(2)}, u32[]{:S(2)}) collective-permute-start(f32[7,8,512]{2,1,0:T(8,128)S(1)} %get-tuple-element.13.refs_0_), channel_id=1, source_target_pairs={{0,1},{1,0},{2,3},{3,2},{4,5},{5,4},{6,7},{7,6},{8,9},{9,8},{10,11... | collective-permute-start | bytes 344072 | tf_op jit(solution)/shard_map/ppermute | solution.py:494
  13.6 1.3 %collective-permute-start.6 = (f32[7,8,512]{2,1,0:T(8,128)S(1)}, f32[7,8,512]{2,1,0:T(8,128)S(1)}, u32[]{:S(2)}, u32[]{:S(2)}) collective-permute-start(f32[7,8,512]{2,1,0:T(8,128)S(1)} %collective-permute-done.2), channel_id=1, source_target_pairs={{0,1},{1,0},{2,3},{3,2},{4,5},{5,4},{6,7},{7,6},{8,9},{9,8},{10,11... | collective-permute-start | bytes 344072 | tf_op jit(solution)/shard_map/ppermute | solution.py:494
  13.8 1.3 %collective-permute-start.4 = (f32[7,8,512]{2,1,0:T(8,128)S(1)}, f32[7,8,512]{2,1,0:T(8,128)S(1)}, u32[]{:S(2)}, u32[]{:S(2)}) collective-permute-start(f32[7,8,512]{2,1,0:T(8,128)S(1)} %collective-permute-done.refs_2_), channel_id=1, source_target_pairs={{0,1},{1,0},{2,3},{3,2},{4,5},{5,4},{6,7},{7,6},{8,9},{9,8},{10,11... | collective-permute-start | bytes 344072 | tf_op jit(solution)/shard_map/ppermute | solution.py:494
  14.1 1.3 %collective-permute-start.5 = (f32[7,8,512]{2,1,0:T(8,128)S(1)}, f32[7,8,512]{2,1,0:T(8,128)S(1)}, u32[]{:S(2)}, u32[]{:S(2)}) collective-permute-start(f32[7,8,512]{2,1,0:T(8,128)S(1)} %collective-permute-done.1.refs_4_), channel_id=1, source_target_pairs={{0,1},{1,0},{2,3},{3,2},{4,5},{5,4},{6,7},{7,6},{8,9},{9,8},{10,11... | collective-permute-start | bytes 344072 | tf_op jit(solution)/shard_map/ppermute | solution.py:494

commit v5 on v4

--- a/solution.py
+++ b/solution.py
@@ -65,7 +65,14 @@
 
 
 def pick(tile, index):
-    return jnp.take_along_axis(tile, index, axis=1, mode="promise_in_bounds")
+    numbers = lax.GatherDimensionNumbers(
+        offset_dims=(),
+        collapsed_slice_dims=(1,),
+        start_index_map=(1,),
+        operand_batching_dims=(0,),
+        start_indices_batching_dims=(0,),
+    )
+    return lax.gather(tile, index[..., None], numbers, (1, 1), mode=lax.GatherScatterMode.PROMISE_IN_BOUNDS)
 
 
 def next_lane(tile, following):
@@ -75,20 +82,19 @@
 
 def rows_summed(parts):
     sub = sublane_index()
-    step = SUBLANES // 2
-    while step:
+    step = 1
+    while step < SUBLANES:
         low = jnp.bitwise_and(sub, step) == 0
-        half = len(parts) // 2
         parts = [
-            jnp.where(low, a, pltpu.roll(b, step, 0)) + jnp.where(low, pltpu.roll(a, SUBLANES - step, 0), b)
-            for a, b in zip(parts[:half], parts[half:])
+            jnp.where(low, a, b) + pltpu.roll(jnp.where(low, b, a), step, 0) for a, b in zip(parts[::2], parts[1::2])
         ]
-        step //= 2
+        step *= 2
     return parts[0]
 
 
 def tile_of(ref, lead, tile):
-    return ref[lead + (slice(None), slice(tile * LANES, (tile + 1) * LANES))]
+    whole = (slice(None),) * (len(ref.shape) - 1 - len(lead))
+    return ref[lead + whole + (slice(tile * LANES, (tile + 1) * LANES),)]
 
 
 def column_center(column, cosine, column_count, cell_count):
@@ -141,26 +147,29 @@
 
 def adjoint_taps(tile, cosine, column_count, cell_count, half):
     spacing = PITCH * cell_count / column_count
-    least = angle_table()[0].min()
-    lane = lane_index()
-    cell = (lane + (tile * LANES - half)).astype(F32)
+    cell = (lane_index() + (tile * LANES - half)).astype(F32)
     inside = (cell >= 0) & (cell < cell_count)
     first = jnp.floor((cell - (cell_count / 2 + 0.5)) * cosine * (1.0 / spacing) + (column_count / 2 - 0.5 - 1e-3)) + 1.0
+    taps = []
+    for tap in range(3):
+        column = first + tap
+        weight = jnp.maximum(0.0, 1.0 - jnp.abs(cell - column_center(column, cosine, column_count, cell_count)))
+        weight = jnp.where(inside & (column >= 0) & (column < column_count), weight, 0.0)
+        taps.append((jnp.clip(column.astype(jnp.int32), 0, column_count - 1), weight))
+    return taps
+
+
+def adjoint_tiles(tile, tap, column_count, cell_count, half):
+    spacing = PITCH * cell_count / column_count
+    least = angle_table()[0].min()
     ends = [
         (tile * LANES - half + e - cell_count / 2 - 0.5) * c / spacing + column_count / 2 + 0.5
         for e in (0, LANES - 1)
         for c in (1.0, least)
     ]
-    taps = []
-    for tap in range(3):
-        column = first + tap
-        weight = jnp.maximum(0.0, 1.0 - jnp.abs(cell - column_center(column, cosine, column_count, cell_count)))
-        weight = jnp.where(inside & (column >= 0) & (column < column_count), weight, 0.0)
-        place = jnp.clip(column.astype(jnp.int32), 0, column_count - 1)
-        low = min(max(math.floor(min(ends) + tap - 0.6), 0), column_count - 1) // LANES
-        high = min(max(math.ceil(max(ends) + tap + 0.6), 0), column_count - 1) // LANES
-        taps.append((place, weight, range(low, high + 1)))
-    return taps
+    low = min(max(math.floor(min(ends) + tap - 0.6), 0), column_count - 1) // LANES
+    high = min(max(math.ceil(max(ends) + tap + 0.6), 0), column_count - 1) // LANES
+    return range(low, high + 1)
 
 
 def store_line(line, base_ref, bend_ref):
@@ -182,9 +191,9 @@
     before, out = None, []
     for tile in range(tiles + 1):
         cut = slice(tile * LANES, (tile + 1) * LANES)
-        low = pick(jnp.broadcast_to(base_ref[row : row + 1, cut], (SUBLANES, LANES)), index)
-        rise = pick(jnp.broadcast_to(bend_ref[row : row + 1, cut], (SUBLANES, LANES)), index)
-        after = low + share * rise
+        low = jnp.broadcast_to(base_ref[row : row + 1, cut], (SUBLANES, LANES))
+        rise = jnp.broadcast_to(bend_ref[row : row + 1, cut], (SUBLANES, LANES))
+        after = pick(low + share * rise, index)
         if tile:
             out.append(jnp.where(near, before, after))
         before = after
@@ -196,14 +205,27 @@
     member = jnp.bitwise_and(sublane_index(), members - 1)
     cosine, _, flat = angle_facts(spread_scalars(lambda k: angle_ref[subset_ref[k]], members, member))
     lifts = spread_scalars(lambda k: lift_ref[subset_ref[k]], members, member).astype(F32)
-    tangents = [
-        angle_facts(jnp.full((SUBLANES, LANES), angle_ref[subset_ref[k]], jnp.int32))[1] for k in range(members)
-    ]
-    return cosine, flat, lifts, tangents
+    return cosine, flat, lifts
+
+
+def member_tangents(angle_ref, subset_ref):
+    indices = [angle_ref[subset_ref[k]] for k in range(subset_ref.shape[0])]
+    return [angle_facts(jnp.full((SUBLANES, LANES), i, jnp.int32))[1] for i in indices]
 
 
 def project_kernel(
-    angle_ref, subset_ref, volume_ref, measured_ref, block_ref, cover_ref, part_sum_ref, part_up_ref, cell_ref, slope_ref
+    angle_ref,
+    subset_ref,
+    volume_ref,
+    measured_ref,
+    block_ref,
+    cover_ref,
+    rise_ref,
+    first_ref,
+    part_ref,
+    end_ref,
+    cell_ref,
+    slope_ref,
 ):
     slab_depth, row_count, cell_count = volume_ref.shape
     row_share, view_count, column_count = measured_ref.shape
@@ -223,69 +245,64 @@
                     measured_ref[row, pl.ds(view, 1), side * width : (side + 1) * width]
                 )
 
+    for depth in range(slab_depth):
+        for group in range(groups):
+            band = slice(group * SUBLANES, (group + 1) * SUBLANES)
+            cells = [tile_of(volume_ref, (depth, band), tile) for tile in range(tiles)] + [zero]
+            for tile in range(tiles):
+                rise_ref[depth, band, tile * LANES : (tile + 1) * LANES] = (
+                    next_lane(cells[tile], cells[tile + 1]) - cells[tile]
+                )
+            first_ref[depth, band, :] = column_of(cells[0], 0)
+
     def one_view(view, carry):
         _, tangent, _ = angle_facts(jnp.full((SUBLANES, LANES), angle_ref[view], jnp.int32))
-        first_sum, first_up, last_sum, last_up, all_up = zero, zero, zero, zero, zero
+        low_end, high_end = zero, zero
+        sums = [[zero] * (tiles + 1) for _ in range(slab_depth)]
         for group in range(groups):
+            band = slice(group * SUBLANES, (group + 1) * SUBLANES)
             whole, fraction = shear_steps(group, row_count, tangent)
-            near = lane + (whole + half) < LANES
-            first_sum += jnp.where(near, 0.0, 1.0)
-            first_up += jnp.where(near, 0.0, fraction)
-            last_sum += jnp.where(near, 1.0, 0.0)
-            last_up += jnp.where(near, fraction, 0.0)
-            all_up += fraction
-        for tile, pair in ((0, (first_sum, first_up)), (tiles, (last_sum, last_up)), (1, (zero, all_up))):
-            cut = slice(tile * LANES, (tile + 1) * LANES)
-            part_sum_ref[slab_depth, view, :, cut], part_up_ref[slab_depth, view, :, cut] = pair
-        for depth in range(slab_depth):
-            sums, ups = [zero] * (tiles + 1), [zero] * (tiles + 1)
-            for group in range(groups):
-                whole, fraction = shear_steps(group, row_count, tangent)
-                place = lane + (whole + half)
-                index = jnp.bitwise_and(place, LANES - 1)
-                near = place < LANES
-                before = zero
+            place = lane + (whole + half)
+            index = jnp.bitwise_and(place, LANES - 1)
+            near, last = place < LANES, index == LANES - 1
+            enter = jnp.where(last, fraction, 0.0)
+            low_end = low_end + jnp.where(near, enter, 1.0)
+            high_end = high_end + jnp.where(near, 1.0 - enter, 0.0)
+            for depth in range(slab_depth):
+                before = enter * first_ref[depth, band, :]
                 for tile in range(tiles + 1):
                     after = zero
                     if tile < tiles:
-                        cells = volume_ref[
-                            depth, group * SUBLANES : (group + 1) * SUBLANES, tile * LANES : (tile + 1) * LANES
-                        ]
-                        after = pick(cells, index)
-                    moved = jnp.where(near, before, after)
-                    sums[tile] = sums[tile] + moved
-                    ups[tile] = ups[tile] + fraction * moved
+                        at = (depth, band)
+                        after = pick(tile_of(volume_ref, at, tile) + fraction * tile_of(rise_ref, at, tile), index)
+                    sums[depth][tile] = sums[depth][tile] + jnp.where(near, before, after)
                     before = after
+        end_ref[0, view, :, :] = low_end
+        end_ref[1, view, :, :] = high_end
+        for depth in range(slab_depth):
             for tile in range(tiles + 1):
-                cut = slice(tile * LANES, (tile + 1) * LANES)
-                part_sum_ref[depth, view, :, cut] = sums[tile]
-                part_up_ref[depth, view, :, cut] = ups[tile]
+                part_ref[depth, view, :, tile * LANES : (tile + 1) * LANES] = sums[depth][tile]
         return carry
 
-    lax.fori_loop(0, view_count, one_view, 0)
+    lax.fori_loop(0, view_count, one_view, 0, unroll=4)
 
     shift = LANES - half
-    for depth in range(slab_depth + 1):
-        collapsed = []
-        held = lambda ref, tile: rows_summed([tile_of(ref, (depth, view), tile) for view in range(view_count)])
-        if depth < slab_depth:
-            sums = [held(part_sum_ref, tile) for tile in range(tiles + 1)]
-            ups = [held(part_up_ref, tile) for tile in range(tiles + 1)]
-        else:
-            sums = [held(part_sum_ref, 0)] + [zero + float(row_count)] * (tiles - 1) + [held(part_sum_ref, tiles)]
-            ups = [held(part_up_ref, 0)] + [held(part_up_ref, 1)] * (tiles - 1) + [held(part_up_ref, tiles)]
-        ups.append(zero)
-        for tile in range(tiles + 1):
-            cells = sums[tile] - ups[tile] + next_lane(ups[tile], ups[tile + 1])
-            cell = lane + (tile * LANES - shift)
-            if tile in (0, tiles):
-                cells = jnp.where((cell >= 0) & (cell < cell_count), cells, 0.0)
-            collapsed.append(cells)
-        collapsed.append(zero)
+    inside = [None] * (tiles + 1)
+    inside[0], inside[tiles] = lane >= shift, lane < shift
+
+    def store(at, line):
+        line = [jnp.where(mask, cells, 0.0) if mask is not None else cells for cells, mask in zip(line, inside)] + [zero]
         for tile in range(tiles + 1):
             cut = slice(tile * LANES, (tile + 1) * LANES)
-            cell_ref[depth, :, cut] = collapsed[tile]
-            slope_ref[depth, :, cut] = next_lane(collapsed[tile], collapsed[tile + 1]) - collapsed[tile]
+            cell_ref[at, :, cut] = line[tile]
+            slope_ref[at, :, cut] = next_lane(line[tile], line[tile + 1]) - line[tile]
+
+    views = range(view_count)
+    for depth in range(slab_depth):
+        store(depth, [rows_summed([tile_of(part_ref, (depth, v), t) for v in views]) for t in range(tiles + 1)])
+    flat = zero + float(row_count)
+    ends = [rows_summed([end_ref[e, v, :, :] for v in views]) for e in range(2)]
+    store(slab_depth, [ends[0]] + [flat] * (tiles - 1) + [ends[1]])
 
     cosine, _, _ = angle_facts(spread_scalars(lambda v: angle_ref[v], view_count, sub))
     factor = 1.0 / (row_count * cosine)
@@ -300,22 +317,38 @@
         ends = [column_center(tile * LANES + e, c, column_count, cell_count) for e in (0, LANES - 1) for c in (1.0, least)]
         low = min(max(math.floor(min(ends) - 1e-2) + shift, shift - 2), shift + cell_count) // LANES
         high = min(max(math.floor(max(ends) + 1e-2) + shift, shift - 2), shift + cell_count) // LANES
-        for depth in range(slab_depth + 1):
-            cells, slope = zero, zero
-            for source in range(low, high + 1):
-                here = block == source
-                cells = jnp.where(here, pick(tile_of(cell_ref, (depth,), source), index), cells)
-                slope = jnp.where(here, pick(tile_of(slope_ref, (depth,), source), index), slope)
-            profile = (cells + fraction * slope) * factor
-            if depth == slab_depth:
-                cover_ref[:, tile * LANES : (tile + 1) * LANES] = profile
-            else:
-                side, inner = divmod(tile * LANES, width)
-                block_ref[depth * 2 + side, :, inner : inner + LANES] = profile
+        cells, slopes = [zero] * slab_depth + [flat], [zero] * (slab_depth + 1)
+        for source in range(low, high + 1):
+            here = block == source
+            for at in range(slab_depth + 1):
+                if at == slab_depth and source not in (0, tiles):
+                    continue
+                cells[at] = jnp.where(here, pick(tile_of(cell_ref, (at,), source), index), cells[at])
+                slopes[at] = jnp.where(here, pick(tile_of(slope_ref, (at,), source), index), slopes[at])
+        profiles = [(c + fraction * s) * factor for c, s in zip(cells, slopes)]
+        side, inner = divmod(tile * LANES, width)
+        for depth in range(slab_depth):
+            block_ref[depth * 2 + side, :, inner : inner + LANES] = profiles[depth]
+        cover_ref[:, tile * LANES : (tile + 1) * LANES] = profiles[slab_depth]
 
 
 def divisor_kernel(
-    slab_count, order, angle_ref, lift_ref, subset_ref, cover_ref, bound_ref, own_ref, rows_ref, edge_ref, bend_ref, sub_ref
+    slab_count,
+    order,
+    angle_ref,
+    lift_ref,
+    subset_ref,
+    cover_ref,
+    bound_ref,
+    own_ref,
+    rows_ref,
+    own_cone_ref,
+    cone_ref,
+    place_ref,
+    tap_ref,
+    edge_ref,
+    bend_ref,
+    sub_ref,
 ):
     slab_depth, row_count, cell_count = bound_ref.shape
     row_share, view_count, column_count = own_ref.shape
@@ -329,14 +362,24 @@
 
     _, _, flat = angle_facts(spread_scalars(lambda v: angle_ref[v], view_count, sub))
     lifts = spread_scalars(lambda v: lift_ref[v], view_count, sub).astype(F32)
+    lane = lane_index()
+    origin = slabs_of(slab, order)
+    source = sum(jnp.where(lane >= slab_depth * b, 1, 0) for b in range(1, len(order)))
+    slices = spread_scalars(lambda b: origin[b], len(order), source) * slab_depth + (lane - source * slab_depth)
+    held = (slices >= 0) & (slices < total_slices)
+    slices = slices.astype(F32)
     for row in range(row_share):
         sample = cone_sample((slab * row_share + row).astype(F32), lifts, flat, total_rows, total_slices)
+        weights = jnp.where(held, jnp.maximum(0.0, 1.0 - jnp.abs(sample - slices)), 0.0)
+        for place in range(slab_depth * len(order)):
+            own_cone_ref[place, row, :, :] = column_of(weights, place)
         total = cone_total(sample, total_slices)
         for tile in range(columns):
             cut = slice(tile * LANES, (tile + 1) * LANES)
             own_ref[row, :, cut] = 1.0 / jnp.maximum(total * cover_ref[:, cut], LEN_FLOOR)
 
-    cosine, flat, lifts, tangents = subset_angles(angle_ref, lift_ref, subset_ref)
+    cosine, flat, lifts = subset_angles(angle_ref, lift_ref, subset_ref)
+    tangents = member_tangents(angle_ref, subset_ref)
     for member in range(subset_count):
         view = pl.ds(subset_ref[member], 1)
         for side in range(2):
@@ -345,6 +388,8 @@
     sample, weights = subset_cone(slab, slab_count, order, slab_depth, row_share, flat, lifts)
     total = cone_total(sample, total_slices)
     for place in range(row_share * len(order)):
+        for z, w in enumerate(weights):
+            cone_ref[place, z, :, :] = column_of(w, place)
         length = column_of(total, place)
         for tile in range(width // LANES):
             cut = slice(tile * LANES, (tile + 1) * LANES)
@@ -354,7 +399,10 @@
     line = []
     for tile in range(tiles + 1):
         taps = adjoint_taps(tile, cosine, column_count, cell_count, row_count // 2)
-        line.append(sum(weight for _, weight, _ in taps) * factor)
+        for tap, (place, weight) in enumerate(taps):
+            place_ref[tile, tap, :, :] = place
+            tap_ref[tile, tap, :, :] = weight * factor
+        line.append(sum(weight for _, weight in taps) * factor)
     store_line(line, edge_ref, bend_ref)
     slice_total = []
     for depth in range(slab_depth):
@@ -380,16 +428,18 @@
 
 
 def update_kernel(
-    slab_count,
     order,
     angle_ref,
-    lift_ref,
     subset_ref,
     volume_ref,
     measured_ref,
     bound_ref,
     own_ref,
     rows_ref,
+    own_cone_ref,
+    cone_ref,
+    place_ref,
+    tap_ref,
     *refs,
 ):
     blocks = refs[: len(order)]
@@ -397,38 +447,24 @@
     slab_depth, row_count, cell_count = volume_ref.shape
     row_share, view_count, column_count = measured_ref.shape
     subset_count = subset_ref.shape[0]
-    total_rows, total_slices = row_share * slab_count, slab_depth * slab_count
     tiles, columns = cell_count // LANES, column_count // LANES
     width = column_count // 2
-    lane, sub = lane_index(), sublane_index()
     zero = jnp.zeros((SUBLANES, LANES), F32)
-    slab = lax.axis_index("slab")
-    odd = lax.rem(slab, 2)
-    origin = slabs_of(slab, order)
+    odd = lax.rem(lax.axis_index("slab"), 2)
     mate_block, other_block = (blocks[order.index(away)] for away in (1, -1))
 
-    _, _, flat = angle_facts(spread_scalars(lambda v: angle_ref[v], view_count, sub))
-    lifts = spread_scalars(lambda v: lift_ref[v], view_count, sub).astype(F32)
-    source = sum(jnp.where(lane >= slab_depth * b, 1, 0) for b in range(1, len(order)))
-    slices = spread_scalars(lambda b: origin[b], len(order), source) * slab_depth + (lane - source * slab_depth)
-    held = (slices >= 0) & (slices < total_slices)
-    slices = slices.astype(F32)
-    for row in range(row_share):
-        sample = cone_sample((slab * row_share + row).astype(F32), lifts, flat, total_rows, total_slices)
-        weights = jnp.where(held, jnp.maximum(0.0, 1.0 - jnp.abs(sample - slices)), 0.0)
-        image = [zero] * columns
+    for tile in range(columns):
+        side, inner = divmod(tile * LANES, width)
+        image = [zero] * row_share
         for place, block in enumerate(blocks):
             for depth in range(slab_depth):
-                weight = column_of(weights, place * slab_depth + depth)
-                for tile in range(columns):
-                    side, inner = divmod(tile * LANES, width)
-                    image[tile] = image[tile] + weight * block[depth * 2 + side, :, inner : inner + LANES]
-        for tile in range(columns):
-            cut = slice(tile * LANES, (tile + 1) * LANES)
-            residual_ref[row, :, cut] = (measured_ref[row, :, cut] - image[tile]) * own_ref[row, :, cut]
-
-    cosine, flat, lifts, tangents = subset_angles(angle_ref, lift_ref, subset_ref)
-    factor = 1.0 / (row_count * cosine)
+                cells = block[depth * 2 + side, :, inner : inner + LANES]
+                for row in range(row_share):
+                    image[row] = image[row] + own_cone_ref[place * slab_depth + depth, row, :, :] * cells
+        cut = slice(tile * LANES, (tile + 1) * LANES)
+        for row in range(row_share):
+            residual_ref[row, :, cut] = (measured_ref[row, :, cut] - image[row]) * own_ref[row, :, cut]
+
     for member in range(subset_count):
         view = pl.ds(subset_ref[member], 1)
         for side in range(2):
@@ -440,11 +476,10 @@
                 profile_ref[1 + depth, at, :] = blocks[0][depth * 2 + side, view, :]
             profile_ref[1 + slab_depth, at, :] = jnp.where(odd == 0, mate[1], other[1])
 
-    _, weights = subset_cone(slab, slab_count, order, slab_depth, row_share, flat, lifts)
     inner_tiles = width // LANES
     spread = [[zero] * inner_tiles for _ in range(slab_depth)]
     for place in range(row_share * len(order)):
-        weight = [column_of(w, place) for w in weights]
+        weight = [cone_ref[place, z, :, :] for z in range(slab_depth + 2)]
         block, row = blocks[place // row_share], place % row_share
         for tile in range(inner_tiles):
             cut = slice(tile * LANES, (tile + 1) * LANES)
@@ -465,29 +500,35 @@
     line = []
     for tile in range(tiles + 1):
         value = zero
-        for place, weight, at_tiles in adjoint_taps(tile, cosine, column_count, cell_count, row_count // 2):
+        for tap in range(3):
+            place = place_ref[tile, tap, :, :]
             block, index = jnp.right_shift(place, 7), jnp.bitwise_and(place, LANES - 1)
             found = zero
-            for at in at_tiles:
+            for at in adjoint_tiles(tile, tap, column_count, cell_count, row_count // 2):
                 found = jnp.where(block == at, pick(tile_of(spread_ref, (), at), index), found)
-            value = value + weight * found
-        line.append(value * factor)
+            value = value + tap_ref[tile, tap, :, :] * found
+        line.append(value)
     store_line(line, cell_ref, slope_ref)
+
+    tangents = member_tangents(angle_ref, subset_ref)
 
     def one_group(group, carry):
         band = pl.ds(pl.multiple_of(group * SUBLANES, SUBLANES), SUBLANES)
-        steps = [adjoint_steps(group, row_count, tangent) for tangent in tangents]
+        back = [[zero] * tiles for _ in range(slab_depth)]
+        for member in range(subset_count):
+            step = adjoint_steps(group, row_count, tangents[member])
+            for depth in range(slab_depth):
+                line = sheared(cell_ref, slope_ref, depth * subset_count + member, step, tiles)
+                back[depth] = [b + a for b, a in zip(back[depth], line)]
         for depth in range(slab_depth):
-            back = [zero] * tiles
-            for member in range(subset_count):
-                line = sheared(cell_ref, slope_ref, depth * subset_count + member, steps[member], tiles)
-                back = [b + a for b, a in zip(back, line)]
             for tile in range(tiles):
                 cut = slice(tile * LANES, (tile + 1) * LANES)
-                updated_ref[depth, band, cut] = volume_ref[depth, band, cut] + back[tile] * bound_ref[depth, band, cut]
+                updated_ref[depth, band, cut] = (
+                    volume_ref[depth, band, cut] + back[depth][tile] * bound_ref[depth, band, cut]
+                )
         return carry
 
-    lax.fori_loop(0, row_count // SUBLANES, one_group, 0)
+    lax.fori_loop(0, row_count // SUBLANES, one_group, 0, unroll=2)
 
 
 def swapped(block):
@@ -549,7 +590,12 @@
         ),
         in_specs=[smem, smem, vmem, vmem],
         out_specs=(vmem, vmem),
-        scratch_shapes=[pltpu.VMEM((slab_depth + 1, view_count, SUBLANES, wide), F32)] * 2
+        scratch_shapes=[
+            pltpu.VMEM(volume.shape, F32),
+            pltpu.VMEM((slab_depth, row_count, LANES), F32),
+            pltpu.VMEM((slab_depth, view_count, SUBLANES, wide), F32),
+            pltpu.VMEM((2, view_count, SUBLANES, LANES), F32),
+        ]
         + [pltpu.VMEM((slab_depth + 1, SUBLANES, wide), F32)] * 2,
         name="project",
     )(view_angle, subset, volume, measured)
@@ -562,21 +608,25 @@
             pltpu.VMEM(volume.shape, F32),
             pltpu.VMEM(measured.shape, F32),
             pltpu.VMEM((row_share * len(order), SUBLANES, column_count // 2), F32),
+            pltpu.VMEM((slab_depth * len(order), row_share, SUBLANES, LANES), F32),
+            pltpu.VMEM((row_share * len(order), slab_depth + 2, SUBLANES, LANES), F32),
+            pltpu.VMEM((tiles + 1, 3, SUBLANES, LANES), jnp.int32),
+            pltpu.VMEM((tiles + 1, 3, SUBLANES, LANES), F32),
         ),
         in_specs=[smem] * 3 + [vmem],
-        out_specs=(vmem,) * 3,
+        out_specs=(vmem,) * 7,
         scratch_shapes=[pltpu.VMEM((SUBLANES, wide), F32)] * 2 + [pltpu.VMEM((SUBLANES, column_count // 2), F32)],
         cost_estimate=pl.CostEstimate(flops=4_000_000, bytes_accessed=8_000_000, transcendentals=0),
         name="divisors",
     )
     blocks, divisors = gathered(own, reach, lambda: divide(view_angle, view_lift, subset, cover))
     return pl.pallas_call(
-        functools.partial(update_kernel, slab_count, order),
+        functools.partial(update_kernel, order),
         out_shape=(
             jax.ShapeDtypeStruct(measured.shape, F32),
             jax.ShapeDtypeStruct(volume.shape, F32),
         ),
-        in_specs=[smem] * 3 + [vmem] * (5 + len(order)),
+        in_specs=[smem] * 2 + [vmem] * (2 + len(divisors) + len(order)),
         out_specs=(vmem, vmem),
         scratch_shapes=[
             pltpu.VMEM((slab_depth + 2, SUBLANES, column_count // 2), F32),
@@ -584,7 +634,7 @@
         ]
         + [pltpu.VMEM((SUBLANES, wide), F32)] * 2,
         name="update",
-    )(view_angle, view_lift, subset, volume, measured, *map(here, (*divisors, *blocks)))
+    )(view_angle, subset, *map(here, (volume, measured, *divisors, *blocks)))
 
 
 def solution(mesh):

time: 20.2 us -> 21.1 us (1.045)
  local copies, waits for them, and re-layouts: 0 us -> 4.57 us
  Pallas kernels: 10.8 us -> 8.34 us
  waiting for transfers between devices: 4.07 us -> 2.72 us
    unnamed x0 -> x12, local copies, waits for them, and re-layouts: none -> 4.57 us
    pallas_call x1, Pallas kernels: 4.63 us -> 3.04 us  [per_device(): pl.pallas_call(functools.partial(update_kernel, order), out_shape=(jax.Sh...]
    ppermute x3, waiting for transfers between devices: 2.9 us -> 1.56 us  [from_chip(): return lax.ppermute(block, 'slab', pairs)]
    pallas_call x1, Pallas kernels: 3.86 us -> 3.13 us  [per_device(): pl.pallas_call(project_kernel, out_shape=(pltpu.VMEM(block_shape, F32), p...]
  transfers between devices with their start and end apart: 7 -> 7, of which waited for: 4 -> 4; matrix products, arithmetic and copies ran while one was open for 0% -> 0% of each run, Pallas kernels for 12% -> 10%
where the time goes in v5:
time: 21.1 us; the launch traced here: 20.8 us
  Pallas kernels  8.34 us (40%)
  local copies, waits for them, and re-layouts  4.57 us (22%)
  starting transfers between devices  4.51 us (21%)
  waiting for transfers between devices  2.72 us (13%)
  between operations  0.67 us (3%)
    unnamed x12, local copies, waits for them, and re-layouts  4.57 us
    pallas_call x1, Pallas kernels, per_device(): pl.pallas_call(project_kernel, out_shape=(pltpu.VMEM(block_shape, F32), p...  3.13 us
    ppermute x3, starting transfers between devices, from_chip(): return lax.ppermute(block, 'slab', pairs)  3.12 us
    pallas_call x1, Pallas kernels, per_device(): pl.pallas_call(functools.partial(update_kernel, order), out_shape=(jax.Sh...  3.04 us
    pallas_call x1, Pallas kernels, per_device(): divide(view_angle, view_lift, subset, cover)  2.17 us
    ppermute x3, waiting for transfers between devices, from_chip(): return lax.ppermute(block, 'slab', pairs)  1.56 us
    ppermute x4, starting transfers between devices, swapped(): lax.ppermute(block, 'slab', [(i, i ^ 1) for i in range(lax.axis_size('sla...  1.38 us
    ppermute x4, waiting for transfers between devices, swapped(): lax.ppermute(block, 'slab', [(i, i ^ 1) for i in range(lax.axis_size('sla...  1.16 us
  transfers between devices with their start and end apart: 7, of which 4 were waited for; matrix products, arithmetic and copies ran while one was open for 0% of the time, Pallas kernels for 10%

profile of v5, /device:TPU:0, one launch (start us, length us, event | category | flops | bytes accessed | tf_op | source)
XLA Modules:
  0.0 20.8 jit_solution(16341033735602176077)
XLA Ops:
  0.6 0.0 copy-start.3
  0.6 3.1 %project.1 = (f32[7,8,512]{2,1,0:T(8,128)S(1)}, f32[8,1024]{1,0:T(8,128)S(1)}) custom-call(s32[8]{0:T(128)} %angle_ref.5, s32[4]{0:T(128)} %subset_ref.5, f32[2,64,1024]{2,1,0:T(8,128)} %volume_ref.3, f32[3,8,1024]{2,1,0:T(8,128)} %measured_ref.3), custom_call_target="tpu_custom_call" | custom-call | tf_op jit(solution)/shard_map/project/pallas_call | solution.py:585
  3.8 0.5 %collective-permute-start.2 = (f32[7,8,512]{2,1,0:T(8,128)S(1)}, f32[7,8,512]{2,1,0:T(8,128)S(1)}, u32[]{:S(2)}, u32[]{:S(2)}) collective-permute-start(f32[7,8,512]{2,1,0:T(8,128)S(1)} %get-tuple-element.21.refs_0_), channel_id=1, source_target_pairs={{4,0},{6,2},{8,4},{1,5},{10,6},{3,7},{12,8},{5,9},{14,10},{7,11},{... | collective-permute-start | bytes 344072 | tf_op jit(solution)/shard_map/ppermute | solution.py:547
  4.2 2.1 %collective-permute-start.1 = (f32[7,8,512]{2,1,0:T(8,128)S(1)}, f32[7,8,512]{2,1,0:T(8,128)S(1)}, u32[]{:S(2)}, u32[]{:S(2)}) collective-permute-start(f32[7,8,512]{2,1,0:T(8,128)S(1)} %get-tuple-element.21.refs_0_), channel_id=1, source_target_pairs={{2,0},{4,2},{1,3},{6,4},{3,5},{8,6},{5,7},{10,8},{7,9},{12,10},{9,... | collective-permute-start | bytes 344072 | tf_op jit(solution)/shard_map/ppermute | solution.py:547
  6.4 0.5 %collective-permute-start = (f32[7,8,512]{2,1,0:T(8,128)S(1)}, f32[7,8,512]{2,1,0:T(8,128)S(1)}, u32[]{:S(2)}, u32[]{:S(2)}) collective-permute-start(f32[7,8,512]{2,1,0:T(8,128)S(1)} %get-tuple-element.21.refs_0_), channel_id=1, source_target_pairs={{3,1},{0,2},{5,3},{2,4},{7,5},{4,6},{9,7},{6,8},{11,9},{8,10},{13,... | collective-permute-start | bytes 344072 | tf_op jit(solution)/shard_map/ppermute | solution.py:547
  6.9 0.7 %collective-permute-start.3 = (f32[7,8,512]{2,1,0:T(8,128)S(1)}, f32[7,8,512]{2,1,0:T(8,128)S(1)}, u32[]{:S(2)}, u32[]{:S(2)}) collective-permute-start(f32[7,8,512]{2,1,0:T(8,128)S(1)} %get-tuple-element.21.refs_0_), channel_id=1, source_target_pairs={{0,1},{1,0},{2,3},{3,2},{4,5},{5,4},{6,7},{7,6},{8,9},{9,8},{10,11... | collective-permute-start | bytes 344072 | tf_op jit(solution)/shard_map/ppermute | solution.py:535
  7.6 2.2 %divisors.1 = (f32[2,64,1024]{2,1,0:T(8,128)S(1)}, f32[3,8,1024]{2,1,0:T(8,128)S(1)}, f32[21,8,512]{2,1,0:T(8,128)S(1)}, f32[14,3,8,128]{3,2,1,0:T(8,128)S(1)}, ...) custom-call(s32[8]{0:T(128)} %angle_ref.5, s32[8]{0:T(128)} %lift_ref.1, ...), custom_call_target="tpu_custom_call" | custom-call | flops 4000000 | bytes 8000000 | tf_op jit(solution)/shard_map/divisors/pallas_call | solution.py:622
  9.8 0.0 copy-start.1
  9.8 0.8 %copy-done.1 = f32[2,64,1024]{2,1,0:T(8,128)} copy-done((f32[2,64,1024]{2,1,0:T(8,128)}, f32[2,64,1024]{2,1,0:T(8,128)S(1)}, u32[]{:S(2)}) %copy-start.1) | copy-done | bytes 524312
  10.6 0.0 copy-start.4
  10.6 0.7 %copy-done.4 = f32[21,8,512]{2,1,0:T(8,128)} copy-done((f32[21,8,512]{2,1,0:T(8,128)}, f32[21,8,512]{2,1,0:T(8,128)S(1)}, u32[]{:S(2)}) %copy-start.4) | copy-done | bytes 344088
  11.3 0.0 collective-permute-done.2
  11.3 0.0 collective-permute-done.1.refs_4_
  11.3 1.6 %collective-permute-done.refs_2_ = f32[7,8,512]{2,1,0:T(8,128)S(1)} collective-permute-done((f32[7,8,512]{2,1,0:T(8,128)S(1)}, f32[7,8,512]{2,1,0:T(8,128)S(1)}, u32[]{:S(2)}, u32[]{:S(2)}) %collective-permute-start) | collective-permute-done | bytes 114720 | tf_op jit(solution)/shard_map/ppermute | solution.py:547
  12.9 0.2 collective-permute-start.6
  13.0 0.4 %collective-permute-start.4 = (f32[7,8,512]{2,1,0:T(8,128)S(1)}, f32[7,8,512]{2,1,0:T(8,128)S(1)}, u32[]{:S(2)}, u32[]{:S(2)}) collective-permute-start(f32[7,8,512]{2,1,0:T(8,128)S(1)} %collective-permute-done.refs_2_), channel_id=1, source_target_pairs={{0,1},{1,0},{2,3},{3,2},{4,5},{5,4},{6,7},{7,6},{8,9},{9,8},{10,11... | collective-permute-start | bytes 344072 | tf_op jit(solution)/shard_map/ppermute | solution.py:535
  13.4 0.2 collective-permute-start.5
  13.5 0.0 collective-permute-done.3.refs_1_
  13.5 0.7 %collective-permute-done.6.refs_6_ = f32[7,8,512]{2,1,0:T(8,128)S(1)} collective-permute-done((f32[7,8,512]{2,1,0:T(8,128)S(1)}, f32[7,8,512]{2,1,0:T(8,128)S(1)}, u32[]{:S(2)}, u32[]{:S(2)}) %collective-permute-start.6) | collective-permute-done | bytes 114720 | tf_op jit(solution)/shard_map/ppermute | solution.py:535
  14.2 0.2 collective-permute-done.4.refs_3_
  14.4 0.3 %collective-permute-done.5.refs_5_ = f32[7,8,512]{2,1,0:T(8,128)S(1)} collective-permute-done((f32[7,8,512]{2,1,0:T(8,128)S(1)}, f32[7,8,512]{2,1,0:T(8,128)S(1)}, u32[]{:S(2)}, u32[]{:S(2)}) %collective-permute-start.5) | collective-permute-done | bytes 114720 | tf_op jit(solution)/shard_map/ppermute | solution.py:535
  14.7 0.0 copy-done.3
  14.7 0.0 copy-start
  14.7 1.0 %copy-done = f32[2,64,1024]{2,1,0:T(8,128)S(1)} copy-done((f32[2,64,1024]{2,1,0:T(8,128)S(1)}, f32[2,64,1024]{2,1,0:T(8,128)}, u32[]{:S(2)}) %copy-start) | copy-done | bytes 524312
  15.8 0.0 copy-start.2
  15.8 1.0 %copy-done.2 = f32[2,64,1024]{2,1,0:T(8,128)S(1)} copy-done((f32[2,64,1024]{2,1,0:T(8,128)S(1)}, f32[2,64,1024]{2,1,0:T(8,128)}, u32[]{:S(2)}) %copy-start.2) | copy-done | bytes 524312
  16.8 0.0 copy-start.5
  16.8 1.0 %copy-done.5 = f32[21,8,512]{2,1,0:T(8,128)S(1)} copy-done((f32[21,8,512]{2,1,0:T(8,128)S(1)}, f32[21,8,512]{2,1,0:T(8,128)}, u32[]{:S(2)}) %copy-start.5) | copy-done | bytes 344088
  17.8 3.0 %update.1 = (f32[3,8,1024]{2,1,0:T(8,128)}, f32[2,64,1024]{2,1,0:T(8,128)}) custom-call(s32[8]{0:T(128)} %angle_ref.5, s32[4]{0:T(128)} %subset_ref.5, f32[2,64,1024]{2,1,0:T(8,128)S(1)} %copy-done, f32[3,8,1024]{2,1,0:T(8,128)S(1)} %copy-done.3, f32[2,64,1024]{2,1,0:T(8,128)S(1)} %copy-done.2, f32[3,8,1024]{2,1,0:T(8,128)S(1)} %get-tuple-element.31.own_ref, ...), custom_call_target="tpu_custom_call" | custom-call | tf_op jit(solution)/shard_map/update/pallas_call | solution.py:623
Async XLA Ops:
  0.6 14.1 %copy-start.3 = (f32[3,8,1024]{2,1,0:T(8,128)S(1)}, f32[3,8,1024]{2,1,0:T(8,128)}, u32[]{:S(2)}) copy-start(f32[3,8,1024]{2,1,0:T(8,128)} %measured_ref.3) | copy-start | bytes 294916
  3.8 7.5 %collective-permute-start.2 = (f32[7,8,512]{2,1,0:T(8,128)S(1)}, f32[7,8,512]{2,1,0:T(8,128)S(1)}, u32[]{:S(2)}, u32[]{:S(2)}) collective-permute-start(f32[7,8,512]{2,1,0:T(8,128)S(1)} %get-tuple-element.21.refs_0_), channel_id=1, source_target_pairs={{4,0},{6,2},{8,4},{1,5},{10,6},{3,7},{12,8},{5,9},{14,10},{7,11},{... | collective-permute-start | bytes 344072 | tf_op jit(solution)/shard_map/ppermute | solution.py:547
  4.2 7.1 %collective-permute-start.1 = (f32[7,8,512]{2,1,0:T(8,128)S(1)}, f32[7,8,512]{2,1,0:T(8,128)S(1)}, u32[]{:S(2)}, u32[]{:S(2)}) collective-permute-start(f32[7,8,512]{2,1,0:T(8,128)S(1)} %get-tuple-element.21.refs_0_), channel_id=1, source_target_pairs={{2,0},{4,2},{1,3},{6,4},{3,5},{8,6},{5,7},{10,8},{7,9},{12,10},{9,... | collective-permute-start | bytes 344072 | tf_op jit(solution)/shard_map/ppermute | solution.py:547
  6.4 6.5 %collective-permute-start = (f32[7,8,512]{2,1,0:T(8,128)S(1)}, f32[7,8,512]{2,1,0:T(8,128)S(1)}, u32[]{:S(2)}, u32[]{:S(2)}) collective-permute-start(f32[7,8,512]{2,1,0:T(8,128)S(1)} %get-tuple-element.21.refs_0_), channel_id=1, source_target_pairs={{3,1},{0,2},{5,3},{2,4},{7,5},{4,6},{9,7},{6,8},{11,9},{8,10},{13,... | collective-permute-start | bytes 344072 | tf_op jit(solution)/shard_map/ppermute | solution.py:547
  6.9 6.6 %collective-permute-start.3 = (f32[7,8,512]{2,1,0:T(8,128)S(1)}, f32[7,8,512]{2,1,0:T(8,128)S(1)}, u32[]{:S(2)}, u32[]{:S(2)}) collective-permute-start(f32[7,8,512]{2,1,0:T(8,128)S(1)} %get-tuple-element.21.refs_0_), channel_id=1, source_target_pairs={{0,1},{1,0},{2,3},{3,2},{4,5},{5,4},{6,7},{7,6},{8,9},{9,8},{10,11... | collective-permute-start | bytes 344072 | tf_op jit(solution)/shard_map/ppermute | solution.py:535
  9.8 0.8 %copy-start.1 = (f32[2,64,1024]{2,1,0:T(8,128)}, f32[2,64,1024]{2,1,0:T(8,128)S(1)}, u32[]{:S(2)}) copy-start(f32[2,64,1024]{2,1,0:T(8,128)S(1)} %get-tuple-element.30.bound_ref) | copy-start | bytes 1572868
  10.6 0.7 %copy-start.4 = (f32[21,8,512]{2,1,0:T(8,128)}, f32[21,8,512]{2,1,0:T(8,128)S(1)}, u32[]{:S(2)}) copy-start(f32[21,8,512]{2,1,0:T(8,128)S(1)} %get-tuple-element.32.rows_ref) | copy-start | bytes 1032196
  12.9 1.3 %collective-permute-start.6 = (f32[7,8,512]{2,1,0:T(8,128)S(1)}, f32[7,8,512]{2,1,0:T(8,128)S(1)}, u32[]{:S(2)}, u32[]{:S(2)}) collective-permute-start(f32[7,8,512]{2,1,0:T(8,128)S(1)} %collective-permute-done.2), channel_id=1, source_target_pairs={{0,1},{1,0},{2,3},{3,2},{4,5},{5,4},{6,7},{7,6},{8,9},{9,8},{10,11... | collective-permute-start | bytes 344072 | tf_op jit(solution)/shard_map/ppermute | solution.py:535
  13.0 1.3 %collective-permute-start.4 = (f32[7,8,512]{2,1,0:T(8,128)S(1)}, f32[7,8,512]{2,1,0:T(8,128)S(1)}, u32[]{:S(2)}, u32[]{:S(2)}) collective-permute-start(f32[7,8,512]{2,1,0:T(8,128)S(1)} %collective-permute-done.refs_2_), channel_id=1, source_target_pairs={{0,1},{1,0},{2,3},{3,2},{4,5},{5,4},{6,7},{7,6},{8,9},{9,8},{10,11... | collective-permute-start | bytes 344072 | tf_op jit(solution)/shard_map/ppermute | solution.py:535
  13.4 1.3 %collective-permute-start.5 = (f32[7,8,512]{2,1,0:T(8,128)S(1)}, f32[7,8,512]{2,1,0:T(8,128)S(1)}, u32[]{:S(2)}, u32[]{:S(2)}) collective-permute-start(f32[7,8,512]{2,1,0:T(8,128)S(1)} %collective-permute-done.1.refs_4_), channel_id=1, source_target_pairs={{0,1},{1,0},{2,3},{3,2},{4,5},{5,4},{6,7},{7,6},{8,9},{9,8},{10,11... | collective-permute-start | bytes 344072 | tf_op jit(solution)/shard_map/ppermute | solution.py:535
  14.7 1.0 %copy-start = (f32[2,64,1024]{2,1,0:T(8,128)S(1)}, f32[2,64,1024]{2,1,0:T(8,128)}, u32[]{:S(2)}) copy-start(f32[2,64,1024]{2,1,0:T(8,128)} %volume_ref.3) | copy-start | bytes 1572868
  15.8 1.0 %copy-start.2 = (f32[2,64,1024]{2,1,0:T(8,128)S(1)}, f32[2,64,1024]{2,1,0:T(8,128)}, u32[]{:S(2)}) copy-start(f32[2,64,1024]{2,1,0:T(8,128)} %copy-done.1) | copy-start | bytes 1572868
  16.8 1.0 %copy-start.5 = (f32[21,8,512]{2,1,0:T(8,128)S(1)}, f32[21,8,512]{2,1,0:T(8,128)}, u32[]{:S(2)}) copy-start(f32[21,8,512]{2,1,0:T(8,128)} %copy-done.4) | copy-start | bytes 1032196

commit v6 on v5

--- a/solution.py
+++ b/solution.py
@@ -18,6 +18,7 @@
 LANES = 128
 SUBLANES = 8
 F32 = jnp.float32
+VMEM_LIMIT = 8 * 1024 * 1024
 
 
 def angle_table():
@@ -579,6 +580,7 @@
     subset_count = subset.shape[0]
     tiles = cell_count // LANES
     reach = slab_reach(slab_count, slab_depth, row_share)
+    small = pltpu.CompilerParams(vmem_limit_bytes=VMEM_LIMIT)
     smem, vmem = pl.BlockSpec(memory_space=pltpu.SMEM), pl.BlockSpec(memory_space=pltpu.VMEM)
     wide = (tiles + 1) * LANES
     block_shape = (2 * slab_depth + row_share, SUBLANES, column_count // 2)
@@ -597,6 +599,7 @@
             pltpu.VMEM((2, view_count, SUBLANES, LANES), F32),
         ]
         + [pltpu.VMEM((slab_depth + 1, SUBLANES, wide), F32)] * 2,
+        compiler_params=small,
         name="project",
     )(view_angle, subset, volume, measured)
     here = lambda x: pltpu.with_memory_space_constraint(x, pltpu.VMEM)
@@ -617,6 +620,7 @@
         out_specs=(vmem,) * 7,
         scratch_shapes=[pltpu.VMEM((SUBLANES, wide), F32)] * 2 + [pltpu.VMEM((SUBLANES, column_count // 2), F32)],
         cost_estimate=pl.CostEstimate(flops=4_000_000, bytes_accessed=8_000_000, transcendentals=0),
+        compiler_params=small,
         name="divisors",
     )
     blocks, divisors = gathered(own, reach, lambda: divide(view_angle, view_lift, subset, cover))
@@ -633,6 +637,7 @@
             pltpu.VMEM((SUBLANES, column_count), F32),
         ]
         + [pltpu.VMEM((SUBLANES, wide), F32)] * 2,
+        compiler_params=small,
         name="update",
     )(view_angle, subset, *map(here, (volume, measured, *divisors, *blocks)))
 

time: 21.1 us -> 20.7 us (0.981)
  waiting for transfers between devices: 2.72 us -> 4.35 us
  local copies, waits for them, and re-layouts: 4.57 us -> 3.25 us
  Pallas kernels: 8.34 us -> 7.7 us
    ppermute x3, waiting for transfers between devices: 1.56 us -> 3.19 us  [from_chip(): return lax.ppermute(block, 'slab', pairs)]
    unnamed x12 -> x14, local copies, waits for them, and re-layouts: 4.57 us -> 3.25 us
    pallas_call x1, Pallas kernels: 3.13 us -> 2.71 us  [per_device(): pl.pallas_call(project_kernel, out_shape=(pltpu.VMEM(block_shape, F32), p...]
where the time goes in v6:
time: 20.7 us; the launch traced here: 20.5 us
  Pallas kernels  7.7 us (37%)
  starting transfers between devices  4.51 us (22%)
  waiting for transfers between devices  4.35 us (21%)
  local copies, waits for them, and re-layouts  3.25 us (16%)
  between operations  0.68 us (3%)
    unnamed x14, local copies, waits for them, and re-layouts  3.25 us
    ppermute x3, waiting for transfers between devices, from_chip(): return lax.ppermute(block, 'slab', pairs)  3.19 us
    ppermute x3, starting transfers between devices, from_chip(): return lax.ppermute(block, 'slab', pairs)  3.12 us
    pallas_call x1, Pallas kernels, per_device(): pl.pallas_call(functools.partial(update_kernel, order), out_shape=(jax.Sh...  2.94 us
    pallas_call x1, Pallas kernels, per_device(): pl.pallas_call(project_kernel, out_shape=(pltpu.VMEM(block_shape, F32), p...  2.71 us
    pallas_call x1, Pallas kernels, per_device(): divide(view_angle, view_lift, subset, cover)  2.05 us
    ppermute x4, starting transfers between devices, swapped(): lax.ppermute(block, 'slab', [(i, i ^ 1) for i in range(lax.axis_size('sla...  1.38 us
    ppermute x4, waiting for transfers between devices, swapped(): lax.ppermute(block, 'slab', [(i, i ^ 1) for i in range(lax.axis_size('sla...  1.16 us
  transfers between devices with their start and end apart: 7, of which 4 were waited for; matrix products, arithmetic and copies ran while one was open for 0% of the time, Pallas kernels for 10%

profile of v6, /device:TPU:0, one launch (start us, length us, event | category | flops | bytes accessed | tf_op | source)
XLA Modules:
  0.0 20.5 jit_solution(496591613178073106)
XLA Ops:
  0.6 0.0 copy-start
  0.6 1.0 %copy-done = f32[2,64,1024]{2,1,0:T(8,128)S(1)} copy-done((f32[2,64,1024]{2,1,0:T(8,128)S(1)}, f32[2,64,1024]{2,1,0:T(8,128)}, u32[]{:S(2)}) %copy-start) | copy-done | bytes 524312
  1.7 0.0 copy-start.2
  1.7 0.9 %copy-done.2 = f32[3,8,1024]{2,1,0:T(8,128)S(1)} copy-done((f32[3,8,1024]{2,1,0:T(8,128)S(1)}, f32[3,8,1024]{2,1,0:T(8,128)}, u32[]{:S(2)}) %copy-start.2) | copy-done | bytes 98328
  2.6 0.0 copy-start.4
  2.6 0.7 %copy-done.4 = s32[8]{0:T(128)S(1)} copy-done((s32[8]{0:T(128)S(1)}, s32[8]{0:T(128)}, u32[]{:S(2)}) %copy-start.4) | copy-done | bytes 56
  3.2 0.0 copy-start.5
  3.2 0.7 %copy-done.5 = s32[4]{0:T(128)S(1)} copy-done((s32[4]{0:T(128)S(1)}, s32[4]{0:T(128)}, u32[]{:S(2)}) %copy-start.5) | copy-done | bytes 40
  3.9 0.0 copy-start.1
  3.9 0.0 copy-start.3
  3.9 2.7 %project.1 = (f32[7,8,512]{2,1,0:T(8,128)S(1)}, f32[8,1024]{1,0:T(8,128)S(1)}) custom-call(s32[8]{0:T(128)S(1)} %copy-done.4, s32[4]{0:T(128)S(1)} %copy-done.5, f32[2,64,1024]{2,1,0:T(8,128)S(1)} %copy-done, f32[3,8,1024]{2,1,0:T(8,128)S(1)} %copy-done.2), custom_call_target="tpu_custom_call" | custom-call | tf_op jit(solution)/shard_map/project/pallas_call | solution.py:587
  6.6 0.0 copy-start.6
  6.6 0.5 %collective-permute-start.2 = (f32[7,8,512]{2,1,0:T(8,128)S(1)}, f32[7,8,512]{2,1,0:T(8,128)S(1)}, u32[]{:S(2)}, u32[]{:S(2)}) collective-permute-start(f32[7,8,512]{2,1,0:T(8,128)S(1)} %get-tuple-element.21.refs_0_), channel_id=1, source_target_pairs={{4,0},{6,2},{8,4},{1,5},{10,6},{3,7},{12,8},{5,9},{14,10},{7,11},{... | collective-permute-start | bytes 344072 | tf_op jit(solution)/shard_map/ppermute | solution.py:548
  7.1 2.1 %collective-permute-start.1 = (f32[7,8,512]{2,1,0:T(8,128)S(1)}, f32[7,8,512]{2,1,0:T(8,128)S(1)}, u32[]{:S(2)}, u32[]{:S(2)}) collective-permute-start(f32[7,8,512]{2,1,0:T(8,128)S(1)} %get-tuple-element.21.refs_0_), channel_id=1, source_target_pairs={{2,0},{4,2},{1,3},{6,4},{3,5},{8,6},{5,7},{10,8},{7,9},{12,10},{9,... | collective-permute-start | bytes 344072 | tf_op jit(solution)/shard_map/ppermute | solution.py:548
  9.2 0.5 %collective-permute-start = (f32[7,8,512]{2,1,0:T(8,128)S(1)}, f32[7,8,512]{2,1,0:T(8,128)S(1)}, u32[]{:S(2)}, u32[]{:S(2)}) collective-permute-start(f32[7,8,512]{2,1,0:T(8,128)S(1)} %get-tuple-element.21.refs_0_), channel_id=1, source_target_pairs={{3,1},{0,2},{5,3},{2,4},{7,5},{4,6},{9,7},{6,8},{11,9},{8,10},{13,... | collective-permute-start | bytes 344072 | tf_op jit(solution)/shard_map/ppermute | solution.py:548
  9.7 0.7 %collective-permute-start.3 = (f32[7,8,512]{2,1,0:T(8,128)S(1)}, f32[7,8,512]{2,1,0:T(8,128)S(1)}, u32[]{:S(2)}, u32[]{:S(2)}) collective-permute-start(f32[7,8,512]{2,1,0:T(8,128)S(1)} %get-tuple-element.21.refs_0_), channel_id=1, source_target_pairs={{0,1},{1,0},{2,3},{3,2},{4,5},{5,4},{6,7},{7,6},{8,9},{9,8},{10,11... | collective-permute-start | bytes 344072 | tf_op jit(solution)/shard_map/ppermute | solution.py:536
  10.4 0.0 copy-done.6
  10.4 2.0 %divisors.1 = (f32[2,64,1024]{2,1,0:T(8,128)S(1)}, f32[3,8,1024]{2,1,0:T(8,128)S(1)}, f32[21,8,512]{2,1,0:T(8,128)S(1)}, f32[14,3,8,128]{3,2,1,0:T(8,128)S(1)}, ...) custom-call(s32[8]{0:T(128)S(1)} %copy-done.4, s32[8]{0:T(128)S(1)} %copy-done.6, ...), custom_call_target="tpu_custom_call" | custom-call | flops 4000000 | bytes 8000000 | tf_op jit(solution)/shard_map/divisors/pallas_call | solution.py:626
  12.5 0.0 collective-permute-done.2
  12.5 0.0 collective-permute-done.1.refs_4_
  12.5 3.2 %collective-permute-done.refs_2_ = f32[7,8,512]{2,1,0:T(8,128)S(1)} collective-permute-done((f32[7,8,512]{2,1,0:T(8,128)S(1)}, f32[7,8,512]{2,1,0:T(8,128)S(1)}, u32[]{:S(2)}, u32[]{:S(2)}) %collective-permute-start) | collective-permute-done | bytes 114720 | tf_op jit(solution)/shard_map/ppermute | solution.py:548
  15.7 0.2 collective-permute-start.6
  15.9 0.4 %collective-permute-start.4 = (f32[7,8,512]{2,1,0:T(8,128)S(1)}, f32[7,8,512]{2,1,0:T(8,128)S(1)}, u32[]{:S(2)}, u32[]{:S(2)}) collective-permute-start(f32[7,8,512]{2,1,0:T(8,128)S(1)} %collective-permute-done.refs_2_), channel_id=1, source_target_pairs={{0,1},{1,0},{2,3},{3,2},{4,5},{5,4},{6,7},{7,6},{8,9},{9,8},{10,11... | collective-permute-start | bytes 344072 | tf_op jit(solution)/shard_map/ppermute | solution.py:536
  16.2 0.2 collective-permute-start.5
  16.4 0.0 collective-permute-done.3.refs_1_
  16.4 0.7 %collective-permute-done.6.refs_6_ = f32[7,8,512]{2,1,0:T(8,128)S(1)} collective-permute-done((f32[7,8,512]{2,1,0:T(8,128)S(1)}, f32[7,8,512]{2,1,0:T(8,128)S(1)}, u32[]{:S(2)}, u32[]{:S(2)}) %collective-permute-start.6) | collective-permute-done | bytes 114720 | tf_op jit(solution)/shard_map/ppermute | solution.py:536
  17.0 0.2 collective-permute-done.4.refs_3_
  17.2 0.3 %collective-permute-done.5.refs_5_ = f32[7,8,512]{2,1,0:T(8,128)S(1)} collective-permute-done((f32[7,8,512]{2,1,0:T(8,128)S(1)}, f32[7,8,512]{2,1,0:T(8,128)S(1)}, u32[]{:S(2)}, u32[]{:S(2)}) %collective-permute-start.5) | collective-permute-done | bytes 114720 | tf_op jit(solution)/shard_map/ppermute | solution.py:536
  17.5 0.0 copy-done.1
  17.5 0.0 copy-done.3
  17.5 2.9 %update.1 = (f32[3,8,1024]{2,1,0:T(8,128)}, f32[2,64,1024]{2,1,0:T(8,128)}) custom-call(s32[8]{0:T(128)S(1)} %copy-done.4, s32[4]{0:T(128)S(1)} %copy-done.5, f32[2,64,1024]{2,1,0:T(8,128)S(1)} %copy-done.1, f32[3,8,1024]{2,1,0:T(8,128)S(1)} %copy-done.3, f32[2,64,1024]{2,1,0:T(8,128)S(1)} %get-tuple-element.30.bound_ref, ...), custom_call_target="tpu_custom_call" | custom-call | tf_op jit(solution)/shard_map/update/pallas_call | solution.py:627
Async XLA Ops:
  0.6 1.0 %copy-start = (f32[2,64,1024]{2,1,0:T(8,128)S(1)}, f32[2,64,1024]{2,1,0:T(8,128)}, u32[]{:S(2)}) copy-start(f32[2,64,1024]{2,1,0:T(8,128)} %volume_ref.3) | copy-start | bytes 1572868
  1.7 0.9 %copy-start.2 = (f32[3,8,1024]{2,1,0:T(8,128)S(1)}, f32[3,8,1024]{2,1,0:T(8,128)}, u32[]{:S(2)}) copy-start(f32[3,8,1024]{2,1,0:T(8,128)} %measured_ref.3) | copy-start | bytes 294916
  2.6 0.7 %copy-start.4 = (s32[8]{0:T(128)S(1)}, s32[8]{0:T(128)}, u32[]{:S(2)}) copy-start(s32[8]{0:T(128)} %angle_ref.5) | copy-start | bytes 100
  3.2 0.7 %copy-start.5 = (s32[4]{0:T(128)S(1)}, s32[4]{0:T(128)}, u32[]{:S(2)}) copy-start(s32[4]{0:T(128)} %subset_ref.5) | copy-start | bytes 52
  3.9 13.7 %copy-start.1 = (f32[2,64,1024]{2,1,0:T(8,128)S(1)}, f32[2,64,1024]{2,1,0:T(8,128)}, u32[]{:S(2)}) copy-start(f32[2,64,1024]{2,1,0:T(8,128)} %volume_ref.3) | copy-start | bytes 1572868
  3.9 13.7 %copy-start.3 = (f32[3,8,1024]{2,1,0:T(8,128)S(1)}, f32[3,8,1024]{2,1,0:T(8,128)}, u32[]{:S(2)}) copy-start(f32[3,8,1024]{2,1,0:T(8,128)} %measured_ref.3) | copy-start | bytes 294916
  6.6 3.9 %copy-start.6 = (s32[8]{0:T(128)S(1)}, s32[8]{0:T(128)}, u32[]{:S(2)}) copy-start(s32[8]{0:T(128)} %lift_ref.1) | copy-start | bytes 100
  6.6 5.9 %collective-permute-start.2 = (f32[7,8,512]{2,1,0:T(8,128)S(1)}, f32[7,8,512]{2,1,0:T(8,128)S(1)}, u32[]{:S(2)}, u32[]{:S(2)}) collective-permute-start(f32[7,8,512]{2,1,0:T(8,128)S(1)} %get-tuple-element.21.refs_0_), channel_id=1, source_target_pairs={{4,0},{6,2},{8,4},{1,5},{10,6},{3,7},{12,8},{5,9},{14,10},{7,11},{... | collective-permute-start | bytes 344072 | tf_op jit(solution)/shard_map/ppermute | solution.py:548
  7.1 5.4 %collective-permute-start.1 = (f32[7,8,512]{2,1,0:T(8,128)S(1)}, f32[7,8,512]{2,1,0:T(8,128)S(1)}, u32[]{:S(2)}, u32[]{:S(2)}) collective-permute-start(f32[7,8,512]{2,1,0:T(8,128)S(1)} %get-tuple-element.21.refs_0_), channel_id=1, source_target_pairs={{2,0},{4,2},{1,3},{6,4},{3,5},{8,6},{5,7},{10,8},{7,9},{12,10},{9,... | collective-permute-start | bytes 344072 | tf_op jit(solution)/shard_map/ppermute | solution.py:548
  9.2 6.5 %collective-permute-start = (f32[7,8,512]{2,1,0:T(8,128)S(1)}, f32[7,8,512]{2,1,0:T(8,128)S(1)}, u32[]{:S(2)}, u32[]{:S(2)}) collective-permute-start(f32[7,8,512]{2,1,0:T(8,128)S(1)} %get-tuple-element.21.refs_0_), channel_id=1, source_target_pairs={{3,1},{0,2},{5,3},{2,4},{7,5},{4,6},{9,7},{6,8},{11,9},{8,10},{13,... | collective-permute-start | bytes 344072 | tf_op jit(solution)/shard_map/ppermute | solution.py:548
  9.7 6.6 %collective-permute-start.3 = (f32[7,8,512]{2,1,0:T(8,128)S(1)}, f32[7,8,512]{2,1,0:T(8,128)S(1)}, u32[]{:S(2)}, u32[]{:S(2)}) collective-permute-start(f32[7,8,512]{2,1,0:T(8,128)S(1)} %get-tuple-element.21.refs_0_), channel_id=1, source_target_pairs={{0,1},{1,0},{2,3},{3,2},{4,5},{5,4},{6,7},{7,6},{8,9},{9,8},{10,11... | collective-permute-start | bytes 344072 | tf_op jit(solution)/shard_map/ppermute | solution.py:536
  15.7 1.3 %collective-permute-start.6 = (f32[7,8,512]{2,1,0:T(8,128)S(1)}, f32[7,8,512]{2,1,0:T(8,128)S(1)}, u32[]{:S(2)}, u32[]{:S(2)}) collective-permute-start(f32[7,8,512]{2,1,0:T(8,128)S(1)} %collective-permute-done.2), channel_id=1, source_target_pairs={{0,1},{1,0},{2,3},{3,2},{4,5},{5,4},{6,7},{7,6},{8,9},{9,8},{10,11... | collective-permute-start | bytes 344072 | tf_op jit(solution)/shard_map/ppermute | solution.py:536
  15.9 1.3 %collective-permute-start.4 = (f32[7,8,512]{2,1,0:T(8,128)S(1)}, f32[7,8,512]{2,1,0:T(8,128)S(1)}, u32[]{:S(2)}, u32[]{:S(2)}) collective-permute-start(f32[7,8,512]{2,1,0:T(8,128)S(1)} %collective-permute-done.refs_2_), channel_id=1, source_target_pairs={{0,1},{1,0},{2,3},{3,2},{4,5},{5,4},{6,7},{7,6},{8,9},{9,8},{10,11... | collective-permute-start | bytes 344072 | tf_op jit(solution)/shard_map/ppermute | solution.py:536
  16.2 1.3 %collective-permute-start.5 = (f32[7,8,512]{2,1,0:T(8,128)S(1)}, f32[7,8,512]{2,1,0:T(8,128)S(1)}, u32[]{:S(2)}, u32[]{:S(2)}) collective-permute-start(f32[7,8,512]{2,1,0:T(8,128)S(1)} %collective-permute-done.1.refs_4_), channel_id=1, source_target_pairs={{0,1},{1,0},{2,3},{3,2},{4,5},{5,4},{6,7},{7,6},{8,9},{9,8},{10,11... | collective-permute-start | bytes 344072 | tf_op jit(solution)/shard_map/ppermute | solution.py:536

commit v7 on v6

--- a/solution.py
+++ b/solution.py
@@ -580,6 +580,8 @@
     subset_count = subset.shape[0]
     tiles = cell_count // LANES
     reach = slab_reach(slab_count, slab_depth, row_share)
+    here = lambda x: pltpu.with_memory_space_constraint(x, pltpu.VMEM)
+    there = lambda x: pltpu.with_memory_space_constraint(x, pltpu.HBM)
     small = pltpu.CompilerParams(vmem_limit_bytes=VMEM_LIMIT)
     smem, vmem = pl.BlockSpec(memory_space=pltpu.SMEM), pl.BlockSpec(memory_space=pltpu.VMEM)
     wide = (tiles + 1) * LANES
@@ -601,8 +603,7 @@
         + [pltpu.VMEM((slab_depth + 1, SUBLANES, wide), F32)] * 2,
         compiler_params=small,
         name="project",
-    )(view_angle, subset, volume, measured)
-    here = lambda x: pltpu.with_memory_space_constraint(x, pltpu.VMEM)
+    )(*map(there, (view_angle, subset, volume, measured)))
     cover = here(cover)
     order = window(reach)
     divide = pl.pallas_call(

time: 20.7 us -> 17.9 us (0.86)
  local copies, waits for them, and re-layouts: 3.25 us -> 0.03 us
  Pallas kernels: 7.7 us -> 8.14 us
    unnamed x14 -> x10, local copies, waits for them, and re-layouts: 3.25 us -> 0.03 us
    pallas_call x1, Pallas kernels: 2.71 us -> 3.15 us  [per_device(): pl.pallas_call(project_kernel, out_shape=(pltpu.VMEM(block_shape, F32), p...]
  transfers between devices with their start and end apart: 7 -> 7, of which waited for: 4 -> 4; matrix products, arithmetic and copies ran while one was open for 0% -> 0% of each run, Pallas kernels for 10% -> 12%
where the time goes in v7:
time: 17.9 us; the launch traced here: 17.7 us
  Pallas kernels  8.14 us (45%)
  starting transfers between devices  4.51 us (25%)
  waiting for transfers between devices  4.35 us (24%)
  between operations  0.71 us (4%)
    ppermute x3, waiting for transfers between devices, from_chip(): return lax.ppermute(block, 'slab', pairs)  3.18 us
    pallas_call x1, Pallas kernels, per_device(): pl.pallas_call(project_kernel, out_shape=(pltpu.VMEM(block_shape, F32), p...  3.15 us
    ppermute x3, starting transfers between devices, from_chip(): return lax.ppermute(block, 'slab', pairs)  3.12 us
    pallas_call x1, Pallas kernels, per_device(): pl.pallas_call(functools.partial(update_kernel, order), out_shape=(jax.Sh...  2.94 us
    pallas_call x1, Pallas kernels, per_device(): divide(view_angle, view_lift, subset, cover)  2.05 us
    ppermute x4, starting transfers between devices, swapped(): lax.ppermute(block, 'slab', [(i, i ^ 1) for i in range(lax.axis_size('sla...  1.38 us
    ppermute x4, waiting for transfers between devices, swapped(): lax.ppermute(block, 'slab', [(i, i ^ 1) for i in range(lax.axis_size('sla...  1.16 us
  transfers between devices with their start and end apart: 7, of which 4 were waited for; matrix products, arithmetic and copies ran while one was open for 0% of the time, Pallas kernels for 12%

profile of v7, /device:TPU:0, one launch (start us, length us, event | category | flops | bytes accessed | tf_op | source)
XLA Modules:
  0.0 17.7 jit_solution(13914978578968038906)
XLA Ops:
  0.6 0.0 copy-start
  0.6 0.0 copy-start.1
  0.6 3.2 %project.1 = (f32[7,8,512]{2,1,0:T(8,128)S(1)}, f32[8,1024]{1,0:T(8,128)S(1)}) custom-call(s32[8]{0:T(128)} %angle_ref.5, s32[4]{0:T(128)} %subset_ref.5, f32[2,64,1024]{2,1,0:T(8,128)} %volume_ref.3, f32[3,8,1024]{2,1,0:T(8,128)} %measured_ref.3), custom_call_target="tpu_custom_call" | custom-call | tf_op jit(solution)/shard_map/project/pallas_call | solution.py:589
  3.8 0.0 copy-start.2
  3.8 0.0 copy-start.3
  3.8 0.0 copy-start.4
  3.8 0.5 %collective-permute-start.2 = (f32[7,8,512]{2,1,0:T(8,128)S(1)}, f32[7,8,512]{2,1,0:T(8,128)S(1)}, u32[]{:S(2)}, u32[]{:S(2)}) collective-permute-start(f32[7,8,512]{2,1,0:T(8,128)S(1)} %get-tuple-element.21.refs_0_), channel_id=1, source_target_pairs={{4,0},{6,2},{8,4},{1,5},{10,6},{3,7},{12,8},{5,9},{14,10},{7,11},{... | collective-permute-start | bytes 344072 | tf_op jit(solution)/shard_map/ppermute | solution.py:548
  4.3 2.1 %collective-permute-start.1 = (f32[7,8,512]{2,1,0:T(8,128)S(1)}, f32[7,8,512]{2,1,0:T(8,128)S(1)}, u32[]{:S(2)}, u32[]{:S(2)}) collective-permute-start(f32[7,8,512]{2,1,0:T(8,128)S(1)} %get-tuple-element.21.refs_0_), channel_id=1, source_target_pairs={{2,0},{4,2},{1,3},{6,4},{3,5},{8,6},{5,7},{10,8},{7,9},{12,10},{9,... | collective-permute-start | bytes 344072 | tf_op jit(solution)/shard_map/ppermute | solution.py:548
  6.4 0.5 %collective-permute-start = (f32[7,8,512]{2,1,0:T(8,128)S(1)}, f32[7,8,512]{2,1,0:T(8,128)S(1)}, u32[]{:S(2)}, u32[]{:S(2)}) collective-permute-start(f32[7,8,512]{2,1,0:T(8,128)S(1)} %get-tuple-element.21.refs_0_), channel_id=1, source_target_pairs={{3,1},{0,2},{5,3},{2,4},{7,5},{4,6},{9,7},{6,8},{11,9},{8,10},{13,... | collective-permute-start | bytes 344072 | tf_op jit(solution)/shard_map/ppermute | solution.py:548
  7.0 0.7 %collective-permute-start.3 = (f32[7,8,512]{2,1,0:T(8,128)S(1)}, f32[7,8,512]{2,1,0:T(8,128)S(1)}, u32[]{:S(2)}, u32[]{:S(2)}) collective-permute-start(f32[7,8,512]{2,1,0:T(8,128)S(1)} %get-tuple-element.21.refs_0_), channel_id=1, source_target_pairs={{0,1},{1,0},{2,3},{3,2},{4,5},{5,4},{6,7},{7,6},{8,9},{9,8},{10,11... | collective-permute-start | bytes 344072 | tf_op jit(solution)/shard_map/ppermute | solution.py:536
  7.7 0.0 copy-done.2
  7.7 0.0 copy-done.3
  7.7 0.0 copy-done.4
  7.7 2.0 %divisors.1 = (f32[2,64,1024]{2,1,0:T(8,128)S(1)}, f32[3,8,1024]{2,1,0:T(8,128)S(1)}, f32[21,8,512]{2,1,0:T(8,128)S(1)}, f32[14,3,8,128]{3,2,1,0:T(8,128)S(1)}, ...) custom-call(s32[8]{0:T(128)S(1)} %copy-done.2, s32[8]{0:T(128)S(1)} %copy-done.4, ...), custom_call_target="tpu_custom_call" | custom-call | flops 4000000 | bytes 8000000 | tf_op jit(solution)/shard_map/divisors/pallas_call | solution.py:627
  9.7 0.0 collective-permute-done.2
  9.8 0.0 collective-permute-done.1.refs_4_
  9.8 3.2 %collective-permute-done.refs_2_ = f32[7,8,512]{2,1,0:T(8,128)S(1)} collective-permute-done((f32[7,8,512]{2,1,0:T(8,128)S(1)}, f32[7,8,512]{2,1,0:T(8,128)S(1)}, u32[]{:S(2)}, u32[]{:S(2)}) %collective-permute-start) | collective-permute-done | bytes 114720 | tf_op jit(solution)/shard_map/ppermute | solution.py:548
  12.9 0.2 collective-permute-start.6
  13.1 0.4 %collective-permute-start.4 = (f32[7,8,512]{2,1,0:T(8,128)S(1)}, f32[7,8,512]{2,1,0:T(8,128)S(1)}, u32[]{:S(2)}, u32[]{:S(2)}) collective-permute-start(f32[7,8,512]{2,1,0:T(8,128)S(1)} %collective-permute-done.refs_2_), channel_id=1, source_target_pairs={{0,1},{1,0},{2,3},{3,2},{4,5},{5,4},{6,7},{7,6},{8,9},{9,8},{10,11... | collective-permute-start | bytes 344072 | tf_op jit(solution)/shard_map/ppermute | solution.py:536
  13.5 0.2 collective-permute-start.5
  13.6 0.0 collective-permute-done.3.refs_1_
  13.6 0.7 %collective-permute-done.6.refs_6_ = f32[7,8,512]{2,1,0:T(8,128)S(1)} collective-permute-done((f32[7,8,512]{2,1,0:T(8,128)S(1)}, f32[7,8,512]{2,1,0:T(8,128)S(1)}, u32[]{:S(2)}, u32[]{:S(2)}) %collective-permute-start.6) | collective-permute-done | bytes 114720 | tf_op jit(solution)/shard_map/ppermute | solution.py:536
  14.3 0.2 collective-permute-done.4.refs_3_
  14.4 0.3 %collective-permute-done.5.refs_5_ = f32[7,8,512]{2,1,0:T(8,128)S(1)} collective-permute-done((f32[7,8,512]{2,1,0:T(8,128)S(1)}, f32[7,8,512]{2,1,0:T(8,128)S(1)}, u32[]{:S(2)}, u32[]{:S(2)}) %collective-permute-start.5) | collective-permute-done | bytes 114720 | tf_op jit(solution)/shard_map/ppermute | solution.py:536
  14.8 0.0 copy-done
  14.8 0.0 copy-done.1
  14.8 2.9 %update.1 = (f32[3,8,1024]{2,1,0:T(8,128)}, f32[2,64,1024]{2,1,0:T(8,128)}) custom-call(s32[8]{0:T(128)S(1)} %copy-done.2, s32[4]{0:T(128)S(1)} %copy-done.3, f32[2,64,1024]{2,1,0:T(8,128)S(1)} %copy-done, f32[3,8,1024]{2,1,0:T(8,128)S(1)} %copy-done.1, f32[2,64,1024]{2,1,0:T(8,128)S(1)} %get-tuple-element.30.bound_ref, ...), custom_call_target="tpu_custom_call" | custom-call | tf_op jit(solution)/shard_map/update/pallas_call | solution.py:628
Async XLA Ops:
  0.6 14.2 %copy-start = (f32[2,64,1024]{2,1,0:T(8,128)S(1)}, f32[2,64,1024]{2,1,0:T(8,128)}, u32[]{:S(2)}) copy-start(f32[2,64,1024]{2,1,0:T(8,128)} %volume_ref.3) | copy-start | bytes 1572868
  0.6 14.1 %copy-start.1 = (f32[3,8,1024]{2,1,0:T(8,128)S(1)}, f32[3,8,1024]{2,1,0:T(8,128)}, u32[]{:S(2)}) copy-start(f32[3,8,1024]{2,1,0:T(8,128)} %measured_ref.3) | copy-start | bytes 294916
  3.8 3.9 %copy-start.2 = (s32[8]{0:T(128)S(1)}, s32[8]{0:T(128)}, u32[]{:S(2)}) copy-start(s32[8]{0:T(128)} %angle_ref.5) | copy-start | bytes 100
  3.8 3.9 %copy-start.3 = (s32[4]{0:T(128)S(1)}, s32[4]{0:T(128)}, u32[]{:S(2)}) copy-start(s32[4]{0:T(128)} %subset_ref.5) | copy-start | bytes 52
  3.8 3.9 %copy-start.4 = (s32[8]{0:T(128)S(1)}, s32[8]{0:T(128)}, u32[]{:S(2)}) copy-start(s32[8]{0:T(128)} %lift_ref.1) | copy-start | bytes 100
  3.8 5.9 %collective-permute-start.2 = (f32[7,8,512]{2,1,0:T(8,128)S(1)}, f32[7,8,512]{2,1,0:T(8,128)S(1)}, u32[]{:S(2)}, u32[]{:S(2)}) collective-permute-start(f32[7,8,512]{2,1,0:T(8,128)S(1)} %get-tuple-element.21.refs_0_), channel_id=1, source_target_pairs={{4,0},{6,2},{8,4},{1,5},{10,6},{3,7},{12,8},{5,9},{14,10},{7,11},{... | collective-permute-start | bytes 344072 | tf_op jit(solution)/shard_map/ppermute | solution.py:548
  4.3 5.4 %collective-permute-start.1 = (f32[7,8,512]{2,1,0:T(8,128)S(1)}, f32[7,8,512]{2,1,0:T(8,128)S(1)}, u32[]{:S(2)}, u32[]{:S(2)}) collective-permute-start(f32[7,8,512]{2,1,0:T(8,128)S(1)} %get-tuple-element.21.refs_0_), channel_id=1, source_target_pairs={{2,0},{4,2},{1,3},{6,4},{3,5},{8,6},{5,7},{10,8},{7,9},{12,10},{9,... | collective-permute-start | bytes 344072 | tf_op jit(solution)/shard_map/ppermute | solution.py:548
  6.4 6.5 %collective-permute-start = (f32[7,8,512]{2,1,0:T(8,128)S(1)}, f32[7,8,512]{2,1,0:T(8,128)S(1)}, u32[]{:S(2)}, u32[]{:S(2)}) collective-permute-start(f32[7,8,512]{2,1,0:T(8,128)S(1)} %get-tuple-element.21.refs_0_), channel_id=1, source_target_pairs={{3,1},{0,2},{5,3},{2,4},{7,5},{4,6},{9,7},{6,8},{11,9},{8,10},{13,... | collective-permute-start | bytes 344072 | tf_op jit(solution)/shard_map/ppermute | solution.py:548
  7.0 6.6 %collective-permute-start.3 = (f32[7,8,512]{2,1,0:T(8,128)S(1)}, f32[7,8,512]{2,1,0:T(8,128)S(1)}, u32[]{:S(2)}, u32[]{:S(2)}) collective-permute-start(f32[7,8,512]{2,1,0:T(8,128)S(1)} %get-tuple-element.21.refs_0_), channel_id=1, source_target_pairs={{0,1},{1,0},{2,3},{3,2},{4,5},{5,4},{6,7},{7,6},{8,9},{9,8},{10,11... | collective-permute-start | bytes 344072 | tf_op jit(solution)/shard_map/ppermute | solution.py:536
  12.9 1.3 %collective-permute-start.6 = (f32[7,8,512]{2,1,0:T(8,128)S(1)}, f32[7,8,512]{2,1,0:T(8,128)S(1)}, u32[]{:S(2)}, u32[]{:S(2)}) collective-permute-start(f32[7,8,512]{2,1,0:T(8,128)S(1)} %collective-permute-done.2), channel_id=1, source_target_pairs={{0,1},{1,0},{2,3},{3,2},{4,5},{5,4},{6,7},{7,6},{8,9},{9,8},{10,11... | collective-permute-start | bytes 344072 | tf_op jit(solution)/shard_map/ppermute | solution.py:536
  13.1 1.3 %collective-permute-start.4 = (f32[7,8,512]{2,1,0:T(8,128)S(1)}, f32[7,8,512]{2,1,0:T(8,128)S(1)}, u32[]{:S(2)}, u32[]{:S(2)}) collective-permute-start(f32[7,8,512]{2,1,0:T(8,128)S(1)} %collective-permute-done.refs_2_), channel_id=1, source_target_pairs={{0,1},{1,0},{2,3},{3,2},{4,5},{5,4},{6,7},{7,6},{8,9},{9,8},{10,11... | collective-permute-start | bytes 344072 | tf_op jit(solution)/shard_map/ppermute | solution.py:536
  13.5 1.3 %collective-permute-start.5 = (f32[7,8,512]{2,1,0:T(8,128)S(1)}, f32[7,8,512]{2,1,0:T(8,128)S(1)}, u32[]{:S(2)}, u32[]{:S(2)}) collective-permute-start(f32[7,8,512]{2,1,0:T(8,128)S(1)} %collective-permute-done.1.refs_4_), channel_id=1, source_target_pairs={{0,1},{1,0},{2,3},{3,2},{4,5},{5,4},{6,7},{7,6},{8,9},{9,8},{10,11... | collective-permute-start | bytes 344072 | tf_op jit(solution)/shard_map/ppermute | solution.py:536

commit v8 on v7

--- a/solution.py
+++ b/solution.py
@@ -444,7 +444,7 @@
     *refs,
 ):
     blocks = refs[: len(order)]
-    residual_ref, updated_ref, profile_ref, spread_ref, cell_ref, slope_ref = refs[len(order) :]
+    residual_ref, updated_ref, profile_ref, spread_ref, cell_ref, slope_ref, rest_ref, new_ref, sent = refs[len(order) :]
     slab_depth, row_count, cell_count = volume_ref.shape
     row_share, view_count, column_count = measured_ref.shape
     subset_count = subset_ref.shape[0]
@@ -454,6 +454,7 @@
     odd = lax.rem(lax.axis_index("slab"), 2)
     mate_block, other_block = (blocks[order.index(away)] for away in (1, -1))
 
+    groups = row_count // SUBLANES
     for tile in range(columns):
         side, inner = divmod(tile * LANES, width)
         image = [zero] * row_share
@@ -464,7 +465,9 @@
                     image[row] = image[row] + own_cone_ref[place * slab_depth + depth, row, :, :] * cells
         cut = slice(tile * LANES, (tile + 1) * LANES)
         for row in range(row_share):
-            residual_ref[row, :, cut] = (measured_ref[row, :, cut] - image[row]) * own_ref[row, :, cut]
+            rest_ref[row, :, cut] = (measured_ref[row, :, cut] - image[row]) * own_ref[row, :, cut]
+    copies = [pltpu.make_async_copy(rest_ref, residual_ref, sent.at[groups])]
+    copies[0].start()
 
     for member in range(subset_count):
         view = pl.ds(subset_ref[member], 1)
@@ -512,9 +515,8 @@
     store_line(line, cell_ref, slope_ref)
 
     tangents = member_tangents(angle_ref, subset_ref)
-
-    def one_group(group, carry):
-        band = pl.ds(pl.multiple_of(group * SUBLANES, SUBLANES), SUBLANES)
+    for group in range(groups):
+        band = slice(group * SUBLANES, (group + 1) * SUBLANES)
         back = [[zero] * tiles for _ in range(slab_depth)]
         for member in range(subset_count):
             step = adjoint_steps(group, row_count, tangents[member])
@@ -524,12 +526,13 @@
         for depth in range(slab_depth):
             for tile in range(tiles):
                 cut = slice(tile * LANES, (tile + 1) * LANES)
-                updated_ref[depth, band, cut] = (
+                new_ref[depth, band, cut] = (
                     volume_ref[depth, band, cut] + back[depth][tile] * bound_ref[depth, band, cut]
                 )
-        return carry
-
-    lax.fori_loop(0, row_count // SUBLANES, one_group, 0, unroll=2)
+        copies.append(pltpu.make_async_copy(new_ref.at[:, band, :], updated_ref.at[:, band, :], sent.at[group]))
+        copies[-1].start()
+    for copy in copies:
+        copy.wait()
 
 
 def swapped(block):
@@ -561,15 +564,16 @@
 
 
 def gathered(own, reach, meanwhile):
-    received = [from_chip(own, distance) for distance in fetches(reach)]
+    received = {distance: from_chip(own, distance) for distance in fetches(reach)}
     blocks = {0: own, 1: swapped(own)}
     done = meanwhile()
-    received, done = lax.optimization_barrier((received, done))
-    for distance, block in zip(fetches(reach), received):
-        if 2 * abs(distance) <= reach:
-            blocks[2 * distance] = block
-        if abs(1 - 2 * distance) <= reach:
-            blocks[1 - 2 * distance] = swapped(block)
+    for part in ([d for d in received if abs(d) > 1], [-1, 1]):
+        arrived, done = lax.optimization_barrier(([received[d] for d in part], done))
+        for distance, block in zip(part, arrived):
+            if 2 * abs(distance) <= reach:
+                blocks[2 * distance] = block
+            if abs(1 - 2 * distance) <= reach:
+                blocks[1 - 2 * distance] = swapped(block)
     return [blocks[away] for away in window(reach)], done
 
 
@@ -632,12 +636,16 @@
             jax.ShapeDtypeStruct(volume.shape, F32),
         ),
         in_specs=[smem] * 2 + [vmem] * (2 + len(divisors) + len(order)),
-        out_specs=(vmem, vmem),
+        out_specs=(pl.BlockSpec(memory_space=pl.ANY),) * 2,
         scratch_shapes=[
             pltpu.VMEM((slab_depth + 2, SUBLANES, column_count // 2), F32),
             pltpu.VMEM((SUBLANES, column_count), F32),
-        ]
-        + [pltpu.VMEM((SUBLANES, wide), F32)] * 2,
+            pltpu.VMEM((SUBLANES, wide), F32),
+            pltpu.VMEM((SUBLANES, wide), F32),
+            pltpu.VMEM(measured.shape, F32),
+            pltpu.VMEM(volume.shape, F32),
+            pltpu.SemaphoreType.DMA((row_count // SUBLANES + 1,)),
+        ],
         compiler_params=small,
         name="update",
     )(view_angle, subset, *map(here, (volume, measured, *divisors, *blocks)))

time: 17.9 us -> 17.5 us (0.978)
  Pallas kernels: 8.14 us -> 7.82 us
    pallas_call x1, Pallas kernels: 2.94 us -> 2.62 us  [per_device(): pl.pallas_call(functools.partial(update_kernel, order), out_shape=(jax.Sh...]
where the time goes in v8:
time: 17.5 us; the launch traced here: 17.4 us
  Pallas kernels  7.82 us (45%)
  starting transfers between devices  4.51 us (26%)
  waiting for transfers between devices  4.35 us (25%)
  between operations  0.71 us (4%)
    ppermute x3, waiting for transfers between devices, from_chip(): return lax.ppermute(block, 'slab', pairs)  3.18 us
    pallas_call x1, Pallas kernels, per_device(): pl.pallas_call(project_kernel, out_shape=(pltpu.VMEM(block_shape, F32), p...  3.15 us
    ppermute x3, starting transfers between devices, from_chip(): return lax.ppermute(block, 'slab', pairs)  3.12 us
    pallas_call x1, Pallas kernels, per_device(): pl.pallas_call(functools.partial(update_kernel, order), out_shape=(jax.Sh...  2.62 us
    pallas_call x1, Pallas kernels, per_device(): divide(view_angle, view_lift, subset, cover)  2.05 us
    ppermute x4, starting transfers between devices, swapped(): lax.ppermute(block, 'slab', [(i, i ^ 1) for i in range(lax.axis_size('sla...  1.38 us
    ppermute x4, waiting for transfers between devices, swapped(): lax.ppermute(block, 'slab', [(i, i ^ 1) for i in range(lax.axis_size('sla...  1.16 us
  transfers between devices with their start and end apart: 7, of which 4 were waited for; matrix products, arithmetic and copies ran while one was open for 0% of the time, Pallas kernels for 12%

profile of v8, /device:TPU:0, one launch (start us, length us, event | category | flops | bytes accessed | tf_op | source)
XLA Modules:
  0.0 17.4 jit_solution(11524941592517316858)
XLA Ops:
  0.6 0.0 copy-start
  0.6 0.0 copy-start.1
  0.6 3.2 %project.1 = (f32[7,8,512]{2,1,0:T(8,128)S(1)}, f32[8,1024]{1,0:T(8,128)S(1)}) custom-call(s32[8]{0:T(128)} %angle_ref.5, s32[4]{0:T(128)} %subset_ref.5, f32[2,64,1024]{2,1,0:T(8,128)} %volume_ref.3, f32[3,8,1024]{2,1,0:T(8,128)} %measured_ref.3), custom_call_target="tpu_custom_call" | custom-call | tf_op jit(solution)/shard_map/project/pallas_call | solution.py:593
  3.8 0.0 copy-start.2
  3.8 0.0 copy-start.3
  3.8 0.0 copy-start.4
  3.8 0.5 %collective-permute-start.2 = (f32[7,8,512]{2,1,0:T(8,128)S(1)}, f32[7,8,512]{2,1,0:T(8,128)S(1)}, u32[]{:S(2)}, u32[]{:S(2)}) collective-permute-start(f32[7,8,512]{2,1,0:T(8,128)S(1)} %get-tuple-element.28.refs_0_), channel_id=1, source_target_pairs={{4,0},{6,2},{8,4},{1,5},{10,6},{3,7},{12,8},{5,9},{14,10},{7,11},{... | collective-permute-start | bytes 344072 | tf_op jit(solution)/shard_map/ppermute | solution.py:551
  4.3 2.1 %collective-permute-start.1 = (f32[7,8,512]{2,1,0:T(8,128)S(1)}, f32[7,8,512]{2,1,0:T(8,128)S(1)}, u32[]{:S(2)}, u32[]{:S(2)}) collective-permute-start(f32[7,8,512]{2,1,0:T(8,128)S(1)} %get-tuple-element.28.refs_0_), channel_id=1, source_target_pairs={{2,0},{4,2},{1,3},{6,4},{3,5},{8,6},{5,7},{10,8},{7,9},{12,10},{9,... | collective-permute-start | bytes 344072 | tf_op jit(solution)/shard_map/ppermute | solution.py:551
  6.4 0.5 %collective-permute-start = (f32[7,8,512]{2,1,0:T(8,128)S(1)}, f32[7,8,512]{2,1,0:T(8,128)S(1)}, u32[]{:S(2)}, u32[]{:S(2)}) collective-permute-start(f32[7,8,512]{2,1,0:T(8,128)S(1)} %get-tuple-element.28.refs_0_), channel_id=1, source_target_pairs={{3,1},{0,2},{5,3},{2,4},{7,5},{4,6},{9,7},{6,8},{11,9},{8,10},{13,... | collective-permute-start | bytes 344072 | tf_op jit(solution)/shard_map/ppermute | solution.py:551
  7.0 0.7 %collective-permute-start.3 = (f32[7,8,512]{2,1,0:T(8,128)S(1)}, f32[7,8,512]{2,1,0:T(8,128)S(1)}, u32[]{:S(2)}, u32[]{:S(2)}) collective-permute-start(f32[7,8,512]{2,1,0:T(8,128)S(1)} %get-tuple-element.28.refs_0_), channel_id=1, source_target_pairs={{0,1},{1,0},{2,3},{3,2},{4,5},{5,4},{6,7},{7,6},{8,9},{9,8},{10,11... | collective-permute-start | bytes 344072 | tf_op jit(solution)/shard_map/ppermute | solution.py:539
  7.7 0.0 copy-done.2
  7.7 0.0 copy-done.3
  7.7 0.0 copy-done.4
  7.7 2.0 %divisors.1 = (f32[2,64,1024]{2,1,0:T(8,128)S(1)}, f32[3,8,1024]{2,1,0:T(8,128)S(1)}, f32[21,8,512]{2,1,0:T(8,128)S(1)}, f32[14,3,8,128]{3,2,1,0:T(8,128)S(1)}, ...) custom-call(s32[8]{0:T(128)S(1)} %copy-done.2, s32[8]{0:T(128)S(1)} %copy-done.4, ...), custom_call_target="tpu_custom_call" | custom-call | flops 4000000 | bytes 8000000 | tf_op jit(solution)/shard_map/divisors/pallas_call | solution.py:631
  9.7 0.0 collective-permute-done.2
  9.8 0.0 collective-permute-done.1.refs_4_
  9.8 3.2 %collective-permute-done.refs_2_ = f32[7,8,512]{2,1,0:T(8,128)S(1)} collective-permute-done((f32[7,8,512]{2,1,0:T(8,128)S(1)}, f32[7,8,512]{2,1,0:T(8,128)S(1)}, u32[]{:S(2)}, u32[]{:S(2)}) %collective-permute-start) | collective-permute-done | bytes 114720 | tf_op jit(solution)/shard_map/ppermute | solution.py:551
  12.9 0.2 collective-permute-start.4
  13.1 0.4 %collective-permute-start.5 = (f32[7,8,512]{2,1,0:T(8,128)S(1)}, f32[7,8,512]{2,1,0:T(8,128)S(1)}, u32[]{:S(2)}, u32[]{:S(2)}) collective-permute-start(f32[7,8,512]{2,1,0:T(8,128)S(1)} %collective-permute-done.1.refs_4_), channel_id=1, source_target_pairs={{0,1},{1,0},{2,3},{3,2},{4,5},{5,4},{6,7},{7,6},{8,9},{9,8},{10,11... | collective-permute-start | bytes 344072 | tf_op jit(solution)/shard_map/ppermute | solution.py:539
  13.5 0.2 collective-permute-start.6
  13.6 0.0 collective-permute-done.3.refs_1_
  13.6 0.7 %collective-permute-done.4.refs_3_ = f32[7,8,512]{2,1,0:T(8,128)S(1)} collective-permute-done((f32[7,8,512]{2,1,0:T(8,128)S(1)}, f32[7,8,512]{2,1,0:T(8,128)S(1)}, u32[]{:S(2)}, u32[]{:S(2)}) %collective-permute-start.4) | collective-permute-done | bytes 114720 | tf_op jit(solution)/shard_map/ppermute | solution.py:539
  14.3 0.2 collective-permute-done.5.refs_5_
  14.4 0.3 %collective-permute-done.6.refs_6_ = f32[7,8,512]{2,1,0:T(8,128)S(1)} collective-permute-done((f32[7,8,512]{2,1,0:T(8,128)S(1)}, f32[7,8,512]{2,1,0:T(8,128)S(1)}, u32[]{:S(2)}, u32[]{:S(2)}) %collective-permute-start.6) | collective-permute-done | bytes 114720 | tf_op jit(solution)/shard_map/ppermute | solution.py:539
  14.8 0.0 copy-done
  14.8 0.0 copy-done.1
  14.8 2.6 %update.1 = (f32[3,8,1024]{2,1,0:T(8,128)}, f32[2,64,1024]{2,1,0:T(8,128)}) custom-call(s32[8]{0:T(128)S(1)} %copy-done.2, s32[4]{0:T(128)S(1)} %copy-done.3, f32[2,64,1024]{2,1,0:T(8,128)S(1)} %copy-done, f32[3,8,1024]{2,1,0:T(8,128)S(1)} %copy-done.1, f32[2,64,1024]{2,1,0:T(8,128)S(1)} %get-tuple-element.44.bound_ref, ...), custom_call_target="tpu_custom_call" | custom-call | tf_op jit(solution)/shard_map/update/pallas_call | solution.py:632
Async XLA Ops:
  0.6 14.2 %copy-start = (f32[2,64,1024]{2,1,0:T(8,128)S(1)}, f32[2,64,1024]{2,1,0:T(8,128)}, u32[]{:S(2)}) copy-start(f32[2,64,1024]{2,1,0:T(8,128)} %volume_ref.3) | copy-start | bytes 1572868
  0.6 14.1 %copy-start.1 = (f32[3,8,1024]{2,1,0:T(8,128)S(1)}, f32[3,8,1024]{2,1,0:T(8,128)}, u32[]{:S(2)}) copy-start(f32[3,8,1024]{2,1,0:T(8,128)} %measured_ref.3) | copy-start | bytes 294916
  3.8 3.9 %copy-start.2 = (s32[8]{0:T(128)S(1)}, s32[8]{0:T(128)}, u32[]{:S(2)}) copy-start(s32[8]{0:T(128)} %angle_ref.5) | copy-start | bytes 100
  3.8 3.9 %copy-start.3 = (s32[4]{0:T(128)S(1)}, s32[4]{0:T(128)}, u32[]{:S(2)}) copy-start(s32[4]{0:T(128)} %subset_ref.5) | copy-start | bytes 52
  3.8 3.9 %copy-start.4 = (s32[8]{0:T(128)S(1)}, s32[8]{0:T(128)}, u32[]{:S(2)}) copy-start(s32[8]{0:T(128)} %lift_ref.1) | copy-start | bytes 100
  3.8 5.9 %collective-permute-start.2 = (f32[7,8,512]{2,1,0:T(8,128)S(1)}, f32[7,8,512]{2,1,0:T(8,128)S(1)}, u32[]{:S(2)}, u32[]{:S(2)}) collective-permute-start(f32[7,8,512]{2,1,0:T(8,128)S(1)} %get-tuple-element.28.refs_0_), channel_id=1, source_target_pairs={{4,0},{6,2},{8,4},{1,5},{10,6},{3,7},{12,8},{5,9},{14,10},{7,11},{... | collective-permute-start | bytes 344072 | tf_op jit(solution)/shard_map/ppermute | solution.py:551
  4.3 5.4 %collective-permute-start.1 = (f32[7,8,512]{2,1,0:T(8,128)S(1)}, f32[7,8,512]{2,1,0:T(8,128)S(1)}, u32[]{:S(2)}, u32[]{:S(2)}) collective-permute-start(f32[7,8,512]{2,1,0:T(8,128)S(1)} %get-tuple-element.28.refs_0_), channel_id=1, source_target_pairs={{2,0},{4,2},{1,3},{6,4},{3,5},{8,6},{5,7},{10,8},{7,9},{12,10},{9,... | collective-permute-start | bytes 344072 | tf_op jit(solution)/shard_map/ppermute | solution.py:551
  6.4 6.5 %collective-permute-start = (f32[7,8,512]{2,1,0:T(8,128)S(1)}, f32[7,8,512]{2,1,0:T(8,128)S(1)}, u32[]{:S(2)}, u32[]{:S(2)}) collective-permute-start(f32[7,8,512]{2,1,0:T(8,128)S(1)} %get-tuple-element.28.refs_0_), channel_id=1, source_target_pairs={{3,1},{0,2},{5,3},{2,4},{7,5},{4,6},{9,7},{6,8},{11,9},{8,10},{13,... | collective-permute-start | bytes 344072 | tf_op jit(solution)/shard_map/ppermute | solution.py:551
  7.0 6.6 %collective-permute-start.3 = (f32[7,8,512]{2,1,0:T(8,128)S(1)}, f32[7,8,512]{2,1,0:T(8,128)S(1)}, u32[]{:S(2)}, u32[]{:S(2)}) collective-permute-start(f32[7,8,512]{2,1,0:T(8,128)S(1)} %get-tuple-element.28.refs_0_), channel_id=1, source_target_pairs={{0,1},{1,0},{2,3},{3,2},{4,5},{5,4},{6,7},{7,6},{8,9},{9,8},{10,11... | collective-permute-start | bytes 344072 | tf_op jit(solution)/shard_map/ppermute | solution.py:539
  12.9 1.3 %collective-permute-start.4 = (f32[7,8,512]{2,1,0:T(8,128)S(1)}, f32[7,8,512]{2,1,0:T(8,128)S(1)}, u32[]{:S(2)}, u32[]{:S(2)}) collective-permute-start(f32[7,8,512]{2,1,0:T(8,128)S(1)} %collective-permute-done.refs_2_), channel_id=1, source_target_pairs={{0,1},{1,0},{2,3},{3,2},{4,5},{5,4},{6,7},{7,6},{8,9},{9,8},{10,11... | collective-permute-start | bytes 344072 | tf_op jit(solution)/shard_map/ppermute | solution.py:539
  13.1 1.3 %collective-permute-start.5 = (f32[7,8,512]{2,1,0:T(8,128)S(1)}, f32[7,8,512]{2,1,0:T(8,128)S(1)}, u32[]{:S(2)}, u32[]{:S(2)}) collective-permute-start(f32[7,8,512]{2,1,0:T(8,128)S(1)} %collective-permute-done.1.refs_4_), channel_id=1, source_target_pairs={{0,1},{1,0},{2,3},{3,2},{4,5},{5,4},{6,7},{7,6},{8,9},{9,8},{10,11... | collective-permute-start | bytes 344072 | tf_op jit(solution)/shard_map/ppermute | solution.py:539
  13.5 1.3 %collective-permute-start.6 = (f32[7,8,512]{2,1,0:T(8,128)S(1)}, f32[7,8,512]{2,1,0:T(8,128)S(1)}, u32[]{:S(2)}, u32[]{:S(2)}) collective-permute-start(f32[7,8,512]{2,1,0:T(8,128)S(1)} %collective-permute-done.2), channel_id=1, source_target_pairs={{0,1},{1,0},{2,3},{3,2},{4,5},{5,4},{6,7},{7,6},{8,9},{9,8},{10,11... | collective-permute-start | bytes 344072 | tf_op jit(solution)/shard_map/ppermute | solution.py:539

commit v9 on v8

--- a/solution.py
+++ b/solution.py
@@ -18,6 +18,7 @@
 LANES = 128
 SUBLANES = 8
 F32 = jnp.float32
+FULL, NEAR, NEAR_SHARED, FAR = range(4)
 VMEM_LIMIT = 8 * 1024 * 1024
 
 
@@ -126,12 +127,23 @@
     return jnp.broadcast_to(tile[:, at : at + 1], (SUBLANES, LANES))
 
 
-def subset_cone(slab, slab_count, order, slab_depth, row_share, flat, lifts):
+def slabs_of(slab, order):
+    return [slab + (1 - 2 * lax.rem(slab, 2)) * away for away in order]
+
+
+def turned(slab, kinds):
+    odd = lax.rem(slab, 2)
+    return [{NEAR: 1 - odd, NEAR_SHARED: odd}.get(kind, 0) for kind in kinds]
+
+
+def subset_cone(slab, slab_count, order, kinds, slab_depth, row_share, flat, lifts):
     lane = lane_index()
     total_rows, total_slices = row_share * slab_count, slab_depth * slab_count
-    origin = slabs_of(slab, order)
+    origin, turns = slabs_of(slab, order), turned(slab, kinds)
     source = sum(jnp.where(lane >= row_share * b, 1, 0) for b in range(1, len(order)))
-    rows = spread_scalars(lambda b: origin[b], len(order), source) * row_share + (lane - source * row_share)
+    within = lane - source * row_share
+    within = jnp.where(spread_scalars(lambda b: turns[b], len(order), source) == 1, row_share - 1 - within, within)
+    rows = spread_scalars(lambda b: origin[b], len(order), source) * row_share + within
     real = (rows >= 0) & (rows < total_rows) & (lane < row_share * len(order))
     sample = cone_sample(rows.astype(F32), lifts, flat, total_rows, total_slices)
     weights = []
@@ -140,10 +152,6 @@
         use = real & (at >= 0) & (at < total_slices)
         weights.append(jnp.where(use, jnp.maximum(0.0, 1.0 - jnp.abs(sample - at.astype(F32))), 0.0))
     return sample, weights
-
-
-def slabs_of(slab, order):
-    return [slab + (1 - 2 * lax.rem(slab, 2)) * away for away in order]
 
 
 def adjoint_taps(tile, cosine, column_count, cell_count, half):
@@ -215,11 +223,16 @@
 
 
 def project_kernel(
+    slab_count,
     angle_ref,
+    lift_ref,
     subset_ref,
     volume_ref,
     measured_ref,
     block_ref,
+    near_ref,
+    low_ref,
+    high_ref,
     cover_ref,
     rise_ref,
     first_ref,
@@ -238,13 +251,40 @@
     zero = jnp.zeros((SUBLANES, LANES), F32)
     width = column_count // 2
 
-    for row in range(row_share):
-        for member in range(subset_count):
-            view = subset_ref[member]
-            for side in range(2):
-                block_ref[2 * slab_depth + row, side * subset_count + member : side * subset_count + member + 1, :] = (
-                    measured_ref[row, pl.ds(view, 1), side * width : (side + 1) * width]
-                )
+    assert (slab_depth, row_share) == (2, 3)
+    slab = lax.axis_index("slab")
+    odd = lax.rem(slab, 2)
+    grows = odd == 1
+    far_row = jnp.where(grows, 2, 0)
+    for member in range(subset_count):
+        view = pl.ds(subset_ref[member], 1)
+        for side in range(2):
+            at, cut = side * subset_count + member, slice(side * width, (side + 1) * width)
+            rows = [measured_ref[row, view, cut] for row in range(row_share)]
+            for row in range(row_share):
+                block_ref[2 * slab_depth + row, at : at + 1, :] = rows[row]
+            near_ref[2 * slab_depth, at : at + 1, :] = rows[1]
+            near_ref[2 * slab_depth + 1, at : at + 1, :] = measured_ref[far_row, view, cut]
+            low_ref[2 * slab_depth, at : at + 1, :] = rows[2]
+            high_ref[2 * slab_depth, at : at + 1, :] = rows[2]
+
+    cosine, _, flat = angle_facts(spread_scalars(lambda v: angle_ref[v], view_count, sub))
+    lifts = spread_scalars(lambda v: lift_ref[v], view_count, sub).astype(F32)
+    ends = [
+        cone_sample((slab * row_share + row).astype(F32), lifts, flat, row_share * slab_count, slab_depth * slab_count)
+        - (slab * slab_depth).astype(F32)
+        for row in (0, row_share - 1)
+    ]
+    picked = sub == subset_ref[0]
+    for member in range(1, subset_count):
+        picked = picked | (sub == subset_ref[member])
+    picked = jnp.where(picked, 1, 0)
+    as_int = lambda mask: jnp.where(mask, 1, 0)
+    near_up, near_down = picked * as_int(ends[1] > 0.75), picked * as_int(ends[0] < 0.25)
+    far_up, far_down = picked * as_int(ends[1] > 2.5), picked * as_int(ends[0] < -1.5)
+    near_places = [(near_up * odd) == 1, (near_down * (1 - odd)) == 1]
+    high_places = (far_up * odd + far_down * (1 - odd)) == 1
+    low_places = (far_up * (1 - odd) + far_down * odd) == 1
 
     for depth in range(slab_depth):
         for group in range(groups):
@@ -301,11 +341,10 @@
     views = range(view_count)
     for depth in range(slab_depth):
         store(depth, [rows_summed([tile_of(part_ref, (depth, v), t) for v in views]) for t in range(tiles + 1)])
-    flat = zero + float(row_count)
+    level = zero + float(row_count)
     ends = [rows_summed([end_ref[e, v, :, :] for v in views]) for e in range(2)]
-    store(slab_depth, [ends[0]] + [flat] * (tiles - 1) + [ends[1]])
-
-    cosine, _, _ = angle_facts(spread_scalars(lambda v: angle_ref[v], view_count, sub))
+    store(slab_depth, [ends[0]] + [level] * (tiles - 1) + [ends[1]])
+
     factor = 1.0 / (row_count * cosine)
     least = angle_table()[0].min()
     for tile in range(column_count // LANES):
@@ -318,7 +357,7 @@
         ends = [column_center(tile * LANES + e, c, column_count, cell_count) for e in (0, LANES - 1) for c in (1.0, least)]
         low = min(max(math.floor(min(ends) - 1e-2) + shift, shift - 2), shift + cell_count) // LANES
         high = min(max(math.floor(max(ends) + 1e-2) + shift, shift - 2), shift + cell_count) // LANES
-        cells, slopes = [zero] * slab_depth + [flat], [zero] * (slab_depth + 1)
+        cells, slopes = [zero] * slab_depth + [level], [zero] * (slab_depth + 1)
         for source in range(low, high + 1):
             here = block == source
             for at in range(slab_depth + 1):
@@ -329,13 +368,20 @@
         profiles = [(c + fraction * s) * factor for c, s in zip(cells, slopes)]
         side, inner = divmod(tile * LANES, width)
         for depth in range(slab_depth):
-            block_ref[depth * 2 + side, :, inner : inner + LANES] = profiles[depth]
+            to = (depth * 2 + side, slice(None), slice(inner, inner + LANES))
+            measured = tile_of(measured_ref, (depth,), tile)
+            last = tile_of(measured_ref, (depth * (row_share - 1),), tile)
+            block_ref[to] = profiles[depth]
+            near_ref[to] = jnp.where(near_places[depth], last, profiles[depth])
+            low_ref[to] = jnp.where(low_places, measured, profiles[depth])
+            high_ref[to] = jnp.where(high_places, measured, profiles[depth])
         cover_ref[:, tile * LANES : (tile + 1) * LANES] = profiles[slab_depth]
 
 
 def divisor_kernel(
     slab_count,
     order,
+    kinds,
     angle_ref,
     lift_ref,
     subset_ref,
@@ -386,7 +432,7 @@
         for side in range(2):
             at = slice(side * subset_count + member, side * subset_count + member + 1)
             sub_ref[at, :] = cover_ref[view, side * width : (side + 1) * width]
-    sample, weights = subset_cone(slab, slab_count, order, slab_depth, row_share, flat, lifts)
+    sample, weights = subset_cone(slab, slab_count, order, kinds, slab_depth, row_share, flat, lifts)
     total = cone_total(sample, total_slices)
     for place in range(row_share * len(order)):
         for z, w in enumerate(weights):
@@ -430,6 +476,7 @@
 
 def update_kernel(
     order,
+    kinds,
     angle_ref,
     subset_ref,
     volume_ref,
@@ -444,14 +491,16 @@
     *refs,
 ):
     blocks = refs[: len(order)]
-    residual_ref, updated_ref, profile_ref, spread_ref, cell_ref, slope_ref, rest_ref, new_ref, sent = refs[len(order) :]
+    residual_ref, updated_ref, profile_ref, spread_ref, cell_ref, slope_ref, rest_ref, new_ref, row_ref, sent = refs[len(order) :]
     slab_depth, row_count, cell_count = volume_ref.shape
     row_share, view_count, column_count = measured_ref.shape
     subset_count = subset_ref.shape[0]
     tiles, columns = cell_count // LANES, column_count // LANES
     width = column_count // 2
     zero = jnp.zeros((SUBLANES, LANES), F32)
-    odd = lax.rem(lax.axis_index("slab"), 2)
+    slab = lax.axis_index("slab")
+    odd = lax.rem(slab, 2)
+    turns = turned(slab, kinds)
     mate_block, other_block = (blocks[order.index(away)] for away in (1, -1))
 
     groups = row_count // SUBLANES
@@ -480,17 +529,29 @@
                 profile_ref[1 + depth, at, :] = blocks[0][depth * 2 + side, view, :]
             profile_ref[1 + slab_depth, at, :] = jnp.where(odd == 0, mate[1], other[1])
 
+    moved = [(b, j) for b, kind in enumerate(kinds) for j in range({FULL: 0, FAR: 2}.get(kind, 1))]
+    for at_row, (b, j) in enumerate(moved):
+        depth = turns[b] if kinds[b] in (NEAR, NEAR_SHARED) else j
+        for member in range(subset_count):
+            view = pl.ds(subset_ref[member], 1)
+            for side in range(2):
+                at = slice(side * subset_count + member, side * subset_count + member + 1)
+                row_ref[at_row, at, :] = blocks[b][depth * 2 + side, view, :]
+
     inner_tiles = width // LANES
     spread = [[zero] * inner_tiles for _ in range(slab_depth)]
     for place in range(row_share * len(order)):
         weight = [cone_ref[place, z, :, :] for z in range(slab_depth + 2)]
-        block, row = blocks[place // row_share], place % row_share
+        block, row = divmod(place, row_share)
+        here = (block, row) in moved
+        held = row_ref if here else blocks[block]
+        at_row = moved.index((block, row)) if here else 2 * slab_depth + row - sum(b == block for b, _ in moved)
         for tile in range(inner_tiles):
             cut = slice(tile * LANES, (tile + 1) * LANES)
             image = weight[0] * profile_ref[0, :, cut]
             for z in range(1, slab_depth + 2):
                 image = image + weight[z] * profile_ref[z, :, cut]
-            rest = (block[2 * slab_depth + row, :, cut] - image) * rows_ref[place, :, cut]
+            rest = (held[at_row, :, cut] - image) * rows_ref[place, :, cut]
             for depth in range(slab_depth):
                 spread[depth][tile] = spread[depth][tile] + weight[1 + depth] * rest
     for depth in range(slab_depth):
@@ -556,25 +617,29 @@
 
 
 def window(reach):
-    order = [0, 1]
+    order, kinds = [0, 1], [FULL, FULL]
     for distance in fetches(reach):
-        order += [at for at in (2 * distance, 1 - 2 * distance) if abs(at) <= reach]
+        near = distance == 1
+        for away, kind in ((2 * distance, NEAR if near else FAR), (1 - 2 * distance, NEAR_SHARED if near else FAR)):
+            if abs(away) <= reach:
+                order.append(away)
+                kinds.append(kind)
     assert sorted(order) == list(range(-reach, reach + 1))
-    return tuple(order)
-
-
-def gathered(own, reach, meanwhile):
-    received = {distance: from_chip(own, distance) for distance in fetches(reach)}
+    return tuple(order), tuple(kinds)
+
+
+def gathered(own, near, low, high, reach, meanwhile):
+    sent = {distance: near if distance == 1 else high if distance > 0 else low for distance in fetches(reach)}
+    received = {distance: from_chip(block, distance) for distance, block in sent.items()}
     blocks = {0: own, 1: swapped(own)}
     done = meanwhile()
-    for part in ([d for d in received if abs(d) > 1], [-1, 1]):
-        arrived, done = lax.optimization_barrier(([received[d] for d in part], done))
-        for distance, block in zip(part, arrived):
-            if 2 * abs(distance) <= reach:
-                blocks[2 * distance] = block
-            if abs(1 - 2 * distance) <= reach:
-                blocks[1 - 2 * distance] = swapped(block)
-    return [blocks[away] for away in window(reach)], done
+    arrived, done = lax.optimization_barrier((list(received.values()), done))
+    for distance, block in zip(received, arrived):
+        if 2 * abs(distance) <= reach:
+            blocks[2 * distance] = block
+        if abs(1 - 2 * distance) <= reach:
+            blocks[1 - 2 * distance] = swapped(block)
+    return [blocks[away] for away in window(reach)[0]], done
 
 
 def per_device(volume, measured, view_angle, view_lift, subset):
@@ -589,15 +654,18 @@
     small = pltpu.CompilerParams(vmem_limit_bytes=VMEM_LIMIT)
     smem, vmem = pl.BlockSpec(memory_space=pltpu.SMEM), pl.BlockSpec(memory_space=pltpu.VMEM)
     wide = (tiles + 1) * LANES
-    block_shape = (2 * slab_depth + row_share, SUBLANES, column_count // 2)
-    own, cover = pl.pallas_call(
-        project_kernel,
+    block_of = lambda rows: pltpu.VMEM((2 * slab_depth + rows, SUBLANES, column_count // 2), F32)
+    own, near, low, high, cover = pl.pallas_call(
+        functools.partial(project_kernel, slab_count),
         out_shape=(
-            pltpu.VMEM(block_shape, F32),
+            block_of(row_share),
+            block_of(2),
+            block_of(1),
+            block_of(1),
             pltpu.VMEM((view_count, column_count), F32),
         ),
-        in_specs=[smem, smem, vmem, vmem],
-        out_specs=(vmem, vmem),
+        in_specs=[smem] * 3 + [vmem] * 2,
+        out_specs=(vmem,) * 5,
         scratch_shapes=[
             pltpu.VMEM(volume.shape, F32),
             pltpu.VMEM((slab_depth, row_count, LANES), F32),
@@ -607,11 +675,11 @@
         + [pltpu.VMEM((slab_depth + 1, SUBLANES, wide), F32)] * 2,
         compiler_params=small,
         name="project",
-    )(*map(there, (view_angle, subset, volume, measured)))
+    )(*map(there, (view_angle, view_lift, subset, volume, measured)))
     cover = here(cover)
-    order = window(reach)
+    order, kinds = window(reach)
     divide = pl.pallas_call(
-        functools.partial(divisor_kernel, slab_count, order),
+        functools.partial(divisor_kernel, slab_count, order, kinds),
         out_shape=(
             pltpu.VMEM(volume.shape, F32),
             pltpu.VMEM(measured.shape, F32),
@@ -628,9 +696,9 @@
         compiler_params=small,
         name="divisors",
     )
-    blocks, divisors = gathered(own, reach, lambda: divide(view_angle, view_lift, subset, cover))
+    blocks, divisors = gathered(own, near, low, high, reach, lambda: divide(view_angle, view_lift, subset, cover))
     return pl.pallas_call(
-        functools.partial(update_kernel, order),
+        functools.partial(update_kernel, order, kinds),
         out_shape=(
             jax.ShapeDtypeStruct(measured.shape, F32),
             jax.ShapeDtypeStruct(volume.shape, F32),
@@ -644,6 +712,7 @@
             pltpu.VMEM((SUBLANES, wide), F32),
             pltpu.VMEM(measured.shape, F32),
             pltpu.VMEM(volume.shape, F32),
+            pltpu.VMEM((2 * len(order), SUBLANES, column_count // 2), F32),
             pltpu.SemaphoreType.DMA((row_count // SUBLANES + 1,)),
         ],
         compiler_params=small,

time: 17.5 us -> 17.2 us (0.983)
  waiting for transfers between devices: 4.35 us -> 3.03 us
  starting transfers between devices: 4.51 us -> 5.51 us
    ppermute x3, waiting for transfers between devices: 3.18 us -> 1.75 us  [from_chip(): return lax.ppermute(block, 'slab', pairs)]
    ppermute x4, starting transfers between devices: 1.38 us -> 2.41 us  [swapped(): lax.ppermute(block, 'slab', [(i, i ^ 1) for i in range(lax.axis_size('sla...]
  transfers between devices with their start and end apart: 7 -> 7, of which waited for: 4 -> 3; matrix products, arithmetic and copies ran while one was open for 0% -> 0% of each run, Pallas kernels for 12% -> 12%
where the time goes in v9:
time: 17.2 us; the launch traced here: 17.1 us
  Pallas kernels  7.84 us (46%)
  starting transfers between devices  5.51 us (32%)
  waiting for transfers between devices  3.03 us (18%)
  between operations  0.69 us (4%)
    pallas_call x1, Pallas kernels, per_device(): pl.pallas_call(functools.partial(project_kernel, slab_count), out_shape=(...  3.13 us
    ppermute x3, starting transfers between devices, from_chip(): return lax.ppermute(block, 'slab', pairs)  3.1 us
    pallas_call x1, Pallas kernels, per_device(): pl.pallas_call(functools.partial(update_kernel, order, kinds), out_shape=...  2.66 us
    ppermute x4, starting transfers between devices, swapped(): lax.ppermute(block, 'slab', [(i, i ^ 1) for i in range(lax.axis_size('sla...  2.41 us
    pallas_call x1, Pallas kernels, per_device(): divide(view_angle, view_lift, subset, cover)  2.05 us
    ppermute x3, waiting for transfers between devices, from_chip(): return lax.ppermute(block, 'slab', pairs)  1.75 us
    ppermute x4, waiting for transfers between devices, swapped(): lax.ppermute(block, 'slab', [(i, i ^ 1) for i in range(lax.axis_size('sla...  1.28 us
  transfers between devices with their start and end apart: 7, of which 3 were waited for; matrix products, arithmetic and copies ran while one was open for 0% of the time, Pallas kernels for 12%

profile of v9, /device:TPU:0, one launch (start us, length us, event | category | flops | bytes accessed | tf_op | source)
XLA Modules:
  0.0 17.1 jit_solution(9541963427280992597)
XLA Ops:
  0.6 0.0 copy-start
  0.6 0.0 copy-start.1
  0.6 3.1 %project.1 = (f32[7,8,512]{2,1,0:T(8,128)S(1)}, f32[6,8,512]{2,1,0:T(8,128)S(1)}, f32[5,8,512]{2,1,0:T(8,128)S(1)}, f32[5,8,512]{2,1,0:T(8,128)S(1)}, f32[8,1024]{1,0:T(8,128)S(1)}) custom-call(s32[8]{0:T(128)} %angle_ref.5, s32[8]{0:T(128)} %lift_ref.3, s32[4]{0:T(128)} %subset_ref.5, f32[2,64,1024]{2,1,0:T(8,128)} %volume_ref.3, f32[3,8,1024]{2,1,0:T(8,128)} %measured_ref.3), custom_call_target="tpu_custom_call" | custom-call | tf_op jit(solution)/shard_map/project/pallas_call | solution.py:658
  3.8 0.5 %collective-permute-start.1 = (f32[6,8,512]{2,1,0:T(8,128)S(1)}, f32[6,8,512]{2,1,0:T(8,128)S(1)}, u32[]{:S(2)}, u32[]{:S(2)}) collective-permute-start(f32[6,8,512]{2,1,0:T(8,128)S(1)} %get-tuple-element.25), channel_id=1, source_target_pairs={{2,0},{4,2},{1,3},{6,4},{3,5},{8,6},{5,7},{10,8},{7,9},{12,10},{9,... | collective-permute-start | bytes 294920 | tf_op jit(solution)/shard_map/ppermute | solution.py:612
  4.3 2.6 %collective-permute-start = (f32[5,8,512]{2,1,0:T(8,128)S(1)}, f32[5,8,512]{2,1,0:T(8,128)S(1)}, u32[]{:S(2)}, u32[]{:S(2)}) collective-permute-start(f32[5,8,512]{2,1,0:T(8,128)S(1)} %get-tuple-element.24), channel_id=1, source_target_pairs={{3,1},{0,2},{5,3},{2,4},{7,5},{4,6},{9,7},{6,8},{11,9},{8,10},{13,... | collective-permute-start | bytes 245768 | tf_op jit(solution)/shard_map/ppermute | solution.py:612
  6.9 0.0 collective-permute-start.2
  6.9 0.0 copy-start.2
  6.9 0.0 copy-start.3
  6.9 0.0 copy-start.4
  6.9 1.9 %collective-permute-start.3 = (f32[7,8,512]{2,1,0:T(8,128)S(1)}, f32[7,8,512]{2,1,0:T(8,128)S(1)}, u32[]{:S(2)}, u32[]{:S(2)}) collective-permute-start(f32[7,8,512]{2,1,0:T(8,128)S(1)} %get-tuple-element.42.refs_0_), channel_id=1, source_target_pairs={{0,1},{1,0},{2,3},{3,2},{4,5},{5,4},{6,7},{7,6},{8,9},{9,8},{10,11... | collective-permute-start | bytes 344072 | tf_op jit(solution)/shard_map/ppermute | solution.py:600
  8.8 0.0 copy-done.2
  8.8 0.0 copy-done.3
  8.8 0.0 copy-done.4
  8.8 2.0 %divisors.1 = (f32[2,64,1024]{2,1,0:T(8,128)S(1)}, f32[3,8,1024]{2,1,0:T(8,128)S(1)}, f32[21,8,512]{2,1,0:T(8,128)S(1)}, f32[14,3,8,128]{3,2,1,0:T(8,128)S(1)}, ...) custom-call(s32[8]{0:T(128)S(1)} %copy-done.2, s32[8]{0:T(128)S(1)} %copy-done.4, ...), custom_call_target="tpu_custom_call" | custom-call | flops 4000000 | bytes 8000000 | tf_op jit(solution)/shard_map/divisors/pallas_call | solution.py:699
  10.9 0.0 collective-permute-done.refs_2_
  10.9 1.7 %collective-permute-done.2 = f32[5,8,512]{2,1,0:T(8,128)S(1)} collective-permute-done((f32[5,8,512]{2,1,0:T(8,128)S(1)}, f32[5,8,512]{2,1,0:T(8,128)S(1)}, u32[]{:S(2)}, u32[]{:S(2)}) %collective-permute-start.2) | collective-permute-done | bytes 81952 | tf_op jit(solution)/shard_map/ppermute | solution.py:612
  12.6 0.0 collective-permute-done.1.refs_4_
  12.6 0.0 collective-permute-start.5
  12.6 0.5 %collective-permute-start.6 = (f32[5,8,512]{2,1,0:T(8,128)S(1)}, f32[5,8,512]{2,1,0:T(8,128)S(1)}, u32[]{:S(2)}, u32[]{:S(2)}) collective-permute-start(f32[5,8,512]{2,1,0:T(8,128)S(1)} %collective-permute-done.2), channel_id=1, source_target_pairs={{0,1},{1,0},{2,3},{3,2},{4,5},{5,4},{6,7},{7,6},{8,9},{9,8},{10,11... | collective-permute-start | bytes 245768 | tf_op jit(solution)/shard_map/ppermute | solution.py:600
  13.1 0.0 collective-permute-start.4
  13.1 0.0 collective-permute-done.3.refs_1_
  13.1 0.9 %collective-permute-done.6.refs_6_ = f32[5,8,512]{2,1,0:T(8,128)S(1)} collective-permute-done((f32[5,8,512]{2,1,0:T(8,128)S(1)}, f32[5,8,512]{2,1,0:T(8,128)S(1)}, u32[]{:S(2)}, u32[]{:S(2)}) %collective-permute-start.6) | collective-permute-done | bytes 81952 | tf_op jit(solution)/shard_map/ppermute | solution.py:600
  14.1 0.4 %collective-permute-done.4.refs_3_ = f32[5,8,512]{2,1,0:T(8,128)S(1)} collective-permute-done((f32[5,8,512]{2,1,0:T(8,128)S(1)}, f32[5,8,512]{2,1,0:T(8,128)S(1)}, u32[]{:S(2)}, u32[]{:S(2)}) %collective-permute-start.4) | collective-permute-done | bytes 81952 | tf_op jit(solution)/shard_map/ppermute | solution.py:600
  14.4 0.0 collective-permute-done.5.refs_5_
  14.4 0.0 copy-done
  14.4 0.0 copy-done.1
  14.4 2.7 %update.1 = (f32[3,8,1024]{2,1,0:T(8,128)}, f32[2,64,1024]{2,1,0:T(8,128)}) custom-call(s32[8]{0:T(128)S(1)} %copy-done.2, s32[4]{0:T(128)S(1)} %copy-done.3, f32[2,64,1024]{2,1,0:T(8,128)S(1)} %copy-done, f32[3,8,1024]{2,1,0:T(8,128)S(1)} %copy-done.1, f32[2,64,1024]{2,1,0:T(8,128)S(1)} %get-tuple-element.35.bound_ref, ...), custom_call_target="tpu_custom_call" | custom-call | tf_op jit(solution)/shard_map/update/pallas_call | solution.py:700
Async XLA Ops:
  0.6 13.8 %copy-start = (f32[2,64,1024]{2,1,0:T(8,128)S(1)}, f32[2,64,1024]{2,1,0:T(8,128)}, u32[]{:S(2)}) copy-start(f32[2,64,1024]{2,1,0:T(8,128)} %volume_ref.3) | copy-start | bytes 1572868
  0.6 13.8 %copy-start.1 = (f32[3,8,1024]{2,1,0:T(8,128)S(1)}, f32[3,8,1024]{2,1,0:T(8,128)}, u32[]{:S(2)}) copy-start(f32[3,8,1024]{2,1,0:T(8,128)} %measured_ref.3) | copy-start | bytes 294916
  3.8 8.8 %collective-permute-start.1 = (f32[6,8,512]{2,1,0:T(8,128)S(1)}, f32[6,8,512]{2,1,0:T(8,128)S(1)}, u32[]{:S(2)}, u32[]{:S(2)}) collective-permute-start(f32[6,8,512]{2,1,0:T(8,128)S(1)} %get-tuple-element.25), channel_id=1, source_target_pairs={{2,0},{4,2},{1,3},{6,4},{3,5},{8,6},{5,7},{10,8},{7,9},{12,10},{9,... | collective-permute-start | bytes 294920 | tf_op jit(solution)/shard_map/ppermute | solution.py:612
  4.3 6.6 %collective-permute-start = (f32[5,8,512]{2,1,0:T(8,128)S(1)}, f32[5,8,512]{2,1,0:T(8,128)S(1)}, u32[]{:S(2)}, u32[]{:S(2)}) collective-permute-start(f32[5,8,512]{2,1,0:T(8,128)S(1)} %get-tuple-element.24), channel_id=1, source_target_pairs={{3,1},{0,2},{5,3},{2,4},{7,5},{4,6},{9,7},{6,8},{11,9},{8,10},{13,... | collective-permute-start | bytes 245768 | tf_op jit(solution)/shard_map/ppermute | solution.py:612
  6.9 5.7 %collective-permute-start.2 = (f32[5,8,512]{2,1,0:T(8,128)S(1)}, f32[5,8,512]{2,1,0:T(8,128)S(1)}, u32[]{:S(2)}, u32[]{:S(2)}) collective-permute-start(f32[5,8,512]{2,1,0:T(8,128)S(1)} %get-tuple-element.26), channel_id=1, source_target_pairs={{4,0},{6,2},{8,4},{1,5},{10,6},{3,7},{12,8},{5,9},{14,10},{7,11},{... | collective-permute-start | bytes 245768 | tf_op jit(solution)/shard_map/ppermute | solution.py:612
  6.9 1.9 %copy-start.2 = (s32[8]{0:T(128)S(1)}, s32[8]{0:T(128)}, u32[]{:S(2)}) copy-start(s32[8]{0:T(128)} %angle_ref.5) | copy-start | bytes 100
  6.9 1.9 %copy-start.3 = (s32[4]{0:T(128)S(1)}, s32[4]{0:T(128)}, u32[]{:S(2)}) copy-start(s32[4]{0:T(128)} %subset_ref.5) | copy-start | bytes 52
  6.9 1.9 %copy-start.4 = (s32[8]{0:T(128)S(1)}, s32[8]{0:T(128)}, u32[]{:S(2)}) copy-start(s32[8]{0:T(128)} %lift_ref.3) | copy-start | bytes 100
  6.9 6.2 %collective-permute-start.3 = (f32[7,8,512]{2,1,0:T(8,128)S(1)}, f32[7,8,512]{2,1,0:T(8,128)S(1)}, u32[]{:S(2)}, u32[]{:S(2)}) collective-permute-start(f32[7,8,512]{2,1,0:T(8,128)S(1)} %get-tuple-element.42.refs_0_), channel_id=1, source_target_pairs={{0,1},{1,0},{2,3},{3,2},{4,5},{5,4},{6,7},{7,6},{8,9},{9,8},{10,11... | collective-permute-start | bytes 344072 | tf_op jit(solution)/shard_map/ppermute | solution.py:600
  12.6 1.8 %collective-permute-start.5 = (f32[6,8,512]{2,1,0:T(8,128)S(1)}, f32[6,8,512]{2,1,0:T(8,128)S(1)}, u32[]{:S(2)}, u32[]{:S(2)}) collective-permute-start(f32[6,8,512]{2,1,0:T(8,128)S(1)} %collective-permute-done.1.refs_4_), channel_id=1, source_target_pairs={{0,1},{1,0},{2,3},{3,2},{4,5},{5,4},{6,7},{7,6},{8,9},{9,8},{10,11... | collective-permute-start | bytes 294920 | tf_op jit(solution)/shard_map/ppermute | solution.py:600
  12.6 1.4 %collective-permute-start.6 = (f32[5,8,512]{2,1,0:T(8,128)S(1)}, f32[5,8,512]{2,1,0:T(8,128)S(1)}, u32[]{:S(2)}, u32[]{:S(2)}) collective-permute-start(f32[5,8,512]{2,1,0:T(8,128)S(1)} %collective-permute-done.2), channel_id=1, source_target_pairs={{0,1},{1,0},{2,3},{3,2},{4,5},{5,4},{6,7},{7,6},{8,9},{9,8},{10,11... | collective-permute-start | bytes 245768 | tf_op jit(solution)/shard_map/ppermute | solution.py:600
  13.1 1.3 %collective-permute-start.4 = (f32[5,8,512]{2,1,0:T(8,128)S(1)}, f32[5,8,512]{2,1,0:T(8,128)S(1)}, u32[]{:S(2)}, u32[]{:S(2)}) collective-permute-start(f32[5,8,512]{2,1,0:T(8,128)S(1)} %collective-permute-done.refs_2_), channel_id=1, source_target_pairs={{0,1},{1,0},{2,3},{3,2},{4,5},{5,4},{6,7},{7,6},{8,9},{9,8},{10,11... | collective-permute-start | bytes 245768 | tf_op jit(solution)/shard_map/ppermute | solution.py:600

commit v10 on v9

--- a/solution.py
+++ b/solution.py
@@ -631,8 +631,9 @@
 def gathered(own, near, low, high, reach, meanwhile):
     sent = {distance: near if distance == 1 else high if distance > 0 else low for distance in fetches(reach)}
     received = {distance: from_chip(block, distance) for distance, block in sent.items()}
+    done = meanwhile()
+    own, done = lax.optimization_barrier((own, done))
     blocks = {0: own, 1: swapped(own)}
-    done = meanwhile()
     arrived, done = lax.optimization_barrier((list(received.values()), done))
     for distance, block in zip(received, arrived):
         if 2 * abs(distance) <= reach:

time: 17.2 us -> 17.2 us (level)
  local copies, waits for them, and re-layouts: 0.02 us -> 0.68 us
  starting transfers between devices: 5.51 us -> 4.91 us
    unnamed x10, local copies, waits for them, and re-layouts: 0.02 us -> 0.68 us
    ppermute x4, starting transfers between devices: 2.41 us -> 1.82 us  [swapped(): lax.ppermute(block, 'slab', [(i, i ^ 1) for i in range(lax.axis_size('sla...]
where the time goes in v10:
time: 17.2 us; the launch traced here: 17.1 us
  Pallas kernels  7.84 us (46%)
  starting transfers between devices  4.91 us (29%)
  waiting for transfers between devices  2.97 us (17%)
  local copies, waits for them, and re-layouts  0.68 us (4%)
  between operations  0.68 us (4%)
    pallas_call x1, Pallas kernels, per_device(): pl.pallas_call(functools.partial(project_kernel, slab_count), out_shape=(...  3.13 us
    ppermute x3, starting transfers between devices, from_chip(): return lax.ppermute(block, 'slab', pairs)  3.1 us
    pallas_call x1, Pallas kernels, per_device(): pl.pallas_call(functools.partial(update_kernel, order, kinds), out_shape=...  2.65 us
    pallas_call x1, Pallas kernels, per_device(): divide(view_angle, view_lift, subset, cover)  2.05 us
    ppermute x4, starting transfers between devices, swapped(): lax.ppermute(block, 'slab', [(i, i ^ 1) for i in range(lax.axis_size('sla...  1.82 us
    ppermute x3, waiting for transfers between devices, from_chip(): return lax.ppermute(block, 'slab', pairs)  1.7 us
    ppermute x4, waiting for transfers between devices, swapped(): lax.ppermute(block, 'slab', [(i, i ^ 1) for i in range(lax.axis_size('sla...  1.28 us
    unnamed x10, local copies, waits for them, and re-layouts  0.68 us
  transfers between devices with their start and end apart: 7, of which 3 were waited for; matrix products, arithmetic and copies ran while one was open for 0% of the time, Pallas kernels for 12%

profile of v10, /device:TPU:0, one launch (start us, length us, event | category | flops | bytes accessed | tf_op | source)
XLA Modules:
  0.0 17.1 jit_solution(8838910167110165296)
XLA Ops:
  0.6 0.0 copy-start
  0.6 0.0 copy-start.1
  0.6 3.1 %project.1 = (f32[7,8,512]{2,1,0:T(8,128)S(1)}, f32[6,8,512]{2,1,0:T(8,128)S(1)}, f32[5,8,512]{2,1,0:T(8,128)S(1)}, f32[5,8,512]{2,1,0:T(8,128)S(1)}, f32[8,1024]{1,0:T(8,128)S(1)}) custom-call(s32[8]{0:T(128)} %angle_ref.5, s32[8]{0:T(128)} %lift_ref.3, s32[4]{0:T(128)} %subset_ref.5, f32[2,64,1024]{2,1,0:T(8,128)} %volume_ref.3, f32[3,8,1024]{2,1,0:T(8,128)} %measured_ref.3), custom_call_target="tpu_custom_call" | custom-call | tf_op jit(solution)/shard_map/project/pallas_call | solution.py:659
  3.8 0.5 %collective-permute-start.1 = (f32[6,8,512]{2,1,0:T(8,128)S(1)}, f32[6,8,512]{2,1,0:T(8,128)S(1)}, u32[]{:S(2)}, u32[]{:S(2)}) collective-permute-start(f32[6,8,512]{2,1,0:T(8,128)S(1)} %get-tuple-element.33), channel_id=1, source_target_pairs={{2,0},{4,2},{1,3},{6,4},{3,5},{8,6},{5,7},{10,8},{7,9},{12,10},{9,... | collective-permute-start | bytes 294920 | tf_op jit(solution)/shard_map/ppermute | solution.py:612
  4.3 2.6 %collective-permute-start = (f32[5,8,512]{2,1,0:T(8,128)S(1)}, f32[5,8,512]{2,1,0:T(8,128)S(1)}, u32[]{:S(2)}, u32[]{:S(2)}) collective-permute-start(f32[5,8,512]{2,1,0:T(8,128)S(1)} %get-tuple-element.32), channel_id=1, source_target_pairs={{3,1},{0,2},{5,3},{2,4},{7,5},{4,6},{9,7},{6,8},{11,9},{8,10},{13,... | collective-permute-start | bytes 245768 | tf_op jit(solution)/shard_map/ppermute | solution.py:612
  6.9 0.0 copy-start.2
  6.9 0.0 copy-start.3
  6.9 0.0 copy-start.4
  6.9 0.0 collective-permute-start.2
  6.9 0.6 %copy-done.2 = s32[8]{0:T(128)S(1)} copy-done((s32[8]{0:T(128)S(1)}, s32[8]{0:T(128)}, u32[]{:S(2)}) %copy-start.2) | copy-done | bytes 56
  7.5 0.0 copy-done.3
  7.6 0.0 copy-done.4
  7.6 2.0 %divisors.1 = (f32[2,64,1024]{2,1,0:T(8,128)S(1)}, f32[3,8,1024]{2,1,0:T(8,128)S(1)}, f32[21,8,512]{2,1,0:T(8,128)S(1)}, f32[14,3,8,128]{3,2,1,0:T(8,128)S(1)}, ...) custom-call(s32[8]{0:T(128)S(1)} %copy-done.2, s32[8]{0:T(128)S(1)} %copy-done.4, ...), custom_call_target="tpu_custom_call" | custom-call | flops 4000000 | bytes 8000000 | tf_op jit(solution)/shard_map/divisors/pallas_call | solution.py:700
  9.6 1.3 %collective-permute-start.3 = (f32[7,8,512]{2,1,0:T(8,128)S(1)}, f32[7,8,512]{2,1,0:T(8,128)S(1)}, u32[]{:S(2)}, u32[]{:S(2)}) collective-permute-start(f32[7,8,512]{2,1,0:T(8,128)S(1)} %get-tuple-element.58.refs_0_), channel_id=1, source_target_pairs={{0,1},{1,0},{2,3},{3,2},{4,5},{5,4},{6,7},{7,6},{8,9},{9,8},{10,11... | collective-permute-start | bytes 344072 | tf_op jit(solution)/shard_map/ppermute | solution.py:600
  10.9 0.0 collective-permute-done.refs_2_
  10.9 1.7 %collective-permute-done.2 = f32[5,8,512]{2,1,0:T(8,128)S(1)} collective-permute-done((f32[5,8,512]{2,1,0:T(8,128)S(1)}, f32[5,8,512]{2,1,0:T(8,128)S(1)}, u32[]{:S(2)}, u32[]{:S(2)}) %collective-permute-start.2) | collective-permute-done | bytes 81952 | tf_op jit(solution)/shard_map/ppermute | solution.py:612
  12.6 0.0 collective-permute-done.1.refs_4_
  12.6 0.0 collective-permute-start.5
  12.6 0.5 %collective-permute-start.6 = (f32[5,8,512]{2,1,0:T(8,128)S(1)}, f32[5,8,512]{2,1,0:T(8,128)S(1)}, u32[]{:S(2)}, u32[]{:S(2)}) collective-permute-start(f32[5,8,512]{2,1,0:T(8,128)S(1)} %collective-permute-done.2), channel_id=1, source_target_pairs={{0,1},{1,0},{2,3},{3,2},{4,5},{5,4},{6,7},{7,6},{8,9},{9,8},{10,11... | collective-permute-start | bytes 245768 | tf_op jit(solution)/shard_map/ppermute | solution.py:600
  13.1 0.0 collective-permute-start.4
  13.1 0.0 collective-permute-done.3.refs_1_
  13.1 0.9 %collective-permute-done.6.refs_6_ = f32[5,8,512]{2,1,0:T(8,128)S(1)} collective-permute-done((f32[5,8,512]{2,1,0:T(8,128)S(1)}, f32[5,8,512]{2,1,0:T(8,128)S(1)}, u32[]{:S(2)}, u32[]{:S(2)}) %collective-permute-start.6) | collective-permute-done | bytes 81952 | tf_op jit(solution)/shard_map/ppermute | solution.py:600
  14.1 0.4 %collective-permute-done.4.refs_3_ = f32[5,8,512]{2,1,0:T(8,128)S(1)} collective-permute-done((f32[5,8,512]{2,1,0:T(8,128)S(1)}, f32[5,8,512]{2,1,0:T(8,128)S(1)}, u32[]{:S(2)}, u32[]{:S(2)}) %collective-permute-start.4) | collective-permute-done | bytes 81952 | tf_op jit(solution)/shard_map/ppermute | solution.py:600
  14.4 0.0 collective-permute-done.5.refs_5_
  14.4 0.0 copy-done
  14.4 0.0 copy-done.1
  14.4 2.7 %update.1 = (f32[3,8,1024]{2,1,0:T(8,128)}, f32[2,64,1024]{2,1,0:T(8,128)}) custom-call(s32[8]{0:T(128)S(1)} %copy-done.2, s32[4]{0:T(128)S(1)} %copy-done.3, f32[2,64,1024]{2,1,0:T(8,128)S(1)} %copy-done, f32[3,8,1024]{2,1,0:T(8,128)S(1)} %copy-done.1, f32[2,64,1024]{2,1,0:T(8,128)S(1)} %get-tuple-element.51.bound_ref, ...), custom_call_target="tpu_custom_call" | custom-call | tf_op jit(solution)/shard_map/update/pallas_call | solution.py:701
Async XLA Ops:
  0.6 13.8 %copy-start = (f32[2,64,1024]{2,1,0:T(8,128)S(1)}, f32[2,64,1024]{2,1,0:T(8,128)}, u32[]{:S(2)}) copy-start(f32[2,64,1024]{2,1,0:T(8,128)} %volume_ref.3) | copy-start | bytes 1572868
  0.6 13.8 %copy-start.1 = (f32[3,8,1024]{2,1,0:T(8,128)S(1)}, f32[3,8,1024]{2,1,0:T(8,128)}, u32[]{:S(2)}) copy-start(f32[3,8,1024]{2,1,0:T(8,128)} %measured_ref.3) | copy-start | bytes 294916
  3.8 8.8 %collective-permute-start.1 = (f32[6,8,512]{2,1,0:T(8,128)S(1)}, f32[6,8,512]{2,1,0:T(8,128)S(1)}, u32[]{:S(2)}, u32[]{:S(2)}) collective-permute-start(f32[6,8,512]{2,1,0:T(8,128)S(1)} %get-tuple-element.33), channel_id=1, source_target_pairs={{2,0},{4,2},{1,3},{6,4},{3,5},{8,6},{5,7},{10,8},{7,9},{12,10},{9,... | collective-permute-start | bytes 294920 | tf_op jit(solution)/shard_map/ppermute | solution.py:612
  4.3 6.6 %collective-permute-start = (f32[5,8,512]{2,1,0:T(8,128)S(1)}, f32[5,8,512]{2,1,0:T(8,128)S(1)}, u32[]{:S(2)}, u32[]{:S(2)}) collective-permute-start(f32[5,8,512]{2,1,0:T(8,128)S(1)} %get-tuple-element.32), channel_id=1, source_target_pairs={{3,1},{0,2},{5,3},{2,4},{7,5},{4,6},{9,7},{6,8},{11,9},{8,10},{13,... | collective-permute-start | bytes 245768 | tf_op jit(solution)/shard_map/ppermute | solution.py:612
  6.9 0.7 %copy-start.2 = (s32[8]{0:T(128)S(1)}, s32[8]{0:T(128)}, u32[]{:S(2)}) copy-start(s32[8]{0:T(128)} %angle_ref.5) | copy-start | bytes 100
  6.9 0.7 %copy-start.3 = (s32[4]{0:T(128)S(1)}, s32[4]{0:T(128)}, u32[]{:S(2)}) copy-start(s32[4]{0:T(128)} %subset_ref.5) | copy-start | bytes 52
  6.9 0.7 %copy-start.4 = (s32[8]{0:T(128)S(1)}, s32[8]{0:T(128)}, u32[]{:S(2)}) copy-start(s32[8]{0:T(128)} %lift_ref.3) | copy-start | bytes 100
  6.9 5.7 %collective-permute-start.2 = (f32[5,8,512]{2,1,0:T(8,128)S(1)}, f32[5,8,512]{2,1,0:T(8,128)S(1)}, u32[]{:S(2)}, u32[]{:S(2)}) collective-permute-start(f32[5,8,512]{2,1,0:T(8,128)S(1)} %get-tuple-element.34), channel_id=1, source_target_pairs={{4,0},{6,2},{8,4},{1,5},{10,6},{3,7},{12,8},{5,9},{14,10},{7,11},{... | collective-permute-start | bytes 245768 | tf_op jit(solution)/shard_map/ppermute | solution.py:612
  9.6 3.5 %collective-permute-start.3 = (f32[7,8,512]{2,1,0:T(8,128)S(1)}, f32[7,8,512]{2,1,0:T(8,128)S(1)}, u32[]{:S(2)}, u32[]{:S(2)}) collective-permute-start(f32[7,8,512]{2,1,0:T(8,128)S(1)} %get-tuple-element.58.refs_0_), channel_id=1, source_target_pairs={{0,1},{1,0},{2,3},{3,2},{4,5},{5,4},{6,7},{7,6},{8,9},{9,8},{10,11... | collective-permute-start | bytes 344072 | tf_op jit(solution)/shard_map/ppermute | solution.py:600
  12.6 1.8 %collective-permute-start.5 = (f32[6,8,512]{2,1,0:T(8,128)S(1)}, f32[6,8,512]{2,1,0:T(8,128)S(1)}, u32[]{:S(2)}, u32[]{:S(2)}) collective-permute-start(f32[6,8,512]{2,1,0:T(8,128)S(1)} %collective-permute-done.1.refs_4_), channel_id=1, source_target_pairs={{0,1},{1,0},{2,3},{3,2},{4,5},{5,4},{6,7},{7,6},{8,9},{9,8},{10,11... | collective-permute-start | bytes 294920 | tf_op jit(solution)/shard_map/ppermute | solution.py:600
  12.6 1.4 %collective-permute-start.6 = (f32[5,8,512]{2,1,0:T(8,128)S(1)}, f32[5,8,512]{2,1,0:T(8,128)S(1)}, u32[]{:S(2)}, u32[]{:S(2)}) collective-permute-start(f32[5,8,512]{2,1,0:T(8,128)S(1)} %collective-permute-done.2), channel_id=1, source_target_pairs={{0,1},{1,0},{2,3},{3,2},{4,5},{5,4},{6,7},{7,6},{8,9},{9,8},{10,11... | collective-permute-start | bytes 245768 | tf_op jit(solution)/shard_map/ppermute | solution.py:600
  13.1 1.3 %collective-permute-start.4 = (f32[5,8,512]{2,1,0:T(8,128)S(1)}, f32[5,8,512]{2,1,0:T(8,128)S(1)}, u32[]{:S(2)}, u32[]{:S(2)}) collective-permute-start(f32[5,8,512]{2,1,0:T(8,128)S(1)} %collective-permute-done.refs_2_), channel_id=1, source_target_pairs={{0,1},{1,0},{2,3},{3,2},{4,5},{5,4},{6,7},{7,6},{8,9},{9,8},{10,11... | collective-permute-start | bytes 245768 | tf_op jit(solution)/shard_map/ppermute | solution.py:600

commit v11 on v10

--- a/solution.py
+++ b/solution.py
@@ -613,7 +613,7 @@
 
 
 def fetches(reach):
-    return [s * d for d in range(1, reach // 2 + 2) for s in (-1, 1) if 2 * d - (s > 0) <= reach]
+    return [s * d for d in range(reach // 2 + 1, 0, -1) for s in (1, -1) if 2 * d - (s > 0) <= reach]
 
 
 def window(reach):

time: 17.2 us -> 16.8 us (0.977)
  local copies, waits for them, and re-layouts: 0.68 us -> 0.02 us
  starting transfers between devices: 4.91 us -> 5.19 us
    ppermute x3, starting transfers between devices: 3.1 us -> 4.1 us  [from_chip(): return lax.ppermute(block, 'slab', pairs)]
    ppermute x4, starting transfers between devices: 1.82 us -> 1.09 us  [swapped(): lax.ppermute(block, 'slab', [(i, i ^ 1) for i in range(lax.axis_size('sla...]
    unnamed x10, local copies, waits for them, and re-layouts: 0.68 us -> 0.02 us
where the time goes in v11:
time: 16.8 us; the launch traced here: 16.7 us
  Pallas kernels  7.84 us (47%)
  starting transfers between devices  5.19 us (31%)
  waiting for transfers between devices  2.94 us (18%)
  between operations  0.68 us (4%)
    ppermute x3, starting transfers between devices, from_chip(): return lax.ppermute(block, 'slab', pairs)  4.1 us
    pallas_call x1, Pallas kernels, per_device(): pl.pallas_call(functools.partial(project_kernel, slab_count), out_shape=(...  3.13 us
    pallas_call x1, Pallas kernels, per_device(): pl.pallas_call(functools.partial(update_kernel, order, kinds), out_shape=...  2.65 us
    pallas_call x1, Pallas kernels, per_device(): divide(view_angle, view_lift, subset, cover)  2.06 us
    ppermute x3, waiting for transfers between devices, from_chip(): return lax.ppermute(block, 'slab', pairs)  1.73 us
    ppermute x4, waiting for transfers between devices, swapped(): lax.ppermute(block, 'slab', [(i, i ^ 1) for i in range(lax.axis_size('sla...  1.21 us
    ppermute x4, starting transfers between devices, swapped(): lax.ppermute(block, 'slab', [(i, i ^ 1) for i in range(lax.axis_size('sla...  1.09 us
  transfers between devices with their start and end apart: 7, of which 3 were waited for; matrix products, arithmetic and copies ran while one was open for 0% of the time, Pallas kernels for 12%

profile of v11, /device:TPU:0, one launch (start us, length us, event | category | flops | bytes accessed | tf_op | source)
XLA Modules:
  0.0 16.7 jit_solution(7477782060616792865)
XLA Ops:
  0.6 0.0 copy-start
  0.6 0.0 copy-start.1
  0.6 3.1 %project.1 = (f32[7,8,512]{2,1,0:T(8,128)S(1)}, f32[6,8,512]{2,1,0:T(8,128)S(1)}, f32[5,8,512]{2,1,0:T(8,128)S(1)}, f32[5,8,512]{2,1,0:T(8,128)S(1)}, f32[8,1024]{1,0:T(8,128)S(1)}) custom-call(s32[8]{0:T(128)} %angle_ref.5, s32[8]{0:T(128)} %lift_ref.3, s32[4]{0:T(128)} %subset_ref.5, f32[2,64,1024]{2,1,0:T(8,128)} %volume_ref.3, f32[3,8,1024]{2,1,0:T(8,128)} %measured_ref.3), custom_call_target="tpu_custom_call" | custom-call | tf_op jit(solution)/shard_map/project/pallas_call | solution.py:659
  3.8 0.5 %collective-permute-start.1 = (f32[6,8,512]{2,1,0:T(8,128)S(1)}, f32[6,8,512]{2,1,0:T(8,128)S(1)}, u32[]{:S(2)}, u32[]{:S(2)}) collective-permute-start(f32[6,8,512]{2,1,0:T(8,128)S(1)} %get-tuple-element.33), channel_id=1, source_target_pairs={{2,0},{4,2},{1,3},{6,4},{3,5},{8,6},{5,7},{10,8},{7,9},{12,10},{9,... | collective-permute-start | bytes 294920 | tf_op jit(solution)/shard_map/ppermute | solution.py:612
  4.3 2.1 %collective-permute-start = (f32[5,8,512]{2,1,0:T(8,128)S(1)}, f32[5,8,512]{2,1,0:T(8,128)S(1)}, u32[]{:S(2)}, u32[]{:S(2)}) collective-permute-start(f32[5,8,512]{2,1,0:T(8,128)S(1)} %get-tuple-element.32), channel_id=1, source_target_pairs={{4,0},{6,2},{8,4},{1,5},{10,6},{3,7},{12,8},{5,9},{14,10},{7,11},{... | collective-permute-start | bytes 245768 | tf_op jit(solution)/shard_map/ppermute | solution.py:612
  6.4 0.0 copy-start.2
  6.4 0.0 copy-start.3
  6.4 0.0 copy-start.4
  6.4 1.5 %collective-permute-start.2 = (f32[5,8,512]{2,1,0:T(8,128)S(1)}, f32[5,8,512]{2,1,0:T(8,128)S(1)}, u32[]{:S(2)}, u32[]{:S(2)}) collective-permute-start(f32[5,8,512]{2,1,0:T(8,128)S(1)} %get-tuple-element.34), channel_id=1, source_target_pairs={{3,1},{0,2},{5,3},{2,4},{7,5},{4,6},{9,7},{6,8},{11,9},{8,10},{13,... | collective-permute-start | bytes 245768 | tf_op jit(solution)/shard_map/ppermute | solution.py:612
  7.9 0.0 copy-done.2
  7.9 0.0 copy-done.3
  7.9 0.0 copy-done.4
  7.9 2.1 %divisors.1 = (f32[2,64,1024]{2,1,0:T(8,128)S(1)}, f32[3,8,1024]{2,1,0:T(8,128)S(1)}, f32[21,8,512]{2,1,0:T(8,128)S(1)}, f32[14,3,8,128]{3,2,1,0:T(8,128)S(1)}, ...) custom-call(s32[8]{0:T(128)S(1)} %copy-done.2, s32[8]{0:T(128)S(1)} %copy-done.4, ...), custom_call_target="tpu_custom_call" | custom-call | flops 4000000 | bytes 8000000 | tf_op jit(solution)/shard_map/divisors/pallas_call | solution.py:700
  10.0 0.5 %collective-permute-start.3 = (f32[7,8,512]{2,1,0:T(8,128)S(1)}, f32[7,8,512]{2,1,0:T(8,128)S(1)}, u32[]{:S(2)}, u32[]{:S(2)}) collective-permute-start(f32[7,8,512]{2,1,0:T(8,128)S(1)} %get-tuple-element.58.refs_0_), channel_id=1, source_target_pairs={{0,1},{1,0},{2,3},{3,2},{4,5},{5,4},{6,7},{7,6},{8,9},{9,8},{10,11... | collective-permute-start | bytes 344072 | tf_op jit(solution)/shard_map/ppermute | solution.py:600
  10.5 1.7 %collective-permute-done = f32[5,8,512]{2,1,0:T(8,128)S(1)} collective-permute-done((f32[5,8,512]{2,1,0:T(8,128)S(1)}, f32[5,8,512]{2,1,0:T(8,128)S(1)}, u32[]{:S(2)}, u32[]{:S(2)}) %collective-permute-start) | collective-permute-done | bytes 81952 | tf_op jit(solution)/shard_map/ppermute | solution.py:612
  12.2 0.0 collective-permute-done.2.refs_5_
  12.2 0.0 collective-permute-done.1.refs_3_
  12.2 0.0 collective-permute-start.5
  12.2 0.5 %collective-permute-start.4 = (f32[5,8,512]{2,1,0:T(8,128)S(1)}, f32[5,8,512]{2,1,0:T(8,128)S(1)}, u32[]{:S(2)}, u32[]{:S(2)}) collective-permute-start(f32[5,8,512]{2,1,0:T(8,128)S(1)} %collective-permute-done), channel_id=1, source_target_pairs={{0,1},{1,0},{2,3},{3,2},{4,5},{5,4},{6,7},{7,6},{8,9},{9,8},{10,11... | collective-permute-start | bytes 245768 | tf_op jit(solution)/shard_map/ppermute | solution.py:600
  12.7 0.1 collective-permute-start.6
  12.8 0.0 collective-permute-done.3.refs_1_
  12.8 0.8 %collective-permute-done.4.refs_2_ = f32[5,8,512]{2,1,0:T(8,128)S(1)} collective-permute-done((f32[5,8,512]{2,1,0:T(8,128)S(1)}, f32[5,8,512]{2,1,0:T(8,128)S(1)}, u32[]{:S(2)}, u32[]{:S(2)}) %collective-permute-start.4) | collective-permute-done | bytes 81952 | tf_op jit(solution)/shard_map/ppermute | solution.py:600
  13.7 0.4 %collective-permute-done.6.refs_6_ = f32[5,8,512]{2,1,0:T(8,128)S(1)} collective-permute-done((f32[5,8,512]{2,1,0:T(8,128)S(1)}, f32[5,8,512]{2,1,0:T(8,128)S(1)}, u32[]{:S(2)}, u32[]{:S(2)}) %collective-permute-start.6) | collective-permute-done | bytes 81952 | tf_op jit(solution)/shard_map/ppermute | solution.py:600
  14.0 0.0 collective-permute-done.5.refs_4_
  14.0 0.0 copy-done
  14.0 0.0 copy-done.1
  14.0 2.7 %update.1 = (f32[3,8,1024]{2,1,0:T(8,128)}, f32[2,64,1024]{2,1,0:T(8,128)}) custom-call(s32[8]{0:T(128)S(1)} %copy-done.2, s32[4]{0:T(128)S(1)} %copy-done.3, f32[2,64,1024]{2,1,0:T(8,128)S(1)} %copy-done, f32[3,8,1024]{2,1,0:T(8,128)S(1)} %copy-done.1, f32[2,64,1024]{2,1,0:T(8,128)S(1)} %get-tuple-element.51.bound_ref, ...), custom_call_target="tpu_custom_call" | custom-call | tf_op jit(solution)/shard_map/update/pallas_call | solution.py:701
Async XLA Ops:
  0.6 13.4 %copy-start = (f32[2,64,1024]{2,1,0:T(8,128)S(1)}, f32[2,64,1024]{2,1,0:T(8,128)}, u32[]{:S(2)}) copy-start(f32[2,64,1024]{2,1,0:T(8,128)} %volume_ref.3) | copy-start | bytes 1572868
  0.6 13.4 %copy-start.1 = (f32[3,8,1024]{2,1,0:T(8,128)S(1)}, f32[3,8,1024]{2,1,0:T(8,128)}, u32[]{:S(2)}) copy-start(f32[3,8,1024]{2,1,0:T(8,128)} %measured_ref.3) | copy-start | bytes 294916
  3.8 8.4 %collective-permute-start.1 = (f32[6,8,512]{2,1,0:T(8,128)S(1)}, f32[6,8,512]{2,1,0:T(8,128)S(1)}, u32[]{:S(2)}, u32[]{:S(2)}) collective-permute-start(f32[6,8,512]{2,1,0:T(8,128)S(1)} %get-tuple-element.33), channel_id=1, source_target_pairs={{2,0},{4,2},{1,3},{6,4},{3,5},{8,6},{5,7},{10,8},{7,9},{12,10},{9,... | collective-permute-start | bytes 294920 | tf_op jit(solution)/shard_map/ppermute | solution.py:612
  4.3 7.9 %collective-permute-start = (f32[5,8,512]{2,1,0:T(8,128)S(1)}, f32[5,8,512]{2,1,0:T(8,128)S(1)}, u32[]{:S(2)}, u32[]{:S(2)}) collective-permute-start(f32[5,8,512]{2,1,0:T(8,128)S(1)} %get-tuple-element.32), channel_id=1, source_target_pairs={{4,0},{6,2},{8,4},{1,5},{10,6},{3,7},{12,8},{5,9},{14,10},{7,11},{... | collective-permute-start | bytes 245768 | tf_op jit(solution)/shard_map/ppermute | solution.py:612
  6.4 1.5 %copy-start.2 = (s32[8]{0:T(128)S(1)}, s32[8]{0:T(128)}, u32[]{:S(2)}) copy-start(s32[8]{0:T(128)} %angle_ref.5) | copy-start | bytes 100
  6.4 1.5 %copy-start.3 = (s32[4]{0:T(128)S(1)}, s32[4]{0:T(128)}, u32[]{:S(2)}) copy-start(s32[4]{0:T(128)} %subset_ref.5) | copy-start | bytes 52
  6.4 1.5 %copy-start.4 = (s32[8]{0:T(128)S(1)}, s32[8]{0:T(128)}, u32[]{:S(2)}) copy-start(s32[8]{0:T(128)} %lift_ref.3) | copy-start | bytes 100
  6.4 5.8 %collective-permute-start.2 = (f32[5,8,512]{2,1,0:T(8,128)S(1)}, f32[5,8,512]{2,1,0:T(8,128)S(1)}, u32[]{:S(2)}, u32[]{:S(2)}) collective-permute-start(f32[5,8,512]{2,1,0:T(8,128)S(1)} %get-tuple-element.34), channel_id=1, source_target_pairs={{3,1},{0,2},{5,3},{2,4},{7,5},{4,6},{9,7},{6,8},{11,9},{8,10},{13,... | collective-permute-start | bytes 245768 | tf_op jit(solution)/shard_map/ppermute | solution.py:612
  10.0 2.8 %collective-permute-start.3 = (f32[7,8,512]{2,1,0:T(8,128)S(1)}, f32[7,8,512]{2,1,0:T(8,128)S(1)}, u32[]{:S(2)}, u32[]{:S(2)}) collective-permute-start(f32[7,8,512]{2,1,0:T(8,128)S(1)} %get-tuple-element.58.refs_0_), channel_id=1, source_target_pairs={{0,1},{1,0},{2,3},{3,2},{4,5},{5,4},{6,7},{7,6},{8,9},{9,8},{10,11... | collective-permute-start | bytes 344072 | tf_op jit(solution)/shard_map/ppermute | solution.py:600
  12.2 1.8 %collective-permute-start.5 = (f32[6,8,512]{2,1,0:T(8,128)S(1)}, f32[6,8,512]{2,1,0:T(8,128)S(1)}, u32[]{:S(2)}, u32[]{:S(2)}) collective-permute-start(f32[6,8,512]{2,1,0:T(8,128)S(1)} %collective-permute-done.1.refs_3_), channel_id=1, source_target_pairs={{0,1},{1,0},{2,3},{3,2},{4,5},{5,4},{6,7},{7,6},{8,9},{9,8},{10,11... | collective-permute-start | bytes 294920 | tf_op jit(solution)/shard_map/ppermute | solution.py:600
  12.2 1.4 %collective-permute-start.4 = (f32[5,8,512]{2,1,0:T(8,128)S(1)}, f32[5,8,512]{2,1,0:T(8,128)S(1)}, u32[]{:S(2)}, u32[]{:S(2)}) collective-permute-start(f32[5,8,512]{2,1,0:T(8,128)S(1)} %collective-permute-done), channel_id=1, source_target_pairs={{0,1},{1,0},{2,3},{3,2},{4,5},{5,4},{6,7},{7,6},{8,9},{9,8},{10,11... | collective-permute-start | bytes 245768 | tf_op jit(solution)/shard_map/ppermute | solution.py:600
  12.7 1.3 %collective-permute-start.6 = (f32[5,8,512]{2,1,0:T(8,128)S(1)}, f32[5,8,512]{2,1,0:T(8,128)S(1)}, u32[]{:S(2)}, u32[]{:S(2)}) collective-permute-start(f32[5,8,512]{2,1,0:T(8,128)S(1)} %collective-permute-done.2.refs_5_), channel_id=1, source_target_pairs={{0,1},{1,0},{2,3},{3,2},{4,5},{5,4},{6,7},{7,6},{8,9},{9,8},{10,11... | collective-permute-start | bytes 245768 | tf_op jit(solution)/shard_map/ppermute | solution.py:600

commit v12 on v11

--- a/solution.py
+++ b/solution.py
@@ -266,7 +266,8 @@
             near_ref[2 * slab_depth, at : at + 1, :] = rows[1]
             near_ref[2 * slab_depth + 1, at : at + 1, :] = measured_ref[far_row, view, cut]
             low_ref[2 * slab_depth, at : at + 1, :] = rows[2]
-            high_ref[2 * slab_depth, at : at + 1, :] = rows[2]
+            for more in range(2):
+                high_ref[2 * slab_depth + more, at : at + 1, :] = rows[2]
 
     cosine, _, flat = angle_facts(spread_scalars(lambda v: angle_ref[v], view_count, sub))
     lifts = spread_scalars(lambda v: lift_ref[v], view_count, sub).astype(F32)
@@ -662,7 +663,7 @@
             block_of(row_share),
             block_of(2),
             block_of(1),
-            block_of(1),
+            block_of(2),
             pltpu.VMEM((view_count, column_count), F32),
         ),
         in_specs=[smem] * 3 + [vmem] * 2,

time: 16.8 us -> 16.5 us (0.982); the launches traced: 16.7 us -> 16.1 us
  waiting for transfers between devices: 2.94 us -> 2.06 us
  starting transfers between devices: 5.19 us -> 5.42 us
    ppermute x4, starting transfers between devices: 1.09 us -> 2.27 us  [swapped(): lax.ppermute(block, 'slab', [(i, i ^ 1) for i in range(lax.axis_size('sla...]
    ppermute x3, starting transfers between devices: 4.1 us -> 3.15 us  [from_chip(): return lax.ppermute(block, 'slab', pairs)]
    ppermute x3, waiting for transfers between devices: 1.73 us -> 1.14 us  [from_chip(): return lax.ppermute(block, 'slab', pairs)]
    ppermute x4, waiting for transfers between devices: 1.21 us -> 0.93 us  [swapped(): lax.ppermute(block, 'slab', [(i, i ^ 1) for i in range(lax.axis_size('sla...]
  transfers between devices with their start and end apart: 7 -> 7, of which waited for: 3 -> 2; matrix products, arithmetic and copies ran while one was open for 0% -> 0% of each run, Pallas kernels for 12% -> 13%
where the time goes in v12:
time: 16.5 us; the launch traced here: 16.1 us
  Pallas kernels  7.84 us (48%)
  starting transfers between devices  5.42 us (33%)
  waiting for transfers between devices  2.06 us (12%)
  between operations  0.68 us (4%)
    ppermute x3, starting transfers between devices, from_chip(): return lax.ppermute(block, 'slab', pairs)  3.15 us
    pallas_call x1, Pallas kernels, per_device(): pl.pallas_call(functools.partial(project_kernel, slab_count), out_shape=(...  3.14 us
    pallas_call x1, Pallas kernels, per_device(): pl.pallas_call(functools.partial(update_kernel, order, kinds), out_shape=...  2.65 us
    ppermute x4, starting transfers between devices, swapped(): lax.ppermute(block, 'slab', [(i, i ^ 1) for i in range(lax.axis_size('sla...  2.27 us
    pallas_call x1, Pallas kernels, per_device(): divide(view_angle, view_lift, subset, cover)  2.05 us
    ppermute x3, waiting for transfers between devices, from_chip(): return lax.ppermute(block, 'slab', pairs)  1.14 us
    ppermute x4, waiting for transfers between devices, swapped(): lax.ppermute(block, 'slab', [(i, i ^ 1) for i in range(lax.axis_size('sla...  0.93 us
  transfers between devices with their start and end apart: 7, of which 2 were waited for; matrix products, arithmetic and copies ran while one was open for 0% of the time, Pallas kernels for 13%

profile of v12, /device:TPU:0, one launch (start us, length us, event | category | flops | bytes accessed | tf_op | source)
XLA Modules:
  0.0 16.1 jit_solution(3860194753382620676)
XLA Ops:
  0.6 0.0 copy-start
  0.6 0.0 copy-start.1
  0.6 3.1 %project.1 = (f32[7,8,512]{2,1,0:T(8,128)S(1)}, f32[6,8,512]{2,1,0:T(8,128)S(1)}, f32[5,8,512]{2,1,0:T(8,128)S(1)}, f32[6,8,512]{2,1,0:T(8,128)S(1)}, f32[8,1024]{1,0:T(8,128)S(1)}) custom-call(s32[8]{0:T(128)} %angle_ref.5, s32[8]{0:T(128)} %lift_ref.3, s32[4]{0:T(128)} %subset_ref.5, f32[2,64,1024]{2,1,0:T(8,128)} %volume_ref.3, f32[3,8,1024]{2,1,0:T(8,128)} %measured_ref.3), custom_call_target="tpu_custom_call" | custom-call | tf_op jit(solution)/shard_map/project/pallas_call | solution.py:660
  3.8 0.5 %collective-permute-start = (f32[6,8,512]{2,1,0:T(8,128)S(1)}, f32[6,8,512]{2,1,0:T(8,128)S(1)}, u32[]{:S(2)}, u32[]{:S(2)}) collective-permute-start(f32[6,8,512]{2,1,0:T(8,128)S(1)} %get-tuple-element.32), channel_id=1, source_target_pairs={{4,0},{6,2},{8,4},{1,5},{10,6},{3,7},{12,8},{5,9},{14,10},{7,11},{... | collective-permute-start | bytes 294920 | tf_op jit(solution)/shard_map/ppermute | solution.py:613
  4.3 2.1 %collective-permute-start.1 = (f32[6,8,512]{2,1,0:T(8,128)S(1)}, f32[6,8,512]{2,1,0:T(8,128)S(1)}, u32[]{:S(2)}, u32[]{:S(2)}) collective-permute-start(f32[6,8,512]{2,1,0:T(8,128)S(1)} %get-tuple-element.33), channel_id=1, source_target_pairs={{2,0},{4,2},{1,3},{6,4},{3,5},{8,6},{5,7},{10,8},{7,9},{12,10},{9,... | collective-permute-start | bytes 294920 | tf_op jit(solution)/shard_map/ppermute | solution.py:613
  6.4 0.0 copy-start.2
  6.4 0.0 copy-start.3
  6.4 0.0 copy-start.4
  6.4 0.6 %collective-permute-start.2 = (f32[5,8,512]{2,1,0:T(8,128)S(1)}, f32[5,8,512]{2,1,0:T(8,128)S(1)}, u32[]{:S(2)}, u32[]{:S(2)}) collective-permute-start(f32[5,8,512]{2,1,0:T(8,128)S(1)} %get-tuple-element.34), channel_id=1, source_target_pairs={{3,1},{0,2},{5,3},{2,4},{7,5},{4,6},{9,7},{6,8},{11,9},{8,10},{13,... | collective-permute-start | bytes 245768 | tf_op jit(solution)/shard_map/ppermute | solution.py:613
  7.0 0.1 copy-done.2
  7.0 0.0 copy-done.3
  7.1 0.0 copy-done.4
  7.1 2.1 %divisors.1 = (f32[2,64,1024]{2,1,0:T(8,128)S(1)}, f32[3,8,1024]{2,1,0:T(8,128)S(1)}, f32[21,8,512]{2,1,0:T(8,128)S(1)}, f32[14,3,8,128]{3,2,1,0:T(8,128)S(1)}, ...) custom-call(s32[8]{0:T(128)S(1)} %copy-done.2, s32[8]{0:T(128)S(1)} %copy-done.4, ...), custom_call_target="tpu_custom_call" | custom-call | flops 4000000 | bytes 8000000 | tf_op jit(solution)/shard_map/divisors/pallas_call | solution.py:701
  9.1 1.3 %collective-permute-start.3 = (f32[7,8,512]{2,1,0:T(8,128)S(1)}, f32[7,8,512]{2,1,0:T(8,128)S(1)}, u32[]{:S(2)}, u32[]{:S(2)}) collective-permute-start(f32[7,8,512]{2,1,0:T(8,128)S(1)} %get-tuple-element.58.refs_0_), channel_id=1, source_target_pairs={{0,1},{1,0},{2,3},{3,2},{4,5},{5,4},{6,7},{7,6},{8,9},{9,8},{10,11... | collective-permute-start | bytes 344072 | tf_op jit(solution)/shard_map/ppermute | solution.py:601
  10.4 1.1 %collective-permute-done.2.refs_5_ = f32[5,8,512]{2,1,0:T(8,128)S(1)} collective-permute-done((f32[5,8,512]{2,1,0:T(8,128)S(1)}, f32[5,8,512]{2,1,0:T(8,128)S(1)}, u32[]{:S(2)}, u32[]{:S(2)}) %collective-permute-start.2) | collective-permute-done | bytes 81952 | tf_op jit(solution)/shard_map/ppermute | solution.py:613
  11.6 0.0 collective-permute-done
  11.6 0.0 collective-permute-done.1.refs_3_
  11.6 0.5 %collective-permute-start.4 = (f32[6,8,512]{2,1,0:T(8,128)S(1)}, f32[6,8,512]{2,1,0:T(8,128)S(1)}, u32[]{:S(2)}, u32[]{:S(2)}) collective-permute-start(f32[6,8,512]{2,1,0:T(8,128)S(1)} %collective-permute-done), channel_id=1, source_target_pairs={{0,1},{1,0},{2,3},{3,2},{4,5},{5,4},{6,7},{7,6},{8,9},{9,8},{10,11... | collective-permute-start | bytes 294920 | tf_op jit(solution)/shard_map/ppermute | solution.py:601
  12.0 0.1 collective-permute-start.5
  12.1 0.5 %collective-permute-start.6 = (f32[5,8,512]{2,1,0:T(8,128)S(1)}, f32[5,8,512]{2,1,0:T(8,128)S(1)}, u32[]{:S(2)}, u32[]{:S(2)}) collective-permute-start(f32[5,8,512]{2,1,0:T(8,128)S(1)} %collective-permute-done.2.refs_5_), channel_id=1, source_target_pairs={{0,1},{1,0},{2,3},{3,2},{4,5},{5,4},{6,7},{7,6},{8,9},{9,8},{10,11... | collective-permute-start | bytes 245768 | tf_op jit(solution)/shard_map/ppermute | solution.py:601
  12.5 0.0 collective-permute-done.3.refs_1_
  12.6 0.9 %collective-permute-done.6.refs_6_ = f32[5,8,512]{2,1,0:T(8,128)S(1)} collective-permute-done((f32[5,8,512]{2,1,0:T(8,128)S(1)}, f32[5,8,512]{2,1,0:T(8,128)S(1)}, u32[]{:S(2)}, u32[]{:S(2)}) %collective-permute-start.6) | collective-permute-done | bytes 81952 | tf_op jit(solution)/shard_map/ppermute | solution.py:601
  13.5 0.0 collective-permute-done.4.refs_2_
  13.5 0.0 collective-permute-done.5.refs_4_
  13.5 0.0 copy-done
  13.5 0.0 copy-done.1
  13.5 2.7 %update.1 = (f32[3,8,1024]{2,1,0:T(8,128)}, f32[2,64,1024]{2,1,0:T(8,128)}) custom-call(s32[8]{0:T(128)S(1)} %copy-done.2, s32[4]{0:T(128)S(1)} %copy-done.3, f32[2,64,1024]{2,1,0:T(8,128)S(1)} %copy-done, f32[3,8,1024]{2,1,0:T(8,128)S(1)} %copy-done.1, f32[2,64,1024]{2,1,0:T(8,128)S(1)} %get-tuple-element.51.bound_ref, ...), custom_call_target="tpu_custom_call" | custom-call | tf_op jit(solution)/shard_map/update/pallas_call | solution.py:702
Async XLA Ops:
  0.6 12.9 %copy-start = (f32[2,64,1024]{2,1,0:T(8,128)S(1)}, f32[2,64,1024]{2,1,0:T(8,128)}, u32[]{:S(2)}) copy-start(f32[2,64,1024]{2,1,0:T(8,128)} %volume_ref.3) | copy-start | bytes 1572868
  0.6 12.8 %copy-start.1 = (f32[3,8,1024]{2,1,0:T(8,128)S(1)}, f32[3,8,1024]{2,1,0:T(8,128)}, u32[]{:S(2)}) copy-start(f32[3,8,1024]{2,1,0:T(8,128)} %measured_ref.3) | copy-start | bytes 294916
  3.8 7.8 %collective-permute-start = (f32[6,8,512]{2,1,0:T(8,128)S(1)}, f32[6,8,512]{2,1,0:T(8,128)S(1)}, u32[]{:S(2)}, u32[]{:S(2)}) collective-permute-start(f32[6,8,512]{2,1,0:T(8,128)S(1)} %get-tuple-element.32), channel_id=1, source_target_pairs={{4,0},{6,2},{8,4},{1,5},{10,6},{3,7},{12,8},{5,9},{14,10},{7,11},{... | collective-permute-start | bytes 294920 | tf_op jit(solution)/shard_map/ppermute | solution.py:613
  4.3 7.3 %collective-permute-start.1 = (f32[6,8,512]{2,1,0:T(8,128)S(1)}, f32[6,8,512]{2,1,0:T(8,128)S(1)}, u32[]{:S(2)}, u32[]{:S(2)}) collective-permute-start(f32[6,8,512]{2,1,0:T(8,128)S(1)} %get-tuple-element.33), channel_id=1, source_target_pairs={{2,0},{4,2},{1,3},{6,4},{3,5},{8,6},{5,7},{10,8},{7,9},{12,10},{9,... | collective-permute-start | bytes 294920 | tf_op jit(solution)/shard_map/ppermute | solution.py:613
  6.4 0.7 %copy-start.2 = (s32[8]{0:T(128)S(1)}, s32[8]{0:T(128)}, u32[]{:S(2)}) copy-start(s32[8]{0:T(128)} %angle_ref.5) | copy-start | bytes 100
  6.4 0.7 %copy-start.3 = (s32[4]{0:T(128)S(1)}, s32[4]{0:T(128)}, u32[]{:S(2)}) copy-start(s32[4]{0:T(128)} %subset_ref.5) | copy-start | bytes 52
  6.4 0.7 %copy-start.4 = (s32[8]{0:T(128)S(1)}, s32[8]{0:T(128)}, u32[]{:S(2)}) copy-start(s32[8]{0:T(128)} %lift_ref.3) | copy-start | bytes 100
  6.4 5.2 %collective-permute-start.2 = (f32[5,8,512]{2,1,0:T(8,128)S(1)}, f32[5,8,512]{2,1,0:T(8,128)S(1)}, u32[]{:S(2)}, u32[]{:S(2)}) collective-permute-start(f32[5,8,512]{2,1,0:T(8,128)S(1)} %get-tuple-element.34), channel_id=1, source_target_pairs={{3,1},{0,2},{5,3},{2,4},{7,5},{4,6},{9,7},{6,8},{11,9},{8,10},{13,... | collective-permute-start | bytes 245768 | tf_op jit(solution)/shard_map/ppermute | solution.py:613
  9.1 3.4 %collective-permute-start.3 = (f32[7,8,512]{2,1,0:T(8,128)S(1)}, f32[7,8,512]{2,1,0:T(8,128)S(1)}, u32[]{:S(2)}, u32[]{:S(2)}) collective-permute-start(f32[7,8,512]{2,1,0:T(8,128)S(1)} %get-tuple-element.58.refs_0_), channel_id=1, source_target_pairs={{0,1},{1,0},{2,3},{3,2},{4,5},{5,4},{6,7},{7,6},{8,9},{9,8},{10,11... | collective-permute-start | bytes 344072 | tf_op jit(solution)/shard_map/ppermute | solution.py:601
  11.6 1.9 %collective-permute-start.4 = (f32[6,8,512]{2,1,0:T(8,128)S(1)}, f32[6,8,512]{2,1,0:T(8,128)S(1)}, u32[]{:S(2)}, u32[]{:S(2)}) collective-permute-start(f32[6,8,512]{2,1,0:T(8,128)S(1)} %collective-permute-done), channel_id=1, source_target_pairs={{0,1},{1,0},{2,3},{3,2},{4,5},{5,4},{6,7},{7,6},{8,9},{9,8},{10,11... | collective-permute-start | bytes 294920 | tf_op jit(solution)/shard_map/ppermute | solution.py:601
  12.0 1.4 %collective-permute-start.5 = (f32[6,8,512]{2,1,0:T(8,128)S(1)}, f32[6,8,512]{2,1,0:T(8,128)S(1)}, u32[]{:S(2)}, u32[]{:S(2)}) collective-permute-start(f32[6,8,512]{2,1,0:T(8,128)S(1)} %collective-permute-done.1.refs_3_), channel_id=1, source_target_pairs={{0,1},{1,0},{2,3},{3,2},{4,5},{5,4},{6,7},{7,6},{8,9},{9,8},{10,11... | collective-permute-start | bytes 294920 | tf_op jit(solution)/shard_map/ppermute | solution.py:601
  12.1 1.4 %collective-permute-start.6 = (f32[5,8,512]{2,1,0:T(8,128)S(1)}, f32[5,8,512]{2,1,0:T(8,128)S(1)}, u32[]{:S(2)}, u32[]{:S(2)}) collective-permute-start(f32[5,8,512]{2,1,0:T(8,128)S(1)} %collective-permute-done.2.refs_5_), channel_id=1, source_target_pairs={{0,1},{1,0},{2,3},{3,2},{4,5},{5,4},{6,7},{7,6},{8,9},{9,8},{10,11... | collective-permute-start | bytes 245768 | tf_op jit(solution)/shard_map/ppermute | solution.py:601

commit v13 on v12

--- a/solution.py
+++ b/solution.py
@@ -326,7 +326,7 @@
                 part_ref[depth, view, :, tile * LANES : (tile + 1) * LANES] = sums[depth][tile]
         return carry
 
-    lax.fori_loop(0, view_count, one_view, 0, unroll=4)
+    lax.fori_loop(0, view_count, one_view, 0, unroll=8)
 
     shift = LANES - half
     inside = [None] * (tiles + 1)

time: 16.5 us -> 16.3 us (0.988)
  no operation moved by 1% of the time
where the time goes in v13:
time: 16.3 us; the launch traced here: 16 us
  Pallas kernels  7.69 us (47%)
  starting transfers between devices  5.42 us (33%)
  waiting for transfers between devices  2.06 us (13%)
  between operations  0.68 us (4%)
    ppermute x3, starting transfers between devices, from_chip(): return lax.ppermute(block, 'slab', pairs)  3.15 us
    pallas_call x1, Pallas kernels, per_device(): pl.pallas_call(functools.partial(project_kernel, slab_count), out_shape=(...  2.98 us
    pallas_call x1, Pallas kernels, per_device(): pl.pallas_call(functools.partial(update_kernel, order, kinds), out_shape=...  2.65 us
    ppermute x4, starting transfers between devices, swapped(): lax.ppermute(block, 'slab', [(i, i ^ 1) for i in range(lax.axis_size('sla...  2.27 us
    pallas_call x1, Pallas kernels, per_device(): divide(view_angle, view_lift, subset, cover)  2.05 us
    ppermute x3, waiting for transfers between devices, from_chip(): return lax.ppermute(block, 'slab', pairs)  1.14 us
    ppermute x4, waiting for transfers between devices, swapped(): lax.ppermute(block, 'slab', [(i, i ^ 1) for i in range(lax.axis_size('sla...  0.93 us
  transfers between devices with their start and end apart: 7, of which 2 were waited for; matrix products, arithmetic and copies ran while one was open for 0% of the time, Pallas kernels for 13%

profile of v13, /device:TPU:0, one launch (start us, length us, event | category | flops | bytes accessed | tf_op | source)
XLA Modules:
  0.0 16.0 jit_solution(12381075128819992147)
XLA Ops:
  0.6 0.0 copy-start
  0.6 0.0 copy-start.1
  0.6 3.0 %project.1 = (f32[7,8,512]{2,1,0:T(8,128)S(1)}, f32[6,8,512]{2,1,0:T(8,128)S(1)}, f32[5,8,512]{2,1,0:T(8,128)S(1)}, f32[6,8,512]{2,1,0:T(8,128)S(1)}, f32[8,1024]{1,0:T(8,128)S(1)}) custom-call(s32[8]{0:T(128)} %angle_ref.5, s32[8]{0:T(128)} %lift_ref.3, s32[4]{0:T(128)} %subset_ref.5, f32[2,64,1024]{2,1,0:T(8,128)} %volume_ref.3, f32[3,8,1024]{2,1,0:T(8,128)} %measured_ref.3), custom_call_target="tpu_custom_call" | custom-call | tf_op jit(solution)/shard_map/project/pallas_call | solution.py:660
  3.6 0.5 %collective-permute-start = (f32[6,8,512]{2,1,0:T(8,128)S(1)}, f32[6,8,512]{2,1,0:T(8,128)S(1)}, u32[]{:S(2)}, u32[]{:S(2)}) collective-permute-start(f32[6,8,512]{2,1,0:T(8,128)S(1)} %get-tuple-element.32), channel_id=1, source_target_pairs={{4,0},{6,2},{8,4},{1,5},{10,6},{3,7},{12,8},{5,9},{14,10},{7,11},{... | collective-permute-start | bytes 294920 | tf_op jit(solution)/shard_map/ppermute | solution.py:613
  4.1 2.1 %collective-permute-start.1 = (f32[6,8,512]{2,1,0:T(8,128)S(1)}, f32[6,8,512]{2,1,0:T(8,128)S(1)}, u32[]{:S(2)}, u32[]{:S(2)}) collective-permute-start(f32[6,8,512]{2,1,0:T(8,128)S(1)} %get-tuple-element.33), channel_id=1, source_target_pairs={{2,0},{4,2},{1,3},{6,4},{3,5},{8,6},{5,7},{10,8},{7,9},{12,10},{9,... | collective-permute-start | bytes 294920 | tf_op jit(solution)/shard_map/ppermute | solution.py:613
  6.2 0.0 copy-start.2
  6.2 0.0 copy-start.3
  6.2 0.0 copy-start.4
  6.2 0.6 %collective-permute-start.2 = (f32[5,8,512]{2,1,0:T(8,128)S(1)}, f32[5,8,512]{2,1,0:T(8,128)S(1)}, u32[]{:S(2)}, u32[]{:S(2)}) collective-permute-start(f32[5,8,512]{2,1,0:T(8,128)S(1)} %get-tuple-element.34), channel_id=1, source_target_pairs={{3,1},{0,2},{5,3},{2,4},{7,5},{4,6},{9,7},{6,8},{11,9},{8,10},{13,... | collective-permute-start | bytes 245768 | tf_op jit(solution)/shard_map/ppermute | solution.py:613
  6.8 0.1 copy-done.2
  6.9 0.0 copy-done.3
  6.9 0.0 copy-done.4
  6.9 2.1 %divisors.1 = (f32[2,64,1024]{2,1,0:T(8,128)S(1)}, f32[3,8,1024]{2,1,0:T(8,128)S(1)}, f32[21,8,512]{2,1,0:T(8,128)S(1)}, f32[14,3,8,128]{3,2,1,0:T(8,128)S(1)}, ...) custom-call(s32[8]{0:T(128)S(1)} %copy-done.2, s32[8]{0:T(128)S(1)} %copy-done.4, ...), custom_call_target="tpu_custom_call" | custom-call | flops 4000000 | bytes 8000000 | tf_op jit(solution)/shard_map/divisors/pallas_call | solution.py:701
  9.0 1.3 %collective-permute-start.3 = (f32[7,8,512]{2,1,0:T(8,128)S(1)}, f32[7,8,512]{2,1,0:T(8,128)S(1)}, u32[]{:S(2)}, u32[]{:S(2)}) collective-permute-start(f32[7,8,512]{2,1,0:T(8,128)S(1)} %get-tuple-element.58.refs_0_), channel_id=1, source_target_pairs={{0,1},{1,0},{2,3},{3,2},{4,5},{5,4},{6,7},{7,6},{8,9},{9,8},{10,11... | collective-permute-start | bytes 344072 | tf_op jit(solution)/shard_map/ppermute | solution.py:601
  10.3 1.1 %collective-permute-done.2.refs_5_ = f32[5,8,512]{2,1,0:T(8,128)S(1)} collective-permute-done((f32[5,8,512]{2,1,0:T(8,128)S(1)}, f32[5,8,512]{2,1,0:T(8,128)S(1)}, u32[]{:S(2)}, u32[]{:S(2)}) %collective-permute-start.2) | collective-permute-done | bytes 81952 | tf_op jit(solution)/shard_map/ppermute | solution.py:613
  11.4 0.0 collective-permute-done
  11.4 0.0 collective-permute-done.1.refs_3_
  11.4 0.5 %collective-permute-start.4 = (f32[6,8,512]{2,1,0:T(8,128)S(1)}, f32[6,8,512]{2,1,0:T(8,128)S(1)}, u32[]{:S(2)}, u32[]{:S(2)}) collective-permute-start(f32[6,8,512]{2,1,0:T(8,128)S(1)} %collective-permute-done), channel_id=1, source_target_pairs={{0,1},{1,0},{2,3},{3,2},{4,5},{5,4},{6,7},{7,6},{8,9},{9,8},{10,11... | collective-permute-start | bytes 294920 | tf_op jit(solution)/shard_map/ppermute | solution.py:601
  11.9 0.1 collective-permute-start.5
  11.9 0.5 %collective-permute-start.6 = (f32[5,8,512]{2,1,0:T(8,128)S(1)}, f32[5,8,512]{2,1,0:T(8,128)S(1)}, u32[]{:S(2)}, u32[]{:S(2)}) collective-permute-start(f32[5,8,512]{2,1,0:T(8,128)S(1)} %collective-permute-done.2.refs_5_), channel_id=1, source_target_pairs={{0,1},{1,0},{2,3},{3,2},{4,5},{5,4},{6,7},{7,6},{8,9},{9,8},{10,11... | collective-permute-start | bytes 245768 | tf_op jit(solution)/shard_map/ppermute | solution.py:601
  12.4 0.0 collective-permute-done.3.refs_1_
  12.4 0.9 %collective-permute-done.6.refs_6_ = f32[5,8,512]{2,1,0:T(8,128)S(1)} collective-permute-done((f32[5,8,512]{2,1,0:T(8,128)S(1)}, f32[5,8,512]{2,1,0:T(8,128)S(1)}, u32[]{:S(2)}, u32[]{:S(2)}) %collective-permute-start.6) | collective-permute-done | bytes 81952 | tf_op jit(solution)/shard_map/ppermute | solution.py:601
  13.3 0.0 collective-permute-done.4.refs_2_
  13.3 0.0 collective-permute-done.5.refs_4_
  13.3 0.0 copy-done
  13.3 0.0 copy-done.1
  13.3 2.7 %update.1 = (f32[3,8,1024]{2,1,0:T(8,128)}, f32[2,64,1024]{2,1,0:T(8,128)}) custom-call(s32[8]{0:T(128)S(1)} %copy-done.2, s32[4]{0:T(128)S(1)} %copy-done.3, f32[2,64,1024]{2,1,0:T(8,128)S(1)} %copy-done, f32[3,8,1024]{2,1,0:T(8,128)S(1)} %copy-done.1, f32[2,64,1024]{2,1,0:T(8,128)S(1)} %get-tuple-element.51.bound_ref, ...), custom_call_target="tpu_custom_call" | custom-call | tf_op jit(solution)/shard_map/update/pallas_call | solution.py:702
Async XLA Ops:
  0.6 12.7 %copy-start = (f32[2,64,1024]{2,1,0:T(8,128)S(1)}, f32[2,64,1024]{2,1,0:T(8,128)}, u32[]{:S(2)}) copy-start(f32[2,64,1024]{2,1,0:T(8,128)} %volume_ref.3) | copy-start | bytes 1572868
  0.6 12.7 %copy-start.1 = (f32[3,8,1024]{2,1,0:T(8,128)S(1)}, f32[3,8,1024]{2,1,0:T(8,128)}, u32[]{:S(2)}) copy-start(f32[3,8,1024]{2,1,0:T(8,128)} %measured_ref.3) | copy-start | bytes 294916
  3.6 7.8 %collective-permute-start = (f32[6,8,512]{2,1,0:T(8,128)S(1)}, f32[6,8,512]{2,1,0:T(8,128)S(1)}, u32[]{:S(2)}, u32[]{:S(2)}) collective-permute-start(f32[6,8,512]{2,1,0:T(8,128)S(1)} %get-tuple-element.32), channel_id=1, source_target_pairs={{4,0},{6,2},{8,4},{1,5},{10,6},{3,7},{12,8},{5,9},{14,10},{7,11},{... | collective-permute-start | bytes 294920 | tf_op jit(solution)/shard_map/ppermute | solution.py:613
  4.1 7.3 %collective-permute-start.1 = (f32[6,8,512]{2,1,0:T(8,128)S(1)}, f32[6,8,512]{2,1,0:T(8,128)S(1)}, u32[]{:S(2)}, u32[]{:S(2)}) collective-permute-start(f32[6,8,512]{2,1,0:T(8,128)S(1)} %get-tuple-element.33), channel_id=1, source_target_pairs={{2,0},{4,2},{1,3},{6,4},{3,5},{8,6},{5,7},{10,8},{7,9},{12,10},{9,... | collective-permute-start | bytes 294920 | tf_op jit(solution)/shard_map/ppermute | solution.py:613
  6.2 0.7 %copy-start.2 = (s32[8]{0:T(128)S(1)}, s32[8]{0:T(128)}, u32[]{:S(2)}) copy-start(s32[8]{0:T(128)} %angle_ref.5) | copy-start | bytes 100
  6.2 0.7 %copy-start.3 = (s32[4]{0:T(128)S(1)}, s32[4]{0:T(128)}, u32[]{:S(2)}) copy-start(s32[4]{0:T(128)} %subset_ref.5) | copy-start | bytes 52
  6.2 0.7 %copy-start.4 = (s32[8]{0:T(128)S(1)}, s32[8]{0:T(128)}, u32[]{:S(2)}) copy-start(s32[8]{0:T(128)} %lift_ref.3) | copy-start | bytes 100
  6.2 5.2 %collective-permute-start.2 = (f32[5,8,512]{2,1,0:T(8,128)S(1)}, f32[5,8,512]{2,1,0:T(8,128)S(1)}, u32[]{:S(2)}, u32[]{:S(2)}) collective-permute-start(f32[5,8,512]{2,1,0:T(8,128)S(1)} %get-tuple-element.34), channel_id=1, source_target_pairs={{3,1},{0,2},{5,3},{2,4},{7,5},{4,6},{9,7},{6,8},{11,9},{8,10},{13,... | collective-permute-start | bytes 245768 | tf_op jit(solution)/shard_map/ppermute | solution.py:613
  9.0 3.4 %collective-permute-start.3 = (f32[7,8,512]{2,1,0:T(8,128)S(1)}, f32[7,8,512]{2,1,0:T(8,128)S(1)}, u32[]{:S(2)}, u32[]{:S(2)}) collective-permute-start(f32[7,8,512]{2,1,0:T(8,128)S(1)} %get-tuple-element.58.refs_0_), channel_id=1, source_target_pairs={{0,1},{1,0},{2,3},{3,2},{4,5},{5,4},{6,7},{7,6},{8,9},{9,8},{10,11... | collective-permute-start | bytes 344072 | tf_op jit(solution)/shard_map/ppermute | solution.py:601
  11.4 1.9 %collective-permute-start.4 = (f32[6,8,512]{2,1,0:T(8,128)S(1)}, f32[6,8,512]{2,1,0:T(8,128)S(1)}, u32[]{:S(2)}, u32[]{:S(2)}) collective-permute-start(f32[6,8,512]{2,1,0:T(8,128)S(1)} %collective-permute-done), channel_id=1, source_target_pairs={{0,1},{1,0},{2,3},{3,2},{4,5},{5,4},{6,7},{7,6},{8,9},{9,8},{10,11... | collective-permute-start | bytes 294920 | tf_op jit(solution)/shard_map/ppermute | solution.py:601
  11.9 1.4 %collective-permute-start.5 = (f32[6,8,512]{2,1,0:T(8,128)S(1)}, f32[6,8,512]{2,1,0:T(8,128)S(1)}, u32[]{:S(2)}, u32[]{:S(2)}) collective-permute-start(f32[6,8,512]{2,1,0:T(8,128)S(1)} %collective-permute-done.1.refs_3_), channel_id=1, source_target_pairs={{0,1},{1,0},{2,3},{3,2},{4,5},{5,4},{6,7},{7,6},{8,9},{9,8},{10,11... | collective-permute-start | bytes 294920 | tf_op jit(solution)/shard_map/ppermute | solution.py:601
  11.9 1.4 %collective-permute-start.6 = (f32[5,8,512]{2,1,0:T(8,128)S(1)}, f32[5,8,512]{2,1,0:T(8,128)S(1)}, u32[]{:S(2)}, u32[]{:S(2)}) collective-permute-start(f32[5,8,512]{2,1,0:T(8,128)S(1)} %collective-permute-done.2.refs_5_), channel_id=1, source_target_pairs={{0,1},{1,0},{2,3},{3,2},{4,5},{5,4},{6,7},{7,6},{8,9},{9,8},{10,11... | collective-permute-start | bytes 245768 | tf_op jit(solution)/shard_map/ppermute | solution.py:601

commit v14 on v13

--- a/solution.py
+++ b/solution.py
@@ -73,6 +73,17 @@
         start_index_map=(1,),
         operand_batching_dims=(0,),
         start_indices_batching_dims=(0,),
+    )
+    return lax.gather(tile, index[..., None], numbers, (1, 1), mode=lax.GatherScatterMode.PROMISE_IN_BOUNDS)
+
+
+def pick_rows(tile, index):
+    numbers = lax.GatherDimensionNumbers(
+        offset_dims=(),
+        collapsed_slice_dims=(0,),
+        start_index_map=(0,),
+        operand_batching_dims=(1,),
+        start_indices_batching_dims=(1,),
     )
     return lax.gather(tile, index[..., None], numbers, (1, 1), mode=lax.GatherScatterMode.PROMISE_IN_BOUNDS)
 
@@ -394,6 +405,8 @@
     cone_ref,
     place_ref,
     tap_ref,
+    tangent_ref,
+    view_ref,
     edge_ref,
     bend_ref,
     sub_ref,
@@ -429,6 +442,9 @@
     cosine, flat, lifts = subset_angles(angle_ref, lift_ref, subset_ref)
     tangents = member_tangents(angle_ref, subset_ref)
     for member in range(subset_count):
+        tangent_ref[member, :, :] = tangents[member]
+    view_ref[...] = spread_scalars(lambda k: subset_ref[k], subset_count, jnp.bitwise_and(sub, subset_count - 1))
+    for member in range(subset_count):
         view = pl.ds(subset_ref[member], 1)
         for side in range(2):
             at = slice(side * subset_count + member, side * subset_count + member + 1)
@@ -478,8 +494,6 @@
 def update_kernel(
     order,
     kinds,
-    angle_ref,
-    subset_ref,
     volume_ref,
     measured_ref,
     bound_ref,
@@ -489,13 +503,15 @@
     cone_ref,
     place_ref,
     tap_ref,
+    tangent_ref,
+    view_ref,
     *refs,
 ):
     blocks = refs[: len(order)]
     residual_ref, updated_ref, profile_ref, spread_ref, cell_ref, slope_ref, rest_ref, new_ref, row_ref, sent = refs[len(order) :]
     slab_depth, row_count, cell_count = volume_ref.shape
     row_share, view_count, column_count = measured_ref.shape
-    subset_count = subset_ref.shape[0]
+    subset_count = tangent_ref.shape[0]
     tiles, columns = cell_count // LANES, column_count // LANES
     width = column_count // 2
     zero = jnp.zeros((SUBLANES, LANES), F32)
@@ -519,27 +535,36 @@
     copies = [pltpu.make_async_copy(rest_ref, residual_ref, sent.at[groups])]
     copies[0].start()
 
-    for member in range(subset_count):
-        view = pl.ds(subset_ref[member], 1)
-        for side in range(2):
-            at = slice(side * subset_count + member, side * subset_count + member + 1)
-            other = other_block[(slab_depth - 1) * 2 + side, view, :], other_block[side, view, :]
-            mate = mate_block[(slab_depth - 1) * 2 + side, view, :], mate_block[side, view, :]
-            profile_ref[0, at, :] = jnp.where(odd == 0, other[0], mate[0])
-            for depth in range(slab_depth):
-                profile_ref[1 + depth, at, :] = blocks[0][depth * 2 + side, view, :]
-            profile_ref[1 + slab_depth, at, :] = jnp.where(odd == 0, mate[1], other[1])
+    chosen, first_side = view_ref[...], sublane_index() < subset_count
+
+    def of_members(read, tile):
+        return jnp.where(first_side, pick_rows(read(0, tile), chosen), pick_rows(read(1, tile), chosen))
+
+    inner_tiles = width // LANES
+    for tile in range(inner_tiles):
+        cut = slice(tile * LANES, (tile + 1) * LANES)
+        last, first = (slab_depth - 1) * 2, 0
+        below = lambda side, t: jnp.where(
+            odd == 0, tile_of(other_block, (last + side,), t), tile_of(mate_block, (last + side,), t)
+        )
+        above = lambda side, t: jnp.where(
+            odd == 0, tile_of(mate_block, (first + side,), t), tile_of(other_block, (first + side,), t)
+        )
+        profile_ref[0, :, cut] = of_members(below, tile)
+        for depth in range(slab_depth):
+            profile_ref[1 + depth, :, cut] = of_members(
+                lambda side, t: tile_of(blocks[0], (depth * 2 + side,), t), tile
+            )
+        profile_ref[1 + slab_depth, :, cut] = of_members(above, tile)
 
     moved = [(b, j) for b, kind in enumerate(kinds) for j in range({FULL: 0, FAR: 2}.get(kind, 1))]
     for at_row, (b, j) in enumerate(moved):
         depth = turns[b] if kinds[b] in (NEAR, NEAR_SHARED) else j
-        for member in range(subset_count):
-            view = pl.ds(subset_ref[member], 1)
-            for side in range(2):
-                at = slice(side * subset_count + member, side * subset_count + member + 1)
-                row_ref[at_row, at, :] = blocks[b][depth * 2 + side, view, :]
-
-    inner_tiles = width // LANES
+        for tile in range(inner_tiles):
+            row_ref[at_row, :, tile * LANES : (tile + 1) * LANES] = of_members(
+                lambda side, t: tile_of(blocks[b], (depth * 2 + side,), t), tile
+            )
+
     spread = [[zero] * inner_tiles for _ in range(slab_depth)]
     for place in range(row_share * len(order)):
         weight = [cone_ref[place, z, :, :] for z in range(slab_depth + 2)]
@@ -576,7 +601,7 @@
         line.append(value)
     store_line(line, cell_ref, slope_ref)
 
-    tangents = member_tangents(angle_ref, subset_ref)
+    tangents = [tangent_ref[member, :, :] for member in range(subset_count)]
     for group in range(groups):
         band = slice(group * SUBLANES, (group + 1) * SUBLANES)
         back = [[zero] * tiles for _ in range(slab_depth)]
@@ -690,9 +715,11 @@
             pltpu.VMEM((row_share * len(order), slab_depth + 2, SUBLANES, LANES), F32),
             pltpu.VMEM((tiles + 1, 3, SUBLANES, LANES), jnp.int32),
             pltpu.VMEM((tiles + 1, 3, SUBLANES, LANES), F32),
+            pltpu.VMEM((subset_count, SUBLANES, LANES), F32),
+            pltpu.VMEM((SUBLANES, LANES), jnp.int32),
         ),
         in_specs=[smem] * 3 + [vmem],
-        out_specs=(vmem,) * 7,
+        out_specs=(vmem,) * 9,
         scratch_shapes=[pltpu.VMEM((SUBLANES, wide), F32)] * 2 + [pltpu.VMEM((SUBLANES, column_count // 2), F32)],
         cost_estimate=pl.CostEstimate(flops=4_000_000, bytes_accessed=8_000_000, transcendentals=0),
         compiler_params=small,
@@ -705,7 +732,7 @@
             jax.ShapeDtypeStruct(measured.shape, F32),
             jax.ShapeDtypeStruct(volume.shape, F32),
         ),
-        in_specs=[smem] * 2 + [vmem] * (2 + len(divisors) + len(order)),
+        in_specs=[vmem] * (2 + len(divisors) + len(order)),
         out_specs=(pl.BlockSpec(memory_space=pl.ANY),) * 2,
         scratch_shapes=[
             pltpu.VMEM((slab_depth + 2, SUBLANES, column_count // 2), F32),
@@ -719,7 +746,7 @@
         ],
         compiler_params=small,
         name="update",
-    )(view_angle, subset, *map(here, (volume, measured, *divisors, *blocks)))
+    )(*map(here, (volume, measured, *divisors, *blocks)))
 
 
 def solution(mesh):

time: 16.3 us -> 15.7 us (0.963)
  the two profiles are of different devices: /device:TPU:0 before, /device:TPU:25 now
where the time goes in v14:
time: 15.7 us; the launch traced here: 15.5 us
  Pallas kernels  7.07 us (45%)
  starting transfers between devices  4.18 us (27%)
  waiting for transfers between devices  3.58 us (23%)
  between operations  0.68 us (4%)
    ppermute x3, starting transfers between devices, from_chip(): return lax.ppermute(block, 'slab', pairs)  3.06 us
    pallas_call x1, Pallas kernels, per_device(): pl.pallas_call(functools.partial(project_kernel, slab_count), out_shape=(...  2.98 us
    ppermute x3, waiting for transfers between devices, from_chip(): return lax.ppermute(block, 'slab', pairs)  2.66 us
    pallas_call x1, Pallas kernels, per_device(): divide(view_angle, view_lift, subset, cover)  2.05 us
    pallas_call x1, Pallas kernels, per_device(): pl.pallas_call(functools.partial(update_kernel, order, kinds), out_shape=...  2.04 us
    ppermute x4, starting transfers between devices, swapped(): lax.ppermute(block, 'slab', [(i, i ^ 1) for i in range(lax.axis_size('sla...  1.12 us
    ppermute x4, waiting for transfers between devices, swapped(): lax.ppermute(block, 'slab', [(i, i ^ 1) for i in range(lax.axis_size('sla...  0.93 us
  transfers between devices with their start and end apart: 7, of which 2 were waited for; matrix products, arithmetic and copies ran while one was open for 0% of the time, Pallas kernels for 13%

profile of v14, /device:TPU:25, one launch (start us, length us, event | category | flops | bytes accessed | tf_op | source)
XLA Modules:
  0.0 15.5 jit_solution(8740329361504662661)
XLA Ops:
  0.6 0.0 copy-start
  0.6 0.0 copy-start.1
  0.6 3.0 %project.1 = (f32[7,8,512]{2,1,0:T(8,128)S(1)}, f32[6,8,512]{2,1,0:T(8,128)S(1)}, f32[5,8,512]{2,1,0:T(8,128)S(1)}, f32[6,8,512]{2,1,0:T(8,128)S(1)}, f32[8,1024]{1,0:T(8,128)S(1)}) custom-call(s32[8]{0:T(128)} %angle_ref.3, s32[8]{0:T(128)} %lift_ref.3, s32[4]{0:T(128)} %subset_ref.3, f32[2,64,1024]{2,1,0:T(8,128)} %volume_ref.3, f32[3,8,1024]{2,1,0:T(8,128)} %measured_ref.3), custom_call_target="tpu_custom_call" | custom-call | tf_op jit(solution)/shard_map/project/pallas_call | solution.py:685
  3.6 0.7 %collective-permute-start = (f32[6,8,512]{2,1,0:T(8,128)S(1)}, f32[6,8,512]{2,1,0:T(8,128)S(1)}, u32[]{:S(2)}, u32[]{:S(2)}) collective-permute-start(f32[6,8,512]{2,1,0:T(8,128)S(1)} %get-tuple-element.38), channel_id=1, source_target_pairs={{4,0},{6,2},{8,4},{1,5},{10,6},{3,7},{12,8},{5,9},{14,10},{7,11},{... | collective-permute-start | bytes 294920 | tf_op jit(solution)/shard_map/ppermute | solution.py:638
  4.3 1.2 %collective-permute-start.1 = (f32[6,8,512]{2,1,0:T(8,128)S(1)}, f32[6,8,512]{2,1,0:T(8,128)S(1)}, u32[]{:S(2)}, u32[]{:S(2)}) collective-permute-start(f32[6,8,512]{2,1,0:T(8,128)S(1)} %get-tuple-element.39), channel_id=1, source_target_pairs={{2,0},{4,2},{1,3},{6,4},{3,5},{8,6},{5,7},{10,8},{7,9},{12,10},{9,... | collective-permute-start | bytes 294920 | tf_op jit(solution)/shard_map/ppermute | solution.py:638
  5.6 0.0 copy-start.2
  5.6 0.0 copy-start.3
  5.6 0.0 copy-start.4
  5.6 1.1 %collective-permute-start.2 = (f32[5,8,512]{2,1,0:T(8,128)S(1)}, f32[5,8,512]{2,1,0:T(8,128)S(1)}, u32[]{:S(2)}, u32[]{:S(2)}) collective-permute-start(f32[5,8,512]{2,1,0:T(8,128)S(1)} %get-tuple-element.40), channel_id=1, source_target_pairs={{3,1},{0,2},{5,3},{2,4},{7,5},{4,6},{9,7},{6,8},{11,9},{8,10},{13,... | collective-permute-start | bytes 245768 | tf_op jit(solution)/shard_map/ppermute | solution.py:638
  6.7 0.0 copy-done.2
  6.7 0.0 copy-done.3
  6.7 0.0 copy-done.4
  6.7 2.0 %divisors.1 = (f32[2,64,1024]{2,1,0:T(8,128)S(1)}, f32[3,8,1024]{2,1,0:T(8,128)S(1)}, f32[21,8,512]{2,1,0:T(8,128)S(1)}, f32[14,3,8,128]{3,2,1,0:T(8,128)S(1)}, ...) custom-call(s32[8]{0:T(128)S(1)} %copy-done.2, ...), custom_call_target="tpu_custom_call" | custom-call | flops 4000000 | bytes 8000000 | tf_op jit(solution)/shard_map/divisors/pallas_call | solution.py:728
  8.8 0.2 %collective-permute-start.3 = (f32[7,8,512]{2,1,0:T(8,128)S(1)}, f32[7,8,512]{2,1,0:T(8,128)S(1)}, u32[]{:S(2)}, u32[]{:S(2)}) collective-permute-start(f32[7,8,512]{2,1,0:T(8,128)S(1)} %get-tuple-element.70.refs_0_), channel_id=1, source_target_pairs={{0,1},{1,0},{2,3},{3,2},{4,5},{5,4},{6,7},{7,6},{8,9},{9,8},{10,11... | collective-permute-start | bytes 344072 | tf_op jit(solution)/shard_map/ppermute | solution.py:626
  9.0 2.7 %collective-permute-done.2.refs_5_ = f32[5,8,512]{2,1,0:T(8,128)S(1)} collective-permute-done((f32[5,8,512]{2,1,0:T(8,128)S(1)}, f32[5,8,512]{2,1,0:T(8,128)S(1)}, u32[]{:S(2)}, u32[]{:S(2)}) %collective-permute-start.2) | collective-permute-done | bytes 81952 | tf_op jit(solution)/shard_map/ppermute | solution.py:638
  11.6 0.0 collective-permute-done
  11.6 0.0 collective-permute-done.1.refs_3_
  11.7 0.4 %collective-permute-start.4 = (f32[6,8,512]{2,1,0:T(8,128)S(1)}, f32[6,8,512]{2,1,0:T(8,128)S(1)}, u32[]{:S(2)}, u32[]{:S(2)}) collective-permute-start(f32[6,8,512]{2,1,0:T(8,128)S(1)} %collective-permute-done), channel_id=1, source_target_pairs={{0,1},{1,0},{2,3},{3,2},{4,5},{5,4},{6,7},{7,6},{8,9},{9,8},{10,11... | collective-permute-start | bytes 294920 | tf_op jit(solution)/shard_map/ppermute | solution.py:626
  12.0 0.1 collective-permute-start.5
  12.2 0.4 %collective-permute-start.6 = (f32[5,8,512]{2,1,0:T(8,128)S(1)}, f32[5,8,512]{2,1,0:T(8,128)S(1)}, u32[]{:S(2)}, u32[]{:S(2)}) collective-permute-start(f32[5,8,512]{2,1,0:T(8,128)S(1)} %collective-permute-done.2.refs_5_), channel_id=1, source_target_pairs={{0,1},{1,0},{2,3},{3,2},{4,5},{5,4},{6,7},{7,6},{8,9},{9,8},{10,11... | collective-permute-start | bytes 245768 | tf_op jit(solution)/shard_map/ppermute | solution.py:626
  12.6 0.0 collective-permute-done.3.refs_1_
  12.6 0.9 %collective-permute-done.6.refs_6_ = f32[5,8,512]{2,1,0:T(8,128)S(1)} collective-permute-done((f32[5,8,512]{2,1,0:T(8,128)S(1)}, f32[5,8,512]{2,1,0:T(8,128)S(1)}, u32[]{:S(2)}, u32[]{:S(2)}) %collective-permute-start.6) | collective-permute-done | bytes 81952 | tf_op jit(solution)/shard_map/ppermute | solution.py:626
  13.5 0.0 collective-permute-done.4.refs_2_
  13.5 0.0 collective-permute-done.5.refs_4_
  13.5 0.0 copy-done
  13.5 0.0 copy-done.1
  13.5 2.0 %update.1 = (f32[3,8,1024]{2,1,0:T(8,128)}, f32[2,64,1024]{2,1,0:T(8,128)}) custom-call(f32[2,64,1024]{2,1,0:T(8,128)S(1)} %copy-done, f32[3,8,1024]{2,1,0:T(8,128)S(1)} %copy-done.1, f32[2,64,1024]{2,1,0:T(8,128)S(1)} %get-tuple-element.61.bound_ref, f32[3,8,1024]{2,1,0:T(8,128)S(1)} %get-tuple-element.62.own_ref, ...), custom_call_target="tpu_custom_call" | custom-call | tf_op jit(solution)/shard_map/update/pallas_call | solution.py:729
Async XLA Ops:
  0.6 12.9 %copy-start = (f32[2,64,1024]{2,1,0:T(8,128)S(1)}, f32[2,64,1024]{2,1,0:T(8,128)}, u32[]{:S(2)}) copy-start(f32[2,64,1024]{2,1,0:T(8,128)} %volume_ref.3) | copy-start | bytes 1572868
  0.6 12.8 %copy-start.1 = (f32[3,8,1024]{2,1,0:T(8,128)S(1)}, f32[3,8,1024]{2,1,0:T(8,128)}, u32[]{:S(2)}) copy-start(f32[3,8,1024]{2,1,0:T(8,128)} %measured_ref.3) | copy-start | bytes 294916
  3.6 8.0 %collective-permute-start = (f32[6,8,512]{2,1,0:T(8,128)S(1)}, f32[6,8,512]{2,1,0:T(8,128)S(1)}, u32[]{:S(2)}, u32[]{:S(2)}) collective-permute-start(f32[6,8,512]{2,1,0:T(8,128)S(1)} %get-tuple-element.38), channel_id=1, source_target_pairs={{4,0},{6,2},{8,4},{1,5},{10,6},{3,7},{12,8},{5,9},{14,10},{7,11},{... | collective-permute-start | bytes 294920 | tf_op jit(solution)/shard_map/ppermute | solution.py:638
  4.3 7.3 %collective-permute-start.1 = (f32[6,8,512]{2,1,0:T(8,128)S(1)}, f32[6,8,512]{2,1,0:T(8,128)S(1)}, u32[]{:S(2)}, u32[]{:S(2)}) collective-permute-start(f32[6,8,512]{2,1,0:T(8,128)S(1)} %get-tuple-element.39), channel_id=1, source_target_pairs={{2,0},{4,2},{1,3},{6,4},{3,5},{8,6},{5,7},{10,8},{7,9},{12,10},{9,... | collective-permute-start | bytes 294920 | tf_op jit(solution)/shard_map/ppermute | solution.py:638
  5.6 1.1 %copy-start.2 = (s32[8]{0:T(128)S(1)}, s32[8]{0:T(128)}, u32[]{:S(2)}) copy-start(s32[8]{0:T(128)} %angle_ref.3) | copy-start | bytes 100
  5.6 1.1 %copy-start.3 = (s32[8]{0:T(128)S(1)}, s32[8]{0:T(128)}, u32[]{:S(2)}) copy-start(s32[8]{0:T(128)} %lift_ref.3) | copy-start | bytes 100
  5.6 1.1 %copy-start.4 = (s32[4]{0:T(128)S(1)}, s32[4]{0:T(128)}, u32[]{:S(2)}) copy-start(s32[4]{0:T(128)} %subset_ref.3) | copy-start | bytes 52
  5.6 6.1 %collective-permute-start.2 = (f32[5,8,512]{2,1,0:T(8,128)S(1)}, f32[5,8,512]{2,1,0:T(8,128)S(1)}, u32[]{:S(2)}, u32[]{:S(2)}) collective-permute-start(f32[5,8,512]{2,1,0:T(8,128)S(1)} %get-tuple-element.40), channel_id=1, source_target_pairs={{3,1},{0,2},{5,3},{2,4},{7,5},{4,6},{9,7},{6,8},{11,9},{8,10},{13,... | collective-permute-start | bytes 245768 | tf_op jit(solution)/shard_map/ppermute | solution.py:638
  8.8 3.8 %collective-permute-start.3 = (f32[7,8,512]{2,1,0:T(8,128)S(1)}, f32[7,8,512]{2,1,0:T(8,128)S(1)}, u32[]{:S(2)}, u32[]{:S(2)}) collective-permute-start(f32[7,8,512]{2,1,0:T(8,128)S(1)} %get-tuple-element.70.refs_0_), channel_id=1, source_target_pairs={{0,1},{1,0},{2,3},{3,2},{4,5},{5,4},{6,7},{7,6},{8,9},{9,8},{10,11... | collective-permute-start | bytes 344072 | tf_op jit(solution)/shard_map/ppermute | solution.py:626
  11.7 1.8 %collective-permute-start.4 = (f32[6,8,512]{2,1,0:T(8,128)S(1)}, f32[6,8,512]{2,1,0:T(8,128)S(1)}, u32[]{:S(2)}, u32[]{:S(2)}) collective-permute-start(f32[6,8,512]{2,1,0:T(8,128)S(1)} %collective-permute-done), channel_id=1, source_target_pairs={{0,1},{1,0},{2,3},{3,2},{4,5},{5,4},{6,7},{7,6},{8,9},{9,8},{10,11... | collective-permute-start | bytes 294920 | tf_op jit(solution)/shard_map/ppermute | solution.py:626
  12.0 1.4 %collective-permute-start.5 = (f32[6,8,512]{2,1,0:T(8,128)S(1)}, f32[6,8,512]{2,1,0:T(8,128)S(1)}, u32[]{:S(2)}, u32[]{:S(2)}) collective-permute-start(f32[6,8,512]{2,1,0:T(8,128)S(1)} %collective-permute-done.1.refs_3_), channel_id=1, source_target_pairs={{0,1},{1,0},{2,3},{3,2},{4,5},{5,4},{6,7},{7,6},{8,9},{9,8},{10,11... | collective-permute-start | bytes 294920 | tf_op jit(solution)/shard_map/ppermute | solution.py:626
  12.2 1.3 %collective-permute-start.6 = (f32[5,8,512]{2,1,0:T(8,128)S(1)}, f32[5,8,512]{2,1,0:T(8,128)S(1)}, u32[]{:S(2)}, u32[]{:S(2)}) collective-permute-start(f32[5,8,512]{2,1,0:T(8,128)S(1)} %collective-permute-done.2.refs_5_), channel_id=1, source_target_pairs={{0,1},{1,0},{2,3},{3,2},{4,5},{5,4},{6,7},{7,6},{8,9},{9,8},{10,11... | collective-permute-start | bytes 245768 | tf_op jit(solution)/shard_map/ppermute | solution.py:626

commit v15 on v14

--- a/solution.py
+++ b/solution.py
@@ -233,6 +233,38 @@
     return [angle_facts(jnp.full((SUBLANES, LANES), i, jnp.int32))[1] for i in indices]
 
 
+def store_cells(line, at, half, cell_ref, slope_ref):
+    lane, shift = lane_index(), LANES - half
+    zero = jnp.zeros((SUBLANES, LANES), F32)
+    line = [jnp.where(lane >= shift, line[0], 0.0)] + line[1:-1] + [jnp.where(lane < shift, line[-1], 0.0), zero]
+    for tile in range(len(line) - 1):
+        cut = slice(tile * LANES, (tile + 1) * LANES)
+        cell_ref[at, :, cut] = line[tile]
+        slope_ref[at, :, cut] = next_lane(line[tile], line[tile + 1]) - line[tile]
+
+
+def forward_tap(tile, cosine, column_count, cell_count, shift):
+    least = angle_table()[0].min()
+    column = (lane_index() + tile * LANES).astype(F32)
+    center = column_center(column, cosine, column_count, cell_count)
+    whole = jnp.floor(center)
+    place = jnp.clip(whole.astype(jnp.int32) + shift, shift - 2, shift + cell_count)
+    ends = [column_center(tile * LANES + e, c, column_count, cell_count) for e in (0, LANES - 1) for c in (1.0, least)]
+    low = min(max(math.floor(min(ends) - 1e-2) + shift, shift - 2), shift + cell_count) // LANES
+    high = min(max(math.floor(max(ends) + 1e-2) + shift, shift - 2), shift + cell_count) // LANES
+    return place, center - whole, range(low, high + 1)
+
+
+def resampled(at, place, fraction, sources, level, cell_ref, slope_ref):
+    block, index = jnp.right_shift(place, 7), jnp.bitwise_and(place, LANES - 1)
+    cells, slope = level, jnp.zeros((SUBLANES, LANES), F32)
+    for source in sources:
+        here = block == source
+        cells = jnp.where(here, pick(tile_of(cell_ref, (at,), source), index), cells)
+        slope = jnp.where(here, pick(tile_of(slope_ref, (at,), source), index), slope)
+    return cells + fraction * slope
+
+
 def project_kernel(
     slab_count,
     angle_ref,
@@ -244,11 +276,9 @@
     near_ref,
     low_ref,
     high_ref,
-    cover_ref,
     rise_ref,
     first_ref,
     part_ref,
-    end_ref,
     cell_ref,
     slope_ref,
 ):
@@ -310,7 +340,6 @@
 
     def one_view(view, carry):
         _, tangent, _ = angle_facts(jnp.full((SUBLANES, LANES), angle_ref[view], jnp.int32))
-        low_end, high_end = zero, zero
         sums = [[zero] * (tiles + 1) for _ in range(slab_depth)]
         for group in range(groups):
             band = slice(group * SUBLANES, (group + 1) * SUBLANES)
@@ -319,8 +348,6 @@
             index = jnp.bitwise_and(place, LANES - 1)
             near, last = place < LANES, index == LANES - 1
             enter = jnp.where(last, fraction, 0.0)
-            low_end = low_end + jnp.where(near, enter, 1.0)
-            high_end = high_end + jnp.where(near, 1.0 - enter, 0.0)
             for depth in range(slab_depth):
                 before = enter * first_ref[depth, band, :]
                 for tile in range(tiles + 1):
@@ -330,8 +357,6 @@
                         after = pick(tile_of(volume_ref, at, tile) + fraction * tile_of(rise_ref, at, tile), index)
                     sums[depth][tile] = sums[depth][tile] + jnp.where(near, before, after)
                     before = after
-        end_ref[0, view, :, :] = low_end
-        end_ref[1, view, :, :] = high_end
         for depth in range(slab_depth):
             for tile in range(tiles + 1):
                 part_ref[depth, view, :, tile * LANES : (tile + 1) * LANES] = sums[depth][tile]
@@ -339,55 +364,26 @@
 
     lax.fori_loop(0, view_count, one_view, 0, unroll=8)
 
-    shift = LANES - half
-    inside = [None] * (tiles + 1)
-    inside[0], inside[tiles] = lane >= shift, lane < shift
-
-    def store(at, line):
-        line = [jnp.where(mask, cells, 0.0) if mask is not None else cells for cells, mask in zip(line, inside)] + [zero]
-        for tile in range(tiles + 1):
-            cut = slice(tile * LANES, (tile + 1) * LANES)
-            cell_ref[at, :, cut] = line[tile]
-            slope_ref[at, :, cut] = next_lane(line[tile], line[tile + 1]) - line[tile]
-
-    views = range(view_count)
     for depth in range(slab_depth):
-        store(depth, [rows_summed([tile_of(part_ref, (depth, v), t) for v in views]) for t in range(tiles + 1)])
-    level = zero + float(row_count)
-    ends = [rows_summed([end_ref[e, v, :, :] for v in views]) for e in range(2)]
-    store(slab_depth, [ends[0]] + [level] * (tiles - 1) + [ends[1]])
+        line = [
+            rows_summed([tile_of(part_ref, (depth, view), tile) for view in range(view_count)])
+            for tile in range(tiles + 1)
+        ]
+        store_cells(line, depth, half, cell_ref, slope_ref)
 
     factor = 1.0 / (row_count * cosine)
-    least = angle_table()[0].min()
     for tile in range(column_count // LANES):
-        column = (lane + tile * LANES).astype(F32)
-        center = column_center(column, cosine, column_count, cell_count)
-        whole = jnp.floor(center)
-        fraction = center - whole
-        place = jnp.clip(whole.astype(jnp.int32) + shift, shift - 2, shift + cell_count)
-        block, index = jnp.right_shift(place, 7), jnp.bitwise_and(place, LANES - 1)
-        ends = [column_center(tile * LANES + e, c, column_count, cell_count) for e in (0, LANES - 1) for c in (1.0, least)]
-        low = min(max(math.floor(min(ends) - 1e-2) + shift, shift - 2), shift + cell_count) // LANES
-        high = min(max(math.floor(max(ends) + 1e-2) + shift, shift - 2), shift + cell_count) // LANES
-        cells, slopes = [zero] * slab_depth + [level], [zero] * (slab_depth + 1)
-        for source in range(low, high + 1):
-            here = block == source
-            for at in range(slab_depth + 1):
-                if at == slab_depth and source not in (0, tiles):
-                    continue
-                cells[at] = jnp.where(here, pick(tile_of(cell_ref, (at,), source), index), cells[at])
-                slopes[at] = jnp.where(here, pick(tile_of(slope_ref, (at,), source), index), slopes[at])
-        profiles = [(c + fraction * s) * factor for c, s in zip(cells, slopes)]
+        place, fraction, sources = forward_tap(tile, cosine, column_count, cell_count, LANES - half)
         side, inner = divmod(tile * LANES, width)
         for depth in range(slab_depth):
+            profile = resampled(depth, place, fraction, sources, zero, cell_ref, slope_ref) * factor
             to = (depth * 2 + side, slice(None), slice(inner, inner + LANES))
             measured = tile_of(measured_ref, (depth,), tile)
             last = tile_of(measured_ref, (depth * (row_share - 1),), tile)
-            block_ref[to] = profiles[depth]
-            near_ref[to] = jnp.where(near_places[depth], last, profiles[depth])
-            low_ref[to] = jnp.where(low_places, measured, profiles[depth])
-            high_ref[to] = jnp.where(high_places, measured, profiles[depth])
-        cover_ref[:, tile * LANES : (tile + 1) * LANES] = profiles[slab_depth]
+            block_ref[to] = profile
+            near_ref[to] = jnp.where(near_places[depth], last, profile)
+            low_ref[to] = jnp.where(low_places, measured, profile)
+            high_ref[to] = jnp.where(high_places, measured, profile)
 
 
 def divisor_kernel(
@@ -397,7 +393,7 @@
     angle_ref,
     lift_ref,
     subset_ref,
-    cover_ref,
+    _,
     bound_ref,
     own_ref,
     rows_ref,
@@ -410,6 +406,9 @@
     edge_ref,
     bend_ref,
     sub_ref,
+    cover_ref,
+    cell_ref,
+    slope_ref,
 ):
     slab_depth, row_count, cell_count = bound_ref.shape
     row_share, view_count, column_count = own_ref.shape
@@ -421,9 +420,32 @@
     zero = jnp.zeros((SUBLANES, LANES), F32)
     slab = lax.axis_index("slab")
 
-    _, _, flat = angle_facts(spread_scalars(lambda v: angle_ref[v], view_count, sub))
+    cosine, _, flat = angle_facts(spread_scalars(lambda v: angle_ref[v], view_count, sub))
     lifts = spread_scalars(lambda v: lift_ref[v], view_count, sub).astype(F32)
     lane = lane_index()
+
+    half = row_count // 2
+    ends = [], []
+    for view in range(view_count):
+        _, tangent, _ = angle_facts(jnp.full((SUBLANES, LANES), angle_ref[view], jnp.int32))
+        low_end, high_end = zero, zero
+        for group in range(row_count // SUBLANES):
+            whole, fraction = shear_steps(group, row_count, tangent)
+            place = lane + (whole + half)
+            near = place < LANES
+            enter = jnp.where(jnp.bitwise_and(place, LANES - 1) == LANES - 1, fraction, 0.0)
+            low_end = low_end + jnp.where(near, enter, 1.0)
+            high_end = high_end + jnp.where(near, 1.0 - enter, 0.0)
+        ends[0].append(low_end)
+        ends[1].append(high_end)
+    level = zero + float(row_count)
+    store_cells([rows_summed(ends[0])] + [level] * (tiles - 1) + [rows_summed(ends[1])], 0, half, cell_ref, slope_ref)
+    for tile in range(columns):
+        place, fraction, sources = forward_tap(tile, cosine, column_count, cell_count, LANES - half)
+        sources = [source for source in sources if source in (0, tiles)]
+        cover_ref[:, tile * LANES : (tile + 1) * LANES] = resampled(
+            0, place, fraction, sources, level, cell_ref, slope_ref
+        ) * (1.0 / (row_count * cosine))
     origin = slabs_of(slab, order)
     source = sum(jnp.where(lane >= slab_depth * b, 1, 0) for b in range(1, len(order)))
     slices = spread_scalars(lambda b: origin[b], len(order), source) * slab_depth + (lane - source * slab_depth)
@@ -682,28 +704,25 @@
     smem, vmem = pl.BlockSpec(memory_space=pltpu.SMEM), pl.BlockSpec(memory_space=pltpu.VMEM)
     wide = (tiles + 1) * LANES
     block_of = lambda rows: pltpu.VMEM((2 * slab_depth + rows, SUBLANES, column_count // 2), F32)
-    own, near, low, high, cover = pl.pallas_call(
+    own, near, low, high = pl.pallas_call(
         functools.partial(project_kernel, slab_count),
         out_shape=(
             block_of(row_share),
             block_of(2),
             block_of(1),
             block_of(2),
-            pltpu.VMEM((view_count, column_count), F32),
         ),
         in_specs=[smem] * 3 + [vmem] * 2,
-        out_specs=(vmem,) * 5,
+        out_specs=(vmem,) * 4,
         scratch_shapes=[
             pltpu.VMEM(volume.shape, F32),
             pltpu.VMEM((slab_depth, row_count, LANES), F32),
             pltpu.VMEM((slab_depth, view_count, SUBLANES, wide), F32),
-            pltpu.VMEM((2, view_count, SUBLANES, LANES), F32),
         ]
-        + [pltpu.VMEM((slab_depth + 1, SUBLANES, wide), F32)] * 2,
+        + [pltpu.VMEM((slab_depth, SUBLANES, wide), F32)] * 2,
         compiler_params=small,
         name="project",
     )(*map(there, (view_angle, view_lift, subset, volume, measured)))
-    cover = here(cover)
     order, kinds = window(reach)
     divide = pl.pallas_call(
         functools.partial(divisor_kernel, slab_count, order, kinds),
@@ -718,14 +737,16 @@
             pltpu.VMEM((subset_count, SUBLANES, LANES), F32),
             pltpu.VMEM((SUBLANES, LANES), jnp.int32),
         ),
-        in_specs=[smem] * 3 + [vmem],
+        in_specs=[smem] * 3 + [pl.BlockSpec(memory_space=pl.ANY)],
         out_specs=(vmem,) * 9,
-        scratch_shapes=[pltpu.VMEM((SUBLANES, wide), F32)] * 2 + [pltpu.VMEM((SUBLANES, column_count // 2), F32)],
+        scratch_shapes=[pltpu.VMEM((SUBLANES, wide), F32)] * 2
+        + [pltpu.VMEM((SUBLANES, column_count // 2), F32), pltpu.VMEM((view_count, column_count), F32)]
+        + [pltpu.VMEM((1, SUBLANES, wide), F32)] * 2,
         cost_estimate=pl.CostEstimate(flops=4_000_000, bytes_accessed=8_000_000, transcendentals=0),
         compiler_params=small,
         name="divisors",
     )
-    blocks, divisors = gathered(own, near, low, high, reach, lambda: divide(view_angle, view_lift, subset, cover))
+    blocks, divisors = gathered(own, near, low, high, reach, lambda: divide(view_angle, view_lift, subset, own))
     return pl.pallas_call(
         functools.partial(update_kernel, order, kinds),
         out_shape=(

time: 15.7 us -> 15.7 us (level)
  Pallas kernels: 7.07 us -> 7.27 us
  waiting for transfers between devices: 3.58 us -> 3.42 us
    pallas_call x1, Pallas kernels: 2.05 us -> 2.28 us  [per_device(): divide(view_angle, view_lift, subset, own)]
    ppermute x3, waiting for transfers between devices: 2.66 us -> 2.49 us  [from_chip(): return lax.ppermute(block, 'slab', pairs)]
  transfers between devices with their start and end apart: 7 -> 7, of which waited for: 2 -> 2; matrix products, arithmetic and copies ran while one was open for 0% -> 0% of each run, Pallas kernels for 13% -> 15%
where the time goes in v15:
time: 15.7 us; the launch traced here: 15.5 us
  Pallas kernels  7.27 us (46%)
  starting transfers between devices  4.13 us (26%)
  waiting for transfers between devices  3.42 us (22%)
  between operations  0.7 us (4%)
    ppermute x3, starting transfers between devices, from_chip(): return lax.ppermute(block, 'slab', pairs)  3.06 us
    pallas_call x1, Pallas kernels, per_device(): pl.pallas_call(functools.partial(project_kernel, slab_count), out_shape=(...  2.95 us
    ppermute x3, waiting for transfers between devices, from_chip(): return lax.ppermute(block, 'slab', pairs)  2.49 us
    pallas_call x1, Pallas kernels, per_device(): divide(view_angle, view_lift, subset, own)  2.28 us
    pallas_call x1, Pallas kernels, per_device(): pl.pallas_call(functools.partial(update_kernel, order, kinds), out_shape=...  2.05 us
    ppermute x4, starting transfers between devices, swapped(): lax.ppermute(block, 'slab', [(i, i ^ 1) for i in range(lax.axis_size('sla...  1.07 us
    ppermute x4, waiting for transfers between devices, swapped(): lax.ppermute(block, 'slab', [(i, i ^ 1) for i in range(lax.axis_size('sla...  0.93 us
  transfers between devices with their start and end apart: 7, of which 2 were waited for; matrix products, arithmetic and copies ran while one was open for 0% of the time, Pallas kernels for 15%

profile of v15, /device:TPU:25, one launch (start us, length us, event | category | flops | bytes accessed | tf_op | source)
XLA Modules:
  0.0 15.5 jit_solution(14020887260366588770)
XLA Ops:
  0.6 0.0 copy-start.2
  0.6 0.0 copy-start.3
  0.7 0.0 copy-start.4
  0.7 0.0 copy-start
  0.7 2.9 %project.1 = (f32[7,8,512]{2,1,0:T(8,128)S(1)}, f32[6,8,512]{2,1,0:T(8,128)S(1)}, f32[5,8,512]{2,1,0:T(8,128)S(1)}, f32[6,8,512]{2,1,0:T(8,128)S(1)}) custom-call(s32[8]{0:T(128)} %angle_ref.3, s32[8]{0:T(128)} %lift_ref.3, s32[4]{0:T(128)} %subset_ref.3, f32[2,64,1024]{2,1,0:T(8,128)} %volume_ref.3, f32[3,8,1024]{2,1,0:T(8,128)} %measured_ref.3), custom_call_target="tpu_custom_call" | custom-call | tf_op jit(solution)/shard_map/project/pallas_call | solution.py:707
  3.6 0.0 copy-start.1
  3.6 0.7 %collective-permute-start = (f32[6,8,512]{2,1,0:T(8,128)S(1)}, f32[6,8,512]{2,1,0:T(8,128)S(1)}, u32[]{:S(2)}, u32[]{:S(2)}) collective-permute-start(f32[6,8,512]{2,1,0:T(8,128)S(1)} %get-tuple-element.37), channel_id=1, source_target_pairs={{4,0},{6,2},{8,4},{1,5},{10,6},{3,7},{12,8},{5,9},{14,10},{7,11},{... | collective-permute-start | bytes 294920 | tf_op jit(solution)/shard_map/ppermute | solution.py:660
  4.3 1.2 %collective-permute-start.1 = (f32[6,8,512]{2,1,0:T(8,128)S(1)}, f32[6,8,512]{2,1,0:T(8,128)S(1)}, u32[]{:S(2)}, u32[]{:S(2)}) collective-permute-start(f32[6,8,512]{2,1,0:T(8,128)S(1)} %get-tuple-element.38), channel_id=1, source_target_pairs={{2,0},{4,2},{1,3},{6,4},{3,5},{8,6},{5,7},{10,8},{7,9},{12,10},{9,... | collective-permute-start | bytes 294920 | tf_op jit(solution)/shard_map/ppermute | solution.py:660
  5.6 1.1 %collective-permute-start.2 = (f32[5,8,512]{2,1,0:T(8,128)S(1)}, f32[5,8,512]{2,1,0:T(8,128)S(1)}, u32[]{:S(2)}, u32[]{:S(2)}) collective-permute-start(f32[5,8,512]{2,1,0:T(8,128)S(1)} %get-tuple-element.39), channel_id=1, source_target_pairs={{3,1},{0,2},{5,3},{2,4},{7,5},{4,6},{9,7},{6,8},{11,9},{8,10},{13,... | collective-permute-start | bytes 245768 | tf_op jit(solution)/shard_map/ppermute | solution.py:660
  6.7 0.0 copy-done.2
  6.7 0.0 copy-done.3
  6.7 0.0 copy-done.4
  6.7 2.3 %divisors.1 = (f32[2,64,1024]{2,1,0:T(8,128)S(1)}, f32[3,8,1024]{2,1,0:T(8,128)S(1)}, f32[21,8,512]{2,1,0:T(8,128)S(1)}, f32[14,3,8,128]{3,2,1,0:T(8,128)S(1)}, ...) custom-call(s32[8]{0:T(128)S(1)} %copy-done.2, ...), custom_call_target="tpu_custom_call" | custom-call | flops 4000000 | bytes 8000000 | tf_op jit(solution)/shard_map/divisors/pallas_call | solution.py:749
  9.0 0.2 %collective-permute-start.3 = (f32[7,8,512]{2,1,0:T(8,128)S(1)}, f32[7,8,512]{2,1,0:T(8,128)S(1)}, u32[]{:S(2)}, u32[]{:S(2)}) collective-permute-start(f32[7,8,512]{2,1,0:T(8,128)S(1)} %get-tuple-element.68._.refs_0_), channel_id=1, source_target_pairs={{0,1},{1,0},{2,3},{3,2},{4,5},{5,4},{6,7},{7,6},{8,9},{9,8},{10,11... | collective-permute-start | bytes 344072 | tf_op jit(solution)/shard_map/ppermute | solution.py:648
  9.2 2.5 %collective-permute-done.2.refs_5_ = f32[5,8,512]{2,1,0:T(8,128)S(1)} collective-permute-done((f32[5,8,512]{2,1,0:T(8,128)S(1)}, f32[5,8,512]{2,1,0:T(8,128)S(1)}, u32[]{:S(2)}, u32[]{:S(2)}) %collective-permute-start.2) | collective-permute-done | bytes 81952 | tf_op jit(solution)/shard_map/ppermute | solution.py:660
  11.7 0.0 collective-permute-done
  11.7 0.0 collective-permute-done.1.refs_3_
  11.7 0.4 %collective-permute-start.4 = (f32[6,8,512]{2,1,0:T(8,128)S(1)}, f32[6,8,512]{2,1,0:T(8,128)S(1)}, u32[]{:S(2)}, u32[]{:S(2)}) collective-permute-start(f32[6,8,512]{2,1,0:T(8,128)S(1)} %collective-permute-done), channel_id=1, source_target_pairs={{0,1},{1,0},{2,3},{3,2},{4,5},{5,4},{6,7},{7,6},{8,9},{9,8},{10,11... | collective-permute-start | bytes 294920 | tf_op jit(solution)/shard_map/ppermute | solution.py:648
  12.0 0.1 collective-permute-start.5
  12.2 0.4 %collective-permute-start.6 = (f32[5,8,512]{2,1,0:T(8,128)S(1)}, f32[5,8,512]{2,1,0:T(8,128)S(1)}, u32[]{:S(2)}, u32[]{:S(2)}) collective-permute-start(f32[5,8,512]{2,1,0:T(8,128)S(1)} %collective-permute-done.2.refs_5_), channel_id=1, source_target_pairs={{0,1},{1,0},{2,3},{3,2},{4,5},{5,4},{6,7},{7,6},{8,9},{9,8},{10,11... | collective-permute-start | bytes 245768 | tf_op jit(solution)/shard_map/ppermute | solution.py:648
  12.6 0.0 collective-permute-done.3.refs_1_
  12.6 0.9 %collective-permute-done.6.refs_6_ = f32[5,8,512]{2,1,0:T(8,128)S(1)} collective-permute-done((f32[5,8,512]{2,1,0:T(8,128)S(1)}, f32[5,8,512]{2,1,0:T(8,128)S(1)}, u32[]{:S(2)}, u32[]{:S(2)}) %collective-permute-start.6) | collective-permute-done | bytes 81952 | tf_op jit(solution)/shard_map/ppermute | solution.py:648
  13.5 0.0 collective-permute-done.4.refs_2_
  13.5 0.0 collective-permute-done.5.refs_4_
  13.5 0.0 copy-done
  13.5 0.0 copy-done.1
  13.5 2.0 %update.1 = (f32[3,8,1024]{2,1,0:T(8,128)}, f32[2,64,1024]{2,1,0:T(8,128)}) custom-call(f32[2,64,1024]{2,1,0:T(8,128)S(1)} %copy-done, f32[3,8,1024]{2,1,0:T(8,128)S(1)} %copy-done.1, f32[2,64,1024]{2,1,0:T(8,128)S(1)} %get-tuple-element.59.bound_ref, f32[3,8,1024]{2,1,0:T(8,128)S(1)} %get-tuple-element.60.own_ref, ...), custom_call_target="tpu_custom_call" | custom-call | tf_op jit(solution)/shard_map/update/pallas_call | solution.py:750
Async XLA Ops:
  0.6 6.1 %copy-start.2 = (s32[8]{0:T(128)S(1)}, s32[8]{0:T(128)}, u32[]{:S(2)}) copy-start(s32[8]{0:T(128)} %angle_ref.3) | copy-start | bytes 100
  0.6 6.1 %copy-start.3 = (s32[8]{0:T(128)S(1)}, s32[8]{0:T(128)}, u32[]{:S(2)}) copy-start(s32[8]{0:T(128)} %lift_ref.3) | copy-start | bytes 100
  0.7 6.1 %copy-start.4 = (s32[4]{0:T(128)S(1)}, s32[4]{0:T(128)}, u32[]{:S(2)}) copy-start(s32[4]{0:T(128)} %subset_ref.3) | copy-start | bytes 52
  0.7 12.8 %copy-start = (f32[2,64,1024]{2,1,0:T(8,128)S(1)}, f32[2,64,1024]{2,1,0:T(8,128)}, u32[]{:S(2)}) copy-start(f32[2,64,1024]{2,1,0:T(8,128)} %volume_ref.3) | copy-start | bytes 1572868
  3.6 9.9 %copy-start.1 = (f32[3,8,1024]{2,1,0:T(8,128)S(1)}, f32[3,8,1024]{2,1,0:T(8,128)}, u32[]{:S(2)}) copy-start(f32[3,8,1024]{2,1,0:T(8,128)} %measured_ref.3) | copy-start | bytes 294916
  3.6 8.0 %collective-permute-start = (f32[6,8,512]{2,1,0:T(8,128)S(1)}, f32[6,8,512]{2,1,0:T(8,128)S(1)}, u32[]{:S(2)}, u32[]{:S(2)}) collective-permute-start(f32[6,8,512]{2,1,0:T(8,128)S(1)} %get-tuple-element.37), channel_id=1, source_target_pairs={{4,0},{6,2},{8,4},{1,5},{10,6},{3,7},{12,8},{5,9},{14,10},{7,11},{... | collective-permute-start | bytes 294920 | tf_op jit(solution)/shard_map/ppermute | solution.py:660
  4.3 7.3 %collective-permute-start.1 = (f32[6,8,512]{2,1,0:T(8,128)S(1)}, f32[6,8,512]{2,1,0:T(8,128)S(1)}, u32[]{:S(2)}, u32[]{:S(2)}) collective-permute-start(f32[6,8,512]{2,1,0:T(8,128)S(1)} %get-tuple-element.38), channel_id=1, source_target_pairs={{2,0},{4,2},{1,3},{6,4},{3,5},{8,6},{5,7},{10,8},{7,9},{12,10},{9,... | collective-permute-start | bytes 294920 | tf_op jit(solution)/shard_map/ppermute | solution.py:660
  5.6 6.1 %collective-permute-start.2 = (f32[5,8,512]{2,1,0:T(8,128)S(1)}, f32[5,8,512]{2,1,0:T(8,128)S(1)}, u32[]{:S(2)}, u32[]{:S(2)}) collective-permute-start(f32[5,8,512]{2,1,0:T(8,128)S(1)} %get-tuple-element.39), channel_id=1, source_target_pairs={{3,1},{0,2},{5,3},{2,4},{7,5},{4,6},{9,7},{6,8},{11,9},{8,10},{13,... | collective-permute-start | bytes 245768 | tf_op jit(solution)/shard_map/ppermute | solution.py:660
  9.0 3.6 %collective-permute-start.3 = (f32[7,8,512]{2,1,0:T(8,128)S(1)}, f32[7,8,512]{2,1,0:T(8,128)S(1)}, u32[]{:S(2)}, u32[]{:S(2)}) collective-permute-start(f32[7,8,512]{2,1,0:T(8,128)S(1)} %get-tuple-element.68._.refs_0_), channel_id=1, source_target_pairs={{0,1},{1,0},{2,3},{3,2},{4,5},{5,4},{6,7},{7,6},{8,9},{9,8},{10,11... | collective-permute-start | bytes 344072 | tf_op jit(solution)/shard_map/ppermute | solution.py:648
  11.7 1.8 %collective-permute-start.4 = (f32[6,8,512]{2,1,0:T(8,128)S(1)}, f32[6,8,512]{2,1,0:T(8,128)S(1)}, u32[]{:S(2)}, u32[]{:S(2)}) collective-permute-start(f32[6,8,512]{2,1,0:T(8,128)S(1)} %collective-permute-done), channel_id=1, source_target_pairs={{0,1},{1,0},{2,3},{3,2},{4,5},{5,4},{6,7},{7,6},{8,9},{9,8},{10,11... | collective-permute-start | bytes 294920 | tf_op jit(solution)/shard_map/ppermute | solution.py:648
  12.0 1.4 %collective-permute-start.5 = (f32[6,8,512]{2,1,0:T(8,128)S(1)}, f32[6,8,512]{2,1,0:T(8,128)S(1)}, u32[]{:S(2)}, u32[]{:S(2)}) collective-permute-start(f32[6,8,512]{2,1,0:T(8,128)S(1)} %collective-permute-done.1.refs_3_), channel_id=1, source_target_pairs={{0,1},{1,0},{2,3},{3,2},{4,5},{5,4},{6,7},{7,6},{8,9},{9,8},{10,11... | collective-permute-start | bytes 294920 | tf_op jit(solution)/shard_map/ppermute | solution.py:648
  12.2 1.3 %collective-permute-start.6 = (f32[5,8,512]{2,1,0:T(8,128)S(1)}, f32[5,8,512]{2,1,0:T(8,128)S(1)}, u32[]{:S(2)}, u32[]{:S(2)}) collective-permute-start(f32[5,8,512]{2,1,0:T(8,128)S(1)} %collective-permute-done.2.refs_5_), channel_id=1, source_target_pairs={{0,1},{1,0},{2,3},{3,2},{4,5},{5,4},{6,7},{7,6},{8,9},{9,8},{10,11... | collective-permute-start | bytes 245768 | tf_op jit(solution)/shard_map/ppermute | solution.py:648

commit v16 on v14

--- a/solution.py
+++ b/solution.py
@@ -660,7 +660,7 @@
     done = meanwhile()
     own, done = lax.optimization_barrier((own, done))
     blocks = {0: own, 1: swapped(own)}
-    arrived, done = lax.optimization_barrier((list(received.values()), done))
+    arrived = list(received.values())
     for distance, block in zip(received, arrived):
         if 2 * abs(distance) <= reach:
             blocks[2 * distance] = block

time: 15.7 us -> 15.5 us (0.987)
  waiting for transfers between devices: 3.58 us -> 1.29 us
  starting transfers between devices: 4.18 us -> 6.33 us
    ppermute x3, waiting for transfers between devices: 2.66 us -> 0.01 us  [from_chip(): return lax.ppermute(block, 'slab', pairs)]
    ppermute x4, starting transfers between devices: 1.12 us -> 3.27 us  [swapped(): lax.ppermute(block, 'slab', [(i, i ^ 1) for i in range(lax.axis_size('sla...]
    ppermute x4, waiting for transfers between devices: 0.93 us -> 1.28 us  [swapped(): lax.ppermute(block, 'slab', [(i, i ^ 1) for i in range(lax.axis_size('sla...]
  transfers between devices with their start and end apart: 7 -> 7, of which waited for: 2 -> 1; matrix products, arithmetic and copies ran while one was open for 0% -> 0% of each run, Pallas kernels for 13% -> 13%
where the time goes in v16:
time: 15.5 us; the launch traced here: 15.4 us
  Pallas kernels  7.07 us (46%)
  starting transfers between devices  6.33 us (41%)
  waiting for transfers between devices  1.29 us (8%)
  between operations  0.68 us (4%)
    ppermute x4, starting transfers between devices, swapped(): lax.ppermute(block, 'slab', [(i, i ^ 1) for i in range(lax.axis_size('sla...  3.27 us
    ppermute x3, starting transfers between devices, from_chip(): return lax.ppermute(block, 'slab', pairs)  3.06 us
    pallas_call x1, Pallas kernels, per_device(): pl.pallas_call(functools.partial(project_kernel, slab_count), out_shape=(...  2.98 us
    pallas_call x1, Pallas kernels, per_device(): divide(view_angle, view_lift, subset, cover)  2.05 us
    pallas_call x1, Pallas kernels, per_device(): pl.pallas_call(functools.partial(update_kernel, order, kinds), out_shape=...  2.04 us
    ppermute x4, waiting for transfers between devices, swapped(): lax.ppermute(block, 'slab', [(i, i ^ 1) for i in range(lax.axis_size('sla...  1.28 us
  transfers between devices with their start and end apart: 7, of which 1 were waited for; matrix products, arithmetic and copies ran while one was open for 0% of the time, Pallas kernels for 13%

profile of v16, /device:TPU:25, one launch (start us, length us, event | category | flops | bytes accessed | tf_op | source)
XLA Modules:
  0.0 15.4 jit_solution(6137817237440380192)
XLA Ops:
  0.6 0.0 copy-start
  0.6 0.0 copy-start.1
  0.6 3.0 %project.1 = (f32[7,8,512]{2,1,0:T(8,128)S(1)}, f32[6,8,512]{2,1,0:T(8,128)S(1)}, f32[5,8,512]{2,1,0:T(8,128)S(1)}, f32[6,8,512]{2,1,0:T(8,128)S(1)}, f32[8,1024]{1,0:T(8,128)S(1)}) custom-call(s32[8]{0:T(128)} %angle_ref.3, s32[8]{0:T(128)} %lift_ref.3, s32[4]{0:T(128)} %subset_ref.3, f32[2,64,1024]{2,1,0:T(8,128)} %volume_ref.3, f32[3,8,1024]{2,1,0:T(8,128)} %measured_ref.3), custom_call_target="tpu_custom_call" | custom-call | tf_op jit(solution)/shard_map/project/pallas_call | solution.py:685
  3.6 0.7 %collective-permute-start.1 = (f32[6,8,512]{2,1,0:T(8,128)S(1)}, f32[6,8,512]{2,1,0:T(8,128)S(1)}, u32[]{:S(2)}, u32[]{:S(2)}) collective-permute-start(f32[6,8,512]{2,1,0:T(8,128)S(1)} %get-tuple-element.47), channel_id=1, source_target_pairs={{4,0},{6,2},{8,4},{1,5},{10,6},{3,7},{12,8},{5,9},{14,10},{7,11},{... | collective-permute-start | bytes 294920 | tf_op jit(solution)/shard_map/ppermute | solution.py:638
  4.3 1.2 %collective-permute-start.3 = (f32[6,8,512]{2,1,0:T(8,128)S(1)}, f32[6,8,512]{2,1,0:T(8,128)S(1)}, u32[]{:S(2)}, u32[]{:S(2)}) collective-permute-start(f32[6,8,512]{2,1,0:T(8,128)S(1)} %get-tuple-element.48), channel_id=1, source_target_pairs={{2,0},{4,2},{1,3},{6,4},{3,5},{8,6},{5,7},{10,8},{7,9},{12,10},{9,... | collective-permute-start | bytes 294920 | tf_op jit(solution)/shard_map/ppermute | solution.py:638
  5.6 0.0 copy-start.2
  5.6 0.0 copy-start.3
  5.6 0.0 copy-start.4
  5.6 1.1 %collective-permute-start.5 = (f32[5,8,512]{2,1,0:T(8,128)S(1)}, f32[5,8,512]{2,1,0:T(8,128)S(1)}, u32[]{:S(2)}, u32[]{:S(2)}) collective-permute-start(f32[5,8,512]{2,1,0:T(8,128)S(1)} %get-tuple-element.49), channel_id=1, source_target_pairs={{3,1},{0,2},{5,3},{2,4},{7,5},{4,6},{9,7},{6,8},{11,9},{8,10},{13,... | collective-permute-start | bytes 245768 | tf_op jit(solution)/shard_map/ppermute | solution.py:638
  6.7 0.0 copy-done.2
  6.7 0.0 copy-done.3
  6.7 0.0 copy-done.4
  6.7 2.0 %divisors.1 = (f32[2,64,1024]{2,1,0:T(8,128)S(1)}, f32[3,8,1024]{2,1,0:T(8,128)S(1)}, f32[21,8,512]{2,1,0:T(8,128)S(1)}, f32[14,3,8,128]{3,2,1,0:T(8,128)S(1)}, ...) custom-call(s32[8]{0:T(128)S(1)} %copy-done.2, ...), custom_call_target="tpu_custom_call" | custom-call | flops 4000000 | bytes 8000000 | tf_op jit(solution)/shard_map/divisors/pallas_call | solution.py:728
  8.8 0.2 %collective-permute-start = (f32[7,8,512]{2,1,0:T(8,128)S(1)}, f32[7,8,512]{2,1,0:T(8,128)S(1)}, u32[]{:S(2)}, u32[]{:S(2)}) collective-permute-start(f32[7,8,512]{2,1,0:T(8,128)S(1)} %get-tuple-element.46.refs_0_), channel_id=1, source_target_pairs={{0,1},{1,0},{2,3},{3,2},{4,5},{5,4},{6,7},{7,6},{8,9},{9,8},{10,11... | collective-permute-start | bytes 344072 | tf_op jit(solution)/shard_map/ppermute | solution.py:626
  9.0 0.0 collective-permute-done.1
  9.0 0.3 %collective-permute-start.2 = (f32[6,8,512]{2,1,0:T(8,128)S(1)}, f32[6,8,512]{2,1,0:T(8,128)S(1)}, u32[]{:S(2)}, u32[]{:S(2)}) collective-permute-start(f32[6,8,512]{2,1,0:T(8,128)S(1)} %collective-permute-done.1), channel_id=1, source_target_pairs={{0,1},{1,0},{2,3},{3,2},{4,5},{5,4},{6,7},{7,6},{8,9},{9,8},{10,11... | collective-permute-start | bytes 294920 | tf_op jit(solution)/shard_map/ppermute | solution.py:626
  9.3 0.0 collective-permute-done.3.refs_3_
  9.3 2.7 %collective-permute-start.4 = (f32[6,8,512]{2,1,0:T(8,128)S(1)}, f32[6,8,512]{2,1,0:T(8,128)S(1)}, u32[]{:S(2)}, u32[]{:S(2)}) collective-permute-start(f32[6,8,512]{2,1,0:T(8,128)S(1)} %collective-permute-done.3.refs_3_), channel_id=1, source_target_pairs={{0,1},{1,0},{2,3},{3,2},{4,5},{5,4},{6,7},{7,6},{8,9},{9,8},{10,11... | collective-permute-start | bytes 294920 | tf_op jit(solution)/shard_map/ppermute | solution.py:626
  12.0 0.0 collective-permute-done.5.refs_5_
  12.0 0.0 collective-permute-start.6
  12.0 0.0 collective-permute-done.refs_1_
  12.1 1.3 %collective-permute-done.6.refs_6_ = f32[5,8,512]{2,1,0:T(8,128)S(1)} collective-permute-done((f32[5,8,512]{2,1,0:T(8,128)S(1)}, f32[5,8,512]{2,1,0:T(8,128)S(1)}, u32[]{:S(2)}, u32[]{:S(2)}) %collective-permute-start.6) | collective-permute-done | bytes 81952 | tf_op jit(solution)/shard_map/ppermute | solution.py:626
  13.3 0.0 collective-permute-done.2.refs_2_
  13.3 0.0 collective-permute-done.4.refs_4_
  13.3 0.0 copy-done
  13.3 0.0 copy-done.1
  13.3 2.0 %update.1 = (f32[3,8,1024]{2,1,0:T(8,128)}, f32[2,64,1024]{2,1,0:T(8,128)}) custom-call(f32[2,64,1024]{2,1,0:T(8,128)S(1)} %copy-done, f32[3,8,1024]{2,1,0:T(8,128)S(1)} %copy-done.1, f32[2,64,1024]{2,1,0:T(8,128)S(1)} %get-tuple-element.37.bound_ref, f32[3,8,1024]{2,1,0:T(8,128)S(1)} %get-tuple-element.38.own_ref, ...), custom_call_target="tpu_custom_call" | custom-call | tf_op jit(solution)/shard_map/update/pallas_call | solution.py:729
Async XLA Ops:
  0.6 12.7 %copy-start = (f32[2,64,1024]{2,1,0:T(8,128)S(1)}, f32[2,64,1024]{2,1,0:T(8,128)}, u32[]{:S(2)}) copy-start(f32[2,64,1024]{2,1,0:T(8,128)} %volume_ref.3) | copy-start | bytes 1572868
  0.6 12.7 %copy-start.1 = (f32[3,8,1024]{2,1,0:T(8,128)S(1)}, f32[3,8,1024]{2,1,0:T(8,128)}, u32[]{:S(2)}) copy-start(f32[3,8,1024]{2,1,0:T(8,128)} %measured_ref.3) | copy-start | bytes 294916
  3.6 5.4 %collective-permute-start.1 = (f32[6,8,512]{2,1,0:T(8,128)S(1)}, f32[6,8,512]{2,1,0:T(8,128)S(1)}, u32[]{:S(2)}, u32[]{:S(2)}) collective-permute-start(f32[6,8,512]{2,1,0:T(8,128)S(1)} %get-tuple-element.47), channel_id=1, source_target_pairs={{4,0},{6,2},{8,4},{1,5},{10,6},{3,7},{12,8},{5,9},{14,10},{7,11},{... | collective-permute-start | bytes 294920 | tf_op jit(solution)/shard_map/ppermute | solution.py:638
  4.3 5.0 %collective-permute-start.3 = (f32[6,8,512]{2,1,0:T(8,128)S(1)}, f32[6,8,512]{2,1,0:T(8,128)S(1)}, u32[]{:S(2)}, u32[]{:S(2)}) collective-permute-start(f32[6,8,512]{2,1,0:T(8,128)S(1)} %get-tuple-element.48), channel_id=1, source_target_pairs={{2,0},{4,2},{1,3},{6,4},{3,5},{8,6},{5,7},{10,8},{7,9},{12,10},{9,... | collective-permute-start | bytes 294920 | tf_op jit(solution)/shard_map/ppermute | solution.py:638
  5.6 1.1 %copy-start.2 = (s32[8]{0:T(128)S(1)}, s32[8]{0:T(128)}, u32[]{:S(2)}) copy-start(s32[8]{0:T(128)} %angle_ref.3) | copy-start | bytes 100
  5.6 1.1 %copy-start.3 = (s32[8]{0:T(128)S(1)}, s32[8]{0:T(128)}, u32[]{:S(2)}) copy-start(s32[8]{0:T(128)} %lift_ref.3) | copy-start | bytes 100
  5.6 1.1 %copy-start.4 = (s32[4]{0:T(128)S(1)}, s32[4]{0:T(128)}, u32[]{:S(2)}) copy-start(s32[4]{0:T(128)} %subset_ref.3) | copy-start | bytes 52
  5.6 6.5 %collective-permute-start.5 = (f32[5,8,512]{2,1,0:T(8,128)S(1)}, f32[5,8,512]{2,1,0:T(8,128)S(1)}, u32[]{:S(2)}, u32[]{:S(2)}) collective-permute-start(f32[5,8,512]{2,1,0:T(8,128)S(1)} %get-tuple-element.49), channel_id=1, source_target_pairs={{3,1},{0,2},{5,3},{2,4},{7,5},{4,6},{9,7},{6,8},{11,9},{8,10},{13,... | collective-permute-start | bytes 245768 | tf_op jit(solution)/shard_map/ppermute | solution.py:638
  8.8 3.3 %collective-permute-start = (f32[7,8,512]{2,1,0:T(8,128)S(1)}, f32[7,8,512]{2,1,0:T(8,128)S(1)}, u32[]{:S(2)}, u32[]{:S(2)}) collective-permute-start(f32[7,8,512]{2,1,0:T(8,128)S(1)} %get-tuple-element.46.refs_0_), channel_id=1, source_target_pairs={{0,1},{1,0},{2,3},{3,2},{4,5},{5,4},{6,7},{7,6},{8,9},{9,8},{10,11... | collective-permute-start | bytes 344072 | tf_op jit(solution)/shard_map/ppermute | solution.py:626
  9.0 4.3 %collective-permute-start.2 = (f32[6,8,512]{2,1,0:T(8,128)S(1)}, f32[6,8,512]{2,1,0:T(8,128)S(1)}, u32[]{:S(2)}, u32[]{:S(2)}) collective-permute-start(f32[6,8,512]{2,1,0:T(8,128)S(1)} %collective-permute-done.1), channel_id=1, source_target_pairs={{0,1},{1,0},{2,3},{3,2},{4,5},{5,4},{6,7},{7,6},{8,9},{9,8},{10,11... | collective-permute-start | bytes 294920 | tf_op jit(solution)/shard_map/ppermute | solution.py:626
  9.3 4.0 %collective-permute-start.4 = (f32[6,8,512]{2,1,0:T(8,128)S(1)}, f32[6,8,512]{2,1,0:T(8,128)S(1)}, u32[]{:S(2)}, u32[]{:S(2)}) collective-permute-start(f32[6,8,512]{2,1,0:T(8,128)S(1)} %collective-permute-done.3.refs_3_), channel_id=1, source_target_pairs={{0,1},{1,0},{2,3},{3,2},{4,5},{5,4},{6,7},{7,6},{8,9},{9,8},{10,11... | collective-permute-start | bytes 294920 | tf_op jit(solution)/shard_map/ppermute | solution.py:626
  12.0 1.3 %collective-permute-start.6 = (f32[5,8,512]{2,1,0:T(8,128)S(1)}, f32[5,8,512]{2,1,0:T(8,128)S(1)}, u32[]{:S(2)}, u32[]{:S(2)}) collective-permute-start(f32[5,8,512]{2,1,0:T(8,128)S(1)} %collective-permute-done.5.refs_5_), channel_id=1, source_target_pairs={{0,1},{1,0},{2,3},{3,2},{4,5},{5,4},{6,7},{7,6},{8,9},{9,8},{10,11... | collective-permute-start | bytes 245768 | tf_op jit(solution)/shard_map/ppermute | solution.py:626
